TPU v7x, 32 devices: a whole 2x2x4 slice. The times are simulated.
32 devices in a mesh: lat: 8 (over z, core), lon: 4 (over y, x).
Axes of the slice: x: 2, y: 2, z: 4, core: 2. Of those that a mesh axis runs over, the one named last changes fastest.
Arguments:
- winds: float32 [2, 72, 11520], P(None, 'lat', 'lon'), as said below
- thickness: float32 [72, 11520], P('lat', 'lon'), may hold values from 0.5 to 1.5
- tracers: bfloat16 [3, 72, 11520], P(None, 'lat', 'lon'), may hold values from 0 to 1
- cutoff: int32 [72], replicated, may hold values from 1 to 360, as said below
Outputs:
- new_winds: float32 [2, 72, 11520], P(None, 'lat', 'lon')
- new_thickness: float32 [72, 11520], P('lat', 'lon')
- tracer_mass: bfloat16 [3, 72, 11520], P(None, 'lat', 'lon')
Inputs may be any that keep to these rules, and one draw needn't show every extreme that they name: `cutoff`: the 12 rows nearest each pole have cutoffs that grow from 1 at the pole row to at most a quarter of 720; every other row has exactly 360, so that the filter leaves it unchanged. `winds`: each wind is the cosine of its row's latitude times a value of order one.
All inputs are finite; a program needn't handle non-finite values.
Results may differ from a plain program's by a relative error of at most 0.001.
Values sent between devices are 32-bit elements; how exact they have to be, the bound alone decides.
No kernel may reach another device: no remote copies, remote signals or barrier semaphores. Data moves between devices by JAX's collectives and lax.ppermute only.
A program may use at most 64 MiB of HBM per device.

v0:
```python
import math

import jax
import jax.numpy as jnp
from jax import lax
from jax.sharding import PartitionSpec as P

LEVELS = 16


TIME_STEP = 0.05
DIFFUSION = 0.5
wave_block = 128


def extended(value, sides, width, wrap):
    for axis, dim in sides:
        size, length = (lax.axis_size(axis), value.shape[dim])
        up = [(i, (i + 1) % size) for i in range(size if wrap else size - 1)]
        down = [(j, i) for i, j in up]
        last = lax.slice_in_dim(value, length - width, length, axis=dim)
        first = lax.slice_in_dim(value, 0, width, axis=dim)
        before = lax.ppermute(last, axis, up)
        after = lax.ppermute(first, axis, down)
        value = jnp.concatenate([before, value, after], axis=dim)
    return value


def shifted(block, axis, distance):
    devices = range(lax.axis_size(axis))
    route = [((i - distance) % len(devices), i) for i in devices]
    return lax.ppermute(block, axis, route)


def grid_rows(first_row, count, nlat):
    index = first_row + jnp.arange(count, dtype=jnp.int32)
    centre = (index.astype(jnp.float32) + 0.5) * (math.pi / nlat) - math.pi / 2

    def face(row_index):
        inside = (row_index >= 0) & (row_index < nlat - 1)
        return jnp.where(
            inside, jnp.sin((row_index + 1).astype(jnp.float32) * (math.pi / nlat)), 0.0
        )

    return (
        jnp.cos(centre)[:, None, None],
        jnp.sin(centre)[:, None, None],
        face(index)[:, None, None],
        face(index - 1)[:, None, None],
    )


def tendencies(
    thick,
    wind_u,
    wind_v,
    tracer,
    thick_e,
    thick_w,
    wind_ue,
    wind_uw,
    tracer_e,
    tracer_w,
    thick_n,
    thick_s,
    wind_vn,
    wind_vs,
    tracer_n,
    tracer_s,
    cos_centre,
    sin_centre,
    cos_north,
    cos_south,
    ratio,
):
    flux_east = 0.5 * (wind_u + wind_ue) * (0.5 * (thick + thick_e))
    flux_west = 0.5 * (wind_uw + wind_u) * (0.5 * (thick_w + thick))
    flux_north = 0.5 * (wind_v + wind_vn) * (0.5 * (thick + thick_n)) * cos_north
    flux_south = 0.5 * (wind_vs + wind_v) * (0.5 * (thick_s + thick)) * cos_south
    thick_tend = -(flux_east - flux_west + ratio * (flux_north - flux_south)) / cos_centre
    wind_u_tend = sin_centre * wind_v - (thick_e - thick_w) / (2.0 * cos_centre)
    wind_v_tend = -sin_centre * wind_u - ratio * (thick_n - thick_s) * 0.5
    zonal_part = flux_east * (0.5 * (tracer + tracer_e)) - flux_west * (0.5 * (tracer_w + tracer))
    merid_part = flux_north * (0.5 * (tracer + tracer_n)) - flux_south * (0.5 * (tracer_s + tracer))
    tracer_flux = (zonal_part + ratio * merid_part) / cos_centre
    laplace = tracer_e + tracer_w + (tracer_n + tracer_s) - 4.0 * tracer
    tracer_mass = thick * tracer + TIME_STEP * (DIFFUSION * laplace - tracer_flux)
    return (thick_tend, wind_u_tend, wind_v_tend, tracer_mass)


def band_filter(block, cuts):
    nlon = block.shape[-1]
    half = nlon // 2
    flat = block.reshape(-1, nlon)
    row_cut = jnp.broadcast_to(cuts, block.shape[:-1]).reshape(-1)
    active = row_cut < half
    highest = jnp.max(jnp.where(active, row_cut, -1))
    passes = (highest + wave_block) // wave_block
    column = jnp.arange(nlon, dtype=jnp.int32)

    def one_block(block_index, total):
        wave = block_index * wave_block + jnp.arange(wave_block, dtype=jnp.int32)
        phase = column[:, None] * wave[None, :] % nlon
        angle = phase.astype(jnp.float32) * (2.0 * math.pi / nlon)
        cosine = jnp.cos(angle)
        sine = jnp.sin(angle)
        weight = jnp.where((wave == 0) | (wave == half), 1.0, 2.0) / nlon
        keep = wave[None, :] <= row_cut[:, None]
        real_part = jnp.dot(
            flat, cosine, precision=lax.Precision.HIGHEST, preferred_element_type=jnp.float32
        )
        imag_part = jnp.dot(
            flat, sine, precision=lax.Precision.HIGHEST, preferred_element_type=jnp.float32
        )
        real_part = jnp.where(keep, real_part * weight, 0.0)
        imag_part = jnp.where(keep, imag_part * weight, 0.0)
        contract = (((1,), (1,)), ((), ()))
        back = lax.dot_general(
            real_part,
            cosine,
            contract,
            precision=lax.Precision.HIGHEST,
            preferred_element_type=jnp.float32,
        )
        back = back + lax.dot_general(
            imag_part,
            sine,
            contract,
            precision=lax.Precision.HIGHEST,
            preferred_element_type=jnp.float32,
        )
        return total + back

    summed = lax.fori_loop(0, passes, one_block, jnp.zeros_like(flat))
    return jnp.where(active[:, None], summed, flat).reshape(block.shape)


def regroup_filter(stacked, cuts):
    turned = jnp.swapaxes(
        lax.all_to_all(stacked, "lon", split_axis=3, concat_axis=2, tiled=True), 2, 3
    )
    worked = jnp.swapaxes(band_filter(turned, cuts[:, None]), 2, 3)
    return lax.all_to_all(worked, "lon", split_axis=2, concat_axis=3, tiled=True)


def local(winds, thickness, tracers, cutoff):
    n_lat = lax.axis_size("lat")
    n_lon = lax.axis_size("lon")
    lat_index = lax.axis_index("lat")
    rows, merged = thickness.shape
    columns = merged // LEVELS
    nlat = rows * n_lat
    nlon = columns * n_lon
    ratio = 2.0 * nlat / nlon
    tracer_wide = tracers.astype(jnp.float32)
    thick = thickness.reshape(rows, columns, LEVELS)
    wind_u = winds[0].reshape(rows, columns, LEVELS)
    wind_v = winds[1].reshape(rows, columns, LEVELS)
    tracer_cells = tracer_wide.reshape(3, rows, columns, LEVELS)
    cos_centre, sin_centre, cos_north, cos_south = grid_rows(lat_index * rows, rows, nlat)
    along_lon = jnp.concatenate([thickness[None], winds[0][None], tracer_wide], axis=0)
    lon_ext = extended(along_lon, (("lon", 2),), LEVELS, True)
    lon_ext = lon_ext.reshape(5, rows, columns + 2, LEVELS)
    along_lat = jnp.concatenate([thickness[None], winds[1][None], tracer_wide], axis=0)
    edge_row = jnp.where(lat_index == n_lat - 1, along_lat[:, -1], along_lat[:, 0])
    across = shifted(edge_row, "lon", n_lon // 2)
    flip = jnp.array([1.0, -1.0, 1.0, 1.0, 1.0], jnp.float32)[:, None, None]
    across = across.reshape(5, columns, LEVELS) * flip
    lat_ext = extended(along_lat, (("lat", 1),), 1, False)
    lat_ext = lat_ext.reshape(5, rows + 2, columns, LEVELS)
    south_row = jnp.where(lat_index == 0, across, lat_ext[:, 0])
    north_row = jnp.where(lat_index == n_lat - 1, across, lat_ext[:, -1])
    east = lon_ext[:, :, 2:]
    west = lon_ext[:, :, :-2]
    north = jnp.concatenate([lat_ext[:, 2:-1], north_row[:, None]], axis=1)
    south = jnp.concatenate([south_row[:, None], lat_ext[:, 1:-2]], axis=1)
    thick_tend, wind_u_tend, wind_v_tend, tracer_mass = tendencies(
        thick,
        wind_u,
        wind_v,
        tracer_cells,
        east[0],
        west[0],
        east[1],
        west[1],
        east[2:],
        west[2:],
        north[0],
        south[0],
        north[1],
        south[1],
        north[2:],
        south[2:],
        cos_centre,
        sin_centre,
        cos_north,
        cos_south,
        ratio,
    )
    tendency = jnp.stack([thick_tend, wind_u_tend, wind_v_tend])
    row_cuts = lax.dynamic_slice_in_dim(cutoff, lat_index * rows, rows)
    filtered = regroup_filter(tendency, row_cuts)
    filtered = filtered.reshape(3, rows, merged)
    new_thickness = thickness + TIME_STEP * filtered[0]
    new_winds = jnp.stack([winds[0] + TIME_STEP * filtered[1], winds[1] + TIME_STEP * filtered[2]])
    return (new_winds, new_thickness, tracer_mass.reshape(3, rows, merged).astype(jnp.bfloat16))


def solution(mesh):
    in_specs = (P(None, "lat", "lon"), P("lat", "lon"), P(None, "lat", "lon"), P())
    out_specs = (P(None, "lat", "lon"), P("lat", "lon"), P(None, "lat", "lon"))
    return jax.shard_map(local, mesh=mesh, in_specs=in_specs, out_specs=out_specs, check_vma=False)
```

profile of v0, /device:TPU:26, one launch (start us, length us, event | category | flops | bytes accessed | tf_op | source)
XLA Modules:
  0.0 193.9 jit_solution(16320622703025467537)
XLA Ops:
  7.3 3.6 %collective-permute-start.3 = (f32[5,1,2880]{2,0,1:T(8,128)}, f32[5,1,2880]{2,0,1:T(8,128)}, u32[]{:S(2)}, u32[]{:S(2)}) collective-permute-start(f32[5,1,2880]{2,0,1:T(8,128)} %get-tuple-element.154), channel_id=1, source_target_pairs={{4,0},{8,4},{12,8},{16,12},{20,16},{24,20},{28,24},{5,1},{9,5},{13... | collective-permute-start | bytes 172808 | tf_op jit(solution)/shard_map/ppermute | solution.py:24
  21.1 3.0 %reshape.194 = f32[3,9,180,16]{3,2,0,1:T(8,128)} reshape(bf16[3,9,2880]{2,0,1:T(4,128)(2,1)} %param.9) | data formatting | bytes 466560 | tf_op jit(solution)/shard_map/reshape | solution.py:159
  31.3 3.5 %copy.254 = f32[3,9,180,16]{2,3,1,0:T(8,128)} copy(f32[3,9,180,16]{3,2,0,1:T(8,128)} %reshape.194) | data formatting | bytes 622080 | tf_op jit(solution)/shard_map/reshape | solution.py:159
  40.0 3.9 %reshape.188 = f32[5,9,182,16]{3,2,0,1:T(8,128)} reshape(f32[5,9,2912]{2,0,1:T(8,128)} %concatenate.19) | data formatting | bytes 1048320 | tf_op jit(solution)/shard_map/reshape | solution.py:163
  43.9 3.7 %fusion.65 = (f32[1,9,180,16]{3,2,0,1:T(8,128)}, f32[1,9,180,16]{3,2,0,1:T(8,128)}, f32[1,9,180,16]{3,2,0,1:T(8,128)}, f32[1,9,180,16]{3,2,0,1:T(8,128)}) fusion(f32[5,9,182,16]{3,2,0,1:T(8,128)} %reshape.188), kind=kLoop, calls=%fused_computation.97 | loop fusion | bytes 829440 | tf_op jit(solution)/shard_map/slice | solution.py:185
  60.7 4.5 %reshape.195 = f32[5,11,180,16]{3,2,0,1:T(8,128)} reshape(f32[5,11,2880]{2,0,1:T(8,128)} %pad_maximum_fusion.2) | data formatting | bytes 1267200 | tf_op jit(solution)/shard_map/reshape | solution.py:170
  65.2 6.7 %fusion.63 = (f32[5,8,180,16]{3,2,0,1:T(8,128)}, f32[5,8,180,16]{3,2,0,1:T(8,128)}) fusion(f32[5,11,180,16]{3,2,0,1:T(8,128)} %reshape.195), kind=kLoop, calls=%fused_computation.95 | loop fusion | bytes 1843200 | tf_op jit(solution)/shard_map/slice | solution.py:176
  80.3 3.7 %copy.283 = f32[5,8,180,16]{2,3,1,0:T(8,128)} copy(f32[5,8,180,16]{3,2,0,1:T(8,128)} %get-tuple-element.144) | data formatting | bytes 921600
  84.0 3.7 %copy.286 = f32[5,8,180,16]{2,3,1,0:T(8,128)} copy(f32[5,8,180,16]{3,2,0,1:T(8,128)} %get-tuple-element.143) | data formatting | bytes 921600
  92.2 5.5 %all-to-all-start = ((f32[3,9,180,16]{2,0,1,3:T(4,128)}), f32[3,9,180,16]{2,0,1,3:T(4,128)}, u32[]{:S(2)}, u32[]{:S(2)}) async-start(f32[3,9,180,16]{2,0,1,3:T(4,128)} %copy.242), calls=%async_computation | async-start | bytes 1179648 | tf_op jit(solution)/shard_map/all_to_all | solution.py:140
  97.7 5.1 %fusion.64 = (f32[3,9,180,16]{3,2,0,1:T(8,128)}, f32[3,9,180,16]{3,2,0,1:T(8,128)}) fusion(f32[5,9,182,16]{3,2,0,1:T(8,128)} %reshape.188), kind=kLoop, calls=%fused_computation.96 | loop fusion | bytes 1244160 | tf_op jit(solution)/shard_map/slice | solution.py:186
  102.8 3.4 %copy.287 = f32[3,9,180,16]{2,3,1,0:T(8,128)} copy(f32[3,9,180,16]{3,2,0,1:T(8,128)} %get-tuple-element.145) | data formatting | bytes 622080
  106.2 3.4 %copy.288 = f32[3,9,180,16]{2,3,1,0:T(8,128)} copy(f32[3,9,180,16]{3,2,0,1:T(8,128)} %get-tuple-element.146) | data formatting | bytes 622080
  114.1 20.3 %while.13 = (s32[]{:T(128)}, f32[108,720]{1,0:T(8,128)S(1)}, s32[]{:T(128)}, f32[108,720]{1,0:T(8,128)}, s32[9]{0:T(128)S(1)}, /*index=5*/s32[]{:T(128)}, s32[]{:T(128)}) while((s32[]{:T(128)}, f32[108,720]{1,0:T(8,128)S(1)}, s32[]{:T(128)}, f32[108,720]{1,0:T(8,128)}, s32[9]{0:T(128)S(1)}, /*index=5*/s32[]{:T(128)}, ...), condition=%wide.region_2.3_spmd.clone, body=%wide.region_1.2_spmd.clone.sunk | while | flops 481314560 | bytes 2093813 | solution.py:134
  114.3 2.9 %fusion.94 = f32[108,128]{1,0:T(8,128)S(1)} fusion(f32[108,720]{1,0:T(8,128)} %get-tuple-element.226, s32[128]{0:T(128)S(1)} %iota_add_fusion.3, f32[128]{0:T(128)S(1)} %fusion.93, s32[108]{0:T(128)S(1)} %le.51), kind=kOutput, calls=%fused_computation.9.clone.1 | convolution fusion | flops 120310272 | bytes 367792 | tf_op jit(solution)/shard_map/while/body/dot_general | solution.py:109
  119.2 2.9 %fusion.96 = f32[108,128]{1,0:T(8,128)S(1)} fusion(f32[108,720]{1,0:T(8,128)} %get-tuple-element.226, s32[128]{0:T(128)S(1)} %iota_add_fusion.3, f32[128]{0:T(128)S(1)} %fusion.93, s32[108]{0:T(128)S(1)} %le.51), kind=kOutput, calls=%fused_computation.6.clone.1 | convolution fusion | flops 120310272 | bytes 367792 | tf_op jit(solution)/shard_map/while/body/dot_general | solution.py:112
  124.3 2.9 %fusion.94 = f32[108,128]{1,0:T(8,128)S(1)} fusion(f32[108,720]{1,0:T(8,128)} %get-tuple-element.226, s32[128]{0:T(128)S(1)} %iota_add_fusion.3, f32[128]{0:T(128)S(1)} %fusion.93, s32[108]{0:T(128)S(1)} %le.51), kind=kOutput, calls=%fused_computation.9.clone.1 | convolution fusion | flops 120310272 | bytes 367792 | tf_op jit(solution)/shard_map/while/body/dot_general | solution.py:109
  129.2 2.9 %fusion.96 = f32[108,128]{1,0:T(8,128)S(1)} fusion(f32[108,720]{1,0:T(8,128)} %get-tuple-element.226, s32[128]{0:T(128)S(1)} %iota_add_fusion.3, f32[128]{0:T(128)S(1)} %fusion.93, s32[108]{0:T(128)S(1)} %le.51), kind=kOutput, calls=%fused_computation.6.clone.1 | convolution fusion | flops 120310272 | bytes 367792 | tf_op jit(solution)/shard_map/while/body/dot_general | solution.py:112
  137.3 3.9 %copy.245 = f32[3,9,720,4]{1,3,0,2:T(4,128)} copy(f32[3,9,720,4]{2,3,1,0:T(4,128)S(1)} %bitcast.70) | data formatting | bytes 622080 | tf_op jit(solution)/shard_map/transpose | solution.py:142
  141.1 6.8 %reshape.196 = f32[4,1,19440]{2,1,0:T(1,128)} reshape(f32[720,3,4,9]{3,2,1,0:T(4,128)} %bitcast.61) | data formatting | bytes 622080
  147.9 4.2 %all-to-all-start.1 = ((f32[4,1,19440]{2,1,0:T(1,128)}), f32[4,1,19440]{2,1,0:T(1,128)S(1)}, u32[]{:S(2)}, u32[]{:S(2)}) async-start(f32[4,1,19440]{2,1,0:T(1,128)} %reshape.196), calls=%async_computation.1 | async-start | bytes 622592 | tf_op jit(solution)/shard_map/all_to_all | solution.py:143
  155.8 3.1 %convert_element_type.51 = bf16[3,9,2880]{2,0,1:T(4,128)(2,1)} reshape(bf16[3,9,180,16]{3,2,0,1:T(8,128)(2,1)} %copy.262) | data formatting | bytes 311040 | tf_op jit(solution)/shard_map/convert_element_type | solution.py:206
  162.6 7.5 %reshape.197 = f32[720,3,4,9]{3,2,1,0:T(4,128)} reshape(f32[4,19440]{1,0:T(4,128)S(1)} %reduce.1) | data formatting | bytes 622080
  170.1 5.8 %copy.274 = f32[3,9,4,180,4]{3,2,4,1,0:T(4,128)} copy(f32[3,9,4,180,4]{1,4,0,3,2:T(4,128)} %bitcast.60) | data formatting | bytes 622080 | tf_op jit(solution)/shard_map/all_to_all | solution.py:143
  (139 shorter events, 95.2 us)
Async XLA Ops:
  0.6 15.9 %copy-start.24 = (s32[72]{0:T(128)S(1)}, s32[72]{0:T(128)}, u32[]{:S(2)}) copy-start(s32[72]{0:T(128)} %param.10) | copy-start | bytes 868
  1.9 16.1 %copy-start.4 = (f32[1,9,2880]{2,0,1:T(1,128)}, f32[1,9,2880]{2,0,1:T(1,128)S(1)}, u32[]{:S(2)}) copy-start(f32[1,9,2880]{2,0,1:T(1,128)S(1)} %get-tuple-element.168) | copy-start | bytes 311044
  1.9 16.1 %copy-start.9 = (f32[1,9,2880]{2,0,1:T(1,128)}, f32[1,9,2880]{2,0,1:T(1,128)S(1)}, u32[]{:S(2)}) copy-start(f32[1,9,2880]{2,0,1:T(1,128)S(1)} %get-tuple-element.167) | copy-start | bytes 311044
  2.9 15.0 %copy-start.1 = (f32[3,9,2880]{2,0,1:T(4,128)}, f32[3,9,2880]{2,0,1:T(4,128)S(1)}, u32[]{:S(2)}) copy-start(f32[3,9,2880]{2,0,1:T(4,128)S(1)} %convert_element_type.47) | copy-start | bytes 933124
  4.1 13.8 %copy-start.7 = (f32[1,9,2880]{2,0,1:T(1,128)}, f32[1,9,2880]{2,0,1:T(1,128)S(1)}, u32[]{:S(2)}) copy-start(f32[1,9,2880]{2,0,1:T(1,128)S(1)} %copy.216) | copy-start | bytes 311044
  4.2 15.7 %copy-start.3 = (f32[9,2880]{1,0:T(8,128)S(1)}, f32[9,2880]{1,0:T(8,128)}, u32[]{:S(2)}) copy-start(f32[9,2880]{1,0:T(8,128)} %param.8) | copy-start | bytes 311044
  4.6 7.9 %copy-start.2 = (f32[5,9,2880]{2,0,1:T(8,128)}, f32[5,9,2880]{2,0,1:T(8,128)S(1)}, u32[]{:S(2)}) copy-start(f32[5,9,2880]{2,0,1:T(8,128)S(1)} %get-tuple-element.159) | copy-start | bytes 1555204
  5.4 53.0 %collective-permute-start.2 = (f32[5,1,2880]{2,0,1:T(8,128)}, f32[5,1,2880]{2,0,1:T(8,128)}, u32[]{:S(2)}, u32[]{:S(2)}) collective-permute-start(f32[5,1,2880]{2,0,1:T(8,128)} %get-tuple-element.155), channel_id=1, source_target_pairs={{0,4},{4,8},{8,12},{12,16},{16,20},{20,24},{24,28},{1,5},{5,9},{9,... | collective-permute-start | bytes 172808 | tf_op jit(solution)/shard_map/ppermute | solution.py:23
  7.3 51.1 %collective-permute-start.3 = (f32[5,1,2880]{2,0,1:T(8,128)}, f32[5,1,2880]{2,0,1:T(8,128)}, u32[]{:S(2)}, u32[]{:S(2)}) collective-permute-start(f32[5,1,2880]{2,0,1:T(8,128)} %get-tuple-element.154), channel_id=1, source_target_pairs={{4,0},{8,4},{12,8},{16,12},{20,16},{24,20},{28,24},{5,1},{9,5},{13... | collective-permute-start | bytes 172808 | tf_op jit(solution)/shard_map/ppermute | solution.py:24
  10.9 65.7 %collective-permute-start.4 = (f32[5,2880]{1,0:T(8,128)}, f32[5,2880]{1,0:T(8,128)}, u32[]{:S(2)}, u32[]{:S(2)}) collective-permute-start(f32[5,2880]{1,0:T(8,128)} %get-tuple-element.153), channel_id=1, source_target_pairs={{2,0},{3,1},{0,2},{1,3},{6,4},{7,5},{4,6},{5,7},{10,8},{11,9},{8,1... | collective-permute-start | bytes 172808 | tf_op jit(solution)/shard_map/ppermute | solution.py:32
  13.2 24.4 %collective-permute-start = (f32[5,9,16]{2,0,1:T(8,128)}, f32[5,9,16]{2,0,1:T(8,128)S(1)}, u32[]{:S(2)}, u32[]{:S(2)}) collective-permute-start(f32[5,9,16]{2,0,1:T(8,128)} %get-tuple-element.152), channel_id=1, source_target_pairs={{0,1},{1,2},{2,3},{3,0},{4,5},{5,6},{6,7},{7,4},{8,9},{9,10},{10,1... | collective-permute-start | bytes 8648 | tf_op jit(solution)/shard_map/ppermute | solution.py:23
  13.7 24.0 %collective-permute-start.1 = (f32[5,9,16]{2,0,1:T(8,128)}, f32[5,9,16]{2,0,1:T(8,128)S(1)}, u32[]{:S(2)}, u32[]{:S(2)}) collective-permute-start(f32[5,9,16]{2,0,1:T(8,128)} %get-tuple-element.151), channel_id=1, source_target_pairs={{1,0},{2,1},{3,2},{0,3},{5,4},{6,5},{7,6},{4,7},{9,8},{10,9},{11,1... | collective-permute-start | bytes 8648 | tf_op jit(solution)/shard_map/ppermute | solution.py:24
  29.1 7.8 %copy-start.19 = (pred[9]{0:T(512)(128)(4,1)S(1)}, pred[9]{0:T(512)(128)(4,1)}, u32[]{:S(2)}) copy-start(pred[9]{0:T(512)(128)(4,1)} %copy-done.18) | copy-start | bytes 31
  47.6 8.7 %copy-start.22 = (f32[9]{0:T(128)S(1)}, f32[9]{0:T(128)}, u32[]{:S(2)}) copy-start(f32[9]{0:T(128)} %get-tuple-element.173) | copy-start | bytes 112
  47.6 8.7 %copy-start.23 = (f32[9]{0:T(128)S(1)}, f32[9]{0:T(128)}, u32[]{:S(2)}) copy-start(f32[9]{0:T(128)} %get-tuple-element.174) | copy-start | bytes 112
  49.7 8.6 %copy-start.5 = (f32[1,9,2880]{2,0,1:T(1,128)S(1)}, f32[1,9,2880]{2,0,1:T(1,128)}, u32[]{:S(2)}) copy-start(f32[1,9,2880]{2,0,1:T(1,128)} %copy-done.4) | copy-start | bytes 311044
  49.7 8.6 %copy-start.8 = (f32[1,9,2880]{2,0,1:T(1,128)S(1)}, f32[1,9,2880]{2,0,1:T(1,128)}, u32[]{:S(2)}) copy-start(f32[1,9,2880]{2,0,1:T(1,128)} %copy-done.7) | copy-start | bytes 311044
  84.0 4.8 %copy-start.25 = (f32[9]{0:T(128)S(1)}, f32[9]{0:T(128)}, u32[]{:S(2)}) copy-start(f32[9]{0:T(128)} %get-tuple-element.171) | copy-start | bytes 112
  84.0 4.8 %copy-start.26 = (f32[9]{0:T(128)S(1)}, f32[9]{0:T(128)}, u32[]{:S(2)}) copy-start(f32[9]{0:T(128)} %get-tuple-element.172) | copy-start | bytes 112
  84.0 4.8 %copy-start.27 = (f32[9]{0:T(128)S(1)}, f32[9]{0:T(128)}, u32[]{:S(2)}) copy-start(f32[9]{0:T(128)} %get-tuple-element.176) | copy-start | bytes 112
  92.2 17.5 %all-to-all-start = ((f32[3,9,180,16]{2,0,1,3:T(4,128)}), f32[3,9,180,16]{2,0,1,3:T(4,128)}, u32[]{:S(2)}, u32[]{:S(2)}) async-start(f32[3,9,180,16]{2,0,1,3:T(4,128)} %copy.242), calls=%async_computation | async-start | bytes 1179648 | tf_op jit(solution)/shard_map/all_to_all | solution.py:140
  106.2 7.8 %copy-start.16 = (s32[9]{0:T(128)S(1)}, s32[9]{0:T(128)}, u32[]{:S(2)}) copy-start(s32[9]{0:T(128)} %copy-done.15) | copy-start | bytes 112
  114.1 20.3 %copy-start.17 = (pred[108]{0:T(512)(128)(4,1)S(1)}, pred[108]{0:T(512)(128)(4,1)}, u32[]{:S(2)}) copy-start(pred[108]{0:T(512)(128)(4,1)} %lt.47) | copy-start | bytes 328
  147.9 11.0 %all-to-all-start.1 = ((f32[4,1,19440]{2,1,0:T(1,128)}), f32[4,1,19440]{2,1,0:T(1,128)S(1)}, u32[]{:S(2)}, u32[]{:S(2)}) async-start(f32[4,1,19440]{2,1,0:T(1,128)} %reshape.196), calls=%async_computation.1 | async-start | bytes 622592 | tf_op jit(solution)/shard_map/all_to_all | solution.py:143
  (11 other events, 28.7 us)
where the time goes:
time: 196 us; the launch traced here: 194 us
  local copies, waits for them, and re-layouts  127 us (65%)
  other arithmetic  26.2 us (13%)
  matrix products  19.6 us (10%)
  starting transfers between devices  18.9 us (10%)
    unnamed x72, local copies, waits for them, and re-layouts  46.4 us
    slice x1, local copies, waits for them, and re-layouts, local(): south = jnp.concatenate([south_row[:, None], lat_ext[:, 1:-2]], axis=1)  6.73 us
    reshape x2, local copies, waits for them, and re-layouts, local(): tracer_cells = tracer_wide.reshape(3, rows, columns, LEVELS)  6.5 us
    all_to_all x2, local copies, waits for them, and re-layouts, regroup_filter(): lax.all_to_all(worked, 'lon', split_axis=2, concat_axis=3, tiled=True)  6.34 us
    dot_general x2, matrix products, one_block(): jnp.dot(flat, sine, precision=lax.Precision.HIGHEST, preferred_element_ty...  5.77 us
    dot_general x2, matrix products, one_block(): jnp.dot(flat, cosine, precision=lax.Precision.HIGHEST, preferred_element_...  5.75 us
    all_to_all x1, starting transfers between devices, regroup_filter(): lax.all_to_all(stacked, 'lon', split_axis=3, concat_axis=2, tiled=True)  5.53 us
    ppermute x2, starting transfers between devices, extended(): after = lax.ppermute(first, axis, down)  5.19 us
  transfers between devices with their start and end apart: 7, of which 0 were waited for; matrix products, arithmetic and copies ran while one was open for 41% of the time, Pallas kernels for 0%

commit v1 on v0

v1 whole, which is shorter than its diff:
```python
import functools
import math

import jax
import jax.numpy as jnp
import numpy as np
from jax import lax
from jax.experimental import pallas as pl
from jax.experimental.pallas import tpu as pltpu
from jax.sharding import PartitionSpec as P

LEVELS = 16
TIME_STEP = 0.05
DIFFUSION = 0.5
LANES = 128
PER_TILE = LANES // LEVELS
EXT_ROWS = 16
LIMIT = 48 * 1024 * 1024


class Sizes:
    def __init__(self, rows, merged, n_lat, n_lon):
        self.rows = rows
        self.merged = merged
        self.columns = merged // LEVELS
        self.n_lat = n_lat
        self.n_lon = n_lon
        self.nlat = rows * n_lat
        self.nlon = self.columns * n_lon
        self.ratio = 2.0 * self.nlat / self.nlon
        self.tiles = -(-merged // LANES)
        self.tail = merged - (self.tiles - 1) * LANES
        self.stack = -(-(self.tiles + 1) // 8) * 8
        self.units = 3 * rows
        self.share = -(-self.units // n_lon)
        assert self.tail <= LANES - 2 * LEVELS and rows + 2 <= EXT_ROWS

    def span(self, tile):
        return self.tail if tile == self.tiles - 1 else LANES


def geometry(sz):
    table = np.zeros((sz.n_lat, 3, EXT_ROWS, LANES), np.float64)

    def face(j):
        return math.sin((j + 1) * math.pi / sz.nlat) if 0 <= j < sz.nlat - 1 else 0.0

    for band in range(sz.n_lat):
        for row in range(sz.rows):
            j = band * sz.rows + row
            centre = (j + 0.5) * math.pi / sz.nlat - math.pi / 2
            table[band, 0, row] = 1.0 / math.cos(centre)
            table[band, 1, row] = math.sin(centre)
            table[band, 2, row] = face(j)
        table[band, 2, EXT_ROWS - 1] = face(band * sz.rows - 1)
    return table.astype(np.float32)


def offsets(sz):
    shift, out_tile = np.divmod(np.arange(PER_TILE * sz.stack), sz.stack)
    sector, in_tile = np.divmod(np.arange(sz.n_lon * sz.stack), sz.stack)
    n = (PER_TILE * (out_tile - 1) + shift)[:, None] - (PER_TILE * in_tile + sz.columns * sector)[None, :]
    n = (n + sz.nlon // 2) % sz.nlon - sz.nlon // 2
    with np.errstate(divide="ignore"):
        inverse = np.where(n == 0, 0.0, 1.0 / (sz.nlon * np.sin(np.pi * n / sz.nlon)))
    return n.astype(np.float32), inverse.astype(np.float32)


def pack_kernel(sz, h_ref, w_ref, q_ref, east_ref, west_ref, north_ref, south_ref, across_ref):
    top = lax.axis_index("lat") == sz.n_lat - 1
    last = sz.rows - 1
    for f in range(5):
        to = slice(LEVELS * f, LEVELS * (f + 1))

        def load(lanes, other):
            if f < 2:
                source = (h_ref[:, lanes], w_ref[other, :, lanes])[f]
            else:
                source = q_ref[f - 2, :, lanes].astype(jnp.float32)
            return source

        east_ref[:, to] = load(slice(sz.merged - LEVELS, sz.merged), 0)
        west_ref[:, to] = load(slice(0, LEVELS), 0)
        for t in range(sz.tiles):
            wide = sz.span(t)
            block = load(slice(LANES * t, LANES * t + wide), 1)
            at = sz.stack * f + t
            north_ref[at : at + 1, :wide] = block[last : last + 1]
            south_ref[at : at + 1, :wide] = block[0:1]
            across_ref[at : at + 1, :wide] = jnp.where(top, block[last : last + 1], block[0:1])


def step_kernel(
    sz, h_ref, w_ref, q_ref, from_w, from_e, from_s, from_n, from_a, geo_ref, mass_ref, tend_ref, ext
):
    band = lax.axis_index("lat")
    bottom, top = band == 0, band == sz.n_lat - 1
    lane = lax.broadcasted_iota(jnp.int32, (EXT_ROWS, LANES), 1)
    wide = sz.tiles * LANES
    for f in range(6):
        if f == 0:
            ext[f, : sz.rows, : sz.merged] = h_ref[...]
        elif f == 1:
            ext[f, : sz.rows, : sz.merged] = w_ref[1]
        elif f == 5:
            ext[f, : sz.rows, : sz.merged] = w_ref[0]
        else:
            ext[f, : sz.rows, : sz.merged] = q_ref[f - 2].astype(jnp.float32)
    for f in range(5):
        flip = -1.0 if f == 1 else 1.0
        for t in range(sz.tiles):
            at = slice(sz.stack * f + t, sz.stack * f + t + 1)
            over = from_a[at] * flip
            lanes = slice(LANES * t, LANES * (t + 1))
            ext[f, sz.rows : sz.rows + 1, lanes] = jnp.where(top, over, from_n[at])
            ext[f, EXT_ROWS - 1 : EXT_ROWS, lanes] = jnp.where(bottom, over, from_s[at])
    lane9 = lane[: sz.rows]
    end = (sz.tiles - 1) * LANES
    for place, f in enumerate((0, 5, 2, 3, 4)):
        after = pltpu.roll(from_e[...], (sz.tail - LEVELS * place) % LANES, 1)
        before = pltpu.roll(from_w[...], (LANES - LEVELS - LEVELS * place) % LANES, 1)
        own = ext[f, : sz.rows, end:wide]
        edge = jnp.where(lane9 < LANES - LEVELS, after, before)
        ext[f, : sz.rows, end:wide] = jnp.where(lane9 < sz.tail, own, edge)

    inv_cos = geo_ref[band, 0]
    sin_centre = geo_ref[band, 1]
    cos_face = geo_ref[band, 2]
    ratio = sz.ratio
    tiles = sz.tiles
    rolled = {}

    def tile(f, t):
        t = t % tiles
        return ext[f, :, LANES * t : LANES * (t + 1)]

    def turned(name, t, value, step):
        if (name, t, step) not in rolled:
            rolled[name, t, step] = pltpu.roll(value(t), step % LANES, 1)
        return rolled[name, t, step]

    def east(name, t, value):
        here = turned(name, t, value, -LEVELS)
        return jnp.where(lane < LANES - LEVELS, here, turned(name, (t + 1) % tiles, value, -LEVELS))

    def west(name, t, value):
        here = turned(name, t, value, LEVELS)
        return jnp.where(lane >= LEVELS, here, turned(name, (t - 1) % tiles, value, LEVELS))

    def north(value):
        return pltpu.roll(value, EXT_ROWS - 1, 0)

    def south(value):
        return pltpu.roll(value, 1, 0)

    kept = {}

    def zonal(t):
        t = t % tiles
        if t not in kept:
            thick, wind_u = tile(0, t), tile(5, t)
            thick_e = east("h", t, functools.partial(tile, 0))
            wind_e = east("u", t, functools.partial(tile, 5))
            flux = 0.25 * (wind_u + wind_e) * (thick + thick_e) * inv_cos
            parts = []
            for k in range(3):
                q = tile(2 + k, t)
                q_e = east(k, t, functools.partial(tile, 2 + k))
                parts.append(DIFFUSION * (q_e - q) - flux * (0.5 * (q + q_e)))
            kept[t] = (flux, thick_e, parts)
        return kept[t]

    for t in range(tiles):
        span = sz.span(t)
        lanes = slice(LANES * t, LANES * t + span)
        flux, thick_e, parts = zonal(t)
        thick, wind_u, wind_v = tile(0, t), tile(5, t), tile(1, t)
        flux_w = west("f", t, lambda s: zonal(s)[0])
        thick_w = west("hw", t, functools.partial(tile, 0))
        thick_n = north(thick)
        flux_n = (0.25 * ratio) * (wind_v + north(wind_v)) * (thick + thick_n) * cos_face
        flux_s = south(flux_n)
        thick_tend = -((flux - flux_w) + (flux_n - flux_s) * inv_cos)
        wind_u_tend = sin_centre * wind_v - (thick_e - thick_w) * (0.5 * inv_cos)
        wind_v_tend = -sin_centre * wind_u - (0.5 * ratio) * (thick_n - south(thick))
        for k in range(3):
            q = tile(2 + k, t)
            q_n = north(q)
            zonal_part = parts[k] - west(("p", k), t, lambda s: zonal(s)[2][k])
            lap = q_n + south(q) - 2.0 * q
            over = flux_n * (0.5 * (q + q_n))
            merid_part = DIFFUSION * lap - (over - south(over)) * inv_cos
            mass = thick * q + TIME_STEP * (zonal_part + merid_part)
            mass_ref[k, :, lanes] = mass[: sz.rows, :span].astype(jnp.bfloat16)
        for f, tend in enumerate((thick_tend, wind_u_tend, wind_v_tend)):
            if span < LANES:
                tend = jnp.where(lane < span, tend, 0.0)
            first = sz.stack * sz.rows * f + t
            tend_ref[pl.ds(first, sz.rows, stride=sz.stack), :] = tend[: sz.rows]
    for f in range(3):
        for t in range(tiles, sz.stack):
            first = sz.stack * sz.rows * f + t
            tend_ref[pl.ds(first, sz.rows, stride=sz.stack), :] = jnp.zeros((sz.rows, LANES), jnp.float32)
    spare = sz.stack * sz.units
    if spare < tend_ref.shape[0]:
        tend_ref[spare:, :] = jnp.zeros((tend_ref.shape[0] - spare, LANES), jnp.float32)


def sin_pi(y):
    y = jnp.where(y > 0.5, 1.0 - y, jnp.where(y < -0.5, -1.0 - y, y))
    s = y * y
    series = [(-1) ** i * math.pi ** (2 * i + 1) / math.factorial(2 * i + 1) for i in range(7)]
    total = series[-1]
    for factor in reversed(series[:-1]):
        total = total * s + factor
    return total * y


def filter_kernel(sz, cut_ref, n_ref, inverse_ref, in_ref, out_ref):
    band, sector = lax.axis_index("lat"), lax.axis_index("lon")
    stack, nlon = sz.stack, sz.nlon
    lane = lax.broadcasted_iota(jnp.int32, (stack, LANES), 1)
    n = n_ref[...]
    inverse = inverse_ref[...]
    for i in range(sz.share):
        unit = sector * sz.share + i
        row = lax.rem(unit, sz.rows)
        width = 2 * cut_ref[band * sz.rows + row] + 1
        width = width.astype(jnp.float32)
        turns = n * width
        turns = turns - jnp.round(turns * (0.5 / nlon)) * (2.0 * nlon)
        weights = sin_pi(turns * (1.0 / nlon)) * inverse
        weights = jnp.where(n == 0.0, width * (1.0 / nlon), weights).astype(jnp.bfloat16)
        pieces = [in_ref[s, stack * i : stack * (i + 1)].astype(jnp.bfloat16) for s in range(sz.n_lon)]
        circle = jnp.concatenate(
            [jnp.concatenate(pieces[s:] + pieces[:s], axis=0) for s in range(sz.n_lon)], axis=1
        )
        spread = jnp.dot(weights, circle, preferred_element_type=jnp.float32)
        for s in range(sz.n_lon):
            same = spread[:stack, LANES * s : LANES * (s + 1)]
            carried = None
            for e in range(1, PER_TILE):
                part = spread[stack * e : stack * (e + 1), LANES * s : LANES * (s + 1)]
                part = pltpu.roll(part, LEVELS * e, 1)
                inside = lane >= LEVELS * e
                same = same + jnp.where(inside, part, 0.0)
                over = jnp.where(inside, 0.0, part)
                carried = over if carried is None else carried + over
            out_ref[s, stack * i : stack * (i + 1)] = pltpu.roll(same, stack - 1, 0) + carried


def finish_kernel(sz, cut_ref, h_ref, w_ref, tend_ref, back_ref, new_w_ref, new_h_ref):
    band = lax.axis_index("lat")
    row = lax.broadcasted_iota(jnp.int32, (sz.rows, LANES), 0)
    cuts = jnp.zeros((sz.rows, LANES), jnp.int32)
    for j in range(sz.rows):
        cuts = jnp.where(row == j, cut_ref[band * sz.rows + j], cuts)
    active = cuts < sz.nlon // 2
    for f in range(3):
        for t in range(sz.tiles):
            span = sz.span(t)
            lanes = slice(LANES * t, LANES * t + span)
            at = pl.ds(sz.stack * sz.rows * f + t, sz.rows, stride=sz.stack)
            tend = jnp.where(active, back_ref[at, :], tend_ref[at, :])[:, :span]
            if f == 0:
                new_h_ref[:, lanes] = h_ref[:, lanes] + TIME_STEP * tend
            else:
                new_w_ref[f - 1, :, lanes] = w_ref[f - 1, :, lanes] + TIME_STEP * tend


def local(winds, thickness, tracers, cutoff):
    n_lat = lax.axis_size("lat")
    n_lon = lax.axis_size("lon")
    rows, merged = thickness.shape
    sz = Sizes(rows, merged, n_lat, n_lon)
    f32 = jnp.float32
    vmem = pl.BlockSpec(memory_space=pltpu.VMEM)
    smem = pl.BlockSpec(memory_space=pltpu.SMEM)
    params = pltpu.CompilerParams(vmem_limit_bytes=LIMIT)
    band_rows = jax.ShapeDtypeStruct((5 * sz.stack, LANES), f32)
    edge = jax.ShapeDtypeStruct((rows, LANES), f32)

    to_e, to_w, to_n, to_s, to_a = pl.pallas_call(
        functools.partial(pack_kernel, sz),
        out_shape=(edge, edge, band_rows, band_rows, band_rows),
        in_specs=[vmem] * 3,
        out_specs=(vmem,) * 5,
        compiler_params=params,
        name="pack",
    )(thickness, winds, tracers)

    up = [(i, i + 1) for i in range(n_lat - 1)]
    down = [(i + 1, i) for i in range(n_lat - 1)]
    from_s = lax.ppermute(to_n, "lat", up)
    from_n = lax.ppermute(to_s, "lat", down)
    poles = [
        (band * n_lon + i, band * n_lon + (i + n_lon // 2) % n_lon) for band in (0, n_lat - 1) for i in range(n_lon)
    ]
    from_a = lax.ppermute(to_a, ("lat", "lon"), poles)
    from_w = lax.ppermute(to_e, "lon", [(i, (i + 1) % n_lon) for i in range(n_lon)])
    from_e = lax.ppermute(to_w, "lon", [((i + 1) % n_lon, i) for i in range(n_lon)])

    total = sz.share * n_lon * sz.stack
    mass, tend = pl.pallas_call(
        functools.partial(step_kernel, sz),
        out_shape=(
            jax.ShapeDtypeStruct(tracers.shape, jnp.bfloat16),
            jax.ShapeDtypeStruct((total, LANES), f32),
        ),
        in_specs=[vmem] * 9,
        out_specs=(vmem,) * 2,
        scratch_shapes=[pltpu.VMEM((6, EXT_ROWS, sz.tiles * LANES), f32)],
        compiler_params=params,
        name="step",
    )(thickness, winds, tracers, from_w, from_e, from_s, from_n, from_a, jnp.asarray(geometry(sz)))

    split = (n_lon, sz.share * sz.stack, LANES)
    sent = lax.all_to_all(tend.reshape(split), "lon", 0, 0)
    n, inverse = offsets(sz)
    worked = pl.pallas_call(
        functools.partial(filter_kernel, sz),
        out_shape=jax.ShapeDtypeStruct(split, f32),
        in_specs=[smem] + [vmem] * 3,
        out_specs=vmem,
        compiler_params=params,
        name="filter",
    )(cutoff, jnp.asarray(n), jnp.asarray(inverse), sent)
    back = lax.all_to_all(worked, "lon", 0, 0).reshape(total, LANES)

    new_w, new_h = pl.pallas_call(
        functools.partial(finish_kernel, sz),
        out_shape=(jax.ShapeDtypeStruct(winds.shape, f32), jax.ShapeDtypeStruct(thickness.shape, f32)),
        in_specs=[smem] + [vmem] * 4,
        out_specs=(vmem,) * 2,
        compiler_params=params,
        name="finish",
    )(cutoff, thickness, winds, tend, back)
    return new_w, new_h, mass


def solution(mesh):
    in_specs = (P(None, "lat", "lon"), P("lat", "lon"), P(None, "lat", "lon"), P())
    out_specs = (P(None, "lat", "lon"), P("lat", "lon"), P(None, "lat", "lon"))
    return jax.shard_map(local, mesh=mesh, in_specs=in_specs, out_specs=out_specs, check_vma=False)
```

time: 196 us -> 41.6 us (0.21)
  the two profiles are of different devices: /device:TPU:26 before, /device:TPU:0 now
where the time goes in v1:
time: 41.6 us; the launch traced here: 41.2 us
  starting transfers between devices  14.3 us (34%)
  blocking collectives  9.83 us (24%)
  waiting for transfers between devices  7.04 us (17%)
  Pallas kernels  5.75 us (14%)
  local copies, waits for them, and re-layouts  3.52 us (8%)
  between operations  0.74 us (2%)
    all_to_all x1, blocking collectives, local(): sent = lax.all_to_all(tend.reshape(split), 'lon', 0, 0)  9.83 us
    all_to_all x1, waiting for transfers between devices, local(): back = lax.all_to_all(worked, 'lon', 0, 0).reshape(total, LANES)  4.81 us
    ppermute x1, starting transfers between devices, local(): from_a = lax.ppermute(to_a, ('lat', 'lon'), poles)  4.26 us
    unnamed x16, local copies, waits for them, and re-layouts  3.52 us
    all_to_all x1, starting transfers between devices, local(): back = lax.all_to_all(worked, 'lon', 0, 0).reshape(total, LANES)  3.45 us
    pallas_call x1, Pallas kernels, local(): pl.pallas_call(functools.partial(filter_kernel, sz), out_shape=jax.ShapeD...  2.5 us
    ppermute x1, starting transfers between devices, local(): from_s = lax.ppermute(to_n, 'lat', up)  2.35 us
    ppermute x1, waiting for transfers between devices, local(): lax.ppermute(to_e, 'lon', [(i, (i + 1) % n_lon) for i in range(n_lon)])  1.69 us
  transfers between devices with their start and end apart: 6, of which 3 were waited for; matrix products, arithmetic and copies ran while one was open for 2% of the time, Pallas kernels for 0%

profile of v1, /device:TPU:0, one launch (start us, length us, event | category | flops | bytes accessed | tf_op | source)
XLA Modules:
  0.0 41.2 jit_solution(12482891457384511094)
XLA Ops:
  0.6 1.0 %copy.13.q_ref = bf16[3,9,2880]{2,1,0:T(8,128)(2,1)S(1)} copy(bf16[3,9,2880]{2,0,1:T(4,128)(2,1)} %param.9) | data formatting | bytes 311040 | tf_op args[2]
  1.6 0.0 copy-done.5
  1.7 0.9 %copy-done = f32[9,2880]{1,0:T(8,128)S(1)} copy-done((f32[9,2880]{1,0:T(8,128)S(1)}, f32[9,2880]{1,0:T(8,128)}, u32[]{:S(2)}) %copy-start) | copy-done | bytes 103704
  2.6 0.2 pack.1
  2.8 2.4 %collective-permute-start.2 = (f32[120,128]{1,0:T(8,128)S(1)}, f32[120,128]{1,0:T(8,128)S(1)}, u32[]{:S(2)}, u32[]{:S(2)}) collective-permute-start(f32[120,128]{1,0:T(8,128)S(1)} %get-tuple-element.14), channel_id=1, source_target_pairs={{0,4},{4,8},{8,12},{12,16},{16,20},{20,24},{24,28},{1,5},{5,9},{9,... | collective-permute-start | bytes 184328 | tf_op jit(solution)/shard_map/ppermute | solution.py:294
  5.1 1.3 %collective-permute-start.3 = (f32[120,128]{1,0:T(8,128)S(1)}, f32[120,128]{1,0:T(8,128)S(1)}, u32[]{:S(2)}, u32[]{:S(2)}) collective-permute-start(f32[120,128]{1,0:T(8,128)S(1)} %get-tuple-element.15), channel_id=1, source_target_pairs={{4,0},{8,4},{12,8},{16,12},{20,16},{24,20},{28,24},{5,1},{9,5},{13... | collective-permute-start | bytes 184328 | tf_op jit(solution)/shard_map/ppermute | solution.py:295
  6.4 4.3 %collective-permute-start.4 = (f32[120,128]{1,0:T(8,128)S(1)}, f32[120,128]{1,0:T(8,128)S(1)}, u32[]{:S(2)}, u32[]{:S(2)}) collective-permute-start(f32[120,128]{1,0:T(8,128)S(1)} %get-tuple-element.16), channel_id=1, source_target_pairs={{0,2},{1,3},{2,0},{3,1},{28,30},{29,31},{30,28},{31,29}} | collective-permute-start | bytes 184328 | tf_op jit(solution)/shard_map/ppermute | solution.py:299
  10.7 1.5 %collective-permute-start = (f32[9,128]{1,0:T(8,128)S(1)}, f32[9,128]{1,0:T(8,128)S(1)}, u32[]{:S(2)}, u32[]{:S(2)}) collective-permute-start(f32[9,128]{1,0:T(8,128)S(1)} %get-tuple-element.12), channel_id=1, source_target_pairs={{0,1},{1,2},{2,3},{3,0},{4,5},{5,6},{6,7},{7,4},{8,9},{9,10},{10,1... | collective-permute-start | bytes 13832 | tf_op jit(solution)/shard_map/ppermute | solution.py:300
  12.2 1.4 %collective-permute-start.1 = (f32[9,128]{1,0:T(8,128)S(1)}, f32[9,128]{1,0:T(8,128)S(1)}, u32[]{:S(2)}, u32[]{:S(2)}) collective-permute-start(f32[9,128]{1,0:T(8,128)S(1)} %get-tuple-element.13), channel_id=1, source_target_pairs={{1,0},{2,1},{3,2},{0,3},{5,4},{6,5},{7,6},{4,7},{9,8},{10,9},{11,1... | collective-permute-start | bytes 13832 | tf_op jit(solution)/shard_map/ppermute | solution.py:301
  13.7 1.7 %collective-permute-done.from_w = f32[9,128]{1,0:T(8,128)S(1)} collective-permute-done((f32[9,128]{1,0:T(8,128)S(1)}, f32[9,128]{1,0:T(8,128)S(1)}, u32[]{:S(2)}, u32[]{:S(2)}) %collective-permute-start) | collective-permute-done | bytes 4640 | tf_op jit(solution)/shard_map/ppermute | solution.py:300
  15.4 0.5 %collective-permute-done.1.from_e = f32[9,128]{1,0:T(8,128)S(1)} collective-permute-done((f32[9,128]{1,0:T(8,128)S(1)}, f32[9,128]{1,0:T(8,128)S(1)}, u32[]{:S(2)}, u32[]{:S(2)}) %collective-permute-start.1) | collective-permute-done | bytes 4640 | tf_op jit(solution)/shard_map/ppermute | solution.py:301
  15.9 0.0 collective-permute-done.2.from_s
  15.9 0.0 collective-permute-done.3.from_n
  15.9 1.7 %step.1 = (bf16[3,9,2880]{2,1,0:T(8,128)(2,1)S(1)}, f32[672,128]{1,0:T(8,128)S(1)}) custom-call(f32[9,2880]{1,0:T(8,128)S(1)} %copy-done, f32[2,9,2880]{2,1,0:T(8,128)S(1)} %copy.14.w_ref, bf16[3,9,2880]{2,1,0:T(8,128)(2,1)S(1)} %copy.13.q_ref, f32[9,128]{1,0:T(8,128)S(1)} %collective-permute-done.from_w, f32[9,128]{1,0:T(8,128)S(1)} %collective-permute-done.1.from_e, ...), custom_call_target="tpu_custom_call" | custom-call | tf_op jit(solution)/shard_map/step/pallas_call | solution.py:304
  17.6 0.0 copy-start.2
  17.6 0.0 copy-start.3
  17.6 0.0 copy-start.4
  17.6 9.8 %all_to_all.10.in_ref = f32[4,168,128]{2,1,0:T(8,128)S(1)} all-to-all(f32[4,168,128]{2,1,0:T(8,128)S(1)} %bitcast.2), channel_id=1, replica_groups=mesh['lat'=8,'lon'=4] {'lon'}, dimensions={0} | all-to-all | bytes 688128 | tf_op jit(solution)/shard_map/all_to_all | solution.py:318
  27.5 2.5 %filter.1 = f32[4,168,128]{2,1,0:T(8,128)} custom-call(s32[72]{0:T(128)S(1)} %copy-done.4, f32[192,96]{1,0:T(8,128)S(1)} %copy-done.3, f32[192,96]{1,0:T(8,128)S(1)} %copy-done.2, f32[4,168,128]{2,1,0:T(8,128)S(1)} %all_to_all.10.in_ref), custom_call_target="tpu_custom_call" | custom-call | tf_op jit(solution)/shard_map/filter/pallas_call | solution.py:320
  30.0 3.5 %all-to-all-start.1 = ((f32[4,168,128]{2,1,0:T(8,128)}), f32[4,168,128]{2,1,0:T(8,128)S(1)}, u32[]{:S(2)}, u32[]{:S(2)}) async-start(f32[4,168,128]{2,1,0:T(8,128)} %filter.1), calls=%async_computation.1 | async-start | bytes 688128 | tf_op jit(solution)/shard_map/all_to_all | solution.py:328
  33.4 0.8 %copy.16 = bf16[3,9,2880]{2,0,1:T(4,128)(2,1)} copy(bf16[3,9,2880]{2,1,0:T(8,128)(2,1)S(1)} %get-tuple-element.23) | data formatting | bytes 311040
  34.2 4.8 %all-to-all-done.1 = f32[4,168,128]{2,1,0:T(8,128)S(1)} async-done(((f32[4,168,128]{2,1,0:T(8,128)}), f32[4,168,128]{2,1,0:T(8,128)S(1)}, u32[]{:S(2)}, u32[]{:S(2)}) %all-to-all-start.1) | async-done | bytes 344096 | tf_op jit(solution)/shard_map/all_to_all | solution.py:328
  39.0 1.4 %finish.1 = (f32[2,9,2880]{2,1,0:T(8,128)S(1)}, f32[9,2880]{1,0:T(8,128)}) custom-call(s32[72]{0:T(128)S(1)} %copy-done.4, f32[9,2880]{1,0:T(8,128)S(1)} %copy-done, f32[2,9,2880]{2,1,0:T(8,128)S(1)} %copy.14.w_ref, f32[672,128]{1,0:T(8,128)S(1)} %get-tuple-element.17.tend_ref, f32[672,128]{1,0:T(8,128)S(1)} %bitcast.3), custom_call_target="tpu_custom_call" | custom-call | tf_op jit(solution)/shard_map/finish/pallas_call | solution.py:330
  40.4 0.8 %copy.15 = f32[2,9,2880]{2,0,1:T(2,128)} copy(f32[2,9,2880]{2,1,0:T(8,128)S(1)} %get-tuple-element.21) | data formatting | bytes 414720
  (9 shorter events, 0.0 us)
Async XLA Ops:
  0.6 1.0 %copy-start.5 = (f32[2,9,2880]{2,0,1:T(2,128)S(1)}, f32[2,9,2880]{2,0,1:T(2,128)}, u32[]{:S(2)}) copy-start(f32[2,9,2880]{2,0,1:T(2,128)} %param.7) | copy-start | bytes 622084
  1.7 0.9 %copy-start = (f32[9,2880]{1,0:T(8,128)S(1)}, f32[9,2880]{1,0:T(8,128)}, u32[]{:S(2)}) copy-start(f32[9,2880]{1,0:T(8,128)} %h_ref.5) | copy-start | bytes 311044
  2.6 13.3 %copy-start.1 = (f32[8,3,16,128]{3,2,1,0:T(8,128)S(1)}, f32[8,3,16,128]{3,2,1,0:T(8,128)}, u32[]{:S(2)}) copy-start(f32[8,3,16,128]{3,2,1,0:T(8,128)} %constant.6.clone.geo_ref) | copy-start | bytes 589828
  2.8 13.1 %collective-permute-start.2 = (f32[120,128]{1,0:T(8,128)S(1)}, f32[120,128]{1,0:T(8,128)S(1)}, u32[]{:S(2)}, u32[]{:S(2)}) collective-permute-start(f32[120,128]{1,0:T(8,128)S(1)} %get-tuple-element.14), channel_id=1, source_target_pairs={{0,4},{4,8},{8,12},{12,16},{16,20},{20,24},{24,28},{1,5},{5,9},{9,... | collective-permute-start | bytes 184328 | tf_op jit(solution)/shard_map/ppermute | solution.py:294
  5.1 10.8 %collective-permute-start.3 = (f32[120,128]{1,0:T(8,128)S(1)}, f32[120,128]{1,0:T(8,128)S(1)}, u32[]{:S(2)}, u32[]{:S(2)}) collective-permute-start(f32[120,128]{1,0:T(8,128)S(1)} %get-tuple-element.15), channel_id=1, source_target_pairs={{4,0},{8,4},{12,8},{16,12},{20,16},{24,20},{28,24},{5,1},{9,5},{13... | collective-permute-start | bytes 184328 | tf_op jit(solution)/shard_map/ppermute | solution.py:295
  6.4 9.5 %collective-permute-start.4 = (f32[120,128]{1,0:T(8,128)S(1)}, f32[120,128]{1,0:T(8,128)S(1)}, u32[]{:S(2)}, u32[]{:S(2)}) collective-permute-start(f32[120,128]{1,0:T(8,128)S(1)} %get-tuple-element.16), channel_id=1, source_target_pairs={{0,2},{1,3},{2,0},{3,1},{28,30},{29,31},{30,28},{31,29}} | collective-permute-start | bytes 184328 | tf_op jit(solution)/shard_map/ppermute | solution.py:299
  10.7 4.7 %collective-permute-start = (f32[9,128]{1,0:T(8,128)S(1)}, f32[9,128]{1,0:T(8,128)S(1)}, u32[]{:S(2)}, u32[]{:S(2)}) collective-permute-start(f32[9,128]{1,0:T(8,128)S(1)} %get-tuple-element.12), channel_id=1, source_target_pairs={{0,1},{1,2},{2,3},{3,0},{4,5},{5,6},{6,7},{7,4},{8,9},{9,10},{10,1... | collective-permute-start | bytes 13832 | tf_op jit(solution)/shard_map/ppermute | solution.py:300
  12.2 3.7 %collective-permute-start.1 = (f32[9,128]{1,0:T(8,128)S(1)}, f32[9,128]{1,0:T(8,128)S(1)}, u32[]{:S(2)}, u32[]{:S(2)}) collective-permute-start(f32[9,128]{1,0:T(8,128)S(1)} %get-tuple-element.13), channel_id=1, source_target_pairs={{1,0},{2,1},{3,2},{0,3},{5,4},{6,5},{7,6},{4,7},{9,8},{10,9},{11,1... | collective-permute-start | bytes 13832 | tf_op jit(solution)/shard_map/ppermute | solution.py:301
  17.6 9.9 %copy-start.2 = (f32[192,96]{1,0:T(8,128)S(1)}, f32[192,96]{1,0:T(8,128)}, u32[]{:S(2)}) copy-start(f32[192,96]{1,0:T(8,128)} %constant.8.clone.inverse_ref) | copy-start | bytes 221188
  17.6 9.9 %copy-start.3 = (f32[192,96]{1,0:T(8,128)S(1)}, f32[192,96]{1,0:T(8,128)}, u32[]{:S(2)}) copy-start(f32[192,96]{1,0:T(8,128)} %constant.7.clone.n_ref) | copy-start | bytes 221188
  17.6 9.8 %copy-start.4 = (s32[72]{0:T(128)S(1)}, s32[72]{0:T(128)}, u32[]{:S(2)}) copy-start(s32[72]{0:T(128)} %cut_ref.3) | copy-start | bytes 868
  30.0 9.0 %all-to-all-start.1 = ((f32[4,168,128]{2,1,0:T(8,128)}), f32[4,168,128]{2,1,0:T(8,128)S(1)}, u32[]{:S(2)}, u32[]{:S(2)}) async-start(f32[4,168,128]{2,1,0:T(8,128)} %filter.1), calls=%async_computation.1 | async-start | bytes 688128 | tf_op jit(solution)/shard_map/all_to_all | solution.py:328

commit v2 on v1

--- a/solution.py
+++ b/solution.py
@@ -66,18 +66,16 @@
     return n.astype(np.float32), inverse.astype(np.float32)
 
 
-def pack_kernel(sz, h_ref, w_ref, q_ref, east_ref, west_ref, north_ref, south_ref, across_ref):
-    top = lax.axis_index("lat") == sz.n_lat - 1
+def pack_kernel(sz, h_ref, w_ref, q_ref, east_ref, west_ref, near_ref, far_ref):
+    even = lax.rem(lax.axis_index("lat"), 2) == 0
     last = sz.rows - 1
     for f in range(5):
         to = slice(LEVELS * f, LEVELS * (f + 1))
 
         def load(lanes, other):
             if f < 2:
-                source = (h_ref[:, lanes], w_ref[other, :, lanes])[f]
-            else:
-                source = q_ref[f - 2, :, lanes].astype(jnp.float32)
-            return source
+                return (h_ref[:, lanes], w_ref[other, :, lanes])[f]
+            return q_ref[f - 2, :, lanes].astype(jnp.float32)
 
         east_ref[:, to] = load(slice(sz.merged - LEVELS, sz.merged), 0)
         west_ref[:, to] = load(slice(0, LEVELS), 0)
@@ -85,16 +83,15 @@
             wide = sz.span(t)
             block = load(slice(LANES * t, LANES * t + wide), 1)
             at = sz.stack * f + t
-            north_ref[at : at + 1, :wide] = block[last : last + 1]
-            south_ref[at : at + 1, :wide] = block[0:1]
-            across_ref[at : at + 1, :wide] = jnp.where(top, block[last : last + 1], block[0:1])
-
-
-def step_kernel(
-    sz, h_ref, w_ref, q_ref, from_w, from_e, from_s, from_n, from_a, geo_ref, mass_ref, tend_ref, ext
-):
+            near_ref[at : at + 1, :wide] = jnp.where(even, block[last : last + 1], block[0:1])
+            far_ref[at : at + 1, :wide] = jnp.where(even, block[0:1], block[last : last + 1])
+
+
+def step_kernel(sz, h_ref, w_ref, q_ref, from_w, from_e, near_ref, far_ref, geo_ref, mass_ref, *refs):
+    out_refs, (tend_ref, ext) = refs[: sz.n_lon], refs[sz.n_lon :]
     band = lax.axis_index("lat")
-    bottom, top = band == 0, band == sz.n_lat - 1
+    even = lax.rem(band, 2) == 0
+    over_pole = (band == 0) | (band == sz.n_lat - 1)
     lane = lax.broadcasted_iota(jnp.int32, (EXT_ROWS, LANES), 1)
     wide = sz.tiles * LANES
     for f in range(6):
@@ -107,13 +104,13 @@
         else:
             ext[f, : sz.rows, : sz.merged] = q_ref[f - 2].astype(jnp.float32)
     for f in range(5):
-        flip = -1.0 if f == 1 else 1.0
+        flip = jnp.where(over_pole, -1.0, 1.0) if f == 1 else 1.0
         for t in range(sz.tiles):
             at = slice(sz.stack * f + t, sz.stack * f + t + 1)
-            over = from_a[at] * flip
+            near, far = near_ref[at], far_ref[at] * flip
             lanes = slice(LANES * t, LANES * (t + 1))
-            ext[f, sz.rows : sz.rows + 1, lanes] = jnp.where(top, over, from_n[at])
-            ext[f, EXT_ROWS - 1 : EXT_ROWS, lanes] = jnp.where(bottom, over, from_s[at])
+            ext[f, sz.rows : sz.rows + 1, lanes] = jnp.where(even, near, far)
+            ext[f, EXT_ROWS - 1 : EXT_ROWS, lanes] = jnp.where(even, far, near)
     lane9 = lane[: sz.rows]
     end = (sz.tiles - 1) * LANES
     for place, f in enumerate((0, 5, 2, 3, 4)):
@@ -204,6 +201,17 @@
     spare = sz.stack * sz.units
     if spare < tend_ref.shape[0]:
         tend_ref[spare:, :] = jnp.zeros((tend_ref.shape[0] - spare, LANES), jnp.float32)
+    for p, out_ref in enumerate(out_refs):
+        out_ref[...] = tend_ref[piece(sz, p), :]
+
+
+def partner(sz, index, p):
+    return jnp.bitwise_xor(index, p) if isinstance(index, jax.Array) else index ^ p
+
+
+def piece(sz, p):
+    size = sz.share * sz.stack
+    return pl.ds(pl.multiple_of(partner(sz, lax.axis_index("lon"), p) * size, 8), size)
 
 
 def sin_pi(y):
@@ -216,7 +224,11 @@
     return total * y
 
 
-def filter_kernel(sz, cut_ref, n_ref, inverse_ref, in_ref, out_ref):
+def filter_kernel(sz, cut_ref, n_ref, inverse_ref, *refs):
+    in_refs, out_refs, (gathered, results) = refs[: sz.n_lon], refs[sz.n_lon : 2 * sz.n_lon], refs[2 * sz.n_lon :]
+    for p, in_ref in enumerate(in_refs):
+        gathered[piece(sz, p), :] = in_ref[...]
+    size = sz.share * sz.stack
     band, sector = lax.axis_index("lat"), lax.axis_index("lon")
     stack, nlon = sz.stack, sz.nlon
     lane = lax.broadcasted_iota(jnp.int32, (stack, LANES), 1)
@@ -231,7 +243,8 @@
         turns = turns - jnp.round(turns * (0.5 / nlon)) * (2.0 * nlon)
         weights = sin_pi(turns * (1.0 / nlon)) * inverse
         weights = jnp.where(n == 0.0, width * (1.0 / nlon), weights).astype(jnp.bfloat16)
-        pieces = [in_ref[s, stack * i : stack * (i + 1)].astype(jnp.bfloat16) for s in range(sz.n_lon)]
+        starts = [size * s + stack * i for s in range(sz.n_lon)]
+        pieces = [gathered[at : at + stack].astype(jnp.bfloat16) for at in starts]
         circle = jnp.concatenate(
             [jnp.concatenate(pieces[s:] + pieces[:s], axis=0) for s in range(sz.n_lon)], axis=1
         )
@@ -246,10 +259,17 @@
                 same = same + jnp.where(inside, part, 0.0)
                 over = jnp.where(inside, 0.0, part)
                 carried = over if carried is None else carried + over
-            out_ref[s, stack * i : stack * (i + 1)] = pltpu.roll(same, stack - 1, 0) + carried
-
-
-def finish_kernel(sz, cut_ref, h_ref, w_ref, tend_ref, back_ref, new_w_ref, new_h_ref):
+            results[starts[s] : starts[s] + stack] = pltpu.roll(same, stack - 1, 0) + carried
+    for p, out_ref in enumerate(out_refs):
+        out_ref[...] = results[piece(sz, p), :]
+
+
+def finish_kernel(sz, cut_ref, h_ref, w_ref, *refs):
+    tend_refs, back_refs = refs[: sz.n_lon], refs[sz.n_lon : 2 * sz.n_lon]
+    new_w_ref, new_h_ref, tend_ref, back_ref = refs[2 * sz.n_lon :]
+    for p in range(sz.n_lon):
+        tend_ref[piece(sz, p), :] = tend_refs[p][...]
+        back_ref[piece(sz, p), :] = back_refs[p][...]
     band = lax.axis_index("lat")
     row = lax.broadcasted_iota(jnp.int32, (sz.rows, LANES), 0)
     cuts = jnp.zeros((sz.rows, LANES), jnp.int32)
@@ -280,61 +300,66 @@
     band_rows = jax.ShapeDtypeStruct((5 * sz.stack, LANES), f32)
     edge = jax.ShapeDtypeStruct((rows, LANES), f32)
 
-    to_e, to_w, to_n, to_s, to_a = pl.pallas_call(
+    to_e, to_w, to_near, to_far = pl.pallas_call(
         functools.partial(pack_kernel, sz),
-        out_shape=(edge, edge, band_rows, band_rows, band_rows),
+        out_shape=(edge, edge, band_rows, band_rows),
         in_specs=[vmem] * 3,
-        out_specs=(vmem,) * 5,
+        out_specs=(vmem,) * 4,
         compiler_params=params,
         name="pack",
     )(thickness, winds, tracers)
 
-    up = [(i, i + 1) for i in range(n_lat - 1)]
-    down = [(i + 1, i) for i in range(n_lat - 1)]
-    from_s = lax.ppermute(to_n, "lat", up)
-    from_n = lax.ppermute(to_s, "lat", down)
-    poles = [
-        (band * n_lon + i, band * n_lon + (i + n_lon // 2) % n_lon) for band in (0, n_lat - 1) for i in range(n_lon)
-    ]
-    from_a = lax.ppermute(to_a, ("lat", "lon"), poles)
+    near = [(band * n_lon + i, (band ^ 1) * n_lon + i) for band in range(n_lat) for i in range(n_lon)]
+    far = []
+    for band in range(n_lat):
+        other = band - 1 if band % 2 == 0 else band + 1
+        for i in range(n_lon):
+            if 0 <= other < n_lat:
+                far.append((band * n_lon + i, other * n_lon + i))
+            else:
+                far.append((band * n_lon + i, band * n_lon + (i + n_lon // 2) % n_lon))
+    from_near = lax.ppermute(to_near, ("lat", "lon"), near)
+    from_far = lax.ppermute(to_far, ("lat", "lon"), far)
     from_w = lax.ppermute(to_e, "lon", [(i, (i + 1) % n_lon) for i in range(n_lon)])
     from_e = lax.ppermute(to_w, "lon", [((i + 1) % n_lon, i) for i in range(n_lon)])
 
     total = sz.share * n_lon * sz.stack
-    mass, tend = pl.pallas_call(
+    share = jax.ShapeDtypeStruct((sz.share * sz.stack, LANES), f32)
+    all_units = pltpu.VMEM((total, LANES), f32)
+    mass, *tends = pl.pallas_call(
         functools.partial(step_kernel, sz),
-        out_shape=(
-            jax.ShapeDtypeStruct(tracers.shape, jnp.bfloat16),
-            jax.ShapeDtypeStruct((total, LANES), f32),
-        ),
-        in_specs=[vmem] * 9,
-        out_specs=(vmem,) * 2,
-        scratch_shapes=[pltpu.VMEM((6, EXT_ROWS, sz.tiles * LANES), f32)],
+        out_shape=(jax.ShapeDtypeStruct(tracers.shape, jnp.bfloat16),) + (share,) * n_lon,
+        in_specs=[vmem] * 8,
+        out_specs=(vmem,) * (1 + n_lon),
+        scratch_shapes=[all_units, pltpu.VMEM((6, EXT_ROWS, sz.tiles * LANES), f32)],
         compiler_params=params,
         name="step",
-    )(thickness, winds, tracers, from_w, from_e, from_s, from_n, from_a, jnp.asarray(geometry(sz)))
-
-    split = (n_lon, sz.share * sz.stack, LANES)
-    sent = lax.all_to_all(tend.reshape(split), "lon", 0, 0)
+    )(thickness, winds, tracers, from_w, from_e, from_near, from_far, jnp.asarray(geometry(sz)))
+
+    def exchange(shares):
+        pairs = [[(i, partner(sz, i, p)) for i in range(n_lon)] for p in range(n_lon)]
+        return [shares[0]] + [lax.ppermute(shares[p], "lon", pairs[p]) for p in range(1, n_lon)]
+
     n, inverse = offsets(sz)
     worked = pl.pallas_call(
         functools.partial(filter_kernel, sz),
-        out_shape=jax.ShapeDtypeStruct(split, f32),
-        in_specs=[smem] + [vmem] * 3,
-        out_specs=vmem,
+        out_shape=(share,) * n_lon,
+        in_specs=[smem] + [vmem] * (2 + n_lon),
+        out_specs=(vmem,) * n_lon,
+        scratch_shapes=[all_units, all_units],
         compiler_params=params,
         name="filter",
-    )(cutoff, jnp.asarray(n), jnp.asarray(inverse), sent)
-    back = lax.all_to_all(worked, "lon", 0, 0).reshape(total, LANES)
+    )(cutoff, jnp.asarray(n), jnp.asarray(inverse), *exchange(tends))
 
     new_w, new_h = pl.pallas_call(
         functools.partial(finish_kernel, sz),
         out_shape=(jax.ShapeDtypeStruct(winds.shape, f32), jax.ShapeDtypeStruct(thickness.shape, f32)),
-        in_specs=[smem] + [vmem] * 4,
+        in_specs=[smem] + [vmem] * (2 + 2 * n_lon),
         out_specs=(vmem,) * 2,
+        scratch_shapes=[all_units, all_units],
         compiler_params=params,
         name="finish",
-    )(cutoff, thickness, winds, tend, back)
+    )(cutoff, thickness, winds, *tends, *exchange(worked))
     return new_w, new_h, mass
 
 

time: 41.6 us -> 31.9 us (0.77)
  blocking collectives: 9.83 us -> 0 us
  waiting for transfers between devices: 7.04 us -> 9.31 us
  starting transfers between devices: 14.3 us -> 13.1 us
  Pallas kernels: 5.75 us -> 5.11 us
    all_to_all x1 -> x0, blocking collectives: 9.83 us -> none  [local(): sent = lax.all_to_all(tend.reshape(split), 'lon', 0, 0)]
    ppermute x3 -> x8, waiting for transfers between devices: 0.01 us -> 7.09 us  [the longest x6 7.09 us: exchange(): lax.ppermute(shares[p], 'lon', pairs[p])]
    all_to_all x1 -> x0, waiting for transfers between devices: 4.81 us -> none  [local(): back = lax.all_to_all(worked, 'lon', 0, 0).reshape(total, LANES)]
    all_to_all x1 -> x0, starting transfers between devices: 3.45 us -> none  [local(): back = lax.all_to_all(worked, 'lon', 0, 0).reshape(total, LANES)]
    ppermute x3 -> x8, starting transfers between devices: 7.9 us -> 10.2 us  [the longest x6 7.11 us: exchange(): lax.ppermute(shares[p], 'lon', pairs[p])]
    pallas_call x1, Pallas kernels: 2.5 us -> 1.8 us  [local(): pl.pallas_call(functools.partial(filter_kernel, sz), out_shape=(share,) *...]
  transfers between devices with their start and end apart: 6 -> 10, of which waited for: 3 -> 8; matrix products, arithmetic and copies ran while one was open for 2% -> 2% of each run, Pallas kernels for 0% -> 0%
where the time goes in v2:
time: 31.9 us; the launch traced here: 31.7 us
  starting transfers between devices  13.1 us (41%)
  waiting for transfers between devices  9.31 us (29%)
  Pallas kernels  5.11 us (16%)
  local copies, waits for them, and re-layouts  3.51 us (11%)
  between operations  0.69 us (2%)
    ppermute x6, starting transfers between devices, exchange(): lax.ppermute(shares[p], 'lon', pairs[p])  7.11 us
    ppermute x6, waiting for transfers between devices, exchange(): lax.ppermute(shares[p], 'lon', pairs[p])  7.09 us
    unnamed x16, local copies, waits for them, and re-layouts  3.51 us
    ppermute x1, starting transfers between devices, local(): from_far = lax.ppermute(to_far, ('lat', 'lon'), far)  2.59 us
    pallas_call x1, Pallas kernels, local(): pl.pallas_call(functools.partial(filter_kernel, sz), out_shape=(share,) *...  1.8 us
    pallas_call x1, Pallas kernels, local(): pl.pallas_call(functools.partial(step_kernel, sz), out_shape=(jax.ShapeDt...  1.7 us
    ppermute x1, waiting for transfers between devices, local(): lax.ppermute(to_e, 'lon', [(i, (i + 1) % n_lon) for i in range(n_lon)])  1.62 us
    ppermute x1, starting transfers between devices, local(): lax.ppermute(to_e, 'lon', [(i, (i + 1) % n_lon) for i in range(n_lon)])  1.49 us
  transfers between devices with their start and end apart: 10, of which 8 were waited for; matrix products, arithmetic and copies ran while one was open for 2% of the time, Pallas kernels for 0%

profile of v2, /device:TPU:0, one launch (start us, length us, event | category | flops | bytes accessed | tf_op | source)
XLA Modules:
  0.0 31.7 jit_solution(324354502241413725)
XLA Ops:
  0.6 1.0 %copy.13.q_ref = bf16[3,9,2880]{2,1,0:T(8,128)(2,1)S(1)} copy(bf16[3,9,2880]{2,0,1:T(4,128)(2,1)} %param.9) | data formatting | bytes 311040 | tf_op args[2]
  1.7 0.9 %copy-done = f32[9,2880]{1,0:T(8,128)S(1)} copy-done((f32[9,2880]{1,0:T(8,128)S(1)}, f32[9,2880]{1,0:T(8,128)}, u32[]{:S(2)}) %copy-start) | copy-done | bytes 103704
  2.6 0.2 pack.1
  2.7 0.5 %collective-permute-start.2 = (f32[120,128]{1,0:T(8,128)S(1)}, f32[120,128]{1,0:T(8,128)S(1)}, u32[]{:S(2)}, u32[]{:S(2)}) collective-permute-start(f32[120,128]{1,0:T(8,128)S(1)} %get-tuple-element.20), channel_id=1, source_target_pairs={{0,4},{1,5},{2,6},{3,7},{4,0},{5,1},{6,2},{7,3},{8,12},{9,13},{10,... | collective-permute-start | bytes 184328 | tf_op jit(solution)/shard_map/ppermute | solution.py:321
  3.2 2.6 %collective-permute-start.3 = (f32[120,128]{1,0:T(8,128)S(1)}, f32[120,128]{1,0:T(8,128)S(1)}, u32[]{:S(2)}, u32[]{:S(2)}) collective-permute-start(f32[120,128]{1,0:T(8,128)S(1)} %get-tuple-element.21), channel_id=1, source_target_pairs={{0,2},{1,3},{2,0},{3,1},{4,8},{5,9},{6,10},{7,11},{8,4},{9,5},{10,... | collective-permute-start | bytes 184328 | tf_op jit(solution)/shard_map/ppermute | solution.py:322
  5.8 1.5 %collective-permute-start = (f32[9,128]{1,0:T(8,128)S(1)}, f32[9,128]{1,0:T(8,128)S(1)}, u32[]{:S(2)}, u32[]{:S(2)}) collective-permute-start(f32[9,128]{1,0:T(8,128)S(1)} %get-tuple-element.18), channel_id=1, source_target_pairs={{0,1},{1,2},{2,3},{3,0},{4,5},{5,6},{6,7},{7,4},{8,9},{9,10},{10,1... | collective-permute-start | bytes 13832 | tf_op jit(solution)/shard_map/ppermute | solution.py:323
  7.3 1.4 %collective-permute-start.1 = (f32[9,128]{1,0:T(8,128)S(1)}, f32[9,128]{1,0:T(8,128)S(1)}, u32[]{:S(2)}, u32[]{:S(2)}) collective-permute-start(f32[9,128]{1,0:T(8,128)S(1)} %get-tuple-element.19), channel_id=1, source_target_pairs={{1,0},{2,1},{3,2},{0,3},{5,4},{6,5},{7,6},{4,7},{9,8},{10,9},{11,1... | collective-permute-start | bytes 13832 | tf_op jit(solution)/shard_map/ppermute | solution.py:324
  8.8 1.6 %collective-permute-done.from_w = f32[9,128]{1,0:T(8,128)S(1)} collective-permute-done((f32[9,128]{1,0:T(8,128)S(1)}, f32[9,128]{1,0:T(8,128)S(1)}, u32[]{:S(2)}, u32[]{:S(2)}) %collective-permute-start) | collective-permute-done | bytes 4640 | tf_op jit(solution)/shard_map/ppermute | solution.py:323
  10.4 0.6 %collective-permute-done.1.from_e = f32[9,128]{1,0:T(8,128)S(1)} collective-permute-done((f32[9,128]{1,0:T(8,128)S(1)}, f32[9,128]{1,0:T(8,128)S(1)}, u32[]{:S(2)}, u32[]{:S(2)}) %collective-permute-start.1) | collective-permute-done | bytes 4640 | tf_op jit(solution)/shard_map/ppermute | solution.py:324
  11.0 1.7 %step.1 = (bf16[3,9,2880]{2,1,0:T(8,128)(2,1)S(1)}, f32[168,128]{1,0:T(8,128)S(1)}, f32[168,128]{1,0:T(8,128)S(1)}, f32[168,128]{1,0:T(8,128)S(1)}, f32[168,128]{1,0:T(8,128)S(1)}) custom-call(f32[9,2880]{1,0:T(8,128)S(1)} %copy-done, f32[2,9,2880]{2,1,0:T(8,128)S(1)} %copy.14.w_ref, bf16[3,9,2880]{2,1,0:T(8,128)(2,1)S(1)} %copy.13.q_ref, ...), custom_call_target="tpu_custom_call" | custom-call | tf_op jit(solution)/shard_map/step/pallas_call | solution.py:329
  12.7 1.0 %collective-permute-start.4 = (f32[168,128]{1,0:T(8,128)S(1)}, f32[168,128]{1,0:T(8,128)S(1)}, u32[]{:S(2)}, u32[]{:S(2)}) collective-permute-start(f32[168,128]{1,0:T(8,128)S(1)} %get-tuple-element.23.refs_1_), channel_id=1, source_target_pairs={{0,1},{1,0},{2,3},{3,2},{4,5},{5,4},{6,7},{7,6},{8,9},{9,8},{10,11... | collective-permute-start | bytes 258056 | tf_op jit(solution)/shard_map/ppermute | solution.py:341
  13.7 2.0 %collective-permute-start.5 = (f32[168,128]{1,0:T(8,128)S(1)}, f32[168,128]{1,0:T(8,128)S(1)}, u32[]{:S(2)}, u32[]{:S(2)}) collective-permute-start(f32[168,128]{1,0:T(8,128)S(1)} %get-tuple-element.24.refs_2_), channel_id=1, source_target_pairs={{0,2},{1,3},{2,0},{3,1},{4,6},{5,7},{6,4},{7,5},{8,10},{9,11},{10,... | collective-permute-start | bytes 258056 | tf_op jit(solution)/shard_map/ppermute | solution.py:341
  15.7 0.6 %collective-permute-start.6 = (f32[168,128]{1,0:T(8,128)S(1)}, f32[168,128]{1,0:T(8,128)S(1)}, u32[]{:S(2)}, u32[]{:S(2)}) collective-permute-start(f32[168,128]{1,0:T(8,128)S(1)} %get-tuple-element.25.refs_3_), channel_id=1, source_target_pairs={{0,3},{1,2},{2,1},{3,0},{4,7},{5,6},{6,5},{7,4},{8,11},{9,10},{10,... | collective-permute-start | bytes 258056 | tf_op jit(solution)/shard_map/ppermute | solution.py:341
  16.3 1.0 %collective-permute-done.4.refs_1_ = f32[168,128]{1,0:T(8,128)S(1)} collective-permute-done((f32[168,128]{1,0:T(8,128)S(1)}, f32[168,128]{1,0:T(8,128)S(1)}, u32[]{:S(2)}, u32[]{:S(2)}) %collective-permute-start.4) | collective-permute-done | bytes 86048 | tf_op jit(solution)/shard_map/ppermute | solution.py:341
  17.3 1.9 %collective-permute-done.5.refs_2_ = f32[168,128]{1,0:T(8,128)S(1)} collective-permute-done((f32[168,128]{1,0:T(8,128)S(1)}, f32[168,128]{1,0:T(8,128)S(1)}, u32[]{:S(2)}, u32[]{:S(2)}) %collective-permute-start.5) | collective-permute-done | bytes 86048 | tf_op jit(solution)/shard_map/ppermute | solution.py:341
  19.2 1.9 %collective-permute-done.6.refs_3_ = f32[168,128]{1,0:T(8,128)S(1)} collective-permute-done((f32[168,128]{1,0:T(8,128)S(1)}, f32[168,128]{1,0:T(8,128)S(1)}, u32[]{:S(2)}, u32[]{:S(2)}) %collective-permute-start.6) | collective-permute-done | bytes 86048 | tf_op jit(solution)/shard_map/ppermute | solution.py:341
  21.1 1.8 %filter.1 = (f32[168,128]{1,0:T(8,128)S(1)}, f32[168,128]{1,0:T(8,128)S(1)}, f32[168,128]{1,0:T(8,128)S(1)}, f32[168,128]{1,0:T(8,128)S(1)}) custom-call(s32[72]{0:T(128)S(1)} %copy-done.4, f32[192,96]{1,0:T(8,128)S(1)} %copy-done.3, f32[192,96]{1,0:T(8,128)S(1)} %copy-done.2, f32[168,128]{1,0:T(8,128)S(1)} %get-tuple-element.22.refs_0_, ...), custom_call_target="tpu_custom_call" | custom-call | tf_op jit(solution)/shard_map/filter/pallas_call | solution.py:344
  23.0 1.1 %collective-permute-start.8 = (f32[168,128]{1,0:T(8,128)S(1)}, f32[168,128]{1,0:T(8,128)S(1)}, u32[]{:S(2)}, u32[]{:S(2)}) collective-permute-start(f32[168,128]{1,0:T(8,128)S(1)} %get-tuple-element.28), channel_id=1, source_target_pairs={{0,2},{1,3},{2,0},{3,1},{4,6},{5,7},{6,4},{7,5},{8,10},{9,11},{10,... | collective-permute-start | bytes 258056 | tf_op jit(solution)/shard_map/ppermute | solution.py:341
  24.1 2.3 %collective-permute-start.9 = (f32[168,128]{1,0:T(8,128)S(1)}, f32[168,128]{1,0:T(8,128)S(1)}, u32[]{:S(2)}, u32[]{:S(2)}) collective-permute-start(f32[168,128]{1,0:T(8,128)S(1)} %get-tuple-element.29), channel_id=1, source_target_pairs={{0,3},{1,2},{2,1},{3,0},{4,7},{5,6},{6,5},{7,4},{8,11},{9,10},{10,... | collective-permute-start | bytes 258056 | tf_op jit(solution)/shard_map/ppermute | solution.py:341
  26.4 0.8 %copy.16 = bf16[3,9,2880]{2,0,1:T(4,128)(2,1)} copy(bf16[3,9,2880]{2,1,0:T(8,128)(2,1)S(1)} %get-tuple-element.35) | data formatting | bytes 311040
  27.2 0.2 collective-permute-done.7.refs_5_
  27.5 2.0 %collective-permute-done.9.refs_7_ = f32[168,128]{1,0:T(8,128)S(1)} collective-permute-done((f32[168,128]{1,0:T(8,128)S(1)}, f32[168,128]{1,0:T(8,128)S(1)}, u32[]{:S(2)}, u32[]{:S(2)}) %collective-permute-start.9) | collective-permute-done | bytes 86048 | tf_op jit(solution)/shard_map/ppermute | solution.py:341
  29.5 1.5 %finish.1 = (f32[2,9,2880]{2,1,0:T(8,128)S(1)}, f32[9,2880]{1,0:T(8,128)}) custom-call(s32[72]{0:T(128)S(1)} %copy-done.4, f32[9,2880]{1,0:T(8,128)S(1)} %copy-done, f32[2,9,2880]{2,1,0:T(8,128)S(1)} %copy.14.w_ref, f32[168,128]{1,0:T(8,128)S(1)} %get-tuple-element.22.refs_0_, f32[168,128]{1,0:T(8,128)S(1)} %get-tuple-element.23.refs_1_, ...), custom_call_target="tpu_custom_call" | custom-call | tf_op jit(solution)/shard_map/finish/pallas_call | solution.py:354
  30.9 0.8 %copy.15 = f32[2,9,2880]{2,0,1:T(2,128)} copy(f32[2,9,2880]{2,1,0:T(8,128)S(1)} %get-tuple-element.33) | data formatting | bytes 414720
  (16 shorter events, 0.3 us)
Async XLA Ops:
  0.6 1.0 %copy-start.5 = (f32[2,9,2880]{2,0,1:T(2,128)S(1)}, f32[2,9,2880]{2,0,1:T(2,128)}, u32[]{:S(2)}) copy-start(f32[2,9,2880]{2,0,1:T(2,128)} %param.7) | copy-start | bytes 622084
  1.7 0.9 %copy-start = (f32[9,2880]{1,0:T(8,128)S(1)}, f32[9,2880]{1,0:T(8,128)}, u32[]{:S(2)}) copy-start(f32[9,2880]{1,0:T(8,128)} %h_ref.5) | copy-start | bytes 311044
  2.6 8.4 %copy-start.1 = (f32[8,3,16,128]{3,2,1,0:T(8,128)S(1)}, f32[8,3,16,128]{3,2,1,0:T(8,128)}, u32[]{:S(2)}) copy-start(f32[8,3,16,128]{3,2,1,0:T(8,128)} %constant.6.clone.geo_ref) | copy-start | bytes 589828
  2.7 8.2 %collective-permute-start.2 = (f32[120,128]{1,0:T(8,128)S(1)}, f32[120,128]{1,0:T(8,128)S(1)}, u32[]{:S(2)}, u32[]{:S(2)}) collective-permute-start(f32[120,128]{1,0:T(8,128)S(1)} %get-tuple-element.20), channel_id=1, source_target_pairs={{0,4},{1,5},{2,6},{3,7},{4,0},{5,1},{6,2},{7,3},{8,12},{9,13},{10,... | collective-permute-start | bytes 184328 | tf_op jit(solution)/shard_map/ppermute | solution.py:321
  3.2 7.7 %collective-permute-start.3 = (f32[120,128]{1,0:T(8,128)S(1)}, f32[120,128]{1,0:T(8,128)S(1)}, u32[]{:S(2)}, u32[]{:S(2)}) collective-permute-start(f32[120,128]{1,0:T(8,128)S(1)} %get-tuple-element.21), channel_id=1, source_target_pairs={{0,2},{1,3},{2,0},{3,1},{4,8},{5,9},{6,10},{7,11},{8,4},{9,5},{10,... | collective-permute-start | bytes 184328 | tf_op jit(solution)/shard_map/ppermute | solution.py:322
  5.8 4.5 %collective-permute-start = (f32[9,128]{1,0:T(8,128)S(1)}, f32[9,128]{1,0:T(8,128)S(1)}, u32[]{:S(2)}, u32[]{:S(2)}) collective-permute-start(f32[9,128]{1,0:T(8,128)S(1)} %get-tuple-element.18), channel_id=1, source_target_pairs={{0,1},{1,2},{2,3},{3,0},{4,5},{5,6},{6,7},{7,4},{8,9},{9,10},{10,1... | collective-permute-start | bytes 13832 | tf_op jit(solution)/shard_map/ppermute | solution.py:323
  7.3 13.7 %copy-start.2 = (f32[192,96]{1,0:T(8,128)S(1)}, f32[192,96]{1,0:T(8,128)}, u32[]{:S(2)}) copy-start(f32[192,96]{1,0:T(8,128)} %constant.8.clone.inverse_ref) | copy-start | bytes 221188
  7.3 13.7 %copy-start.3 = (f32[192,96]{1,0:T(8,128)S(1)}, f32[192,96]{1,0:T(8,128)}, u32[]{:S(2)}) copy-start(f32[192,96]{1,0:T(8,128)} %constant.7.clone.n_ref) | copy-start | bytes 221188
  7.3 3.7 %collective-permute-start.1 = (f32[9,128]{1,0:T(8,128)S(1)}, f32[9,128]{1,0:T(8,128)S(1)}, u32[]{:S(2)}, u32[]{:S(2)}) collective-permute-start(f32[9,128]{1,0:T(8,128)S(1)} %get-tuple-element.19), channel_id=1, source_target_pairs={{1,0},{2,1},{3,2},{0,3},{5,4},{6,5},{7,6},{4,7},{9,8},{10,9},{11,1... | collective-permute-start | bytes 13832 | tf_op jit(solution)/shard_map/ppermute | solution.py:324
  12.7 4.6 %collective-permute-start.4 = (f32[168,128]{1,0:T(8,128)S(1)}, f32[168,128]{1,0:T(8,128)S(1)}, u32[]{:S(2)}, u32[]{:S(2)}) collective-permute-start(f32[168,128]{1,0:T(8,128)S(1)} %get-tuple-element.23.refs_1_), channel_id=1, source_target_pairs={{0,1},{1,0},{2,3},{3,2},{4,5},{5,4},{6,7},{7,6},{8,9},{9,8},{10,11... | collective-permute-start | bytes 258056 | tf_op jit(solution)/shard_map/ppermute | solution.py:341
  13.7 5.5 %collective-permute-start.5 = (f32[168,128]{1,0:T(8,128)S(1)}, f32[168,128]{1,0:T(8,128)S(1)}, u32[]{:S(2)}, u32[]{:S(2)}) collective-permute-start(f32[168,128]{1,0:T(8,128)S(1)} %get-tuple-element.24.refs_2_), channel_id=1, source_target_pairs={{0,2},{1,3},{2,0},{3,1},{4,6},{5,7},{6,4},{7,5},{8,10},{9,11},{10,... | collective-permute-start | bytes 258056 | tf_op jit(solution)/shard_map/ppermute | solution.py:341
  15.7 5.4 %copy-start.4 = (s32[72]{0:T(128)S(1)}, s32[72]{0:T(128)}, u32[]{:S(2)}) copy-start(s32[72]{0:T(128)} %cut_ref.3) | copy-start | bytes 868
  15.7 5.4 %collective-permute-start.6 = (f32[168,128]{1,0:T(8,128)S(1)}, f32[168,128]{1,0:T(8,128)S(1)}, u32[]{:S(2)}, u32[]{:S(2)}) collective-permute-start(f32[168,128]{1,0:T(8,128)S(1)} %get-tuple-element.25.refs_3_), channel_id=1, source_target_pairs={{0,3},{1,2},{2,1},{3,0},{4,7},{5,6},{6,5},{7,4},{8,11},{9,10},{10,... | collective-permute-start | bytes 258056 | tf_op jit(solution)/shard_map/ppermute | solution.py:341
  22.9 4.6 %collective-permute-start.7 = (f32[168,128]{1,0:T(8,128)S(1)}, f32[168,128]{1,0:T(8,128)S(1)}, u32[]{:S(2)}, u32[]{:S(2)}) collective-permute-start(f32[168,128]{1,0:T(8,128)S(1)} %get-tuple-element.27), channel_id=1, source_target_pairs={{0,1},{1,0},{2,3},{3,2},{4,5},{5,4},{6,7},{7,6},{8,9},{9,8},{10,11... | collective-permute-start | bytes 258056 | tf_op jit(solution)/shard_map/ppermute | solution.py:341
  23.0 4.5 %collective-permute-start.8 = (f32[168,128]{1,0:T(8,128)S(1)}, f32[168,128]{1,0:T(8,128)S(1)}, u32[]{:S(2)}, u32[]{:S(2)}) collective-permute-start(f32[168,128]{1,0:T(8,128)S(1)} %get-tuple-element.28), channel_id=1, source_target_pairs={{0,2},{1,3},{2,0},{3,1},{4,6},{5,7},{6,4},{7,5},{8,10},{9,11},{10,... | collective-permute-start | bytes 258056 | tf_op jit(solution)/shard_map/ppermute | solution.py:341
  24.1 5.4 %collective-permute-start.9 = (f32[168,128]{1,0:T(8,128)S(1)}, f32[168,128]{1,0:T(8,128)S(1)}, u32[]{:S(2)}, u32[]{:S(2)}) collective-permute-start(f32[168,128]{1,0:T(8,128)S(1)} %get-tuple-element.29), channel_id=1, source_target_pairs={{0,3},{1,2},{2,1},{3,0},{4,7},{5,6},{6,5},{7,4},{8,11},{9,10},{10,... | collective-permute-start | bytes 258056 | tf_op jit(solution)/shard_map/ppermute | solution.py:341

commit v3 on v2

v3 whole, which is shorter than its diff:
```python
import functools
import math

import jax
import jax.numpy as jnp
import numpy as np
from jax import lax
from jax.experimental import pallas as pl
from jax.experimental.pallas import tpu as pltpu
from jax.sharding import PartitionSpec as P

LEVELS = 16
TIME_STEP = 0.05
DIFFUSION = 0.5
LANES = 128
PER_TILE = LANES // LEVELS
EXT_ROWS = 16
LIMIT = 48 * 1024 * 1024


class Sizes:
    def __init__(self, rows, merged, n_lat, n_lon):
        self.rows = rows
        self.merged = merged
        self.columns = merged // LEVELS
        self.n_lat = n_lat
        self.n_lon = n_lon
        self.nlat = rows * n_lat
        self.nlon = self.columns * n_lon
        self.ratio = 2.0 * self.nlat / self.nlon
        self.tiles = -(-merged // LANES)
        self.end = (self.tiles - 1) * LANES
        self.tail = merged - self.end
        self.stack = -(-(self.tiles + 1) // 8) * 8
        polar = self.nlat // 6
        self.full = polar // rows
        self.part = polar % rows
        assert self.tail <= LANES - 4 * LEVELS and rows + 2 <= EXT_ROWS and n_lat % 2 == 0

    def span(self, tile):
        return self.tail if tile == self.tiles - 1 else LANES

    def full_bands(self):
        return [b for b in range(self.n_lat) if min(b, self.n_lat - 1 - b) < self.full]

    def part_bands(self):
        return [b for b in range(self.n_lat) if min(b, self.n_lat - 1 - b) == self.full and self.part]

    def part_first(self, band):
        return jnp.where(band < self.n_lat // 2, 0, self.rows - self.part)


def geometry(sz):
    table = np.zeros((sz.n_lat, 3, EXT_ROWS, LANES), np.float64)

    def face(j):
        return math.sin((j + 1) * math.pi / sz.nlat) if 0 <= j < sz.nlat - 1 else 0.0

    for band in range(sz.n_lat):
        for row in range(sz.rows):
            j = band * sz.rows + row
            centre = (j + 0.5) * math.pi / sz.nlat - math.pi / 2
            table[band, 0, row] = 1.0 / math.cos(centre)
            table[band, 1, row] = math.sin(centre)
            table[band, 2, row] = face(j)
        table[band, 2, EXT_ROWS - 1] = face(band * sz.rows - 1)
    return table.astype(np.float32)


def offsets(sz):
    shift, out_tile = np.divmod(np.arange(PER_TILE * sz.stack), sz.stack)
    sector, in_tile = np.divmod(np.arange(sz.n_lon * sz.stack), sz.stack)
    n = (PER_TILE * (out_tile - 1) + shift)[:, None] - (PER_TILE * in_tile + sz.columns * sector)[None, :]
    n = (n + sz.nlon // 2) % sz.nlon - sz.nlon // 2
    with np.errstate(divide="ignore"):
        inverse = np.where(n == 0, 0.0, 1.0 / (sz.nlon * np.sin(np.pi * n / sz.nlon)))
    return n.astype(np.float32), inverse.astype(np.float32)


def rows_kernel(sz, h_hbm, w_hbm, q_hbm, near_ref, far_ref, h_rows, w_rows, q_rows, sems):
    last = sz.rows - 1
    copies = []
    for k, row in enumerate((0, last)):
        copies.append(pltpu.make_async_copy(h_hbm.at[pl.ds(row, 1)], h_rows.at[k], sems.at[k, 0]))
        copies.append(pltpu.make_async_copy(w_hbm.at[row], w_rows.at[k], sems.at[k, 1]))
        copies.append(pltpu.make_async_copy(q_hbm.at[row], q_rows.at[k], sems.at[k, 2]))
    for copy in copies:
        copy.start()
    for copy in copies:
        copy.wait()
    even = lax.rem(lax.axis_index("lat"), 2) == 0
    for t in range(sz.tiles):
        wide = sz.span(t)
        lanes = slice(LANES * t, LANES * t + wide)
        q = [q_rows[k, :, lanes].astype(jnp.float32) for k in range(2)]
        for f in range(5):
            if f == 0:
                first, final = h_rows[0, :, lanes], h_rows[1, :, lanes]
            elif f == 1:
                first, final = w_rows[0, 1:2, lanes], w_rows[1, 1:2, lanes]
            else:
                first, final = q[0][f - 2 : f - 1], q[1][f - 2 : f - 1]
            at = sz.stack * f + t
            near_ref[at : at + 1, :wide] = jnp.where(even, final, first)
            far_ref[at : at + 1, :wide] = jnp.where(even, first, final)


def columns_kernel(sz, h_ref, w_ref, q_ref, after_ref, east_ref, west_ref):
    for f in range(5):
        to = slice(LEVELS * f, LEVELS * (f + 1))

        def load(lanes):
            if f < 2:
                return (h_ref[:, lanes], w_ref[0, :, lanes])[f]
            return q_ref[f - 2, :, lanes].astype(jnp.float32)

        east_ref[:, to] = load(slice(sz.merged - LEVELS, sz.merged))
        west_ref[:, to] = load(slice(0, LEVELS))


def add_rows(sz, ext, fields, near_ref, far_ref):
    band = lax.axis_index("lat")
    even = lax.rem(band, 2) == 0
    over_pole = (band == 0) | (band == sz.n_lat - 1)
    for f in range(fields):
        flip = jnp.where(over_pole, -1.0, 1.0) if f == 1 else 1.0
        for t in range(sz.tiles):
            at = slice(sz.stack * f + t, sz.stack * f + t + 1)
            near, far = near_ref[at], far_ref[at] * flip
            lanes = slice(LANES * t, LANES * (t + 1))
            ext[f, sz.rows : sz.rows + 1, lanes] = jnp.where(even, near, far)
            ext[f, EXT_ROWS - 1 : EXT_ROWS, lanes] = jnp.where(even, far, near)


class Tiles:
    def __init__(self, sz):
        self.sz = sz
        self.lane = lax.broadcasted_iota(jnp.int32, (EXT_ROWS, LANES), 1)
        self.turned = {}

    def turn(self, name, t, value, step):
        key = (name, t % self.sz.tiles, step)
        if key not in self.turned:
            self.turned[key] = pltpu.roll(value(t % self.sz.tiles), step % LANES, 1)
        return self.turned[key]

    def east(self, name, t, value):
        here = self.turn(name, t, value, -LEVELS)
        return jnp.where(self.lane < LANES - LEVELS, here, self.turn(name, t + 1, value, -LEVELS))

    def west(self, name, t, value):
        here = self.turn(name, t, value, LEVELS)
        return jnp.where(self.lane >= LEVELS, here, self.turn(name, t - 1, value, LEVELS))


def north(value):
    return pltpu.roll(value, EXT_ROWS - 1, 0)


def south(value):
    return pltpu.roll(value, 1, 0)


def polar_kernel(sz, h_ref, w_ref, near_ref, far_ref, geo_ref, *refs):
    tend_ref, ext = refs[0], refs[-1]
    band = lax.axis_index("lat")
    ring = Tiles(sz)
    lane = ring.lane
    tiles, stack, rows = sz.tiles, sz.stack, sz.rows
    for f, value in enumerate((h_ref[...], w_ref[1], w_ref[0])):
        ext[f, :rows, sz.end :] = jnp.zeros((rows, LANES), jnp.float32)
        ext[f, :rows, : sz.merged] = value
    add_rows(sz, ext, 2, near_ref, far_ref)
    inv_cos, sin_centre, cos_face = geo_ref[band, 0], geo_ref[band, 1], geo_ref[band, 2]
    ratio = sz.ratio

    def tile(f, t):
        return ext[f, :, LANES * t : LANES * (t + 1)]

    kept = {}

    def zonal(t):
        if t not in kept:
            thick_e = ring.east("h", t, functools.partial(tile, 0))
            wind_e = ring.east("u", t, functools.partial(tile, 2))
            flux = 0.25 * (tile(2, t) + wind_e) * (tile(0, t) + thick_e) * inv_cos
            if t == tiles - 1:
                flux = jnp.where(lane < sz.tail - LEVELS, flux, 0.0)
            kept[t] = (flux, thick_e)
        return kept[t]

    for t in range(tiles):
        flux, thick_e = zonal(t)
        thick, wind_v, wind_u = tile(0, t), tile(1, t), tile(2, t)
        flux_w = ring.west("f", t, lambda s: zonal(s)[0])
        thick_w = ring.west("hw", t, functools.partial(tile, 0))
        thick_n = north(thick)
        flux_n = (0.25 * ratio) * (wind_v + north(wind_v)) * (thick + thick_n) * cos_face
        thick_tend = -((flux - flux_w) + (flux_n - south(flux_n)) * inv_cos)
        wind_u_tend = sin_centre * wind_v - (thick_e - thick_w) * (0.5 * inv_cos)
        wind_v_tend = -sin_centre * wind_u - (0.5 * ratio) * (thick_n - south(thick))
        for f, tend in enumerate((thick_tend, wind_u_tend, wind_v_tend)):
            if t == tiles - 1:
                spare = 0.0
                if f == 0:
                    last = sz.tail - LEVELS
                    columns = [(tile(0, 0), 0), (thick, last), (tile(2, 0), 0), (wind_u, last)]
                    for k, (source, at) in reversed(list(enumerate(columns))):
                        to = sz.tail + LEVELS * k
                        spare = jnp.where(lane < to + LEVELS, pltpu.roll(source, (to - at) % LANES, 1), spare)
                tend = jnp.where(lane < sz.tail, tend, spare)
            tend_ref[pl.ds(stack * rows * f + t, rows, stride=stack), :] = tend[:rows]
    for f in range(3):
        for t in range(tiles, stack):
            tend_ref[pl.ds(stack * rows * f + t, rows, stride=stack), :] = jnp.zeros((rows, LANES), jnp.float32)
    if sz.part:
        size = sz.part * stack
        first = sz.part_first(band)
        for f in range(3):
            start = pl.multiple_of((rows * f + first) * stack, 8)
            refs[1][size * f : size * (f + 1)] = tend_ref[pl.ds(start, size), :]


def rest_kernel(
    sz, h_ref, w_ref, q_ref, from_w, from_e, near_ref, far_ref, geo_ref, new_w_ref, new_h_ref, mass_ref, ext
):
    band = lax.axis_index("lat")
    ring = Tiles(sz)
    lane = ring.lane
    tiles, rows = sz.tiles, sz.rows
    for f in range(6):
        if f < 2 or f == 5:
            value = (h_ref[...], w_ref[1], w_ref[0])[min(f, 2)]
        else:
            value = q_ref[f - 2].astype(jnp.float32)
        ext[f, :rows, : sz.merged] = value
    add_rows(sz, ext, 5, near_ref, far_ref)
    lane9 = lane[:rows]
    for place, f in enumerate((0, 5, 2, 3, 4)):
        after = pltpu.roll(from_e[...], (sz.tail - LEVELS * place) % LANES, 1)
        before = pltpu.roll(from_w[...], (LANES - LEVELS - LEVELS * place) % LANES, 1)
        own = ext[f, :rows, sz.end :]
        edge = jnp.where(lane9 < LANES - LEVELS, after, before)
        ext[f, :rows, sz.end :] = jnp.where(lane9 < sz.tail, own, edge)
    inv_cos, sin_centre, cos_face = geo_ref[band, 0], geo_ref[band, 1], geo_ref[band, 2]
    ratio = sz.ratio

    def tile(f, t):
        return ext[f, :, LANES * t : LANES * (t + 1)]

    kept = {}

    def zonal(t):
        if t not in kept:
            thick_e = ring.east("h", t, functools.partial(tile, 0))
            wind_e = ring.east("u", t, functools.partial(tile, 5))
            flux = 0.25 * (tile(5, t) + wind_e) * (tile(0, t) + thick_e) * inv_cos
            parts = []
            for k in range(3):
                q = tile(2 + k, t)
                q_e = ring.east(k, t, functools.partial(tile, 2 + k))
                parts.append(DIFFUSION * (q_e - q) - flux * (0.5 * (q + q_e)))
            kept[t] = (flux, thick_e, parts)
        return kept[t]

    for t in range(tiles):
        span = sz.span(t)
        lanes = slice(LANES * t, LANES * t + span)
        flux, thick_e, parts = zonal(t)
        thick, wind_u, wind_v = tile(0, t), tile(5, t), tile(1, t)
        flux_w = ring.west("f", t, lambda s: zonal(s)[0])
        thick_w = ring.west("hw", t, functools.partial(tile, 0))
        thick_n = north(thick)
        flux_n = (0.25 * ratio) * (wind_v + north(wind_v)) * (thick + thick_n) * cos_face
        thick_tend = -((flux - flux_w) + (flux_n - south(flux_n)) * inv_cos)
        wind_u_tend = sin_centre * wind_v - (thick_e - thick_w) * (0.5 * inv_cos)
        wind_v_tend = -sin_centre * wind_u - (0.5 * ratio) * (thick_n - south(thick))
        new_h_ref[:, lanes] = (thick + TIME_STEP * thick_tend)[:rows, :span]
        new_w_ref[0, :, lanes] = (wind_u + TIME_STEP * wind_u_tend)[:rows, :span]
        new_w_ref[1, :, lanes] = (wind_v + TIME_STEP * wind_v_tend)[:rows, :span]
        for k in range(3):
            q = tile(2 + k, t)
            q_n = north(q)
            zonal_part = parts[k] - ring.west(("p", k), t, lambda s: zonal(s)[2][k])
            lap = q_n + south(q) - 2.0 * q
            over = flux_n * (0.5 * (q + q_n))
            merid_part = DIFFUSION * lap - (over - south(over)) * inv_cos
            mass = thick * q + TIME_STEP * (zonal_part + merid_part)
            mass_ref[k, :, lanes] = mass[:rows, :span].astype(jnp.bfloat16)


def sin_pi(y):
    y = jnp.where(y > 0.5, 1.0 - y, jnp.where(y < -0.5, -1.0 - y, y))
    s = y * y
    series = [(-1) ** i * math.pi ** (2 * i + 1) / math.factorial(2 * i + 1) for i in range(7)]
    total = series[-1]
    for factor in reversed(series[:-1]):
        total = total * s + factor
    return total * y


def weights_kernel(sz, cut_ref, n_ref, inverse_ref, after_ref, weights_ref):
    band = lax.axis_index("lat")
    size = PER_TILE * sz.stack
    for row in range(sz.rows):
        width = (2 * cut_ref[band * sz.rows + row] + 1).astype(jnp.float32)
        n = n_ref[...]
        turns = n * width
        turns = turns - jnp.round(turns * (0.5 / sz.nlon)) * (2.0 * sz.nlon)
        weights = sin_pi(turns * (1.0 / sz.nlon)) * inverse_ref[...]
        weights = jnp.where(n == 0.0, width * (1.0 / sz.nlon), weights)
        weights_ref[size * row : size * (row + 1)] = weights.astype(jnp.bfloat16)


def filter_rows(sz, pieces, gathered, inv_cos, count, first, weights_ref, results):
    stack, n_lon = sz.stack, sz.n_lon
    lane = lax.broadcasted_iota(jnp.int32, (count, LANES), 1)
    for s, ref in enumerate(pieces):
        gathered[s, : 3 * count * stack] = ref[...]
    sides = [ref[pl.ds(sz.tiles - 1, count, stride=stack), :] for ref in pieces]

    def column(s, k):
        return pltpu.roll(sides[s % n_lon], (-sz.tail - LEVELS * k) % LANES, 1)

    for s in range(n_lon):
        thick_w, thick_e = column(s, 1), column(s + 1, 0)
        flux = 0.25 * (column(s, 3) + column(s + 1, 2)) * (thick_w + thick_e) * inv_cos
        slope = 0.5 * inv_cos
        for f, (west_of, east_of) in enumerate(((flux, flux), (slope * thick_e, slope * thick_w))):
            at = pl.ds(stack * count * f + sz.tiles - 1, count, stride=stack)
            own = gathered[s, at, :]
            own = own - jnp.where(lane >= sz.tail - LEVELS, pltpu.roll(west_of, sz.tail - LEVELS, 1), 0.0)
            gathered[s, at, :] = jnp.where(lane < sz.tail, own, 0.0)
            at = pl.ds(stack * count * f, count, stride=stack)
            after = (s + 1) % n_lon
            gathered[after, at, :] = gathered[after, at, :] + jnp.where(lane < LEVELS, east_of, 0.0)

    wide = lax.broadcasted_iota(jnp.int32, (stack, LANES), 1)
    size = PER_TILE * stack
    for row in range(count):
        starts = [stack * (count * f + row) for f in range(3)]
        circle = jnp.concatenate(
            [jnp.concatenate([gathered[s, at : at + stack] for s in range(n_lon)], axis=0) for at in starts], axis=1
        ).astype(jnp.bfloat16)
        weights = weights_ref[pl.ds(pl.multiple_of(size * (first + row), 16), size), :]
        spread = jnp.dot(weights, circle, preferred_element_type=jnp.float32)
        for f in range(3):
            same = spread[:stack, LANES * f : LANES * (f + 1)]
            carried = None
            for e in range(1, PER_TILE):
                part = spread[stack * e : stack * (e + 1), LANES * f : LANES * (f + 1)]
                part = pltpu.roll(part, LEVELS * e, 1)
                inside = wide >= LEVELS * e
                same = same + jnp.where(inside, part, 0.0)
                over = jnp.where(inside, 0.0, part)
                carried = over if carried is None else carried + over
            start = pl.multiple_of(stack * (sz.rows * f + first + row), 8)
            results[pl.ds(start, stack), :] = pltpu.roll(same, stack - 1, 0) + carried


def filter_kernel(sz, cut_ref, geo_ref, weights_ref, h_ref, w_ref, plain_w_ref, plain_h_ref, *refs):
    n_lon, rows = sz.n_lon, sz.rows
    full_refs, part_refs = refs[:n_lon], refs[n_lon : 2 * n_lon]
    new_w_ref, new_h_ref, gathered, results = refs[-4:]
    band = lax.axis_index("lat")
    from_pole = jnp.minimum(band, sz.n_lat - 1 - band)

    @pl.when(from_pole < sz.full)
    def _():
        filter_rows(sz, full_refs, gathered, geo_ref[band, 0][:rows], rows, 0, weights_ref, results)

    if sz.part:

        @pl.when(from_pole == sz.full)
        def _():
            inv_cos = geo_ref[band, 0]
            low = band < sz.n_lat // 2
            inv_cos = jnp.where(low, inv_cos[: sz.part], inv_cos[rows - sz.part : rows])
            filter_rows(sz, part_refs, gathered, inv_cos, sz.part, sz.part_first(band), weights_ref, results)

    row = lax.broadcasted_iota(jnp.int32, (rows, LANES), 0)
    cuts = jnp.zeros((rows, LANES), jnp.int32)
    for j in range(rows):
        cuts = jnp.where(row == j, cut_ref[band * rows + j], cuts)
    active = cuts < sz.nlon // 2
    for f in range(3):
        for t in range(sz.tiles):
            span = sz.span(t)
            lanes = slice(LANES * t, LANES * t + span)
            tend = results[pl.ds(sz.stack * rows * f + t, rows, stride=sz.stack), :][:, :span]
            if f == 0:
                new = h_ref[:, lanes] + TIME_STEP * tend
                new_h_ref[:, lanes] = jnp.where(active[:, :span], new, plain_h_ref[:, lanes])
            else:
                new = w_ref[f - 1, :, lanes] + TIME_STEP * tend
                new_w_ref[f - 1, :, lanes] = jnp.where(active[:, :span], new, plain_w_ref[f - 1, :, lanes])


def local(winds, thickness, tracers, cutoff):
    n_lat = lax.axis_size("lat")
    n_lon = lax.axis_size("lon")
    rows, merged = thickness.shape
    sz = Sizes(rows, merged, n_lat, n_lon)
    f32 = jnp.float32
    vmem = pl.BlockSpec(memory_space=pltpu.VMEM)
    smem = pl.BlockSpec(memory_space=pltpu.SMEM)
    hbm = pl.BlockSpec(memory_space=pl.ANY)

    def shaped(*shape):
        return jax.ShapeDtypeStruct(shape, f32)

    def call(kernel, name, in_specs, out_shape, scratch=()):
        return pl.pallas_call(
            functools.partial(kernel, sz),
            out_shape=out_shape,
            in_specs=in_specs,
            out_specs=jax.tree.map(lambda _: vmem, out_shape),
            scratch_shapes=list(scratch),
            compiler_params=pltpu.CompilerParams(vmem_limit_bytes=LIMIT),
            name=name,
        )

    def over_circles(value, bands, step):
        pairs = [(b * n_lon + (i + step) % n_lon, b * n_lon + i) for b in bands for i in range(n_lon)]
        return lax.ppermute(value, ("lat", "lon"), pairs)

    geo = jnp.asarray(geometry(sz))
    n, inverse = (jnp.asarray(table) for table in offsets(sz))

    row_pair = shaped(5 * sz.stack, LANES)
    to_near, to_far = call(
        rows_kernel,
        "rows",
        [hbm] * 3,
        (row_pair, row_pair),
        [
            pltpu.VMEM((2, 1, merged), f32),
            pltpu.VMEM((2, 2, merged), f32),
            pltpu.VMEM((2, 3, merged), jnp.bfloat16),
            pltpu.SemaphoreType.DMA((2, 3)),
        ],
    )(thickness, jnp.swapaxes(winds, 0, 1), jnp.swapaxes(tracers, 0, 1))

    near = [(band * n_lon + i, (band ^ 1) * n_lon + i) for band in range(n_lat) for i in range(n_lon)]
    far = []
    for band in range(n_lat):
        other = band - 1 if band % 2 == 0 else band + 1
        for i in range(n_lon):
            if 0 <= other < n_lat:
                far.append((band * n_lon + i, other * n_lon + i))
            else:
                far.append((band * n_lon + i, band * n_lon + (i + n_lon // 2) % n_lon))
    from_near = lax.ppermute(to_near, ("lat", "lon"), near)
    from_far = lax.ppermute(to_far, ("lat", "lon"), far)

    tend_shapes = [shaped(3 * rows * sz.stack, LANES)]
    if sz.part:
        tend_shapes.append(shaped(3 * sz.part * sz.stack, LANES))
    tends = call(
        polar_kernel, "polar", [vmem] * 5, tend_shapes, [pltpu.VMEM((3, EXT_ROWS, sz.tiles * LANES), f32)]
    )(thickness, winds, from_near, from_far, geo)
    circles = []
    for tend, bands in zip(tends, (sz.full_bands(), sz.part_bands())):
        circles += [tend] + [over_circles(tend, bands, step) for step in range(1, n_lon)]

    weights = call(
        weights_kernel,
        "weights",
        [smem, vmem, vmem, hbm],
        jax.ShapeDtypeStruct((rows * PER_TILE * sz.stack, n_lon * sz.stack), jnp.bfloat16),
    )(cutoff, n, inverse, tends[0])

    edge = shaped(rows, LANES)
    to_e, to_w = call(columns_kernel, "columns", [vmem] * 3 + [hbm], (edge, edge))(
        thickness, winds, tracers, tends[0]
    )
    everywhere = range(n_lat)
    from_w = over_circles(to_e, everywhere, n_lon - 1)
    from_e = over_circles(to_w, everywhere, 1)

    plain_w, plain_h, mass = call(
        rest_kernel,
        "rest",
        [vmem] * 8,
        (shaped(*winds.shape), shaped(rows, merged), jax.ShapeDtypeStruct(tracers.shape, jnp.bfloat16)),
        [pltpu.VMEM((6, EXT_ROWS, sz.tiles * LANES), f32)],
    )(thickness, winds, tracers, from_w, from_e, from_near, from_far, geo)

    new_w, new_h = call(
        filter_kernel,
        "filter",
        [smem] + [vmem] * (6 + len(circles)),
        (shaped(*winds.shape), shaped(rows, merged)),
        [
            pltpu.VMEM((n_lon, 3 * rows * sz.stack, LANES), f32),
            pltpu.VMEM((3 * rows * sz.stack, LANES), f32),
        ],
    )(cutoff, geo, weights, thickness, winds, plain_w, plain_h, *circles)
    return new_w, new_h, mass


def solution(mesh):
    in_specs = (P(None, "lat", "lon"), P("lat", "lon"), P(None, "lat", "lon"), P())
    out_specs = (P(None, "lat", "lon"), P("lat", "lon"), P(None, "lat", "lon"))
    return jax.shard_map(local, mesh=mesh, in_specs=in_specs, out_specs=out_specs, check_vma=False)
```

time: 31.9 us -> 38.7 us (1.21)
  starting transfers between devices: 13.1 us -> 17.4 us
  Pallas kernels: 5.11 us -> 6.63 us
  local copies, waits for them, and re-layouts: 3.51 us -> 4.44 us
    ppermute x8, starting transfers between devices: 10 us -> 14.3 us  [over_circles(): return lax.ppermute(value, ('lat', 'lon'), pairs)]
    ppermute x8, waiting for transfers between devices: 9.3 us -> 6.94 us  [over_circles(): return lax.ppermute(value, ('lat', 'lon'), pairs)]
    ppermute x1, waiting for transfers between devices: 0.01 us -> 2.14 us  [local(): from_far = lax.ppermute(to_far, ('lat', 'lon'), far)]
    pallas_call x4 -> x6, Pallas kernels: 5.11 us -> 6.63 us  [the longest x1 2.43 us: local(): call(filter_kernel, 'filter', [smem] + [vmem] * (6 + len(circles)), (shap...]
    unnamed x16 -> x22, local copies, waits for them, and re-layouts: 3.51 us -> 4.44 us
  transfers between devices with their start and end apart: 10 -> 10, of which waited for: 8 -> 3; matrix products, arithmetic and copies ran while one was open for 2% -> 2% of each run, Pallas kernels for 0% -> 8%
where the time goes in v3:
time: 38.7 us; the launch traced here: 38.4 us
  starting transfers between devices  17.4 us (45%)
  waiting for transfers between devices  9.08 us (23%)
  Pallas kernels  6.63 us (17%)
  local copies, waits for them, and re-layouts  4.44 us (11%)
  between operations  0.84 us (2%)
    ppermute x8, starting transfers between devices, over_circles(): return lax.ppermute(value, ('lat', 'lon'), pairs)  14.3 us
    ppermute x8, waiting for transfers between devices, over_circles(): return lax.ppermute(value, ('lat', 'lon'), pairs)  6.94 us
    unnamed x22, local copies, waits for them, and re-layouts  4.44 us
    ppermute x1, starting transfers between devices, local(): from_far = lax.ppermute(to_far, ('lat', 'lon'), far)  2.6 us
    pallas_call x1, Pallas kernels, local(): call(filter_kernel, 'filter', [smem] + [vmem] * (6 + len(circles)), (shap...  2.43 us
    ppermute x1, waiting for transfers between devices, local(): from_far = lax.ppermute(to_far, ('lat', 'lon'), far)  2.14 us
    pallas_call x1, Pallas kernels, local(): call(rest_kernel, 'rest', [vmem] * 8, (shaped(*winds.shape), shaped(rows,...  1.68 us
    pallas_call x1, Pallas kernels, local(): call(weights_kernel, 'weights', [smem, vmem, vmem, hbm], jax.ShapeDtypeSt...  1.43 us
  transfers between devices with their start and end apart: 10, of which 3 were waited for; matrix products, arithmetic and copies ran while one was open for 2% of the time, Pallas kernels for 8%

profile of v3, /device:TPU:0, one launch (start us, length us, event | category | flops | bytes accessed | tf_op | source)
XLA Modules:
  0.0 38.4 jit_solution(1952193305102061517)
XLA Ops:
  0.6 0.9 %copy-done = f32[9,2880]{1,0:T(8,128)S(1)} copy-done((f32[9,2880]{1,0:T(8,128)S(1)}, f32[9,2880]{1,0:T(8,128)}, u32[]{:S(2)}) %copy-start) | copy-done | bytes 103704
  1.6 0.9 %copy-done.3 = f32[2,9,2880]{2,0,1:T(2,128)S(1)} copy-done((f32[2,9,2880]{2,0,1:T(2,128)S(1)}, f32[2,9,2880]{2,0,1:T(2,128)}, u32[]{:S(2)}) %copy-start.3) | copy-done | bytes 207384
  2.5 0.9 %copy-done.4 = bf16[3,9,2880]{2,0,1:T(4,128)(2,1)S(1)} copy-done((bf16[3,9,2880]{2,0,1:T(4,128)(2,1)S(1)}, bf16[3,9,2880]{2,0,1:T(4,128)(2,1)}, u32[]{:S(2)}) %copy-start.4) | copy-done | bytes 155544
  3.4 0.3 rows.1
  3.7 0.5 %collective-permute-start = (f32[120,128]{1,0:T(8,128)S(1)}, f32[120,128]{1,0:T(8,128)S(1)}, u32[]{:S(2)}, u32[]{:S(2)}) collective-permute-start(f32[120,128]{1,0:T(8,128)S(1)} %get-tuple-element.14), channel_id=1, source_target_pairs={{0,4},{1,5},{2,6},{3,7},{4,0},{5,1},{6,2},{7,3},{8,12},{9,13},{10,... | collective-permute-start | bytes 184328 | tf_op jit(solution)/shard_map/ppermute | solution.py:453
  4.2 2.6 %collective-permute-start.1 = (f32[120,128]{1,0:T(8,128)S(1)}, f32[120,128]{1,0:T(8,128)S(1)}, u32[]{:S(2)}, u32[]{:S(2)}) collective-permute-start(f32[120,128]{1,0:T(8,128)S(1)} %get-tuple-element.15), channel_id=1, source_target_pairs={{0,2},{1,3},{2,0},{3,1},{4,8},{5,9},{6,10},{7,11},{8,4},{9,5},{10,... | collective-permute-start | bytes 184328 | tf_op jit(solution)/shard_map/ppermute | solution.py:454
  6.9 2.1 %collective-permute-done.1.far_ref = f32[120,128]{1,0:T(8,128)S(1)} collective-permute-done((f32[120,128]{1,0:T(8,128)S(1)}, f32[120,128]{1,0:T(8,128)S(1)}, u32[]{:S(2)}, u32[]{:S(2)}) %collective-permute-start.1) | collective-permute-done | bytes 61472 | tf_op jit(solution)/shard_map/ppermute | solution.py:454
  9.0 0.8 %polar.1 = (f32[648,128]{1,0:T(8,128)S(1)}, f32[216,128]{1,0:T(8,128)S(1)}) custom-call(f32[9,2880]{1,0:T(8,128)S(1)} %copy-done, f32[2,9,2880]{2,1,0:T(8,128)S(1)} %copy.10.w_ref, f32[120,128]{1,0:T(8,128)S(1)} %collective-permute-done.near_ref, f32[120,128]{1,0:T(8,128)S(1)} %collective-permute-done.1.far_ref, f32[8,3,16,128]{3,2,1,0:T(8,128)S(1)} %copy-done.2), custom_call_target="tpu_custom_call" | custom-call | tf_op jit(solution)/shard_map/polar/pallas_call | solution.py:459
  9.8 3.9 %collective-permute-start.6 = (f32[648,128]{1,0:T(8,128)S(1)}, f32[648,128]{1,0:T(8,128)S(1)}, u32[]{:S(2)}, u32[]{:S(2)}) collective-permute-start(f32[648,128]{1,0:T(8,128)S(1)} %get-tuple-element.16.after_ref.refs_0_), channel_id=1, source_target_pairs={{3,0},{0,1},{1,2},{2,3},{31,28},{28,29},{29,30},{30,31}} | collective-permute-start | bytes 995336 | tf_op jit(solution)/shard_map/ppermute | solution.py:425
  13.7 3.4 %collective-permute-start.5 = (f32[648,128]{1,0:T(8,128)S(1)}, f32[648,128]{1,0:T(8,128)S(1)}, u32[]{:S(2)}, u32[]{:S(2)}) collective-permute-start(f32[648,128]{1,0:T(8,128)S(1)} %get-tuple-element.16.after_ref.refs_0_), channel_id=1, source_target_pairs={{2,0},{3,1},{0,2},{1,3},{30,28},{31,29},{28,30},{29,31}} | collective-permute-start | bytes 995336 | tf_op jit(solution)/shard_map/ppermute | solution.py:425
  17.1 3.3 %collective-permute-start.4 = (f32[648,128]{1,0:T(8,128)S(1)}, f32[648,128]{1,0:T(8,128)S(1)}, u32[]{:S(2)}, u32[]{:S(2)}) collective-permute-start(f32[648,128]{1,0:T(8,128)S(1)} %get-tuple-element.16.after_ref.refs_0_), channel_id=1, source_target_pairs={{1,0},{2,1},{3,2},{0,3},{29,28},{30,29},{31,30},{28,31}} | collective-permute-start | bytes 995336 | tf_op jit(solution)/shard_map/ppermute | solution.py:425
  20.5 0.7 %collective-permute-start.9 = (f32[216,128]{1,0:T(8,128)S(1)}, f32[216,128]{1,0:T(8,128)S(1)}, u32[]{:S(2)}, u32[]{:S(2)}) collective-permute-start(f32[216,128]{1,0:T(8,128)S(1)} %get-tuple-element.21.refs_4_), channel_id=1, source_target_pairs={{7,4},{4,5},{5,6},{6,7},{27,24},{24,25},{25,26},{26,27}} | collective-permute-start | bytes 331784 | tf_op jit(solution)/shard_map/ppermute | solution.py:425
  21.2 0.1 columns.1
  21.3 0.6 %collective-permute-start.2 = (f32[9,128]{1,0:T(8,128)S(1)}, f32[9,128]{1,0:T(8,128)S(1)}, u32[]{:S(2)}, u32[]{:S(2)}) collective-permute-start(f32[9,128]{1,0:T(8,128)S(1)} %get-tuple-element.17), channel_id=1, source_target_pairs={{3,0},{0,1},{1,2},{2,3},{7,4},{4,5},{5,6},{6,7},{11,8},{8,9},{9,10... | collective-permute-start | bytes 13832 | tf_op jit(solution)/shard_map/ppermute | solution.py:425
  22.0 4.3 %collective-permute-done.2.from_w = f32[9,128]{1,0:T(8,128)S(1)} collective-permute-done((f32[9,128]{1,0:T(8,128)S(1)}, f32[9,128]{1,0:T(8,128)S(1)}, u32[]{:S(2)}, u32[]{:S(2)}) %collective-permute-start.2) | collective-permute-done | bytes 4640 | tf_op jit(solution)/shard_map/ppermute | solution.py:425
  26.3 1.0 %collective-permute-start.3 = (f32[9,128]{1,0:T(8,128)S(1)}, f32[9,128]{1,0:T(8,128)S(1)}, u32[]{:S(2)}, u32[]{:S(2)}) collective-permute-start(f32[9,128]{1,0:T(8,128)S(1)} %get-tuple-element.18), channel_id=1, source_target_pairs={{1,0},{2,1},{3,2},{0,3},{5,4},{6,5},{7,6},{4,7},{9,8},{10,9},{11,1... | collective-permute-start | bytes 13832 | tf_op jit(solution)/shard_map/ppermute | solution.py:425
  27.3 2.6 %collective-permute-done.3.from_e = f32[9,128]{1,0:T(8,128)S(1)} collective-permute-done((f32[9,128]{1,0:T(8,128)S(1)}, f32[9,128]{1,0:T(8,128)S(1)}, u32[]{:S(2)}, u32[]{:S(2)}) %collective-permute-start.3) | collective-permute-done | bytes 4640 | tf_op jit(solution)/shard_map/ppermute | solution.py:425
  29.9 0.7 %collective-permute-start.8 = (f32[216,128]{1,0:T(8,128)S(1)}, f32[216,128]{1,0:T(8,128)S(1)}, u32[]{:S(2)}, u32[]{:S(2)}) collective-permute-start(f32[216,128]{1,0:T(8,128)S(1)} %get-tuple-element.21.refs_4_), channel_id=1, source_target_pairs={{6,4},{7,5},{4,6},{5,7},{26,24},{27,25},{24,26},{25,27}} | collective-permute-start | bytes 331784 | tf_op jit(solution)/shard_map/ppermute | solution.py:425
  30.6 0.7 %collective-permute-start.7 = (f32[216,128]{1,0:T(8,128)S(1)}, f32[216,128]{1,0:T(8,128)S(1)}, u32[]{:S(2)}, u32[]{:S(2)}) collective-permute-start(f32[216,128]{1,0:T(8,128)S(1)} %get-tuple-element.21.refs_4_), channel_id=1, source_target_pairs={{5,4},{6,5},{7,6},{4,7},{25,24},{26,25},{27,26},{24,27}} | collective-permute-start | bytes 331784 | tf_op jit(solution)/shard_map/ppermute | solution.py:425
  31.3 1.4 %weights.1.weights_ref = bf16[1728,96]{1,0:T(8,128)(2,1)S(1)} custom-call(s32[72]{0:T(128)S(1)} %copy-done.8, f32[192,96]{1,0:T(8,128)S(1)} %copy-done.7, f32[192,96]{1,0:T(8,128)S(1)} %copy-done.6, f32[648,128]{1,0:T(8,128)S(1)} %get-tuple-element.16.after_ref.refs_0_), custom_call_target="tpu_custom_call" | custom-call | tf_op jit(solution)/shard_map/weights/pallas_call | solution.py:466
  32.7 1.7 %rest.1 = (f32[2,9,2880]{2,1,0:T(8,128)S(1)}, f32[9,2880]{1,0:T(8,128)S(1)}, bf16[3,9,2880]{2,1,0:T(8,128)(2,1)S(1)}) custom-call(f32[9,2880]{1,0:T(8,128)S(1)} %copy-done.1, f32[2,9,2880]{2,1,0:T(8,128)S(1)} %copy.10.w_ref, bf16[3,9,2880]{2,1,0:T(8,128)(2,1)S(1)} %copy.14.q_ref, f32[9,128]{1,0:T(8,128)S(1)} %collective-permute-done.2.from_w, ...), custom_call_target="tpu_custom_call" | custom-call | tf_op jit(solution)/shard_map/rest/pallas_call | solution.py:481
  34.4 0.8 %copy.17 = bf16[3,9,2880]{2,0,1:T(4,128)(2,1)} copy(bf16[3,9,2880]{2,1,0:T(8,128)(2,1)S(1)} %get-tuple-element.27) | data formatting | bytes 311040
  35.2 2.4 %filter.1 = (f32[2,9,2880]{2,1,0:T(8,128)S(1)}, f32[9,2880]{1,0:T(8,128)}) custom-call(s32[72]{0:T(128)S(1)} %copy-done.8, f32[8,3,16,128]{3,2,1,0:T(8,128)S(1)} %copy-done.2, bf16[1728,96]{1,0:T(8,128)(2,1)S(1)} %weights.1.weights_ref, f32[9,2880]{1,0:T(8,128)S(1)} %copy-done.1, f32[2,9,2880]{2,1,0:T(8,128)S(1)} %copy.10.w_ref, ...), custom_call_target="tpu_custom_call" | custom-call | tf_op jit(solution)/shard_map/filter/pallas_call | solution.py:489
  37.6 0.8 %copy.16 = f32[2,9,2880]{2,0,1:T(2,128)} copy(f32[2,9,2880]{2,1,0:T(8,128)S(1)} %get-tuple-element.25) | data formatting | bytes 414720
  (24 shorter events, 0.1 us)
Async XLA Ops:
  0.6 0.9 %copy-start = (f32[9,2880]{1,0:T(8,128)S(1)}, f32[9,2880]{1,0:T(8,128)}, u32[]{:S(2)}) copy-start(f32[9,2880]{1,0:T(8,128)} %h_ref.7) | copy-start | bytes 311044
  1.6 0.9 %copy-start.3 = (f32[2,9,2880]{2,0,1:T(2,128)S(1)}, f32[2,9,2880]{2,0,1:T(2,128)}, u32[]{:S(2)}) copy-start(f32[2,9,2880]{2,0,1:T(2,128)} %param.7) | copy-start | bytes 622084
  2.5 0.9 %copy-start.4 = (bf16[3,9,2880]{2,0,1:T(4,128)(2,1)S(1)}, bf16[3,9,2880]{2,0,1:T(4,128)(2,1)}, u32[]{:S(2)}) copy-start(bf16[3,9,2880]{2,0,1:T(4,128)(2,1)} %param.9) | copy-start | bytes 466564
  3.7 3.2 %collective-permute-start = (f32[120,128]{1,0:T(8,128)S(1)}, f32[120,128]{1,0:T(8,128)S(1)}, u32[]{:S(2)}, u32[]{:S(2)}) collective-permute-start(f32[120,128]{1,0:T(8,128)S(1)} %get-tuple-element.14), channel_id=1, source_target_pairs={{0,4},{1,5},{2,6},{3,7},{4,0},{5,1},{6,2},{7,3},{8,12},{9,13},{10,... | collective-permute-start | bytes 184328 | tf_op jit(solution)/shard_map/ppermute | solution.py:453
  4.2 4.8 %copy-start.2 = (f32[8,3,16,128]{3,2,1,0:T(8,128)S(1)}, f32[8,3,16,128]{3,2,1,0:T(8,128)}, u32[]{:S(2)}) copy-start(f32[8,3,16,128]{3,2,1,0:T(8,128)} %constant.6.clone.geo_ref) | copy-start | bytes 589828
  4.2 4.8 %collective-permute-start.1 = (f32[120,128]{1,0:T(8,128)S(1)}, f32[120,128]{1,0:T(8,128)S(1)}, u32[]{:S(2)}, u32[]{:S(2)}) collective-permute-start(f32[120,128]{1,0:T(8,128)S(1)} %get-tuple-element.15), channel_id=1, source_target_pairs={{0,2},{1,3},{2,0},{3,1},{4,8},{5,9},{6,10},{7,11},{8,4},{9,5},{10,... | collective-permute-start | bytes 184328 | tf_op jit(solution)/shard_map/ppermute | solution.py:454
  6.8 14.3 %copy-start.5 = (bf16[3,9,2880]{2,0,1:T(4,128)(2,1)S(1)}, bf16[3,9,2880]{2,0,1:T(4,128)(2,1)}, u32[]{:S(2)}) copy-start(bf16[3,9,2880]{2,0,1:T(4,128)(2,1)} %param.9) | copy-start | bytes 466564
  9.8 25.4 %collective-permute-start.6 = (f32[648,128]{1,0:T(8,128)S(1)}, f32[648,128]{1,0:T(8,128)S(1)}, u32[]{:S(2)}, u32[]{:S(2)}) collective-permute-start(f32[648,128]{1,0:T(8,128)S(1)} %get-tuple-element.16.after_ref.refs_0_), channel_id=1, source_target_pairs={{3,0},{0,1},{1,2},{2,3},{31,28},{28,29},{29,30},{30,31}} | collective-permute-start | bytes 995336 | tf_op jit(solution)/shard_map/ppermute | solution.py:425
  13.7 21.5 %collective-permute-start.5 = (f32[648,128]{1,0:T(8,128)S(1)}, f32[648,128]{1,0:T(8,128)S(1)}, u32[]{:S(2)}, u32[]{:S(2)}) collective-permute-start(f32[648,128]{1,0:T(8,128)S(1)} %get-tuple-element.16.after_ref.refs_0_), channel_id=1, source_target_pairs={{2,0},{3,1},{0,2},{1,3},{30,28},{31,29},{28,30},{29,31}} | collective-permute-start | bytes 995336 | tf_op jit(solution)/shard_map/ppermute | solution.py:425
  17.1 18.1 %collective-permute-start.4 = (f32[648,128]{1,0:T(8,128)S(1)}, f32[648,128]{1,0:T(8,128)S(1)}, u32[]{:S(2)}, u32[]{:S(2)}) collective-permute-start(f32[648,128]{1,0:T(8,128)S(1)} %get-tuple-element.16.after_ref.refs_0_), channel_id=1, source_target_pairs={{1,0},{2,1},{3,2},{0,3},{29,28},{30,29},{31,30},{28,31}} | collective-permute-start | bytes 995336 | tf_op jit(solution)/shard_map/ppermute | solution.py:425
  20.5 10.1 %collective-permute-start.9 = (f32[216,128]{1,0:T(8,128)S(1)}, f32[216,128]{1,0:T(8,128)S(1)}, u32[]{:S(2)}, u32[]{:S(2)}) collective-permute-start(f32[216,128]{1,0:T(8,128)S(1)} %get-tuple-element.21.refs_4_), channel_id=1, source_target_pairs={{7,4},{4,5},{5,6},{6,7},{27,24},{24,25},{25,26},{26,27}} | collective-permute-start | bytes 331784 | tf_op jit(solution)/shard_map/ppermute | solution.py:425
  21.2 10.1 %copy-start.6 = (f32[192,96]{1,0:T(8,128)S(1)}, f32[192,96]{1,0:T(8,128)}, u32[]{:S(2)}) copy-start(f32[192,96]{1,0:T(8,128)} %constant.8.clone.inverse_ref) | copy-start | bytes 221188
  21.2 10.1 %copy-start.7 = (f32[192,96]{1,0:T(8,128)S(1)}, f32[192,96]{1,0:T(8,128)}, u32[]{:S(2)}) copy-start(f32[192,96]{1,0:T(8,128)} %constant.7.clone.n_ref) | copy-start | bytes 221188
  21.3 10.0 %copy-start.8 = (s32[72]{0:T(128)S(1)}, s32[72]{0:T(128)}, u32[]{:S(2)}) copy-start(s32[72]{0:T(128)} %cut_ref.3) | copy-start | bytes 868
  21.3 4.9 %collective-permute-start.2 = (f32[9,128]{1,0:T(8,128)S(1)}, f32[9,128]{1,0:T(8,128)S(1)}, u32[]{:S(2)}, u32[]{:S(2)}) collective-permute-start(f32[9,128]{1,0:T(8,128)S(1)} %get-tuple-element.17), channel_id=1, source_target_pairs={{3,0},{0,1},{1,2},{2,3},{7,4},{4,5},{5,6},{6,7},{11,8},{8,9},{9,10... | collective-permute-start | bytes 13832 | tf_op jit(solution)/shard_map/ppermute | solution.py:425
  26.2 6.5 %copy-start.1 = (f32[9,2880]{1,0:T(8,128)S(1)}, f32[9,2880]{1,0:T(8,128)}, u32[]{:S(2)}) copy-start(f32[9,2880]{1,0:T(8,128)} %h_ref.7) | copy-start | bytes 311044
  26.3 3.7 %collective-permute-start.3 = (f32[9,128]{1,0:T(8,128)S(1)}, f32[9,128]{1,0:T(8,128)S(1)}, u32[]{:S(2)}, u32[]{:S(2)}) collective-permute-start(f32[9,128]{1,0:T(8,128)S(1)} %get-tuple-element.18), channel_id=1, source_target_pairs={{1,0},{2,1},{3,2},{0,3},{5,4},{6,5},{7,6},{4,7},{9,8},{10,9},{11,1... | collective-permute-start | bytes 13832 | tf_op jit(solution)/shard_map/ppermute | solution.py:425
  29.9 5.3 %collective-permute-start.8 = (f32[216,128]{1,0:T(8,128)S(1)}, f32[216,128]{1,0:T(8,128)S(1)}, u32[]{:S(2)}, u32[]{:S(2)}) collective-permute-start(f32[216,128]{1,0:T(8,128)S(1)} %get-tuple-element.21.refs_4_), channel_id=1, source_target_pairs={{6,4},{7,5},{4,6},{5,7},{26,24},{27,25},{24,26},{25,27}} | collective-permute-start | bytes 331784 | tf_op jit(solution)/shard_map/ppermute | solution.py:425
  30.6 4.6 %collective-permute-start.7 = (f32[216,128]{1,0:T(8,128)S(1)}, f32[216,128]{1,0:T(8,128)S(1)}, u32[]{:S(2)}, u32[]{:S(2)}) collective-permute-start(f32[216,128]{1,0:T(8,128)S(1)} %get-tuple-element.21.refs_4_), channel_id=1, source_target_pairs={{5,4},{6,5},{7,6},{4,7},{25,24},{26,25},{27,26},{24,27}} | collective-permute-start | bytes 331784 | tf_op jit(solution)/shard_map/ppermute | solution.py:425

commit v4 on v3

--- a/solution.py
+++ b/solution.py
@@ -16,6 +16,7 @@
 PER_TILE = LANES // LEVELS
 EXT_ROWS = 16
 LIMIT = 48 * 1024 * 1024
+ALL_VMEM = 64 * 1024 * 1024 - 256 * 1024
 
 
 class Sizes:
@@ -36,6 +37,7 @@
         self.full = polar // rows
         self.part = polar % rows
         assert self.tail <= LANES - 4 * LEVELS and rows + 2 <= EXT_ROWS and n_lat % 2 == 0
+        assert n_lon & (n_lon - 1) == 0
 
     def span(self, tile):
         return self.tail if tile == self.tiles - 1 else LANES
@@ -313,11 +315,13 @@
 
 
 def filter_rows(sz, pieces, gathered, inv_cos, count, first, weights_ref, results):
+    here = lax.axis_index("lon")
     stack, n_lon = sz.stack, sz.n_lon
     lane = lax.broadcasted_iota(jnp.int32, (count, LANES), 1)
-    for s, ref in enumerate(pieces):
-        gathered[s, : 3 * count * stack] = ref[...]
-    sides = [ref[pl.ds(sz.tiles - 1, count, stride=stack), :] for ref in pieces]
+    for turn, ref in enumerate(pieces):
+        eastward = lax.rem(jnp.bitwise_xor(here, turn) - here + n_lon, n_lon)
+        gathered[eastward, : 3 * count * stack] = ref[...]
+    sides = [gathered[s, pl.ds(sz.tiles - 1, count, stride=stack), :] for s in range(n_lon)]
 
     def column(s, k):
         return pltpu.roll(sides[s % n_lon], (-sz.tail - LEVELS * k) % LANES, 1)
@@ -404,25 +408,26 @@
     f32 = jnp.float32
     vmem = pl.BlockSpec(memory_space=pltpu.VMEM)
     smem = pl.BlockSpec(memory_space=pltpu.SMEM)
-    hbm = pl.BlockSpec(memory_space=pl.ANY)
+    hbm = pl.BlockSpec(memory_space=pltpu.HBM)
+    anywhere = pl.BlockSpec(memory_space=pl.ANY)
 
     def shaped(*shape):
         return jax.ShapeDtypeStruct(shape, f32)
 
-    def call(kernel, name, in_specs, out_shape, scratch=()):
+    def call(kernel, name, in_specs, out_shape, scratch=(), limit=LIMIT):
         return pl.pallas_call(
             functools.partial(kernel, sz),
             out_shape=out_shape,
             in_specs=in_specs,
             out_specs=jax.tree.map(lambda _: vmem, out_shape),
             scratch_shapes=list(scratch),
-            compiler_params=pltpu.CompilerParams(vmem_limit_bytes=LIMIT),
+            compiler_params=pltpu.CompilerParams(vmem_limit_bytes=limit),
             name=name,
         )
 
-    def over_circles(value, bands, step):
-        pairs = [(b * n_lon + (i + step) % n_lon, b * n_lon + i) for b in bands for i in range(n_lon)]
-        return lax.ppermute(value, ("lat", "lon"), pairs)
+    def swapped(value, bands, turn):
+        sectors = [(b, i, i ^ turn if b in bands else i) for b in range(n_lat) for i in range(n_lon)]
+        return lax.ppermute(value, ("lat", "lon"), [(b * n_lon + i, b * n_lon + k) for b, i, k in sectors])
 
     geo = jnp.asarray(geometry(sz))
     n, inverse = (jnp.asarray(table) for table in offsets(sz))
@@ -439,6 +444,7 @@
             pltpu.VMEM((2, 3, merged), jnp.bfloat16),
             pltpu.SemaphoreType.DMA((2, 3)),
         ],
+        limit=ALL_VMEM,
     )(thickness, jnp.swapaxes(winds, 0, 1), jnp.swapaxes(tracers, 0, 1))
 
     near = [(band * n_lon + i, (band ^ 1) * n_lon + i) for band in range(n_lat) for i in range(n_lon)]
@@ -461,22 +467,21 @@
     )(thickness, winds, from_near, from_far, geo)
     circles = []
     for tend, bands in zip(tends, (sz.full_bands(), sz.part_bands())):
-        circles += [tend] + [over_circles(tend, bands, step) for step in range(1, n_lon)]
+        circles += [tend] + [swapped(tend, bands, turn) for turn in range(1, n_lon)]
 
     weights = call(
         weights_kernel,
         "weights",
-        [smem, vmem, vmem, hbm],
+        [smem, vmem, vmem, anywhere],
         jax.ShapeDtypeStruct((rows * PER_TILE * sz.stack, n_lon * sz.stack), jnp.bfloat16),
     )(cutoff, n, inverse, tends[0])
 
     edge = shaped(rows, LANES)
-    to_e, to_w = call(columns_kernel, "columns", [vmem] * 3 + [hbm], (edge, edge))(
+    to_e, to_w = call(columns_kernel, "columns", [vmem] * 3 + [anywhere], (edge, edge))(
         thickness, winds, tracers, tends[0]
     )
-    everywhere = range(n_lat)
-    from_w = over_circles(to_e, everywhere, n_lon - 1)
-    from_e = over_circles(to_w, everywhere, 1)
+    from_w = lax.ppermute(to_e, "lon", [(i, (i + 1) % n_lon) for i in range(n_lon)])
+    from_e = lax.ppermute(to_w, "lon", [((i + 1) % n_lon, i) for i in range(n_lon)])
 
     plain_w, plain_h, mass = call(
         rest_kernel,

time: 38.7 us -> 38.5 us (level)
  local copies, waits for them, and re-layouts: 4.44 us -> 2.59 us
  Pallas kernels: 6.63 us -> 8.01 us
  waiting for transfers between devices: 9.08 us -> 9.85 us
  starting transfers between devices: 17.4 us -> 16.9 us
    unnamed x22 -> x16, local copies, waits for them, and re-layouts: 4.44 us -> 2.59 us
    ppermute x8, waiting for transfers between devices: 6.94 us -> 8.43 us  [the longest x1 5.3 us: local(): lax.ppermute(to_e, 'lon', [(i, (i + 1) % n_lon) for i in range(n_lon)])]
    pallas_call x1, Pallas kernels: 0.25 us -> 1.59 us  [local(): call(rows_kernel, 'rows', [hbm] * 3, (row_pair, row_pair), [pltpu.VMEM((2...]
    ppermute x1, waiting for transfers between devices: 2.14 us -> 1.42 us  [local(): from_far = lax.ppermute(to_far, ('lat', 'lon'), far)]
    ppermute x8, starting transfers between devices: 14.3 us -> 13.8 us  [the longest x6 11.2 us: swapped(): lax.ppermute(value, ('lat', 'lon'), [(b * n_lon + i, b * n_lon + k) for b...]
  transfers between devices with their start and end apart: 10 -> 10, of which waited for: 3 -> 3; matrix products, arithmetic and copies ran while one was open for 2% -> 5% of each run, Pallas kernels for 8% -> 8%
where the time goes in v4:
time: 38.5 us; the launch traced here: 38.2 us
  starting transfers between devices  16.9 us (44%)
  waiting for transfers between devices  9.85 us (26%)
  Pallas kernels  8.01 us (21%)
  local copies, waits for them, and re-layouts  2.59 us (7%)
  between operations  0.82 us (2%)
    ppermute x6, starting transfers between devices, swapped(): lax.ppermute(value, ('lat', 'lon'), [(b * n_lon + i, b * n_lon + k) for b...  11.2 us
    ppermute x1, waiting for transfers between devices, local(): lax.ppermute(to_e, 'lon', [(i, (i + 1) % n_lon) for i in range(n_lon)])  5.3 us
    ppermute x1, waiting for transfers between devices, local(): lax.ppermute(to_w, 'lon', [((i + 1) % n_lon, i) for i in range(n_lon)])  3.12 us
    ppermute x1, starting transfers between devices, local(): from_far = lax.ppermute(to_far, ('lat', 'lon'), far)  2.61 us
    unnamed x16, local copies, waits for them, and re-layouts  2.59 us
    pallas_call x1, Pallas kernels, local(): call(filter_kernel, 'filter', [smem] + [vmem] * (6 + len(circles)), (shap...  2.47 us
    ppermute x1, starting transfers between devices, local(): lax.ppermute(to_e, 'lon', [(i, (i + 1) % n_lon) for i in range(n_lon)])  2.01 us
    pallas_call x1, Pallas kernels, local(): call(rest_kernel, 'rest', [vmem] * 8, (shaped(*winds.shape), shaped(rows,...  1.68 us
  transfers between devices with their start and end apart: 10, of which 3 were waited for; matrix products, arithmetic and copies ran while one was open for 5% of the time, Pallas kernels for 8%

profile of v4, /device:TPU:0, one launch (start us, length us, event | category | flops | bytes accessed | tf_op | source)
XLA Modules:
  0.0 38.2 jit_solution(6907573400081721262)
XLA Ops:
  0.6 1.6 %rows.1 = (f32[120,128]{1,0:T(8,128)}, f32[120,128]{1,0:T(8,128)}) custom-call(f32[9,2880]{1,0:T(8,128)} %h_ref.7, f32[9,2,2880]{2,1,0:T(2,128)} %bitcast.2, bf16[9,3,2880]{2,1,0:T(4,128)(2,1)} %bitcast.3), custom_call_target="tpu_custom_call" | custom-call | tf_op jit(solution)/shard_map/rows/pallas_call | solution.py:436
  2.2 0.5 %collective-permute-start = (f32[120,128]{1,0:T(8,128)}, f32[120,128]{1,0:T(8,128)S(1)}, u32[]{:S(2)}, u32[]{:S(2)}) collective-permute-start(f32[120,128]{1,0:T(8,128)} %get-tuple-element.14), channel_id=1, source_target_pairs={{0,4},{1,5},{2,6},{3,7},{4,0},{5,1},{6,2},{7,3},{8,12},{9,13},{10,... | collective-permute-start | bytes 184328 | tf_op jit(solution)/shard_map/ppermute | solution.py:459
  2.7 2.6 %collective-permute-start.1 = (f32[120,128]{1,0:T(8,128)}, f32[120,128]{1,0:T(8,128)S(1)}, u32[]{:S(2)}, u32[]{:S(2)}) collective-permute-start(f32[120,128]{1,0:T(8,128)} %get-tuple-element.15), channel_id=1, source_target_pairs={{0,2},{1,3},{2,0},{3,1},{4,8},{5,9},{6,10},{7,11},{8,4},{9,5},{10,... | collective-permute-start | bytes 184328 | tf_op jit(solution)/shard_map/ppermute | solution.py:460
  5.4 1.0 %copy.10.w_ref = f32[2,9,2880]{2,1,0:T(8,128)S(1)} copy(f32[2,9,2880]{2,0,1:T(2,128)} %param.7) | data formatting | bytes 414720 | tf_op args[0]
  6.4 1.4 %collective-permute-done.1.far_ref = f32[120,128]{1,0:T(8,128)S(1)} collective-permute-done((f32[120,128]{1,0:T(8,128)}, f32[120,128]{1,0:T(8,128)S(1)}, u32[]{:S(2)}, u32[]{:S(2)}) %collective-permute-start.1) | collective-permute-done | bytes 61472 | tf_op jit(solution)/shard_map/ppermute | solution.py:460
  7.8 0.8 %polar.1 = (f32[648,128]{1,0:T(8,128)S(1)}, f32[216,128]{1,0:T(8,128)S(1)}) custom-call(f32[9,2880]{1,0:T(8,128)S(1)} %copy-done, f32[2,9,2880]{2,1,0:T(8,128)S(1)} %copy.10.w_ref, f32[120,128]{1,0:T(8,128)S(1)} %collective-permute-done.near_ref, f32[120,128]{1,0:T(8,128)S(1)} %collective-permute-done.1.far_ref, f32[8,3,16,128]{3,2,1,0:T(8,128)S(1)} %copy-done.1), custom_call_target="tpu_custom_call" | custom-call | tf_op jit(solution)/shard_map/polar/pallas_call | solution.py:465
  8.5 4.9 %collective-permute-start.6 = (f32[648,128]{1,0:T(8,128)S(1)}, f32[648,128]{1,0:T(8,128)S(1)}, u32[]{:S(2)}, u32[]{:S(2)}) collective-permute-start(f32[648,128]{1,0:T(8,128)S(1)} %get-tuple-element.16.after_ref.refs_0_), channel_id=1, source_target_pairs={{0,3},{1,2},{2,1},{3,0},{4,4},{5,5},{6,6},{7,7},{8,8},{9,9},{10,10... | collective-permute-start | bytes 995336 | tf_op jit(solution)/shard_map/ppermute | solution.py:430
  13.4 2.4 %collective-permute-start.5 = (f32[648,128]{1,0:T(8,128)S(1)}, f32[648,128]{1,0:T(8,128)S(1)}, u32[]{:S(2)}, u32[]{:S(2)}) collective-permute-start(f32[648,128]{1,0:T(8,128)S(1)} %get-tuple-element.16.after_ref.refs_0_), channel_id=1, source_target_pairs={{0,2},{1,3},{2,0},{3,1},{4,4},{5,5},{6,6},{7,7},{8,8},{9,9},{10,10... | collective-permute-start | bytes 995336 | tf_op jit(solution)/shard_map/ppermute | solution.py:430
  15.8 2.0 %collective-permute-start.4 = (f32[648,128]{1,0:T(8,128)S(1)}, f32[648,128]{1,0:T(8,128)S(1)}, u32[]{:S(2)}, u32[]{:S(2)}) collective-permute-start(f32[648,128]{1,0:T(8,128)S(1)} %get-tuple-element.16.after_ref.refs_0_), channel_id=1, source_target_pairs={{0,1},{1,0},{2,3},{3,2},{4,4},{5,5},{6,6},{7,7},{8,8},{9,9},{10,10... | collective-permute-start | bytes 995336 | tf_op jit(solution)/shard_map/ppermute | solution.py:430
  17.8 0.7 %collective-permute-start.9 = (f32[216,128]{1,0:T(8,128)S(1)}, f32[216,128]{1,0:T(8,128)S(1)}, u32[]{:S(2)}, u32[]{:S(2)}) collective-permute-start(f32[216,128]{1,0:T(8,128)S(1)} %get-tuple-element.21.refs_4_), channel_id=1, source_target_pairs={{0,0},{1,1},{2,2},{3,3},{4,7},{5,6},{6,5},{7,4},{8,8},{9,9},{10,10... | collective-permute-start | bytes 331784 | tf_op jit(solution)/shard_map/ppermute | solution.py:430
  18.5 0.0 copy-start.2
  18.6 0.0 copy-start.3
  18.6 0.1 columns.1
  18.7 2.0 %collective-permute-start.2 = (f32[9,128]{1,0:T(8,128)S(1)}, f32[9,128]{1,0:T(8,128)S(1)}, u32[]{:S(2)}, u32[]{:S(2)}) collective-permute-start(f32[9,128]{1,0:T(8,128)S(1)} %get-tuple-element.17), channel_id=1, source_target_pairs={{0,1},{1,2},{2,3},{3,0},{4,5},{5,6},{6,7},{7,4},{8,9},{9,10},{10,1... | collective-permute-start | bytes 13832 | tf_op jit(solution)/shard_map/ppermute | solution.py:483
  20.7 5.3 %collective-permute-done.2.from_w = f32[9,128]{1,0:T(8,128)S(1)} collective-permute-done((f32[9,128]{1,0:T(8,128)S(1)}, f32[9,128]{1,0:T(8,128)S(1)}, u32[]{:S(2)}, u32[]{:S(2)}) %collective-permute-start.2) | collective-permute-done | bytes 4640 | tf_op jit(solution)/shard_map/ppermute | solution.py:483
  26.0 0.5 %collective-permute-start.3 = (f32[9,128]{1,0:T(8,128)S(1)}, f32[9,128]{1,0:T(8,128)S(1)}, u32[]{:S(2)}, u32[]{:S(2)}) collective-permute-start(f32[9,128]{1,0:T(8,128)S(1)} %get-tuple-element.18), channel_id=1, source_target_pairs={{1,0},{2,1},{3,2},{0,3},{5,4},{6,5},{7,6},{4,7},{9,8},{10,9},{11,1... | collective-permute-start | bytes 13832 | tf_op jit(solution)/shard_map/ppermute | solution.py:484
  26.5 3.1 %collective-permute-done.3.from_e = f32[9,128]{1,0:T(8,128)S(1)} collective-permute-done((f32[9,128]{1,0:T(8,128)S(1)}, f32[9,128]{1,0:T(8,128)S(1)}, u32[]{:S(2)}, u32[]{:S(2)}) %collective-permute-start.3) | collective-permute-done | bytes 4640 | tf_op jit(solution)/shard_map/ppermute | solution.py:484
  29.6 0.7 %collective-permute-start.8 = (f32[216,128]{1,0:T(8,128)S(1)}, f32[216,128]{1,0:T(8,128)S(1)}, u32[]{:S(2)}, u32[]{:S(2)}) collective-permute-start(f32[216,128]{1,0:T(8,128)S(1)} %get-tuple-element.21.refs_4_), channel_id=1, source_target_pairs={{0,0},{1,1},{2,2},{3,3},{4,6},{5,7},{6,4},{7,5},{8,8},{9,9},{10,10... | collective-permute-start | bytes 331784 | tf_op jit(solution)/shard_map/ppermute | solution.py:430
  30.3 0.7 %collective-permute-start.7 = (f32[216,128]{1,0:T(8,128)S(1)}, f32[216,128]{1,0:T(8,128)S(1)}, u32[]{:S(2)}, u32[]{:S(2)}) collective-permute-start(f32[216,128]{1,0:T(8,128)S(1)} %get-tuple-element.21.refs_4_), channel_id=1, source_target_pairs={{0,0},{1,1},{2,2},{3,3},{4,5},{5,4},{6,7},{7,6},{8,8},{9,9},{10,10... | collective-permute-start | bytes 331784 | tf_op jit(solution)/shard_map/ppermute | solution.py:430
  31.0 1.4 %weights.1.weights_ref = bf16[1728,96]{1,0:T(8,128)(2,1)S(1)} custom-call(s32[72]{0:T(128)S(1)} %copy-done.4, f32[192,96]{1,0:T(8,128)S(1)} %copy-done.3, f32[192,96]{1,0:T(8,128)S(1)} %copy-done.2, f32[648,128]{1,0:T(8,128)S(1)} %get-tuple-element.16.after_ref.refs_0_), custom_call_target="tpu_custom_call" | custom-call | tf_op jit(solution)/shard_map/weights/pallas_call | solution.py:472
  32.4 1.7 %rest.1 = (f32[2,9,2880]{2,1,0:T(8,128)S(1)}, f32[9,2880]{1,0:T(8,128)S(1)}, bf16[3,9,2880]{2,1,0:T(8,128)(2,1)S(1)}) custom-call(f32[9,2880]{1,0:T(8,128)S(1)} %copy-done, f32[2,9,2880]{2,1,0:T(8,128)S(1)} %copy.10.w_ref, bf16[3,9,2880]{2,1,0:T(8,128)(2,1)S(1)} %copy.14.q_ref, f32[9,128]{1,0:T(8,128)S(1)} %collective-permute-done.2.from_w, ...), custom_call_target="tpu_custom_call" | custom-call | tf_op jit(solution)/shard_map/rest/pallas_call | solution.py:486
  34.1 0.8 %copy.17 = bf16[3,9,2880]{2,0,1:T(4,128)(2,1)} copy(bf16[3,9,2880]{2,1,0:T(8,128)(2,1)S(1)} %get-tuple-element.27) | data formatting | bytes 311040
  34.9 2.5 %filter.1 = (f32[2,9,2880]{2,1,0:T(8,128)S(1)}, f32[9,2880]{1,0:T(8,128)}) custom-call(s32[72]{0:T(128)S(1)} %copy-done.4, f32[8,3,16,128]{3,2,1,0:T(8,128)S(1)} %copy-done.1, bf16[1728,96]{1,0:T(8,128)(2,1)S(1)} %weights.1.weights_ref, f32[9,2880]{1,0:T(8,128)S(1)} %copy-done, f32[2,9,2880]{2,1,0:T(8,128)S(1)} %copy.10.w_ref, ...), custom_call_target="tpu_custom_call" | custom-call | tf_op jit(solution)/shard_map/filter/pallas_call | solution.py:494
  37.4 0.8 %copy.16 = f32[2,9,2880]{2,0,1:T(2,128)} copy(f32[2,9,2880]{2,1,0:T(8,128)S(1)} %get-tuple-element.25) | data formatting | bytes 414720
  (18 shorter events, 0.1 us)
Async XLA Ops:
  2.2 4.1 %collective-permute-start = (f32[120,128]{1,0:T(8,128)}, f32[120,128]{1,0:T(8,128)S(1)}, u32[]{:S(2)}, u32[]{:S(2)}) collective-permute-start(f32[120,128]{1,0:T(8,128)} %get-tuple-element.14), channel_id=1, source_target_pairs={{0,4},{1,5},{2,6},{3,7},{4,0},{5,1},{6,2},{7,3},{8,12},{9,13},{10,... | collective-permute-start | bytes 184328 | tf_op jit(solution)/shard_map/ppermute | solution.py:459
  2.7 5.0 %copy-start = (f32[9,2880]{1,0:T(8,128)S(1)}, f32[9,2880]{1,0:T(8,128)}, u32[]{:S(2)}) copy-start(f32[9,2880]{1,0:T(8,128)} %h_ref.7) | copy-start | bytes 311044
  2.7 5.0 %copy-start.1 = (f32[8,3,16,128]{3,2,1,0:T(8,128)S(1)}, f32[8,3,16,128]{3,2,1,0:T(8,128)}, u32[]{:S(2)}) copy-start(f32[8,3,16,128]{3,2,1,0:T(8,128)} %constant.6.clone.geo_ref) | copy-start | bytes 589828
  2.7 5.0 %collective-permute-start.1 = (f32[120,128]{1,0:T(8,128)}, f32[120,128]{1,0:T(8,128)S(1)}, u32[]{:S(2)}, u32[]{:S(2)}) collective-permute-start(f32[120,128]{1,0:T(8,128)} %get-tuple-element.15), channel_id=1, source_target_pairs={{0,2},{1,3},{2,0},{3,1},{4,8},{5,9},{6,10},{7,11},{8,4},{9,5},{10,... | collective-permute-start | bytes 184328 | tf_op jit(solution)/shard_map/ppermute | solution.py:460
  6.3 12.2 %copy-start.5 = (bf16[3,9,2880]{2,0,1:T(4,128)(2,1)S(1)}, bf16[3,9,2880]{2,0,1:T(4,128)(2,1)}, u32[]{:S(2)}) copy-start(bf16[3,9,2880]{2,0,1:T(4,128)(2,1)} %param.9) | copy-start | bytes 466564
  8.5 26.4 %collective-permute-start.6 = (f32[648,128]{1,0:T(8,128)S(1)}, f32[648,128]{1,0:T(8,128)S(1)}, u32[]{:S(2)}, u32[]{:S(2)}) collective-permute-start(f32[648,128]{1,0:T(8,128)S(1)} %get-tuple-element.16.after_ref.refs_0_), channel_id=1, source_target_pairs={{0,3},{1,2},{2,1},{3,0},{4,4},{5,5},{6,6},{7,7},{8,8},{9,9},{10,10... | collective-permute-start | bytes 995336 | tf_op jit(solution)/shard_map/ppermute | solution.py:430
  13.4 21.5 %collective-permute-start.5 = (f32[648,128]{1,0:T(8,128)S(1)}, f32[648,128]{1,0:T(8,128)S(1)}, u32[]{:S(2)}, u32[]{:S(2)}) collective-permute-start(f32[648,128]{1,0:T(8,128)S(1)} %get-tuple-element.16.after_ref.refs_0_), channel_id=1, source_target_pairs={{0,2},{1,3},{2,0},{3,1},{4,4},{5,5},{6,6},{7,7},{8,8},{9,9},{10,10... | collective-permute-start | bytes 995336 | tf_op jit(solution)/shard_map/ppermute | solution.py:430
  15.8 19.1 %collective-permute-start.4 = (f32[648,128]{1,0:T(8,128)S(1)}, f32[648,128]{1,0:T(8,128)S(1)}, u32[]{:S(2)}, u32[]{:S(2)}) collective-permute-start(f32[648,128]{1,0:T(8,128)S(1)} %get-tuple-element.16.after_ref.refs_0_), channel_id=1, source_target_pairs={{0,1},{1,0},{2,3},{3,2},{4,4},{5,5},{6,6},{7,7},{8,8},{9,9},{10,10... | collective-permute-start | bytes 995336 | tf_op jit(solution)/shard_map/ppermute | solution.py:430
  17.8 12.5 %collective-permute-start.9 = (f32[216,128]{1,0:T(8,128)S(1)}, f32[216,128]{1,0:T(8,128)S(1)}, u32[]{:S(2)}, u32[]{:S(2)}) collective-permute-start(f32[216,128]{1,0:T(8,128)S(1)} %get-tuple-element.21.refs_4_), channel_id=1, source_target_pairs={{0,0},{1,1},{2,2},{3,3},{4,7},{5,6},{6,5},{7,4},{8,8},{9,9},{10,10... | collective-permute-start | bytes 331784 | tf_op jit(solution)/shard_map/ppermute | solution.py:430
  18.5 12.4 %copy-start.2 = (f32[192,96]{1,0:T(8,128)S(1)}, f32[192,96]{1,0:T(8,128)}, u32[]{:S(2)}) copy-start(f32[192,96]{1,0:T(8,128)} %constant.8.clone.inverse_ref) | copy-start | bytes 221188
  18.6 12.4 %copy-start.3 = (f32[192,96]{1,0:T(8,128)S(1)}, f32[192,96]{1,0:T(8,128)}, u32[]{:S(2)}) copy-start(f32[192,96]{1,0:T(8,128)} %constant.7.clone.n_ref) | copy-start | bytes 221188
  18.7 12.3 %copy-start.4 = (s32[72]{0:T(128)S(1)}, s32[72]{0:T(128)}, u32[]{:S(2)}) copy-start(s32[72]{0:T(128)} %cut_ref.3) | copy-start | bytes 868
  18.7 7.3 %collective-permute-start.2 = (f32[9,128]{1,0:T(8,128)S(1)}, f32[9,128]{1,0:T(8,128)S(1)}, u32[]{:S(2)}, u32[]{:S(2)}) collective-permute-start(f32[9,128]{1,0:T(8,128)S(1)} %get-tuple-element.17), channel_id=1, source_target_pairs={{0,1},{1,2},{2,3},{3,0},{4,5},{5,6},{6,7},{7,4},{8,9},{9,10},{10,1... | collective-permute-start | bytes 13832 | tf_op jit(solution)/shard_map/ppermute | solution.py:483
  26.0 3.7 %collective-permute-start.3 = (f32[9,128]{1,0:T(8,128)S(1)}, f32[9,128]{1,0:T(8,128)S(1)}, u32[]{:S(2)}, u32[]{:S(2)}) collective-permute-start(f32[9,128]{1,0:T(8,128)S(1)} %get-tuple-element.18), channel_id=1, source_target_pairs={{1,0},{2,1},{3,2},{0,3},{5,4},{6,5},{7,6},{4,7},{9,8},{10,9},{11,1... | collective-permute-start | bytes 13832 | tf_op jit(solution)/shard_map/ppermute | solution.py:484
  29.6 5.3 %collective-permute-start.8 = (f32[216,128]{1,0:T(8,128)S(1)}, f32[216,128]{1,0:T(8,128)S(1)}, u32[]{:S(2)}, u32[]{:S(2)}) collective-permute-start(f32[216,128]{1,0:T(8,128)S(1)} %get-tuple-element.21.refs_4_), channel_id=1, source_target_pairs={{0,0},{1,1},{2,2},{3,3},{4,6},{5,7},{6,4},{7,5},{8,8},{9,9},{10,10... | collective-permute-start | bytes 331784 | tf_op jit(solution)/shard_map/ppermute | solution.py:430
  30.3 4.6 %collective-permute-start.7 = (f32[216,128]{1,0:T(8,128)S(1)}, f32[216,128]{1,0:T(8,128)S(1)}, u32[]{:S(2)}, u32[]{:S(2)}) collective-permute-start(f32[216,128]{1,0:T(8,128)S(1)} %get-tuple-element.21.refs_4_), channel_id=1, source_target_pairs={{0,0},{1,1},{2,2},{3,3},{4,5},{5,4},{6,7},{7,6},{8,8},{9,9},{10,10... | collective-permute-start | bytes 331784 | tf_op jit(solution)/shard_map/ppermute | solution.py:430

commit v5 on v4

--- a/solution.py
+++ b/solution.py
@@ -41,12 +41,6 @@
 
     def span(self, tile):
         return self.tail if tile == self.tiles - 1 else LANES
-
-    def full_bands(self):
-        return [b for b in range(self.n_lat) if min(b, self.n_lat - 1 - b) < self.full]
-
-    def part_bands(self):
-        return [b for b in range(self.n_lat) if min(b, self.n_lat - 1 - b) == self.full and self.part]
 
     def part_first(self, band):
         return jnp.where(band < self.n_lat // 2, 0, self.rows - self.part)
@@ -163,8 +157,7 @@
     return pltpu.roll(value, 1, 0)
 
 
-def polar_kernel(sz, h_ref, w_ref, near_ref, far_ref, geo_ref, *refs):
-    tend_ref, ext = refs[0], refs[-1]
+def polar_kernel(sz, h_ref, w_ref, near_ref, far_ref, geo_ref, tend_ref, ext):
     band = lax.axis_index("lat")
     ring = Tiles(sz)
     lane = ring.lane
@@ -215,12 +208,6 @@
     for f in range(3):
         for t in range(tiles, stack):
             tend_ref[pl.ds(stack * rows * f + t, rows, stride=stack), :] = jnp.zeros((rows, LANES), jnp.float32)
-    if sz.part:
-        size = sz.part * stack
-        first = sz.part_first(band)
-        for f in range(3):
-            start = pl.multiple_of((rows * f + first) * stack, 8)
-            refs[1][size * f : size * (f + 1)] = tend_ref[pl.ds(start, size), :]
 
 
 def rest_kernel(
@@ -314,13 +301,16 @@
         weights_ref[size * row : size * (row + 1)] = weights.astype(jnp.bfloat16)
 
 
-def filter_rows(sz, pieces, gathered, inv_cos, count, first, weights_ref, results):
+def filter_rows(sz, circle_ref, gathered, inv_cos, count, first, weights_ref, results):
     here = lax.axis_index("lon")
     stack, n_lon = sz.stack, sz.n_lon
     lane = lax.broadcasted_iota(jnp.int32, (count, LANES), 1)
-    for turn, ref in enumerate(pieces):
-        eastward = lax.rem(jnp.bitwise_xor(here, turn) - here + n_lon, n_lon)
-        gathered[eastward, : 3 * count * stack] = ref[...]
+    for s in range(n_lon):
+        sector = lax.rem(here + s, n_lon)
+        for f in range(3):
+            start = pl.multiple_of(stack * (sz.rows * f + first), 8)
+            piece = circle_ref[sector, pl.ds(start, count * stack), :]
+            gathered[s, stack * count * f : stack * count * (f + 1)] = piece
     sides = [gathered[s, pl.ds(sz.tiles - 1, count, stride=stack), :] for s in range(n_lon)]
 
     def column(s, k):
@@ -362,16 +352,17 @@
             results[pl.ds(start, stack), :] = pltpu.roll(same, stack - 1, 0) + carried
 
 
-def filter_kernel(sz, cut_ref, geo_ref, weights_ref, h_ref, w_ref, plain_w_ref, plain_h_ref, *refs):
-    n_lon, rows = sz.n_lon, sz.rows
-    full_refs, part_refs = refs[:n_lon], refs[n_lon : 2 * n_lon]
-    new_w_ref, new_h_ref, gathered, results = refs[-4:]
+def filter_kernel(
+    sz, cut_ref, geo_ref, weights_ref, h_ref, w_ref, plain_w_ref, plain_h_ref, circle_ref,
+    new_w_ref, new_h_ref, gathered, results,
+):
+    rows = sz.rows
     band = lax.axis_index("lat")
     from_pole = jnp.minimum(band, sz.n_lat - 1 - band)
 
     @pl.when(from_pole < sz.full)
     def _():
-        filter_rows(sz, full_refs, gathered, geo_ref[band, 0][:rows], rows, 0, weights_ref, results)
+        filter_rows(sz, circle_ref, gathered, geo_ref[band, 0][:rows], rows, 0, weights_ref, results)
 
     if sz.part:
 
@@ -380,7 +371,7 @@
             inv_cos = geo_ref[band, 0]
             low = band < sz.n_lat // 2
             inv_cos = jnp.where(low, inv_cos[: sz.part], inv_cos[rows - sz.part : rows])
-            filter_rows(sz, part_refs, gathered, inv_cos, sz.part, sz.part_first(band), weights_ref, results)
+            filter_rows(sz, circle_ref, gathered, inv_cos, sz.part, sz.part_first(band), weights_ref, results)
 
     row = lax.broadcasted_iota(jnp.int32, (rows, LANES), 0)
     cuts = jnp.zeros((rows, LANES), jnp.int32)
@@ -425,10 +416,6 @@
             name=name,
         )
 
-    def swapped(value, bands, turn):
-        sectors = [(b, i, i ^ turn if b in bands else i) for b in range(n_lat) for i in range(n_lon)]
-        return lax.ppermute(value, ("lat", "lon"), [(b * n_lon + i, b * n_lon + k) for b, i, k in sectors])
-
     geo = jnp.asarray(geometry(sz))
     n, inverse = (jnp.asarray(table) for table in offsets(sz))
 
@@ -459,26 +446,25 @@
     from_near = lax.ppermute(to_near, ("lat", "lon"), near)
     from_far = lax.ppermute(to_far, ("lat", "lon"), far)
 
-    tend_shapes = [shaped(3 * rows * sz.stack, LANES)]
-    if sz.part:
-        tend_shapes.append(shaped(3 * sz.part * sz.stack, LANES))
-    tends = call(
-        polar_kernel, "polar", [vmem] * 5, tend_shapes, [pltpu.VMEM((3, EXT_ROWS, sz.tiles * LANES), f32)]
+    tend = call(
+        polar_kernel,
+        "polar",
+        [vmem] * 5,
+        shaped(3 * rows * sz.stack, LANES),
+        [pltpu.VMEM((3, EXT_ROWS, sz.tiles * LANES), f32)],
     )(thickness, winds, from_near, from_far, geo)
-    circles = []
-    for tend, bands in zip(tends, (sz.full_bands(), sz.part_bands())):
-        circles += [tend] + [swapped(tend, bands, turn) for turn in range(1, n_lon)]
+    circle = lax.all_gather(tend, "lon")
 
     weights = call(
         weights_kernel,
         "weights",
         [smem, vmem, vmem, anywhere],
         jax.ShapeDtypeStruct((rows * PER_TILE * sz.stack, n_lon * sz.stack), jnp.bfloat16),
-    )(cutoff, n, inverse, tends[0])
+    )(cutoff, n, inverse, tend)
 
     edge = shaped(rows, LANES)
     to_e, to_w = call(columns_kernel, "columns", [vmem] * 3 + [anywhere], (edge, edge))(
-        thickness, winds, tracers, tends[0]
+        thickness, winds, tracers, tend
     )
     from_w = lax.ppermute(to_e, "lon", [(i, (i + 1) % n_lon) for i in range(n_lon)])
     from_e = lax.ppermute(to_w, "lon", [((i + 1) % n_lon, i) for i in range(n_lon)])
@@ -494,13 +480,13 @@
     new_w, new_h = call(
         filter_kernel,
         "filter",
-        [smem] + [vmem] * (6 + len(circles)),
+        [smem] + [vmem] * 7,
         (shaped(*winds.shape), shaped(rows, merged)),
         [
             pltpu.VMEM((n_lon, 3 * rows * sz.stack, LANES), f32),
             pltpu.VMEM((3 * rows * sz.stack, LANES), f32),
         ],
-    )(cutoff, geo, weights, thickness, winds, plain_w, plain_h, *circles)
+    )(cutoff, geo, weights, thickness, winds, plain_w, plain_h, circle)
     return new_w, new_h, mass
 
 

time: 38.5 us -> 58.7 us (1.52)
  waiting for transfers between devices: 9.85 us -> 24.6 us
  between operations: 0.82 us -> 14.1 us
  starting transfers between devices: 16.9 us -> 6.21 us
  local copies, waits for them, and re-layouts: 2.59 us -> 4.87 us
  Pallas kernels: 8.01 us -> 8.71 us
    all_gather x0 -> x1, waiting for transfers between devices: none -> 22 us  [local(): circle = lax.all_gather(tend, 'lon')]
    ppermute x6 -> x0, starting transfers between devices: 11.2 us -> none  [swapped(): lax.ppermute(value, ('lat', 'lon'), [(b * n_lon + i, b * n_lon + k) for b...]
    ppermute x1, waiting for transfers between devices: 5.3 us -> 0.12 us  [local(): lax.ppermute(to_e, 'lon', [(i, (i + 1) % n_lon) for i in range(n_lon)])]
    unnamed x16 -> x20, local copies, waits for them, and re-layouts: 2.59 us -> 4.87 us
    ppermute x1, waiting for transfers between devices: 3.12 us -> 1.06 us  [local(): lax.ppermute(to_w, 'lon', [((i + 1) % n_lon, i) for i in range(n_lon)])]
    pallas_call x2, Pallas kernels: 3.22 us -> 3.9 us  [the longest x1 2.43 us: local(): call(filter_kernel, 'filter', [smem] + [vmem] * 7, (shaped(*winds.shape),...]
  transfers between devices with their start and end apart: 10 -> 5, of which waited for: 3 -> 4; matrix products, arithmetic and copies ran while one was open for 5% -> 3% of each run, Pallas kernels for 8% -> 5%
where the time goes in v5:
time: 58.7 us; the launch traced here: 58.5 us
  waiting for transfers between devices  24.6 us (42%)
  between operations  14.1 us (24%)
  Pallas kernels  8.71 us (15%)
  starting transfers between devices  6.21 us (11%)
  local copies, waits for them, and re-layouts  4.87 us (8%)
    all_gather x1, waiting for transfers between devices, local(): circle = lax.all_gather(tend, 'lon')  22 us
    unnamed x20, local copies, waits for them, and re-layouts  4.87 us
    ppermute x1, starting transfers between devices, local(): from_far = lax.ppermute(to_far, ('lat', 'lon'), far)  2.59 us
    pallas_call x1, Pallas kernels, local(): call(filter_kernel, 'filter', [smem] + [vmem] * 7, (shaped(*winds.shape),...  2.43 us
    ppermute x1, starting transfers between devices, local(): lax.ppermute(to_e, 'lon', [(i, (i + 1) % n_lon) for i in range(n_lon)])  2.04 us
    pallas_call x1, Pallas kernels, local(): call(rest_kernel, 'rest', [vmem] * 8, (shaped(*winds.shape), shaped(rows,...  1.68 us
    pallas_call x1, Pallas kernels, local(): call(rows_kernel, 'rows', [hbm] * 3, (row_pair, row_pair), [pltpu.VMEM((2...  1.62 us
    pallas_call x1, Pallas kernels, local(): call(polar_kernel, 'polar', [vmem] * 5, shaped(3 * rows * sz.stack, LANES...  1.47 us
  transfers between devices with their start and end apart: 5, of which 4 were waited for; matrix products, arithmetic and copies ran while one was open for 3% of the time, Pallas kernels for 5%

profile of v5, /device:TPU:0, one launch (start us, length us, event | category | flops | bytes accessed | tf_op | source)
XLA Modules:
  0.0 58.5 jit_solution(12972378744662768168)
XLA Ops:
  7.2 0.0 all-gather.3.cloned.1.call-start
  7.2 1.6 %rows.1 = (f32[120,128]{1,0:T(8,128)}, f32[120,128]{1,0:T(8,128)}) custom-call(f32[9,2880]{1,0:T(8,128)} %h_ref.7, f32[9,2,2880]{2,1,0:T(2,128)} %bitcast.4, bf16[9,3,2880]{2,1,0:T(4,128)(2,1)} %bitcast.5), custom_call_target="tpu_custom_call" | custom-call | tf_op jit(solution)/shard_map/rows/pallas_call | solution.py:423
  8.8 0.0 copy-start.7
  8.9 0.5 collective-permute-start
  9.4 2.6 %collective-permute-start.1 = (f32[120,128]{1,0:T(8,128)}, f32[120,128]{1,0:T(8,128)S(1)}, u32[]{:S(2)}, u32[]{:S(2)}) collective-permute-start(f32[120,128]{1,0:T(8,128)} %get-tuple-element.13), channel_id=1, source_target_pairs={{0,2},{1,3},{2,0},{3,1},{4,8},{5,9},{6,10},{7,11},{8,4},{9,5},{10,... | collective-permute-start | bytes 184328 | tf_op jit(solution)/shard_map/ppermute | solution.py:447
  12.0 1.0 %copy.10.w_ref = f32[2,9,2880]{2,1,0:T(8,128)S(1)} copy(f32[2,9,2880]{2,0,1:T(2,128)} %param.7) | data formatting | bytes 414720 | tf_op args[0]
  13.0 0.0 collective-permute-done.near_ref
  13.0 1.4 %collective-permute-done.1.far_ref = f32[120,128]{1,0:T(8,128)S(1)} collective-permute-done((f32[120,128]{1,0:T(8,128)}, f32[120,128]{1,0:T(8,128)S(1)}, u32[]{:S(2)}, u32[]{:S(2)}) %collective-permute-start.1) | collective-permute-done | bytes 61472 | tf_op jit(solution)/shard_map/ppermute | solution.py:447
  14.4 0.9 %copy-done.1 = f32[8,3,16,128]{3,2,1,0:T(8,128)S(1)} copy-done((f32[8,3,16,128]{3,2,1,0:T(8,128)S(1)}, f32[8,3,16,128]{3,2,1,0:T(8,128)}, u32[]{:S(2)}) %copy-start.1) | copy-done | bytes 196632
  15.3 1.5 %polar.1.after_ref = f32[648,128]{1,0:T(8,128)} custom-call(f32[9,2880]{1,0:T(8,128)S(1)} %copy-done, f32[2,9,2880]{2,1,0:T(8,128)S(1)} %copy.10.w_ref, f32[120,128]{1,0:T(8,128)S(1)} %collective-permute-done.near_ref, f32[120,128]{1,0:T(8,128)S(1)} %collective-permute-done.1.far_ref, f32[8,3,16,128]{3,2,1,0:T(8,128)S(1)} %copy-done.1), custom_call_target="tpu_custom_call" | custom-call | tf_op jit(solution)/shard_map/polar/pallas_call | solution.py:449
  16.8 0.0 all-gather.3.cloned.1.call-update
  16.8 0.0 copy-start.2
  16.9 0.1 columns.1
  17.0 2.0 %collective-permute-start.2 = (f32[9,128]{1,0:T(8,128)S(1)}, f32[9,128]{1,0:T(8,128)S(1)}, u32[]{:S(2)}, u32[]{:S(2)}) collective-permute-start(f32[9,128]{1,0:T(8,128)S(1)} %get-tuple-element.14), channel_id=1, source_target_pairs={{0,1},{1,2},{2,3},{3,0},{4,5},{5,6},{6,7},{7,4},{8,9},{9,10},{10,1... | collective-permute-start | bytes 13832 | tf_op jit(solution)/shard_map/ppermute | solution.py:469
  19.0 1.0 %collective-permute-start.3 = (f32[9,128]{1,0:T(8,128)S(1)}, f32[9,128]{1,0:T(8,128)S(1)}, u32[]{:S(2)}, u32[]{:S(2)}) collective-permute-start(f32[9,128]{1,0:T(8,128)S(1)} %get-tuple-element.15), channel_id=1, source_target_pairs={{1,0},{2,1},{3,2},{0,3},{5,4},{6,5},{7,6},{4,7},{9,8},{10,9},{11,1... | collective-permute-start | bytes 13832 | tf_op jit(solution)/shard_map/ppermute | solution.py:470
  20.0 1.4 %weights.1.weights_ref = bf16[1728,96]{1,0:T(8,128)(2,1)S(1)} custom-call(s32[72]{0:T(128)S(1)} %copy-done.6, f32[192,96]{1,0:T(8,128)S(1)} %copy-done.5, f32[192,96]{1,0:T(8,128)S(1)} %copy-done.4, f32[648,128]{1,0:T(8,128)} %polar.1.after_ref), custom_call_target="tpu_custom_call" | custom-call | tf_op jit(solution)/shard_map/weights/pallas_call | solution.py:458
  21.5 0.1 collective-permute-done.2.from_w
  21.6 1.1 %collective-permute-done.3.from_e = f32[9,128]{1,0:T(8,128)S(1)} collective-permute-done((f32[9,128]{1,0:T(8,128)S(1)}, f32[9,128]{1,0:T(8,128)S(1)}, u32[]{:S(2)}, u32[]{:S(2)}) %collective-permute-start.3) | collective-permute-done | bytes 4640 | tf_op jit(solution)/shard_map/ppermute | solution.py:470
  22.7 1.7 %rest.1 = (f32[2,9,2880]{2,1,0:T(8,128)S(1)}, f32[9,2880]{1,0:T(8,128)S(1)}, bf16[3,9,2880]{2,1,0:T(8,128)(2,1)S(1)}) custom-call(f32[9,2880]{1,0:T(8,128)S(1)} %copy-done, f32[2,9,2880]{2,1,0:T(8,128)S(1)} %copy.10.w_ref, bf16[3,9,2880]{2,1,0:T(8,128)(2,1)S(1)} %copy.14.q_ref, f32[9,128]{1,0:T(8,128)S(1)} %collective-permute-done.2.from_w, ...), custom_call_target="tpu_custom_call" | custom-call | tf_op jit(solution)/shard_map/rest/pallas_call | solution.py:472
  24.3 0.8 %copy.17 = bf16[3,9,2880]{2,0,1:T(4,128)(2,1)} copy(bf16[3,9,2880]{2,1,0:T(8,128)(2,1)S(1)} %get-tuple-element.23) | data formatting | bytes 311040
  25.1 22.0 %all-gather.3.cloned.1.call-done = f32[2592,128]{1,0:T(8,128)} async-done(((f32[648,128]{1,0:T(8,128)}), f32[2592,128]{1,0:T(8,128)}) %all-gather.3.cloned.1.call-update) | async-done | bytes 1327120 | tf_op jit(solution)/shard_map/all_gather | solution.py:456
  47.1 1.3 %copy-done.3 = f32[2592,128]{1,0:T(8,128)S(1)} copy-done((f32[2592,128]{1,0:T(8,128)S(1)}, f32[2592,128]{1,0:T(8,128)}, u32[]{:S(2)}) %copy-start.3) | copy-done | bytes 1327128
  48.4 2.4 %filter.1 = (f32[2,9,2880]{2,1,0:T(8,128)S(1)}, f32[9,2880]{1,0:T(8,128)}) custom-call(s32[72]{0:T(128)S(1)} %copy-done.6, f32[8,3,16,128]{3,2,1,0:T(8,128)S(1)} %copy-done.2, bf16[1728,96]{1,0:T(8,128)(2,1)S(1)} %weights.1.weights_ref, f32[9,2880]{1,0:T(8,128)S(1)} %copy-done, f32[2,9,2880]{2,1,0:T(8,128)S(1)} %copy.10.w_ref, ...), custom_call_target="tpu_custom_call" | custom-call | tf_op jit(solution)/shard_map/filter/pallas_call | solution.py:480
  50.8 0.8 %copy.16 = f32[2,9,2880]{2,0,1:T(2,128)} copy(f32[2,9,2880]{2,1,0:T(8,128)S(1)} %get-tuple-element.21) | data formatting | bytes 414720
  (13 shorter events, 0.1 us)
Async XLA Ops:
  7.2 7.2 %copy-start = (f32[9,2880]{1,0:T(8,128)S(1)}, f32[9,2880]{1,0:T(8,128)}, u32[]{:S(2)}) copy-start(f32[9,2880]{1,0:T(8,128)} %h_ref.7) | copy-start | bytes 311044
  7.2 39.9 %all-gather.3.cloned.1.call-start = ((), (), s32[]{:S(2)}) async-start(), calls=%async_computation | async-start | bytes 1658880 | tf_op jit(solution)/shard_map/all_gather | solution.py:456
  8.8 8.0 %copy-start.7 = (bf16[3,9,2880]{2,0,1:T(4,128)(2,1)S(1)}, bf16[3,9,2880]{2,0,1:T(4,128)(2,1)}, u32[]{:S(2)}) copy-start(bf16[3,9,2880]{2,0,1:T(4,128)(2,1)} %param.9) | copy-start | bytes 466564
  8.9 4.1 %collective-permute-start = (f32[120,128]{1,0:T(8,128)}, f32[120,128]{1,0:T(8,128)S(1)}, u32[]{:S(2)}, u32[]{:S(2)}) collective-permute-start(f32[120,128]{1,0:T(8,128)} %get-tuple-element.12), channel_id=1, source_target_pairs={{0,4},{1,5},{2,6},{3,7},{4,0},{5,1},{6,2},{7,3},{8,12},{9,13},{10,... | collective-permute-start | bytes 184328 | tf_op jit(solution)/shard_map/ppermute | solution.py:446
  9.4 5.0 %collective-permute-start.1 = (f32[120,128]{1,0:T(8,128)}, f32[120,128]{1,0:T(8,128)S(1)}, u32[]{:S(2)}, u32[]{:S(2)}) collective-permute-start(f32[120,128]{1,0:T(8,128)} %get-tuple-element.13), channel_id=1, source_target_pairs={{0,2},{1,3},{2,0},{3,1},{4,8},{5,9},{6,10},{7,11},{8,4},{9,5},{10,... | collective-permute-start | bytes 184328 | tf_op jit(solution)/shard_map/ppermute | solution.py:447
  12.0 8.1 %copy-start.4 = (f32[192,96]{1,0:T(8,128)S(1)}, f32[192,96]{1,0:T(8,128)}, u32[]{:S(2)}) copy-start(f32[192,96]{1,0:T(8,128)} %constant.8.clone.inverse_ref) | copy-start | bytes 221188
  12.0 8.1 %copy-start.5 = (f32[192,96]{1,0:T(8,128)S(1)}, f32[192,96]{1,0:T(8,128)}, u32[]{:S(2)}) copy-start(f32[192,96]{1,0:T(8,128)} %constant.7.clone.n_ref) | copy-start | bytes 221188
  12.0 8.1 %copy-start.6 = (s32[72]{0:T(128)S(1)}, s32[72]{0:T(128)}, u32[]{:S(2)}) copy-start(s32[72]{0:T(128)} %cut_ref.3) | copy-start | bytes 868
  14.4 0.9 %copy-start.1 = (f32[8,3,16,128]{3,2,1,0:T(8,128)S(1)}, f32[8,3,16,128]{3,2,1,0:T(8,128)}, u32[]{:S(2)}) copy-start(f32[8,3,16,128]{3,2,1,0:T(8,128)} %constant.6.clone.geo_ref) | copy-start | bytes 589828
  16.8 5.8 %copy-start.2 = (f32[8,3,16,128]{3,2,1,0:T(8,128)S(1)}, f32[8,3,16,128]{3,2,1,0:T(8,128)}, u32[]{:S(2)}) copy-start(f32[8,3,16,128]{3,2,1,0:T(8,128)} %constant.6.clone.geo_ref) | copy-start | bytes 589828
  17.0 4.6 %collective-permute-start.2 = (f32[9,128]{1,0:T(8,128)S(1)}, f32[9,128]{1,0:T(8,128)S(1)}, u32[]{:S(2)}, u32[]{:S(2)}) collective-permute-start(f32[9,128]{1,0:T(8,128)S(1)} %get-tuple-element.14), channel_id=1, source_target_pairs={{0,1},{1,2},{2,3},{3,0},{4,5},{5,6},{6,7},{7,4},{8,9},{9,10},{10,1... | collective-permute-start | bytes 13832 | tf_op jit(solution)/shard_map/ppermute | solution.py:469
  19.0 3.7 %collective-permute-start.3 = (f32[9,128]{1,0:T(8,128)S(1)}, f32[9,128]{1,0:T(8,128)S(1)}, u32[]{:S(2)}, u32[]{:S(2)}) collective-permute-start(f32[9,128]{1,0:T(8,128)S(1)} %get-tuple-element.15), channel_id=1, source_target_pairs={{1,0},{2,1},{3,2},{0,3},{5,4},{6,5},{7,6},{4,7},{9,8},{10,9},{11,1... | collective-permute-start | bytes 13832 | tf_op jit(solution)/shard_map/ppermute | solution.py:470
  47.1 1.3 %copy-start.3 = (f32[2592,128]{1,0:T(8,128)S(1)}, f32[2592,128]{1,0:T(8,128)}, u32[]{:S(2)}) copy-start(f32[2592,128]{1,0:T(8,128)} %all-gather.3.cloned.1.call-done) | copy-start | bytes 3981316
Sparse Core Ops, SparseCore 0:
  16.9 30.1 all-gather.2

commit v6 on v5

v6 whole, which is shorter than its diff:
```python
import functools
import math

import jax
import jax.numpy as jnp
import numpy as np
from jax import lax
from jax.experimental import pallas as pl
from jax.experimental.pallas import tpu as pltpu
from jax.sharding import PartitionSpec as P

LEVELS = 16
TIME_STEP = 0.05
DIFFUSION = 0.5
LANES = 128
PER_TILE = LANES // LEVELS
EXT_ROWS = 16
LIMIT = 48 * 1024 * 1024
ALL_VMEM = 64 * 1024 * 1024 - 3600 * 1024


class Sizes:
    def __init__(self, rows, merged, n_lat, n_lon):
        self.rows = rows
        self.merged = merged
        self.columns = merged // LEVELS
        self.n_lat = n_lat
        self.n_lon = n_lon
        self.nlat = rows * n_lat
        self.nlon = self.columns * n_lon
        self.ratio = 2.0 * self.nlat / self.nlon
        self.tiles = -(-merged // LANES)
        self.end = (self.tiles - 1) * LANES
        self.tail = merged - self.end
        self.stack = -(-(self.tiles + 1) // 8) * 8
        self.units = 3 * rows
        self.share = -(-self.units // n_lon)
        self.size = self.share * self.stack
        assert self.tail <= LANES - 4 * LEVELS and rows + 2 <= EXT_ROWS and n_lat % 2 == 0
        assert n_lon >= 4 and n_lon & (n_lon - 1) == 0

    def span(self, tile):
        return self.tail if tile == self.tiles - 1 else LANES

    def turns(self, odd):
        middle = list(range(1, self.n_lon - 1))
        return [0, self.n_lon - 1] + (middle[::-1] if odd else middle)

    def partner(self, k):
        odd = lax.rem(lax.axis_index("lat"), 2) == 1
        turn = jnp.where(odd, self.turns(True)[k], self.turns(False)[k])
        return jnp.bitwise_xor(lax.axis_index("lon"), turn)

    def piece(self, k):
        return pl.ds(pl.multiple_of(self.partner(k) * self.size, 8), self.size)


def geometry(sz):
    table = np.zeros((sz.n_lat, 3, EXT_ROWS, LANES), np.float64)

    def face(j):
        return math.sin((j + 1) * math.pi / sz.nlat) if 0 <= j < sz.nlat - 1 else 0.0

    for band in range(sz.n_lat):
        for row in range(sz.rows):
            j = band * sz.rows + row
            centre = (j + 0.5) * math.pi / sz.nlat - math.pi / 2
            table[band, 0, row] = 1.0 / math.cos(centre)
            table[band, 1, row] = math.sin(centre)
            table[band, 2, row] = face(j)
        table[band, 2, EXT_ROWS - 1] = face(band * sz.rows - 1)
    return table.astype(np.float32)


def offsets(sz):
    shift, out_tile = np.divmod(np.arange(PER_TILE * sz.stack), sz.stack)
    sector, in_tile = np.divmod(np.arange(sz.n_lon * sz.stack), sz.stack)
    n = (PER_TILE * (out_tile - 1) + shift)[:, None] - (PER_TILE * in_tile + sz.columns * sector)[None, :]
    n = (n + sz.nlon // 2) % sz.nlon - sz.nlon // 2
    with np.errstate(divide="ignore"):
        inverse = np.where(n == 0, 0.0, 1.0 / (sz.nlon * np.sin(np.pi * n / sz.nlon)))
    return n.astype(np.float32), inverse.astype(np.float32)


def rows_kernel(sz, h_hbm, w_hbm, q_hbm, geo_hbm, near_ref, far_ref, sides_ref, block_ref, geo_ref, h_in, w_in, q_in, sems):
    band = lax.axis_index("lat")
    pairs = ((h_hbm, h_in), (w_hbm, w_in), (q_hbm, q_in), (geo_hbm.at[band], geo_ref))
    copies = [pltpu.make_async_copy(source, to, sems.at[i]) for i, (source, to) in enumerate(pairs)]
    for copy in copies:
        copy.start()
    for copy in copies:
        copy.wait()
    rows, last = sz.rows, sz.rows - 1
    fields = [h_in[...], w_in[:, 1, :]] + [q_in[:, k, :].astype(jnp.float32) for k in range(3)] + [w_in[:, 0, :]]
    for f, value in enumerate(fields):
        block_ref[f, :rows, : sz.merged] = value
    even = lax.rem(band, 2) == 0
    for t in range(sz.tiles):
        wide = sz.span(t)
        lanes = slice(LANES * t, LANES * t + wide)
        for f in range(5):
            first, final = block_ref[f, 0:1, lanes], block_ref[f, last:rows, lanes]
            at = sz.stack * f + t
            near_ref[at : at + 1, :wide] = jnp.where(even, final, first)
            far_ref[at : at + 1, :wide] = jnp.where(even, first, final)
    sides_ref[...] = jnp.zeros(sides_ref.shape, jnp.float32)
    for k, at in enumerate((0, sz.merged - LEVELS)):
        for place, f in enumerate((0, 5, 2, 3, 4)):
            to = slice(LEVELS * place, LEVELS * (place + 1))
            sides_ref[EXT_ROWS * k : EXT_ROWS * k + rows, to] = block_ref[f, :rows, at : at + LEVELS]


def add_rows(sz, ext, fields, near_ref, far_ref):
    band = lax.axis_index("lat")
    even = lax.rem(band, 2) == 0
    over_pole = (band == 0) | (band == sz.n_lat - 1)
    for f in range(fields):
        flip = jnp.where(over_pole, -1.0, 1.0) if f == 1 else 1.0
        for t in range(sz.tiles):
            at = slice(sz.stack * f + t, sz.stack * f + t + 1)
            near, far = near_ref[at], far_ref[at] * flip
            lanes = slice(LANES * t, LANES * (t + 1))
            ext[f, sz.rows : sz.rows + 1, lanes] = jnp.where(even, near, far)
            ext[f, EXT_ROWS - 1 : EXT_ROWS, lanes] = jnp.where(even, far, near)


class Tiles:
    def __init__(self, sz):
        self.sz = sz
        self.lane = lax.broadcasted_iota(jnp.int32, (EXT_ROWS, LANES), 1)
        self.turned = {}

    def turn(self, name, t, value, step):
        key = (name, t % self.sz.tiles, step)
        if key not in self.turned:
            self.turned[key] = pltpu.roll(value(t % self.sz.tiles), step % LANES, 1)
        return self.turned[key]

    def east(self, name, t, value):
        here = self.turn(name, t, value, -LEVELS)
        return jnp.where(self.lane < LANES - LEVELS, here, self.turn(name, t + 1, value, -LEVELS))

    def west(self, name, t, value):
        here = self.turn(name, t, value, LEVELS)
        return jnp.where(self.lane >= LEVELS, here, self.turn(name, t - 1, value, LEVELS))


def north(value):
    return pltpu.roll(value, EXT_ROWS - 1, 0)


def south(value):
    return pltpu.roll(value, 1, 0)


def polar_kernel(sz, block_ref, near_ref, far_ref, sides_ref, geo_ref, *refs):
    out_refs, (tend_ref, ext) = refs[:-2], refs[-2:]
    ring = Tiles(sz)
    lane = ring.lane
    tiles, stack, rows = sz.tiles, sz.stack, sz.rows
    for f, source in enumerate((0, 1, 5)):
        ext[f, :rows, sz.end :] = jnp.zeros((rows, LANES), jnp.float32)
        ext[f, :rows, : sz.merged] = block_ref[source, :rows, : sz.merged]
    add_rows(sz, ext, 2, near_ref, far_ref)
    inv_cos, sin_centre, cos_face = geo_ref[0], geo_ref[1], geo_ref[2]
    ratio = sz.ratio

    def tile(f, t):
        return ext[f, :, LANES * t : LANES * (t + 1)]

    kept = {}

    def zonal(t):
        if t not in kept:
            thick_e = ring.east("h", t, functools.partial(tile, 0))
            wind_e = ring.east("u", t, functools.partial(tile, 2))
            flux = 0.25 * (tile(2, t) + wind_e) * (tile(0, t) + thick_e) * inv_cos
            if t == tiles - 1:
                flux = jnp.where(lane < sz.tail - LEVELS, flux, 0.0)
            kept[t] = (flux, thick_e)
        return kept[t]

    for t in range(tiles):
        flux, thick_e = zonal(t)
        thick, wind_v, wind_u = tile(0, t), tile(1, t), tile(2, t)
        flux_w = ring.west("f", t, lambda s: zonal(s)[0])
        thick_w = ring.west("hw", t, functools.partial(tile, 0))
        thick_n = north(thick)
        flux_n = (0.25 * ratio) * (wind_v + north(wind_v)) * (thick + thick_n) * cos_face
        thick_tend = -((flux - flux_w) + (flux_n - south(flux_n)) * inv_cos)
        wind_u_tend = sin_centre * wind_v - (thick_e - thick_w) * (0.5 * inv_cos)
        wind_v_tend = -sin_centre * wind_u - (0.5 * ratio) * (thick_n - south(thick))
        spare = 0.0
        if t == tiles - 1:
            last = sz.tail - LEVELS
            columns = [(tile(0, 0), 0), (thick, last), (tile(2, 0), 0), (wind_u, last)]
            for k, (source, at) in reversed(list(enumerate(columns))):
                to = sz.tail + LEVELS * k
                spare = jnp.where(lane < to + LEVELS, pltpu.roll(source, (to - at) % LANES, 1), spare)
        for f, tend in enumerate((thick_tend, wind_u_tend, wind_v_tend)):
            if t == tiles - 1:
                tend = jnp.where(lane < sz.tail, tend, spare)
            tend_ref[pl.ds(stack * rows * f + t, rows, stride=stack), :] = tend[:rows]
    for f in range(3):
        for t in range(tiles, stack):
            tend_ref[pl.ds(stack * rows * f + t, rows, stride=stack), :] = jnp.zeros((rows, LANES), jnp.float32)
    used = stack * sz.units
    if used < tend_ref.shape[0]:
        tend_ref[used:, :] = jnp.zeros((tend_ref.shape[0] - used, LANES), jnp.float32)
    here = lax.axis_index("lon")
    for k, out_ref in enumerate(out_refs):
        out_ref[: sz.size] = tend_ref[sz.piece(k), :]
        if k:
            eastward = sz.partner(k) == lax.rem(here + 1, sz.n_lon)
            out_ref[sz.size :] = jnp.where(eastward, sides_ref[EXT_ROWS:], sides_ref[:EXT_ROWS])


def rest_kernel(sz, block_ref, near_ref, far_ref, geo_ref, after_ref, *refs):
    met_refs, (new_w_ref, new_h_ref, mass_ref, ext) = refs[: sz.n_lon - 1], refs[sz.n_lon - 1 :]
    ring = Tiles(sz)
    lane = ring.lane
    tiles, rows = sz.tiles, sz.rows
    ext[:, :rows, : sz.merged] = block_ref[:, :rows, : sz.merged]
    add_rows(sz, ext, 5, near_ref, far_ref)
    lane9 = lane[:rows]
    here = lax.axis_index("lon")
    from_e = from_w = met_refs[0][sz.size :]
    for k, met_ref in enumerate(met_refs[1:], 2):
        from_e = jnp.where(sz.partner(k) == lax.rem(here + 1, sz.n_lon), met_ref[sz.size :], from_e)
        from_w = jnp.where(sz.partner(k) == lax.rem(here + sz.n_lon - 1, sz.n_lon), met_ref[sz.size :], from_w)
    for place, f in enumerate((0, 5, 2, 3, 4)):
        after = pltpu.roll(from_e, (sz.tail - LEVELS * place) % LANES, 1)[:rows]
        before = pltpu.roll(from_w, (LANES - LEVELS - LEVELS * place) % LANES, 1)[:rows]
        own = ext[f, :rows, sz.end :]
        edge = jnp.where(lane9 < LANES - LEVELS, after, before)
        ext[f, :rows, sz.end :] = jnp.where(lane9 < sz.tail, own, edge)
    inv_cos, sin_centre, cos_face = geo_ref[0], geo_ref[1], geo_ref[2]
    ratio = sz.ratio

    def tile(f, t):
        return ext[f, :, LANES * t : LANES * (t + 1)]

    kept = {}

    def zonal(t):
        if t not in kept:
            thick_e = ring.east("h", t, functools.partial(tile, 0))
            wind_e = ring.east("u", t, functools.partial(tile, 5))
            flux = 0.25 * (tile(5, t) + wind_e) * (tile(0, t) + thick_e) * inv_cos
            parts = []
            for k in range(3):
                q = tile(2 + k, t)
                q_e = ring.east(k, t, functools.partial(tile, 2 + k))
                parts.append(DIFFUSION * (q_e - q) - flux * (0.5 * (q + q_e)))
            kept[t] = (flux, thick_e, parts)
        return kept[t]

    for t in range(tiles):
        span = sz.span(t)
        lanes = slice(LANES * t, LANES * t + span)
        flux, thick_e, parts = zonal(t)
        thick, wind_u, wind_v = tile(0, t), tile(5, t), tile(1, t)
        flux_w = ring.west("f", t, lambda s: zonal(s)[0])
        thick_w = ring.west("hw", t, functools.partial(tile, 0))
        thick_n = north(thick)
        flux_n = (0.25 * ratio) * (wind_v + north(wind_v)) * (thick + thick_n) * cos_face
        thick_tend = -((flux - flux_w) + (flux_n - south(flux_n)) * inv_cos)
        wind_u_tend = sin_centre * wind_v - (thick_e - thick_w) * (0.5 * inv_cos)
        wind_v_tend = -sin_centre * wind_u - (0.5 * ratio) * (thick_n - south(thick))
        new_h_ref[:, lanes] = (thick + TIME_STEP * thick_tend)[:rows, :span]
        new_w_ref[0, :, lanes] = (wind_u + TIME_STEP * wind_u_tend)[:rows, :span]
        new_w_ref[1, :, lanes] = (wind_v + TIME_STEP * wind_v_tend)[:rows, :span]
        for k in range(3):
            q = tile(2 + k, t)
            q_n = north(q)
            zonal_part = parts[k] - ring.west(("p", k), t, lambda s: zonal(s)[2][k])
            lap = q_n + south(q) - 2.0 * q
            over = flux_n * (0.5 * (q + q_n))
            merid_part = DIFFUSION * lap - (over - south(over)) * inv_cos
            mass = thick * q + TIME_STEP * (zonal_part + merid_part)
            mass_ref[:, k, lanes] = mass[:rows, :span].astype(jnp.bfloat16)


def sin_pi(y):
    y = jnp.where(y > 0.5, 1.0 - y, jnp.where(y < -0.5, -1.0 - y, y))
    s = y * y
    series = [(-1) ** i * math.pi ** (2 * i + 1) / math.factorial(2 * i + 1) for i in range(7)]
    total = series[-1]
    for factor in reversed(series[:-1]):
        total = total * s + factor
    return total * y


def share_of(sz, i):
    unit = lax.axis_index("lon") * sz.share + i
    return unit // sz.rows, lax.rem(unit, sz.rows)


def weights_kernel(sz, cut_ref, n_ref, inverse_ref, after_ref, weights_ref):
    band = lax.axis_index("lat")
    size = PER_TILE * sz.stack
    for i in range(sz.share):
        width = (2 * cut_ref[band * sz.rows + share_of(sz, i)[1]] + 1).astype(jnp.float32)
        n = n_ref[...]
        turns = n * width
        turns = turns - jnp.round(turns * (0.5 / sz.nlon)) * (2.0 * sz.nlon)
        weights = sin_pi(turns * (1.0 / sz.nlon)) * inverse_ref[...]
        weights = jnp.where(n == 0.0, width * (1.0 / sz.nlon), weights)
        weights_ref[size * i : size * (i + 1)] = weights.astype(jnp.bfloat16)


def filter_kernel(sz, weights_ref, geo_ref, *refs):
    n_lon, stack, share = sz.n_lon, sz.stack, sz.share
    in_refs, out_refs, (gathered, results) = refs[:n_lon], refs[n_lon : 2 * n_lon], refs[2 * n_lon :]
    for k, in_ref in enumerate(in_refs):
        gathered[sz.partner(k)] = in_ref[: sz.size]

    lane = lax.broadcasted_iota(jnp.int32, (share, LANES), 1)
    place = lax.broadcasted_iota(jnp.int32, (share, LANES), 0)
    by_flux = by_thick = jnp.zeros((share, LANES), jnp.float32)
    for i in range(share):
        field, row = share_of(sz, i)
        inv_cos = geo_ref[0, pl.ds(row, 1), :]
        by_flux = jnp.where((place == i) & (field == 0), inv_cos, by_flux)
        by_thick = jnp.where((place == i) & (field == 1), 0.5 * inv_cos, by_thick)
    sides = [gathered[s, pl.ds(sz.tiles - 1, share, stride=stack), :] for s in range(n_lon)]

    def column(s, k):
        return pltpu.roll(sides[s % n_lon], (-sz.tail - LEVELS * k) % LANES, 1)

    for s in range(n_lon):
        thick_w, thick_e = column(s, 1), column(s + 1, 0)
        flux = 0.25 * (column(s, 3) + column(s + 1, 2)) * (thick_w + thick_e) * by_flux
        west_of, east_of = flux + by_thick * thick_e, flux + by_thick * thick_w
        at = pl.ds(sz.tiles - 1, share, stride=stack)
        own = gathered[s, at, :]
        own = own - jnp.where(lane >= sz.tail - LEVELS, pltpu.roll(west_of, sz.tail - LEVELS, 1), 0.0)
        gathered[s, at, :] = jnp.where(lane < sz.tail, own, 0.0)
        at = pl.ds(0, share, stride=stack)
        after = (s + 1) % n_lon
        gathered[after, at, :] = gathered[after, at, :] + jnp.where(lane < LEVELS, east_of, 0.0)

    wide = lax.broadcasted_iota(jnp.int32, (stack, LANES), 1)
    rows = PER_TILE * stack
    for i in range(share):
        here = slice(stack * i, stack * (i + 1))
        pieces = [gathered[s, here].astype(jnp.bfloat16) for s in range(n_lon)]
        circle = jnp.concatenate([jnp.concatenate(pieces[s:] + pieces[:s], axis=0) for s in range(n_lon)], axis=1)
        spread = jnp.dot(weights_ref[rows * i : rows * (i + 1)], circle, preferred_element_type=jnp.float32)
        for s in range(n_lon):
            same = spread[:stack, LANES * s : LANES * (s + 1)]
            carried = None
            for e in range(1, PER_TILE):
                part = spread[stack * e : stack * (e + 1), LANES * s : LANES * (s + 1)]
                part = pltpu.roll(part, LEVELS * e, 1)
                inside = wide >= LEVELS * e
                same = same + jnp.where(inside, part, 0.0)
                over = jnp.where(inside, 0.0, part)
                carried = over if carried is None else carried + over
            results[s, here] = pltpu.roll(same, stack - 1, 0) + carried
    for k, out_ref in enumerate(out_refs):
        out_ref[...] = results[sz.partner(k)]


def finish_kernel(sz, cut_ref, block_ref, plain_w_ref, plain_h_ref, *refs):
    back_refs, (new_w_ref, new_h_ref, back_ref) = refs[: sz.n_lon], refs[sz.n_lon :]
    rows = sz.rows
    for k, ref in enumerate(back_refs):
        back_ref[sz.piece(k), :] = ref[...]
    row = lax.broadcasted_iota(jnp.int32, (rows, LANES), 0)
    cuts = jnp.zeros((rows, LANES), jnp.int32)
    for j in range(rows):
        cuts = jnp.where(row == j, cut_ref[lax.axis_index("lat") * rows + j], cuts)
    active = cuts < sz.nlon // 2
    for f in range(3):
        for t in range(sz.tiles):
            span = sz.span(t)
            lanes = slice(LANES * t, LANES * t + span)
            tend = back_ref[pl.ds(sz.stack * rows * f + t, rows, stride=sz.stack), :][:, :span]
            new = block_ref[(0, 5, 1)[f], :rows, lanes] + TIME_STEP * tend
            if f == 0:
                new_h_ref[:, lanes] = jnp.where(active[:, :span], new, plain_h_ref[:, lanes])
            else:
                new_w_ref[:, f - 1, lanes] = jnp.where(active[:, :span], new, plain_w_ref[f - 1, :, lanes])


def local(winds, thickness, tracers, cutoff):
    n_lat = lax.axis_size("lat")
    n_lon = lax.axis_size("lon")
    rows, merged = thickness.shape
    sz = Sizes(rows, merged, n_lat, n_lon)
    f32 = jnp.float32
    vmem = pl.BlockSpec(memory_space=pltpu.VMEM)
    smem = pl.BlockSpec(memory_space=pltpu.SMEM)
    hbm = pl.BlockSpec(memory_space=pltpu.HBM)
    anywhere = pl.BlockSpec(memory_space=pl.ANY)

    def shaped(*shape):
        return jax.ShapeDtypeStruct(shape, f32)

    def call(kernel, name, in_specs, out_shape, scratch=(), limit=LIMIT):
        return pl.pallas_call(
            functools.partial(kernel, sz),
            out_shape=out_shape,
            in_specs=in_specs,
            out_specs=jax.tree.map(lambda _: vmem, out_shape),
            scratch_shapes=list(scratch),
            compiler_params=pltpu.CompilerParams(vmem_limit_bytes=limit),
            name=name,
        )

    n, inverse = (jnp.asarray(table) for table in offsets(sz))

    wind_rows = jnp.swapaxes(winds, 0, 1)
    tracer_rows = jnp.swapaxes(tracers, 0, 1)
    row_pair = shaped(5 * sz.stack, LANES)
    to_near, to_far, sides, block, geo = call(
        rows_kernel,
        "rows",
        [hbm] * 4,
        (
            row_pair,
            row_pair,
            shaped(2 * EXT_ROWS, LANES),
            shaped(6, EXT_ROWS, sz.tiles * LANES),
            shaped(3, EXT_ROWS, LANES),
        ),
        [
            pltpu.VMEM((rows, merged), f32),
            pltpu.VMEM((rows, 2, merged), f32),
            pltpu.VMEM((rows, 3, merged), jnp.bfloat16),
            pltpu.SemaphoreType.DMA((4,)),
        ],
        limit=ALL_VMEM,
    )(thickness, wind_rows, tracer_rows, jnp.asarray(geometry(sz)))

    near = [(band * n_lon + i, (band ^ 1) * n_lon + i) for band in range(n_lat) for i in range(n_lon)]
    far = []
    for band in range(n_lat):
        other = band - 1 if band % 2 == 0 else band + 1
        for i in range(n_lon):
            if 0 <= other < n_lat:
                far.append((band * n_lon + i, other * n_lon + i))
            else:
                far.append((band * n_lon + i, band * n_lon + (i + n_lon // 2) % n_lon))
    from_near = lax.ppermute(to_near, ("lat", "lon"), near)
    from_far = lax.ppermute(to_far, ("lat", "lon"), far)

    order = [sz.turns(False), sz.turns(True)]

    def meetings(shares):
        got = [shares[0]]
        for k in range(1, n_lon):
            sectors = [(band, i, i ^ order[band % 2][k]) for band in range(n_lat) for i in range(n_lon)]
            got.append(lax.ppermute(shares[k], ("lat", "lon"), [(b * n_lon + i, b * n_lon + j) for b, i, j in sectors]))
        return got

    all_pieces = pltpu.VMEM((n_lon, sz.size, LANES), f32)
    tends = call(
        polar_kernel,
        "polar",
        [vmem] * 5,
        [shaped(sz.size, LANES)] + [shaped(sz.size + EXT_ROWS, LANES)] * (n_lon - 1),
        [pltpu.VMEM((n_lon * sz.size, LANES), f32), pltpu.VMEM((3, EXT_ROWS, sz.tiles * LANES), f32)],
    )(block, from_near, from_far, sides, geo)
    met = meetings(tends)
    weights = call(
        weights_kernel,
        "weights",
        [smem, vmem, vmem, anywhere],
        jax.ShapeDtypeStruct((sz.share * PER_TILE * sz.stack, n_lon * sz.stack), jnp.bfloat16),
    )(cutoff, n, inverse, tends[0])
    worked = call(
        filter_kernel,
        "filter",
        [vmem] * (2 + n_lon),
        [shaped(sz.size, LANES)] * n_lon,
        [all_pieces, all_pieces],
    )(weights, geo, *met)
    back = meetings(worked)

    plain_w, plain_h, mass = call(
        rest_kernel,
        "rest",
        [vmem] * 4 + [anywhere] + [vmem] * (n_lon - 1),
        (shaped(2, rows, merged), shaped(rows, merged), jax.ShapeDtypeStruct(tracer_rows.shape, jnp.bfloat16)),
        [pltpu.VMEM((6, EXT_ROWS, sz.tiles * LANES), f32)],
    )(block, from_near, from_far, geo, worked[0], *met[1:])

    new_w, new_h = call(
        finish_kernel,
        "finish",
        [smem] + [vmem] * (3 + n_lon),
        (shaped(*wind_rows.shape), shaped(rows, merged)),
        [pltpu.VMEM((n_lon * sz.size, LANES), f32)],
    )(cutoff, block, plain_w, plain_h, *back)
    return jnp.swapaxes(new_w, 0, 1), new_h, jnp.swapaxes(mass, 0, 1)


def solution(mesh):
    in_specs = (P(None, "lat", "lon"), P("lat", "lon"), P(None, "lat", "lon"), P())
    out_specs = (P(None, "lat", "lon"), P("lat", "lon"), P(None, "lat", "lon"))
    return jax.shard_map(local, mesh=mesh, in_specs=in_specs, out_specs=out_specs, check_vma=False)
```

time: 58.7 us -> 30.9 us (0.53)
  waiting for transfers between devices: 24.6 us -> 7.06 us
  between operations: 14.1 us -> 0.7 us
  starting transfers between devices: 6.21 us -> 10.3 us
  local copies, waits for them, and re-layouts: 4.87 us -> 2.73 us
  Pallas kernels: 8.71 us -> 9.77 us
    all_gather x1 -> x0, waiting for transfers between devices: 22 us -> none  [local(): circle = lax.all_gather(tend, 'lon')]
    ppermute x2 -> x6, starting transfers between devices: 3.07 us -> 7.21 us  [meetings(): lax.ppermute(shares[k], ('lat', 'lon'), [(b * n_lon + i, b * n_lon + j) f...]
    ppermute x2 -> x6, waiting for transfers between devices: 1.19 us -> 4.64 us  [meetings(): lax.ppermute(shares[k], ('lat', 'lon'), [(b * n_lon + i, b * n_lon + j) f...]
    unnamed x20 -> x16, local copies, waits for them, and re-layouts: 4.87 us -> 2.73 us
    pallas_call x5, Pallas kernels: 7.29 us -> 8.53 us  [the longest x1 2.63 us: local(): call(rest_kernel, 'rest', [vmem] * 4 + [anywhere] + [vmem] * (n_lon - 1),...]
    ppermute x1, waiting for transfers between devices: 1.39 us -> 2.41 us  [local(): from_far = lax.ppermute(to_far, ('lat', 'lon'), far)]
  transfers between devices with their start and end apart: 5 -> 8, of which waited for: 4 -> 5; matrix products, arithmetic and copies ran while one was open for 3% -> 0% of each run, Pallas kernels for 5% -> 13%
where the time goes in v6:
time: 30.9 us; the launch traced here: 30.6 us
  starting transfers between devices  10.3 us (33%)
  Pallas kernels  9.77 us (32%)
  waiting for transfers between devices  7.06 us (23%)
  local copies, waits for them, and re-layouts  2.73 us (9%)
  between operations  0.7 us (2%)
    ppermute x6, starting transfers between devices, meetings(): lax.ppermute(shares[k], ('lat', 'lon'), [(b * n_lon + i, b * n_lon + j) f...  7.21 us
    ppermute x6, waiting for transfers between devices, meetings(): lax.ppermute(shares[k], ('lat', 'lon'), [(b * n_lon + i, b * n_lon + j) f...  4.64 us
    unnamed x16, local copies, waits for them, and re-layouts  2.73 us
    pallas_call x1, Pallas kernels, local(): call(rest_kernel, 'rest', [vmem] * 4 + [anywhere] + [vmem] * (n_lon - 1),...  2.63 us
    ppermute x1, starting transfers between devices, local(): from_far = lax.ppermute(to_far, ('lat', 'lon'), far)  2.59 us
    pallas_call x1, Pallas kernels, local(): call(rows_kernel, 'rows', [hbm] * 4, (row_pair, row_pair, shaped(2 * EXT_...  2.53 us
    ppermute x1, waiting for transfers between devices, local(): from_far = lax.ppermute(to_far, ('lat', 'lon'), far)  2.41 us
    pallas_call x1, Pallas kernels, local(): call(finish_kernel, 'finish', [smem] + [vmem] * (3 + n_lon), (shaped(*win...  1.5 us
  transfers between devices with their start and end apart: 8, of which 5 were waited for; matrix products, arithmetic and copies ran while one was open for 0% of the time, Pallas kernels for 13%

profile of v6, /device:TPU:0, one launch (start us, length us, event | category | flops | bytes accessed | tf_op | source)
XLA Modules:
  0.0 30.6 jit_solution(7878972458447298086)
XLA Ops:
  0.6 0.0 copy-start.4
  0.6 0.0 copy-start.5
  0.7 2.5 %rows.1 = (f32[120,128]{1,0:T(8,128)}, f32[120,128]{1,0:T(8,128)}, f32[32,128]{1,0:T(8,128)}, f32[6,16,2944]{2,1,0:T(8,128)}, f32[3,16,128]{2,1,0:T(8,128)}) custom-call(f32[9,2880]{1,0:T(8,128)} %h_hbm.1, f32[9,2,2880]{2,1,0:T(2,128)} %bitcast.4, bf16[9,3,2880]{2,1,0:T(4,128)(2,1)} %bitcast.5, f32[8,3,16,128]{3,2,1,0:T(8,128)} %constant.8.clone.geo_hbm), custom_call_target="tpu_custom_call" | custom-call | tf_op jit(solution)/shard_map/rows/pallas_call | solution.py:417
  3.2 0.5 %collective-permute-start = (f32[120,128]{1,0:T(8,128)}, f32[120,128]{1,0:T(8,128)S(1)}, u32[]{:S(2)}, u32[]{:S(2)}) collective-permute-start(f32[120,128]{1,0:T(8,128)} %get-tuple-element.22), channel_id=1, source_target_pairs={{0,4},{1,5},{2,6},{3,7},{4,0},{5,1},{6,2},{7,3},{8,12},{9,13},{10,... | collective-permute-start | bytes 184328 | tf_op jit(solution)/shard_map/ppermute | solution.py:446
  3.7 2.6 %collective-permute-start.1 = (f32[120,128]{1,0:T(8,128)}, f32[120,128]{1,0:T(8,128)S(1)}, u32[]{:S(2)}, u32[]{:S(2)}) collective-permute-start(f32[120,128]{1,0:T(8,128)} %get-tuple-element.23), channel_id=1, source_target_pairs={{0,2},{1,3},{2,0},{3,1},{4,8},{5,9},{6,10},{7,11},{8,4},{9,5},{10,... | collective-permute-start | bytes 184328 | tf_op jit(solution)/shard_map/ppermute | solution.py:447
  6.3 2.4 %collective-permute-done.1.far_ref = f32[120,128]{1,0:T(8,128)S(1)} collective-permute-done((f32[120,128]{1,0:T(8,128)}, f32[120,128]{1,0:T(8,128)S(1)}, u32[]{:S(2)}, u32[]{:S(2)}) %collective-permute-start.1) | collective-permute-done | bytes 61472 | tf_op jit(solution)/shard_map/ppermute | solution.py:447
  8.7 1.3 %copy-done = f32[6,16,2944]{2,1,0:T(8,128)S(1)} copy-done((f32[6,16,2944]{2,1,0:T(8,128)S(1)}, f32[6,16,2944]{2,1,0:T(8,128)}, u32[]{:S(2)}) %copy-start) | copy-done | bytes 1130520
  10.0 0.7 %copy-done.2 = f32[3,16,128]{2,1,0:T(8,128)S(1)} copy-done((f32[3,16,128]{2,1,0:T(8,128)S(1)}, f32[3,16,128]{2,1,0:T(8,128)}, u32[]{:S(2)}) %copy-start.2) | copy-done | bytes 24600
  10.7 0.7 %copy-done.6 = f32[32,128]{1,0:T(8,128)S(1)} copy-done((f32[32,128]{1,0:T(8,128)S(1)}, f32[32,128]{1,0:T(8,128)}, u32[]{:S(2)}) %copy-start.6) | copy-done | bytes 16408
  11.4 0.8 %polar.1 = (f32[168,128]{1,0:T(8,128)S(1)}, f32[184,128]{1,0:T(8,128)S(1)}, f32[184,128]{1,0:T(8,128)S(1)}, f32[184,128]{1,0:T(8,128)S(1)}) custom-call(f32[6,16,2944]{2,1,0:T(8,128)S(1)} %copy-done, f32[120,128]{1,0:T(8,128)S(1)} %collective-permute-done.near_ref, f32[120,128]{1,0:T(8,128)S(1)} %collective-permute-done.1.far_ref, f32[32,128]{1,0:T(8,128)S(1)} %copy-done.6, ...), custom_call_target="tpu_custom_call" | custom-call | tf_op jit(solution)/shard_map/polar/pallas_call | solution.py:459
  12.2 3.0 %collective-permute-start.2 = (f32[184,128]{1,0:T(8,128)S(1)}, f32[184,128]{1,0:T(8,128)S(1)}, u32[]{:S(2)}, u32[]{:S(2)}) collective-permute-start(f32[184,128]{1,0:T(8,128)S(1)} %get-tuple-element.27), channel_id=1, source_target_pairs={{0,3},{1,2},{2,1},{3,0},{4,7},{5,6},{6,5},{7,4},{8,11},{9,10},{10,... | collective-permute-start | bytes 282632 | tf_op jit(solution)/shard_map/ppermute | solution.py:455
  15.2 0.5 %collective-permute-start.3 = (f32[184,128]{1,0:T(8,128)S(1)}, f32[184,128]{1,0:T(8,128)S(1)}, u32[]{:S(2)}, u32[]{:S(2)}) collective-permute-start(f32[184,128]{1,0:T(8,128)S(1)} %get-tuple-element.28), channel_id=1, source_target_pairs={{0,1},{1,0},{2,3},{3,2},{4,6},{5,7},{6,4},{7,5},{8,9},{9,8},{10,11... | collective-permute-start | bytes 282632 | tf_op jit(solution)/shard_map/ppermute | solution.py:455
  15.8 0.1 collective-permute-start.4
  15.9 1.2 %weights.1.weights_ref = bf16[1344,96]{1,0:T(8,128)(2,1)S(1)} custom-call(s32[72]{0:T(128)S(1)} %copy-done.7, f32[192,96]{1,0:T(8,128)S(1)} %copy-done.5, f32[192,96]{1,0:T(8,128)S(1)} %copy-done.4, f32[168,128]{1,0:T(8,128)S(1)} %get-tuple-element.26.after_ref.refs_0_), custom_call_target="tpu_custom_call" | custom-call | tf_op jit(solution)/shard_map/weights/pallas_call | solution.py:467
  17.1 1.2 %collective-permute-done.2.refs_1_.refs_0_ = f32[184,128]{1,0:T(8,128)S(1)} collective-permute-done((f32[184,128]{1,0:T(8,128)S(1)}, f32[184,128]{1,0:T(8,128)S(1)}, u32[]{:S(2)}, u32[]{:S(2)}) %collective-permute-start.2) | collective-permute-done | bytes 94240 | tf_op jit(solution)/shard_map/ppermute | solution.py:455
  18.4 2.1 %collective-permute-done.3.refs_2_.refs_1_ = f32[184,128]{1,0:T(8,128)S(1)} collective-permute-done((f32[184,128]{1,0:T(8,128)S(1)}, f32[184,128]{1,0:T(8,128)S(1)}, u32[]{:S(2)}, u32[]{:S(2)}) %collective-permute-start.3) | collective-permute-done | bytes 94240 | tf_op jit(solution)/shard_map/ppermute | solution.py:455
  20.5 1.1 %filter.1 = (f32[168,128]{1,0:T(8,128)S(1)}, f32[168,128]{1,0:T(8,128)S(1)}, f32[168,128]{1,0:T(8,128)S(1)}, f32[168,128]{1,0:T(8,128)S(1)}) custom-call(bf16[1344,96]{1,0:T(8,128)(2,1)S(1)} %weights.1.weights_ref, f32[3,16,128]{2,1,0:T(8,128)S(1)} %copy-done.3, f32[168,128]{1,0:T(8,128)S(1)} %get-tuple-element.26.after_ref.refs_0_, ...), custom_call_target="tpu_custom_call" | custom-call | tf_op jit(solution)/shard_map/filter/pallas_call | solution.py:473
  21.6 1.8 %collective-permute-start.5 = (f32[168,128]{1,0:T(8,128)S(1)}, f32[168,128]{1,0:T(8,128)S(1)}, u32[]{:S(2)}, u32[]{:S(2)}) collective-permute-start(f32[168,128]{1,0:T(8,128)S(1)} %get-tuple-element.33), channel_id=1, source_target_pairs={{0,3},{1,2},{2,1},{3,0},{4,7},{5,6},{6,5},{7,4},{8,11},{9,10},{10,... | collective-permute-start | bytes 258056 | tf_op jit(solution)/shard_map/ppermute | solution.py:455
  23.4 1.1 %collective-permute-start.6 = (f32[168,128]{1,0:T(8,128)S(1)}, f32[168,128]{1,0:T(8,128)S(1)}, u32[]{:S(2)}, u32[]{:S(2)}) collective-permute-start(f32[168,128]{1,0:T(8,128)S(1)} %get-tuple-element.34), channel_id=1, source_target_pairs={{0,1},{1,0},{2,3},{3,2},{4,6},{5,7},{6,4},{7,5},{8,9},{9,8},{10,11... | collective-permute-start | bytes 258056 | tf_op jit(solution)/shard_map/ppermute | solution.py:455
  24.6 0.6 %collective-permute-start.7 = (f32[168,128]{1,0:T(8,128)S(1)}, f32[168,128]{1,0:T(8,128)S(1)}, u32[]{:S(2)}, u32[]{:S(2)}) collective-permute-start(f32[168,128]{1,0:T(8,128)S(1)} %get-tuple-element.35), channel_id=1, source_target_pairs={{0,2},{1,3},{2,0},{3,1},{4,5},{5,4},{6,7},{7,6},{8,10},{9,11},{10,... | collective-permute-start | bytes 258056 | tf_op jit(solution)/shard_map/ppermute | solution.py:455
  25.2 2.6 %rest.1 = (f32[2,9,2880]{2,1,0:T(8,128)S(1)}, f32[9,2880]{1,0:T(8,128)S(1)}, bf16[9,3,2880]{2,1,0:T(4,128)(2,1)}) custom-call(f32[6,16,2944]{2,1,0:T(8,128)S(1)} %copy-done.1, f32[120,128]{1,0:T(8,128)S(1)} %collective-permute-done.near_ref, f32[120,128]{1,0:T(8,128)S(1)} %collective-permute-done.1.far_ref, f32[3,16,128]{2,1,0:T(8,128)S(1)} %copy-done.3, ...), custom_call_target="tpu_custom_call" | custom-call | tf_op jit(solution)/shard_map/rest/pallas_call | solution.py:482
  27.8 1.1 %collective-permute-done.6.refs_2_ = f32[168,128]{1,0:T(8,128)S(1)} collective-permute-done((f32[168,128]{1,0:T(8,128)S(1)}, f32[168,128]{1,0:T(8,128)S(1)}, u32[]{:S(2)}, u32[]{:S(2)}) %collective-permute-start.6) | collective-permute-done | bytes 86048 | tf_op jit(solution)/shard_map/ppermute | solution.py:455
  28.9 0.2 collective-permute-done.7.refs_3_
  29.1 1.5 %finish.1 = (f32[9,2,2880]{2,1,0:T(2,128)}, f32[9,2880]{1,0:T(8,128)}) custom-call(s32[72]{0:T(128)S(1)} %copy-done.7, f32[6,16,2944]{2,1,0:T(8,128)S(1)} %copy-done.1, f32[2,9,2880]{2,1,0:T(8,128)S(1)} %get-tuple-element.31.plain_w_ref, f32[9,2880]{1,0:T(8,128)S(1)} %get-tuple-element.32.plain_h_ref, f32[168,128]{1,0:T(8,128)S(1)} %get-tuple-element.30.after_ref.refs_0_, ...), custom_call_target="tpu_custom_call" | custom-call | tf_op jit(solution)/shard_map/finish/pallas_call | solution.py:490
  (14 shorter events, 0.0 us)
Async XLA Ops:
  0.6 15.3 %copy-start.4 = (f32[192,96]{1,0:T(8,128)S(1)}, f32[192,96]{1,0:T(8,128)}, u32[]{:S(2)}) copy-start(f32[192,96]{1,0:T(8,128)} %constant.7.clone.inverse_ref) | copy-start | bytes 221188
  0.6 15.2 %copy-start.5 = (f32[192,96]{1,0:T(8,128)S(1)}, f32[192,96]{1,0:T(8,128)}, u32[]{:S(2)}) copy-start(f32[192,96]{1,0:T(8,128)} %constant.6.clone.n_ref) | copy-start | bytes 221188
  0.7 15.2 %copy-start.7 = (s32[72]{0:T(128)S(1)}, s32[72]{0:T(128)}, u32[]{:S(2)}) copy-start(s32[72]{0:T(128)} %cut_ref.3) | copy-start | bytes 868
  3.2 3.1 %collective-permute-start = (f32[120,128]{1,0:T(8,128)}, f32[120,128]{1,0:T(8,128)S(1)}, u32[]{:S(2)}, u32[]{:S(2)}) collective-permute-start(f32[120,128]{1,0:T(8,128)} %get-tuple-element.22), channel_id=1, source_target_pairs={{0,4},{1,5},{2,6},{3,7},{4,0},{5,1},{6,2},{7,3},{8,12},{9,13},{10,... | collective-permute-start | bytes 184328 | tf_op jit(solution)/shard_map/ppermute | solution.py:446
  3.7 5.0 %collective-permute-start.1 = (f32[120,128]{1,0:T(8,128)}, f32[120,128]{1,0:T(8,128)S(1)}, u32[]{:S(2)}, u32[]{:S(2)}) collective-permute-start(f32[120,128]{1,0:T(8,128)} %get-tuple-element.23), channel_id=1, source_target_pairs={{0,2},{1,3},{2,0},{3,1},{4,8},{5,9},{6,10},{7,11},{8,4},{9,5},{10,... | collective-permute-start | bytes 184328 | tf_op jit(solution)/shard_map/ppermute | solution.py:447
  8.7 1.3 %copy-start = (f32[6,16,2944]{2,1,0:T(8,128)S(1)}, f32[6,16,2944]{2,1,0:T(8,128)}, u32[]{:S(2)}) copy-start(f32[6,16,2944]{2,1,0:T(8,128)} %get-tuple-element.21.block_ref) | copy-start | bytes 3391492
  10.0 0.7 %copy-start.2 = (f32[3,16,128]{2,1,0:T(8,128)S(1)}, f32[3,16,128]{2,1,0:T(8,128)}, u32[]{:S(2)}) copy-start(f32[3,16,128]{2,1,0:T(8,128)} %get-tuple-element.24.geo_ref) | copy-start | bytes 73732
  10.7 0.7 %copy-start.6 = (f32[32,128]{1,0:T(8,128)S(1)}, f32[32,128]{1,0:T(8,128)}, u32[]{:S(2)}) copy-start(f32[32,128]{1,0:T(8,128)} %get-tuple-element.25.sides_ref) | copy-start | bytes 49156
  11.4 9.1 %copy-start.3 = (f32[3,16,128]{2,1,0:T(8,128)S(1)}, f32[3,16,128]{2,1,0:T(8,128)}, u32[]{:S(2)}) copy-start(f32[3,16,128]{2,1,0:T(8,128)} %get-tuple-element.24.geo_ref) | copy-start | bytes 73732
  11.4 13.7 %copy-start.1 = (f32[6,16,2944]{2,1,0:T(8,128)S(1)}, f32[6,16,2944]{2,1,0:T(8,128)}, u32[]{:S(2)}) copy-start(f32[6,16,2944]{2,1,0:T(8,128)} %get-tuple-element.21.block_ref) | copy-start | bytes 3391492
  12.2 6.1 %collective-permute-start.2 = (f32[184,128]{1,0:T(8,128)S(1)}, f32[184,128]{1,0:T(8,128)S(1)}, u32[]{:S(2)}, u32[]{:S(2)}) collective-permute-start(f32[184,128]{1,0:T(8,128)S(1)} %get-tuple-element.27), channel_id=1, source_target_pairs={{0,3},{1,2},{2,1},{3,0},{4,7},{5,6},{6,5},{7,4},{8,11},{9,10},{10,... | collective-permute-start | bytes 282632 | tf_op jit(solution)/shard_map/ppermute | solution.py:455
  15.2 5.3 %collective-permute-start.3 = (f32[184,128]{1,0:T(8,128)S(1)}, f32[184,128]{1,0:T(8,128)S(1)}, u32[]{:S(2)}, u32[]{:S(2)}) collective-permute-start(f32[184,128]{1,0:T(8,128)S(1)} %get-tuple-element.28), channel_id=1, source_target_pairs={{0,1},{1,0},{2,3},{3,2},{4,6},{5,7},{6,4},{7,5},{8,9},{9,8},{10,11... | collective-permute-start | bytes 282632 | tf_op jit(solution)/shard_map/ppermute | solution.py:455
  15.8 4.7 %collective-permute-start.4 = (f32[184,128]{1,0:T(8,128)S(1)}, f32[184,128]{1,0:T(8,128)S(1)}, u32[]{:S(2)}, u32[]{:S(2)}) collective-permute-start(f32[184,128]{1,0:T(8,128)S(1)} %get-tuple-element.29), channel_id=1, source_target_pairs={{0,2},{1,3},{2,0},{3,1},{4,5},{5,4},{6,7},{7,6},{8,10},{9,11},{10,... | collective-permute-start | bytes 282632 | tf_op jit(solution)/shard_map/ppermute | solution.py:455
  21.6 6.2 %collective-permute-start.5 = (f32[168,128]{1,0:T(8,128)S(1)}, f32[168,128]{1,0:T(8,128)S(1)}, u32[]{:S(2)}, u32[]{:S(2)}) collective-permute-start(f32[168,128]{1,0:T(8,128)S(1)} %get-tuple-element.33), channel_id=1, source_target_pairs={{0,3},{1,2},{2,1},{3,0},{4,7},{5,6},{6,5},{7,4},{8,11},{9,10},{10,... | collective-permute-start | bytes 258056 | tf_op jit(solution)/shard_map/ppermute | solution.py:455
  23.4 5.4 %collective-permute-start.6 = (f32[168,128]{1,0:T(8,128)S(1)}, f32[168,128]{1,0:T(8,128)S(1)}, u32[]{:S(2)}, u32[]{:S(2)}) collective-permute-start(f32[168,128]{1,0:T(8,128)S(1)} %get-tuple-element.34), channel_id=1, source_target_pairs={{0,1},{1,0},{2,3},{3,2},{4,6},{5,7},{6,4},{7,5},{8,9},{9,8},{10,11... | collective-permute-start | bytes 258056 | tf_op jit(solution)/shard_map/ppermute | solution.py:455
  24.6 4.5 %collective-permute-start.7 = (f32[168,128]{1,0:T(8,128)S(1)}, f32[168,128]{1,0:T(8,128)S(1)}, u32[]{:S(2)}, u32[]{:S(2)}) collective-permute-start(f32[168,128]{1,0:T(8,128)S(1)} %get-tuple-element.35), channel_id=1, source_target_pairs={{0,2},{1,3},{2,0},{3,1},{4,5},{5,4},{6,7},{7,6},{8,10},{9,11},{10,... | collective-permute-start | bytes 258056 | tf_op jit(solution)/shard_map/ppermute | solution.py:455

commit v7 on v6

--- a/solution.py
+++ b/solution.py
@@ -16,7 +16,7 @@
 PER_TILE = LANES // LEVELS
 EXT_ROWS = 16
 LIMIT = 48 * 1024 * 1024
-ALL_VMEM = 64 * 1024 * 1024 - 3600 * 1024
+ALL_VMEM = 64 * 1024 * 1024 - 256 * 1024
 
 
 class Sizes:
@@ -36,6 +36,8 @@
         self.units = 3 * rows
         self.share = -(-self.units // n_lon)
         self.size = self.share * self.stack
+        self.pole = self.units - 1
+        self.near_only = self.nlat // 6 < 2 * rows and self.units % self.share > 0
         assert self.tail <= LANES - 4 * LEVELS and rows + 2 <= EXT_ROWS and n_lat % 2 == 0
         assert n_lon >= 4 and n_lon & (n_lon - 1) == 0
 
@@ -82,32 +84,49 @@
     return n.astype(np.float32), inverse.astype(np.float32)
 
 
-def rows_kernel(sz, h_hbm, w_hbm, q_hbm, geo_hbm, near_ref, far_ref, sides_ref, block_ref, geo_ref, h_in, w_in, q_in, sems):
-    band = lax.axis_index("lat")
-    pairs = ((h_hbm, h_in), (w_hbm, w_in), (q_hbm, q_in), (geo_hbm.at[band], geo_ref))
-    copies = [pltpu.make_async_copy(source, to, sems.at[i]) for i, (source, to) in enumerate(pairs)]
+def rows_kernel(sz, h_hbm, w_hbm, q_hbm, near_ref, far_ref, sides_ref, *scratch):
+    row_refs, first_refs, last_refs, sems = scratch[:3], scratch[3:6], scratch[6:9], scratch[9]
+    rows, last = sz.rows, sz.rows - 1
+    copies = []
+    for i, source in enumerate((h_hbm, w_hbm, q_hbm)):
+        for k, row in enumerate((0, last)):
+            one = source.at[pl.ds(row, 1)] if i == 0 else source.at[row]
+            copies.append(pltpu.make_async_copy(one, row_refs[i].at[k], sems.at[i, k]))
+        for k, (start, to) in enumerate(((0, first_refs[i]), (sz.end, last_refs[i]))):
+            lanes = pl.ds(start, to.shape[-1])
+            cut = source.at[:, lanes] if i == 0 else source.at[:, :, lanes]
+            copies.append(pltpu.make_async_copy(cut, to, sems.at[i, 2 + k]))
     for copy in copies:
         copy.start()
     for copy in copies:
         copy.wait()
-    rows, last = sz.rows, sz.rows - 1
-    fields = [h_in[...], w_in[:, 1, :]] + [q_in[:, k, :].astype(jnp.float32) for k in range(3)] + [w_in[:, 0, :]]
-    for f, value in enumerate(fields):
-        block_ref[f, :rows, : sz.merged] = value
-    even = lax.rem(band, 2) == 0
+    even = lax.rem(lax.axis_index("lat"), 2) == 0
+    h_rows, w_rows, q_rows = row_refs
     for t in range(sz.tiles):
         wide = sz.span(t)
         lanes = slice(LANES * t, LANES * t + wide)
+        q = [q_rows[k, :, lanes].astype(jnp.float32) for k in range(2)]
         for f in range(5):
-            first, final = block_ref[f, 0:1, lanes], block_ref[f, last:rows, lanes]
+            if f == 0:
+                first, final = h_rows[0, :, lanes], h_rows[1, :, lanes]
+            elif f == 1:
+                first, final = w_rows[0, 1:2, lanes], w_rows[1, 1:2, lanes]
+            else:
+                first, final = q[0][f - 2 : f - 1], q[1][f - 2 : f - 1]
             at = sz.stack * f + t
             near_ref[at : at + 1, :wide] = jnp.where(even, final, first)
             far_ref[at : at + 1, :wide] = jnp.where(even, first, final)
     sides_ref[...] = jnp.zeros(sides_ref.shape, jnp.float32)
-    for k, at in enumerate((0, sz.merged - LEVELS)):
-        for place, f in enumerate((0, 5, 2, 3, 4)):
-            to = slice(LEVELS * place, LEVELS * (place + 1))
-            sides_ref[EXT_ROWS * k : EXT_ROWS * k + rows, to] = block_ref[f, :rows, at : at + LEVELS]
+    for k, (refs, at) in enumerate(((first_refs, 0), (last_refs, sz.tail - LEVELS))):
+        columns = slice(at, at + LEVELS)
+        for f in range(5):
+            if f == 0:
+                value = refs[0][:, columns]
+            elif f == 1:
+                value = refs[1][:, 0, columns]
+            else:
+                value = refs[2][:, f - 2, columns].astype(jnp.float32)
+            sides_ref[EXT_ROWS * k : EXT_ROWS * k + rows, LEVELS * f : LEVELS * (f + 1)] = value
 
 
 def add_rows(sz, ext, fields, near_ref, far_ref):
@@ -118,7 +137,8 @@
         flip = jnp.where(over_pole, -1.0, 1.0) if f == 1 else 1.0
         for t in range(sz.tiles):
             at = slice(sz.stack * f + t, sz.stack * f + t + 1)
-            near, far = near_ref[at], far_ref[at] * flip
+            near = near_ref[at]
+            far = jnp.zeros_like(near) if far_ref is None else far_ref[at] * flip
             lanes = slice(LANES * t, LANES * (t + 1))
             ext[f, sz.rows : sz.rows + 1, lanes] = jnp.where(even, near, far)
             ext[f, EXT_ROWS - 1 : EXT_ROWS, lanes] = jnp.where(even, far, near)
@@ -153,16 +173,18 @@
     return pltpu.roll(value, 1, 0)
 
 
-def polar_kernel(sz, block_ref, near_ref, far_ref, sides_ref, geo_ref, *refs):
+def polar_kernel(sz, h_ref, w_ref, near_ref, sides_ref, geo_ref, *refs):
+    far_ref, refs = (None, refs) if sz.near_only else (refs[0], refs[1:])
     out_refs, (tend_ref, ext) = refs[:-2], refs[-2:]
+    band = lax.axis_index("lat")
     ring = Tiles(sz)
     lane = ring.lane
     tiles, stack, rows = sz.tiles, sz.stack, sz.rows
-    for f, source in enumerate((0, 1, 5)):
+    for f, value in enumerate((h_ref[...], w_ref[1], w_ref[0])):
         ext[f, :rows, sz.end :] = jnp.zeros((rows, LANES), jnp.float32)
-        ext[f, :rows, : sz.merged] = block_ref[source, :rows, : sz.merged]
+        ext[f, :rows, : sz.merged] = value
     add_rows(sz, ext, 2, near_ref, far_ref)
-    inv_cos, sin_centre, cos_face = geo_ref[0], geo_ref[1], geo_ref[2]
+    inv_cos, sin_centre, cos_face = geo_ref[band, 0], geo_ref[band, 1], geo_ref[band, 2]
     ratio = sz.ratio
 
     def tile(f, t):
@@ -207,6 +229,12 @@
     used = stack * sz.units
     if used < tend_ref.shape[0]:
         tend_ref[used:, :] = jnp.zeros((tend_ref.shape[0] - used, LANES), jnp.float32)
+    if sz.near_only:
+        swap_ends(sz, tend_ref)
+        for t in range(tiles):
+            lanes = slice(LANES * t, LANES * (t + 1))
+            row = jnp.where(band < sz.n_lat // 2, ext[0, 0:1, lanes], ext[0, rows - 1 : rows, lanes])
+            tend_ref[used + t : used + t + 1, :] = row
     here = lax.axis_index("lon")
     for k, out_ref in enumerate(out_refs):
         out_ref[: sz.size] = tend_ref[sz.piece(k), :]
@@ -215,12 +243,18 @@
             out_ref[sz.size :] = jnp.where(eastward, sides_ref[EXT_ROWS:], sides_ref[:EXT_ROWS])
 
 
-def rest_kernel(sz, block_ref, near_ref, far_ref, geo_ref, after_ref, *refs):
+def rest_kernel(sz, h_ref, w_ref, q_ref, near_ref, far_ref, geo_ref, after_ref, *refs):
     met_refs, (new_w_ref, new_h_ref, mass_ref, ext) = refs[: sz.n_lon - 1], refs[sz.n_lon - 1 :]
+    band = lax.axis_index("lat")
     ring = Tiles(sz)
     lane = ring.lane
     tiles, rows = sz.tiles, sz.rows
-    ext[:, :rows, : sz.merged] = block_ref[:, :rows, : sz.merged]
+    for f in range(6):
+        if f < 2 or f == 5:
+            value = (h_ref[...], w_ref[1], w_ref[0])[min(f, 2)]
+        else:
+            value = q_ref[f - 2].astype(jnp.float32)
+        ext[f, :rows, : sz.merged] = value
     add_rows(sz, ext, 5, near_ref, far_ref)
     lane9 = lane[:rows]
     here = lax.axis_index("lon")
@@ -234,7 +268,7 @@
         own = ext[f, :rows, sz.end :]
         edge = jnp.where(lane9 < LANES - LEVELS, after, before)
         ext[f, :rows, sz.end :] = jnp.where(lane9 < sz.tail, own, edge)
-    inv_cos, sin_centre, cos_face = geo_ref[0], geo_ref[1], geo_ref[2]
+    inv_cos, sin_centre, cos_face = geo_ref[band, 0], geo_ref[band, 1], geo_ref[band, 2]
     ratio = sz.ratio
 
     def tile(f, t):
@@ -278,7 +312,7 @@
             over = flux_n * (0.5 * (q + q_n))
             merid_part = DIFFUSION * lap - (over - south(over)) * inv_cos
             mass = thick * q + TIME_STEP * (zonal_part + merid_part)
-            mass_ref[:, k, lanes] = mass[:rows, :span].astype(jnp.bfloat16)
+            mass_ref[k, :, lanes] = mass[:rows, :span].astype(jnp.bfloat16)
 
 
 def sin_pi(y):
@@ -293,10 +327,25 @@
 
 def share_of(sz, i):
     unit = lax.axis_index("lon") * sz.share + i
-    return unit // sz.rows, lax.rem(unit, sz.rows)
-
-
-def weights_kernel(sz, cut_ref, n_ref, inverse_ref, after_ref, weights_ref):
+    row = lax.rem(unit, sz.rows)
+    if sz.near_only:
+        low = lax.axis_index("lat") < sz.n_lat // 2
+        row = jnp.where(low & (unit == sz.pole), 0, row)
+        row = jnp.where(low & (unit == 2 * sz.rows), sz.rows - 1, row)
+    return unit // sz.rows, row
+
+
+def swap_ends(sz, ref):
+    low = lax.axis_index("lat") < sz.n_lat // 2
+    first = slice(2 * sz.rows * sz.stack, (2 * sz.rows + 1) * sz.stack)
+    last = slice(sz.pole * sz.stack, sz.units * sz.stack)
+    a, b = ref[first], ref[last]
+    ref[first] = jnp.where(low, b, a)
+    ref[last] = jnp.where(low, a, b)
+
+
+def weights_kernel(sz, cut_ref, n_ref, inverse_ref, far_ref, after_ref, weights_ref, to_far_ref):
+    to_far_ref[...] = far_ref[...]
     band = lax.axis_index("lat")
     size = PER_TILE * sz.stack
     for i in range(sz.share):
@@ -315,12 +364,13 @@
     for k, in_ref in enumerate(in_refs):
         gathered[sz.partner(k)] = in_ref[: sz.size]
 
+    band = lax.axis_index("lat")
     lane = lax.broadcasted_iota(jnp.int32, (share, LANES), 1)
     place = lax.broadcasted_iota(jnp.int32, (share, LANES), 0)
     by_flux = by_thick = jnp.zeros((share, LANES), jnp.float32)
     for i in range(share):
         field, row = share_of(sz, i)
-        inv_cos = geo_ref[0, pl.ds(row, 1), :]
+        inv_cos = geo_ref[band, 0, pl.ds(row, 1), :]
         by_flux = jnp.where((place == i) & (field == 0), inv_cos, by_flux)
         by_thick = jnp.where((place == i) & (field == 1), 0.5 * inv_cos, by_thick)
     sides = [gathered[s, pl.ds(sz.tiles - 1, share, stride=stack), :] for s in range(n_lon)]
@@ -339,6 +389,14 @@
         at = pl.ds(0, share, stride=stack)
         after = (s + 1) % n_lon
         gathered[after, at, :] = gathered[after, at, :] + jnp.where(lane < LEVELS, east_of, 0.0)
+
+    if sz.near_only:
+        sign = jnp.where(band == 0, 1.0, jnp.where(band == sz.n_lat - 1, -1.0, 0.0))
+        factor = jnp.where(lax.axis_index("lon") == sz.pole // share, 0.5 * sz.ratio * sign, 0.0)
+        at = sz.pole % share * stack
+        for s in range(n_lon):
+            over = gathered[(s + n_lon // 2) % n_lon, at + stack : at + 2 * stack]
+            gathered[s, at : at + stack] = gathered[s, at : at + stack] + factor * over
 
     wide = lax.broadcasted_iota(jnp.int32, (stack, LANES), 1)
     rows = PER_TILE * stack
@@ -362,11 +420,13 @@
         out_ref[...] = results[sz.partner(k)]
 
 
-def finish_kernel(sz, cut_ref, block_ref, plain_w_ref, plain_h_ref, *refs):
+def finish_kernel(sz, cut_ref, h_ref, w_ref, plain_w_ref, plain_h_ref, *refs):
     back_refs, (new_w_ref, new_h_ref, back_ref) = refs[: sz.n_lon], refs[sz.n_lon :]
     rows = sz.rows
     for k, ref in enumerate(back_refs):
         back_ref[sz.piece(k), :] = ref[...]
+    if sz.near_only:
+        swap_ends(sz, back_ref)
     row = lax.broadcasted_iota(jnp.int32, (rows, LANES), 0)
     cuts = jnp.zeros((rows, LANES), jnp.int32)
     for j in range(rows):
@@ -377,10 +437,11 @@
             span = sz.span(t)
             lanes = slice(LANES * t, LANES * t + span)
             tend = back_ref[pl.ds(sz.stack * rows * f + t, rows, stride=sz.stack), :][:, :span]
-            new = block_ref[(0, 5, 1)[f], :rows, lanes] + TIME_STEP * tend
             if f == 0:
+                new = h_ref[:, lanes] + TIME_STEP * tend
                 new_h_ref[:, lanes] = jnp.where(active[:, :span], new, plain_h_ref[:, lanes])
             else:
+                new = w_ref[f - 1, :, lanes] + TIME_STEP * tend
                 new_w_ref[:, f - 1, lanes] = jnp.where(active[:, :span], new, plain_w_ref[f - 1, :, lanes])
 
 
@@ -409,30 +470,27 @@
             name=name,
         )
 
+    geo = jnp.asarray(geometry(sz))
     n, inverse = (jnp.asarray(table) for table in offsets(sz))
 
     wind_rows = jnp.swapaxes(winds, 0, 1)
     tracer_rows = jnp.swapaxes(tracers, 0, 1)
     row_pair = shaped(5 * sz.stack, LANES)
-    to_near, to_far, sides, block, geo = call(
+    kept = [((1,), f32), ((2,), f32), ((3,), jnp.bfloat16)]
+    to_near, to_far, sides = call(
         rows_kernel,
         "rows",
-        [hbm] * 4,
-        (
-            row_pair,
-            row_pair,
-            shaped(2 * EXT_ROWS, LANES),
-            shaped(6, EXT_ROWS, sz.tiles * LANES),
-            shaped(3, EXT_ROWS, LANES),
-        ),
-        [
-            pltpu.VMEM((rows, merged), f32),
-            pltpu.VMEM((rows, 2, merged), f32),
-            pltpu.VMEM((rows, 3, merged), jnp.bfloat16),
-            pltpu.SemaphoreType.DMA((4,)),
-        ],
+        [hbm] * 3,
+        (row_pair, row_pair, shaped(2 * EXT_ROWS, LANES)),
+        [pltpu.VMEM((2,) + count + (merged,), dtype) for count, dtype in kept]
+        + [
+            pltpu.VMEM((rows,) + (count if count != (1,) else ()) + (lanes,), dtype)
+            for lanes in (LANES, sz.tail)
+            for count, dtype in kept
+        ]
+        + [pltpu.SemaphoreType.DMA((3, 4))],
         limit=ALL_VMEM,
-    )(thickness, wind_rows, tracer_rows, jnp.asarray(geometry(sz)))
+    )(thickness, wind_rows, tracer_rows)
 
     near = [(band * n_lon + i, (band ^ 1) * n_lon + i) for band in range(n_lat) for i in range(n_lon)]
     far = []
@@ -444,7 +502,7 @@
             else:
                 far.append((band * n_lon + i, band * n_lon + (i + n_lon // 2) % n_lon))
     from_near = lax.ppermute(to_near, ("lat", "lon"), near)
-    from_far = lax.ppermute(to_far, ("lat", "lon"), far)
+    first_far = () if sz.near_only else (lax.ppermute(to_far, ("lat", "lon"), far),)
 
     order = [sz.turns(False), sz.turns(True)]
 
@@ -459,17 +517,18 @@
     tends = call(
         polar_kernel,
         "polar",
-        [vmem] * 5,
+        [vmem] * (5 + len(first_far)),
         [shaped(sz.size, LANES)] + [shaped(sz.size + EXT_ROWS, LANES)] * (n_lon - 1),
         [pltpu.VMEM((n_lon * sz.size, LANES), f32), pltpu.VMEM((3, EXT_ROWS, sz.tiles * LANES), f32)],
-    )(block, from_near, from_far, sides, geo)
+    )(thickness, winds, from_near, sides, geo, *first_far)
     met = meetings(tends)
-    weights = call(
+    weights, to_far = call(
         weights_kernel,
         "weights",
-        [smem, vmem, vmem, anywhere],
-        jax.ShapeDtypeStruct((sz.share * PER_TILE * sz.stack, n_lon * sz.stack), jnp.bfloat16),
-    )(cutoff, n, inverse, tends[0])
+        [smem, vmem, vmem, vmem, anywhere],
+        (jax.ShapeDtypeStruct((sz.share * PER_TILE * sz.stack, n_lon * sz.stack), jnp.bfloat16), row_pair),
+    )(cutoff, n, inverse, to_far, tends[0])
+    from_far = lax.ppermute(to_far, ("lat", "lon"), far) if sz.near_only else first_far[0]
     worked = call(
         filter_kernel,
         "filter",
@@ -482,19 +541,19 @@
     plain_w, plain_h, mass = call(
         rest_kernel,
         "rest",
-        [vmem] * 4 + [anywhere] + [vmem] * (n_lon - 1),
-        (shaped(2, rows, merged), shaped(rows, merged), jax.ShapeDtypeStruct(tracer_rows.shape, jnp.bfloat16)),
+        [vmem] * 6 + [anywhere] + [vmem] * (n_lon - 1),
+        (shaped(2, rows, merged), shaped(rows, merged), jax.ShapeDtypeStruct(tracers.shape, jnp.bfloat16)),
         [pltpu.VMEM((6, EXT_ROWS, sz.tiles * LANES), f32)],
-    )(block, from_near, from_far, geo, worked[0], *met[1:])
+    )(thickness, winds, tracers, from_near, from_far, geo, worked[0], *met[1:])
 
     new_w, new_h = call(
         finish_kernel,
         "finish",
-        [smem] + [vmem] * (3 + n_lon),
+        [smem] + [vmem] * (4 + n_lon),
         (shaped(*wind_rows.shape), shaped(rows, merged)),
         [pltpu.VMEM((n_lon * sz.size, LANES), f32)],
-    )(cutoff, block, plain_w, plain_h, *back)
-    return jnp.swapaxes(new_w, 0, 1), new_h, jnp.swapaxes(mass, 0, 1)
+    )(cutoff, thickness, winds, plain_w, plain_h, *back)
+    return jnp.swapaxes(new_w, 0, 1), new_h, mass
 
 
 def solution(mesh):

time: 30.9 us -> 27.5 us (0.89)
  Pallas kernels: 9.77 us -> 8.07 us
  waiting for transfers between devices: 7.06 us -> 5.98 us
    ppermute x6, waiting for transfers between devices: 4.64 us -> 2.76 us  [meetings(): lax.ppermute(shares[k], ('lat', 'lon'), [(b * n_lon + i, b * n_lon + j) f...]
    pallas_call x5, Pallas kernels: 8.68 us -> 6.98 us  [the longest x1 1.73 us: local(): call(rows_kernel, 'rows', [hbm] * 3, (row_pair, row_pair, shaped(2 * EXT_...]
    ppermute x1, starting transfers between devices: 2.59 us -> 1.46 us  [local(): lax.ppermute(to_far, ('lat', 'lon'), far)]
    ppermute x6, starting transfers between devices: 7.21 us -> 8.06 us  [meetings(): lax.ppermute(shares[k], ('lat', 'lon'), [(b * n_lon + i, b * n_lon + j) f...]
    ppermute x1, waiting for transfers between devices: 2.41 us -> 3.08 us  [local(): lax.ppermute(to_far, ('lat', 'lon'), far)]
    unnamed x16 -> x19, local copies, waits for them, and re-layouts: 2.73 us -> 2.45 us
  transfers between devices with their start and end apart: 8 -> 8, of which waited for: 5 -> 4; matrix products, arithmetic and copies ran while one was open for 0% -> 6% of each run, Pallas kernels for 13% -> 11%
where the time goes in v7:
time: 27.5 us; the launch traced here: 27.3 us
  starting transfers between devices  10 us (36%)
  Pallas kernels  8.07 us (29%)
  waiting for transfers between devices  5.98 us (22%)
  local copies, waits for them, and re-layouts  2.45 us (9%)
  between operations  0.74 us (3%)
    ppermute x6, starting transfers between devices, meetings(): lax.ppermute(shares[k], ('lat', 'lon'), [(b * n_lon + i, b * n_lon + j) f...  8.06 us
    ppermute x1, waiting for transfers between devices, local(): lax.ppermute(to_far, ('lat', 'lon'), far)  3.08 us
    ppermute x6, waiting for transfers between devices, meetings(): lax.ppermute(shares[k], ('lat', 'lon'), [(b * n_lon + i, b * n_lon + j) f...  2.76 us
    unnamed x19, local copies, waits for them, and re-layouts  2.45 us
    pallas_call x1, Pallas kernels, local(): call(rows_kernel, 'rows', [hbm] * 3, (row_pair, row_pair, shaped(2 * EXT_...  1.73 us
    pallas_call x1, Pallas kernels, local(): call(rest_kernel, 'rest', [vmem] * 6 + [anywhere] + [vmem] * (n_lon - 1),...  1.71 us
    pallas_call x1, Pallas kernels, local(): call(finish_kernel, 'finish', [smem] + [vmem] * (4 + n_lon), (shaped(*win...  1.53 us
    ppermute x1, starting transfers between devices, local(): lax.ppermute(to_far, ('lat', 'lon'), far)  1.46 us
  transfers between devices with their start and end apart: 8, of which 4 were waited for; matrix products, arithmetic and copies ran while one was open for 6% of the time, Pallas kernels for 11%

profile of v7, /device:TPU:0, one launch (start us, length us, event | category | flops | bytes accessed | tf_op | source)
XLA Modules:
  0.0 27.3 jit_solution(13098438952331502513)
XLA Ops:
  0.6 1.7 %rows.1 = (f32[120,128]{1,0:T(8,128)}, f32[120,128]{1,0:T(8,128)}, f32[32,128]{1,0:T(8,128)}) custom-call(f32[9,2880]{1,0:T(8,128)} %h_ref.5, f32[9,2,2880]{2,1,0:T(2,128)} %bitcast.3, bf16[9,3,2880]{2,1,0:T(4,128)(2,1)} %bitcast.4), custom_call_target="tpu_custom_call" | custom-call | tf_op jit(solution)/shard_map/rows/pallas_call | solution.py:480
  2.4 0.0 copy-start
  2.4 0.0 copy-start.1
  2.4 0.5 %collective-permute-start = (f32[120,128]{1,0:T(8,128)}, f32[120,128]{1,0:T(8,128)S(1)}, u32[]{:S(2)}, u32[]{:S(2)}) collective-permute-start(f32[120,128]{1,0:T(8,128)} %get-tuple-element.21), channel_id=1, source_target_pairs={{0,4},{1,5},{2,6},{3,7},{4,0},{5,1},{6,2},{7,3},{8,12},{9,13},{10,... | collective-permute-start | bytes 184328 | tf_op jit(solution)/shard_map/ppermute | solution.py:504
  2.9 1.0 %copy.13.w_ref = f32[2,9,2880]{2,1,0:T(8,128)S(1)} copy(f32[2,9,2880]{2,0,1:T(2,128)} %param.7) | data formatting | bytes 414720 | tf_op args[0]
  3.9 0.1 collective-permute-done.near_ref
  4.0 0.0 copy-start.3
  4.1 0.8 %polar.1 = (f32[168,128]{1,0:T(8,128)S(1)}, f32[184,128]{1,0:T(8,128)S(1)}, f32[184,128]{1,0:T(8,128)S(1)}, f32[184,128]{1,0:T(8,128)S(1)}) custom-call(f32[9,2880]{1,0:T(8,128)S(1)} %copy-done, f32[2,9,2880]{2,1,0:T(8,128)S(1)} %copy.13.w_ref, f32[120,128]{1,0:T(8,128)S(1)} %collective-permute-done.near_ref, f32[32,128]{1,0:T(8,128)S(1)} %copy-done.5, ...), custom_call_target="tpu_custom_call" | custom-call | tf_op jit(solution)/shard_map/polar/pallas_call | solution.py:517
  4.9 3.9 %collective-permute-start.2 = (f32[184,128]{1,0:T(8,128)S(1)}, f32[184,128]{1,0:T(8,128)S(1)}, u32[]{:S(2)}, u32[]{:S(2)}) collective-permute-start(f32[184,128]{1,0:T(8,128)S(1)} %get-tuple-element.27), channel_id=1, source_target_pairs={{0,3},{1,2},{2,1},{3,0},{4,7},{5,6},{6,5},{7,4},{8,11},{9,10},{10,... | collective-permute-start | bytes 282632 | tf_op jit(solution)/shard_map/ppermute | solution.py:513
  8.7 0.5 %collective-permute-start.3 = (f32[184,128]{1,0:T(8,128)S(1)}, f32[184,128]{1,0:T(8,128)S(1)}, u32[]{:S(2)}, u32[]{:S(2)}) collective-permute-start(f32[184,128]{1,0:T(8,128)S(1)} %get-tuple-element.28), channel_id=1, source_target_pairs={{0,1},{1,0},{2,3},{3,2},{4,6},{5,7},{6,4},{7,5},{8,9},{9,8},{10,11... | collective-permute-start | bytes 282632 | tf_op jit(solution)/shard_map/ppermute | solution.py:513
  9.3 0.1 collective-permute-start.4
  9.4 0.6 %copy-done.6 = s32[72]{0:T(128)S(1)} copy-done((s32[72]{0:T(128)S(1)}, s32[72]{0:T(128)}, u32[]{:S(2)}) %copy-start.6) | copy-done | bytes 312
  10.0 1.2 %weights.1 = (bf16[1344,96]{1,0:T(8,128)(2,1)S(1)}, f32[120,128]{1,0:T(8,128)S(1)}) custom-call(s32[72]{0:T(128)S(1)} %copy-done.6, f32[192,96]{1,0:T(8,128)S(1)} %copy-done.3, f32[192,96]{1,0:T(8,128)S(1)} %copy-done.2, f32[120,128]{1,0:T(8,128)S(1)} %copy-done.4, f32[168,128]{1,0:T(8,128)S(1)} %get-tuple-element.24.after_ref.refs_0_), custom_call_target="tpu_custom_call" | custom-call | tf_op jit(solution)/shard_map/weights/pallas_call | solution.py:525
  11.3 0.6 %collective-permute-done.2.refs_1_.refs_0_ = f32[184,128]{1,0:T(8,128)S(1)} collective-permute-done((f32[184,128]{1,0:T(8,128)S(1)}, f32[184,128]{1,0:T(8,128)S(1)}, u32[]{:S(2)}, u32[]{:S(2)}) %collective-permute-start.2) | collective-permute-done | bytes 94240 | tf_op jit(solution)/shard_map/ppermute | solution.py:513
  11.8 2.2 %collective-permute-done.3.refs_2_.refs_1_ = f32[184,128]{1,0:T(8,128)S(1)} collective-permute-done((f32[184,128]{1,0:T(8,128)S(1)}, f32[184,128]{1,0:T(8,128)S(1)}, u32[]{:S(2)}, u32[]{:S(2)}) %collective-permute-start.3) | collective-permute-done | bytes 94240 | tf_op jit(solution)/shard_map/ppermute | solution.py:513
  14.0 1.1 %filter.1 = (f32[168,128]{1,0:T(8,128)S(1)}, f32[168,128]{1,0:T(8,128)S(1)}, f32[168,128]{1,0:T(8,128)S(1)}, f32[168,128]{1,0:T(8,128)S(1)}) custom-call(bf16[1344,96]{1,0:T(8,128)(2,1)S(1)} %get-tuple-element.26.weights_ref, f32[8,3,16,128]{3,2,1,0:T(8,128)S(1)} %copy-done.1, f32[168,128]{1,0:T(8,128)S(1)} %get-tuple-element.24.after_ref.refs_0_, ...), custom_call_target="tpu_custom_call" | custom-call | tf_op jit(solution)/shard_map/filter/pallas_call | solution.py:532
  15.1 1.8 %collective-permute-start.5 = (f32[168,128]{1,0:T(8,128)S(1)}, f32[168,128]{1,0:T(8,128)S(1)}, u32[]{:S(2)}, u32[]{:S(2)}) collective-permute-start(f32[168,128]{1,0:T(8,128)S(1)} %get-tuple-element.33), channel_id=1, source_target_pairs={{0,3},{1,2},{2,1},{3,0},{4,7},{5,6},{6,5},{7,4},{8,11},{9,10},{10,... | collective-permute-start | bytes 258056 | tf_op jit(solution)/shard_map/ppermute | solution.py:513
  16.9 1.2 %collective-permute-start.6 = (f32[168,128]{1,0:T(8,128)S(1)}, f32[168,128]{1,0:T(8,128)S(1)}, u32[]{:S(2)}, u32[]{:S(2)}) collective-permute-start(f32[168,128]{1,0:T(8,128)S(1)} %get-tuple-element.34), channel_id=1, source_target_pairs={{0,1},{1,0},{2,3},{3,2},{4,6},{5,7},{6,4},{7,5},{8,9},{9,8},{10,11... | collective-permute-start | bytes 258056 | tf_op jit(solution)/shard_map/ppermute | solution.py:513
  18.1 0.6 %collective-permute-start.7 = (f32[168,128]{1,0:T(8,128)S(1)}, f32[168,128]{1,0:T(8,128)S(1)}, u32[]{:S(2)}, u32[]{:S(2)}) collective-permute-start(f32[168,128]{1,0:T(8,128)S(1)} %get-tuple-element.35), channel_id=1, source_target_pairs={{0,2},{1,3},{2,0},{3,1},{4,5},{5,4},{6,7},{7,6},{8,10},{9,11},{10,... | collective-permute-start | bytes 258056 | tf_op jit(solution)/shard_map/ppermute | solution.py:513
  18.7 1.5 %collective-permute-start.1 = (f32[120,128]{1,0:T(8,128)S(1)}, f32[120,128]{1,0:T(8,128)S(1)}, u32[]{:S(2)}, u32[]{:S(2)}) collective-permute-start(f32[120,128]{1,0:T(8,128)S(1)} %get-tuple-element.25), channel_id=1, source_target_pairs={{0,2},{1,3},{2,0},{3,1},{4,8},{5,9},{6,10},{7,11},{8,4},{9,5},{10,... | collective-permute-start | bytes 184328 | tf_op jit(solution)/shard_map/ppermute | solution.py:531
  20.2 3.1 %collective-permute-done.1.far_ref = f32[120,128]{1,0:T(8,128)S(1)} collective-permute-done((f32[120,128]{1,0:T(8,128)S(1)}, f32[120,128]{1,0:T(8,128)S(1)}, u32[]{:S(2)}, u32[]{:S(2)}) %collective-permute-start.1) | collective-permute-done | bytes 61472 | tf_op jit(solution)/shard_map/ppermute | solution.py:531
  23.2 1.7 %rest.1 = (f32[2,9,2880]{2,1,0:T(8,128)S(1)}, f32[9,2880]{1,0:T(8,128)S(1)}, bf16[3,9,2880]{2,1,0:T(8,128)(2,1)S(1)}) custom-call(f32[9,2880]{1,0:T(8,128)S(1)} %copy-done, f32[2,9,2880]{2,1,0:T(8,128)S(1)} %copy.13.w_ref, bf16[3,9,2880]{2,1,0:T(8,128)(2,1)S(1)} %copy.12.q_ref, f32[120,128]{1,0:T(8,128)S(1)} %collective-permute-done.near_ref, ...), custom_call_target="tpu_custom_call" | custom-call | tf_op jit(solution)/shard_map/rest/pallas_call | solution.py:541
  25.0 0.8 %copy.14 = bf16[3,9,2880]{2,0,1:T(4,128)(2,1)} copy(bf16[3,9,2880]{2,1,0:T(8,128)(2,1)S(1)} %get-tuple-element.41) | data formatting | bytes 311040
  25.7 1.5 %finish.1 = (f32[9,2,2880]{2,1,0:T(2,128)}, f32[9,2880]{1,0:T(8,128)}) custom-call(s32[72]{0:T(128)S(1)} %copy-done.6, f32[9,2880]{1,0:T(8,128)S(1)} %copy-done, f32[2,9,2880]{2,1,0:T(8,128)S(1)} %copy.13.w_ref, f32[2,9,2880]{2,1,0:T(8,128)S(1)} %get-tuple-element.31.plain_w_ref, f32[9,2880]{1,0:T(8,128)S(1)} %get-tuple-element.32.plain_h_ref, ...), custom_call_target="tpu_custom_call" | custom-call | tf_op jit(solution)/shard_map/finish/pallas_call | solution.py:549
  (17 shorter events, 0.1 us)
Async XLA Ops:
  2.4 1.7 %copy-start = (f32[9,2880]{1,0:T(8,128)S(1)}, f32[9,2880]{1,0:T(8,128)}, u32[]{:S(2)}) copy-start(f32[9,2880]{1,0:T(8,128)} %h_ref.5) | copy-start | bytes 311044
  2.4 1.7 %copy-start.1 = (f32[8,3,16,128]{3,2,1,0:T(8,128)S(1)}, f32[8,3,16,128]{3,2,1,0:T(8,128)}, u32[]{:S(2)}) copy-start(f32[8,3,16,128]{3,2,1,0:T(8,128)} %constant.6.clone.geo_ref) | copy-start | bytes 589828
  2.4 1.6 %copy-start.5 = (f32[32,128]{1,0:T(8,128)S(1)}, f32[32,128]{1,0:T(8,128)}, u32[]{:S(2)}) copy-start(f32[32,128]{1,0:T(8,128)} %get-tuple-element.23.sides_ref) | copy-start | bytes 49156
  2.4 1.6 %collective-permute-start = (f32[120,128]{1,0:T(8,128)}, f32[120,128]{1,0:T(8,128)S(1)}, u32[]{:S(2)}, u32[]{:S(2)}) collective-permute-start(f32[120,128]{1,0:T(8,128)} %get-tuple-element.21), channel_id=1, source_target_pairs={{0,4},{1,5},{2,6},{3,7},{4,0},{5,1},{6,2},{7,3},{8,12},{9,13},{10,... | collective-permute-start | bytes 184328 | tf_op jit(solution)/shard_map/ppermute | solution.py:504
  4.0 5.3 %copy-start.2 = (f32[192,96]{1,0:T(8,128)S(1)}, f32[192,96]{1,0:T(8,128)}, u32[]{:S(2)}) copy-start(f32[192,96]{1,0:T(8,128)} %constant.8.clone.inverse_ref) | copy-start | bytes 221188
  4.0 5.3 %copy-start.3 = (f32[192,96]{1,0:T(8,128)S(1)}, f32[192,96]{1,0:T(8,128)}, u32[]{:S(2)}) copy-start(f32[192,96]{1,0:T(8,128)} %constant.7.clone.n_ref) | copy-start | bytes 221188
  4.1 5.3 %copy-start.4 = (f32[120,128]{1,0:T(8,128)S(1)}, f32[120,128]{1,0:T(8,128)}, u32[]{:S(2)}) copy-start(f32[120,128]{1,0:T(8,128)} %get-tuple-element.22.far_ref) | copy-start | bytes 184324
  4.9 7.0 %collective-permute-start.2 = (f32[184,128]{1,0:T(8,128)S(1)}, f32[184,128]{1,0:T(8,128)S(1)}, u32[]{:S(2)}, u32[]{:S(2)}) collective-permute-start(f32[184,128]{1,0:T(8,128)S(1)} %get-tuple-element.27), channel_id=1, source_target_pairs={{0,3},{1,2},{2,1},{3,0},{4,7},{5,6},{6,5},{7,4},{8,11},{9,10},{10,... | collective-permute-start | bytes 282632 | tf_op jit(solution)/shard_map/ppermute | solution.py:513
  8.7 5.3 %collective-permute-start.3 = (f32[184,128]{1,0:T(8,128)S(1)}, f32[184,128]{1,0:T(8,128)S(1)}, u32[]{:S(2)}, u32[]{:S(2)}) collective-permute-start(f32[184,128]{1,0:T(8,128)S(1)} %get-tuple-element.28), channel_id=1, source_target_pairs={{0,1},{1,0},{2,3},{3,2},{4,6},{5,7},{6,4},{7,5},{8,9},{9,8},{10,11... | collective-permute-start | bytes 282632 | tf_op jit(solution)/shard_map/ppermute | solution.py:513
  9.3 4.8 %collective-permute-start.4 = (f32[184,128]{1,0:T(8,128)S(1)}, f32[184,128]{1,0:T(8,128)S(1)}, u32[]{:S(2)}, u32[]{:S(2)}) collective-permute-start(f32[184,128]{1,0:T(8,128)S(1)} %get-tuple-element.29), channel_id=1, source_target_pairs={{0,2},{1,3},{2,0},{3,1},{4,5},{5,4},{6,7},{7,6},{8,10},{9,11},{10,... | collective-permute-start | bytes 282632 | tf_op jit(solution)/shard_map/ppermute | solution.py:513
  9.4 0.7 %copy-start.6 = (s32[72]{0:T(128)S(1)}, s32[72]{0:T(128)}, u32[]{:S(2)}) copy-start(s32[72]{0:T(128)} %cut_ref.3) | copy-start | bytes 868
  14.0 6.1 %copy-start.7 = (bf16[3,9,2880]{2,0,1:T(4,128)(2,1)S(1)}, bf16[3,9,2880]{2,0,1:T(4,128)(2,1)}, u32[]{:S(2)}) copy-start(bf16[3,9,2880]{2,0,1:T(4,128)(2,1)} %param.9) | copy-start | bytes 466564
  15.1 10.6 %collective-permute-start.5 = (f32[168,128]{1,0:T(8,128)S(1)}, f32[168,128]{1,0:T(8,128)S(1)}, u32[]{:S(2)}, u32[]{:S(2)}) collective-permute-start(f32[168,128]{1,0:T(8,128)S(1)} %get-tuple-element.33), channel_id=1, source_target_pairs={{0,3},{1,2},{2,1},{3,0},{4,7},{5,6},{6,5},{7,4},{8,11},{9,10},{10,... | collective-permute-start | bytes 258056 | tf_op jit(solution)/shard_map/ppermute | solution.py:513
  16.9 8.8 %collective-permute-start.6 = (f32[168,128]{1,0:T(8,128)S(1)}, f32[168,128]{1,0:T(8,128)S(1)}, u32[]{:S(2)}, u32[]{:S(2)}) collective-permute-start(f32[168,128]{1,0:T(8,128)S(1)} %get-tuple-element.34), channel_id=1, source_target_pairs={{0,1},{1,0},{2,3},{3,2},{4,6},{5,7},{6,4},{7,5},{8,9},{9,8},{10,11... | collective-permute-start | bytes 258056 | tf_op jit(solution)/shard_map/ppermute | solution.py:513
  18.1 7.6 %collective-permute-start.7 = (f32[168,128]{1,0:T(8,128)S(1)}, f32[168,128]{1,0:T(8,128)S(1)}, u32[]{:S(2)}, u32[]{:S(2)}) collective-permute-start(f32[168,128]{1,0:T(8,128)S(1)} %get-tuple-element.35), channel_id=1, source_target_pairs={{0,2},{1,3},{2,0},{3,1},{4,5},{5,4},{6,7},{7,6},{8,10},{9,11},{10,... | collective-permute-start | bytes 258056 | tf_op jit(solution)/shard_map/ppermute | solution.py:513
  18.7 4.6 %collective-permute-start.1 = (f32[120,128]{1,0:T(8,128)S(1)}, f32[120,128]{1,0:T(8,128)S(1)}, u32[]{:S(2)}, u32[]{:S(2)}) collective-permute-start(f32[120,128]{1,0:T(8,128)S(1)} %get-tuple-element.25), channel_id=1, source_target_pairs={{0,2},{1,3},{2,0},{3,1},{4,8},{5,9},{6,10},{7,11},{8,4},{9,5},{10,... | collective-permute-start | bytes 184328 | tf_op jit(solution)/shard_map/ppermute | solution.py:531

commit v8 on v7

--- a/solution.py
+++ b/solution.py
@@ -173,9 +173,11 @@
     return pltpu.roll(value, 1, 0)
 
 
-def polar_kernel(sz, h_ref, w_ref, near_ref, sides_ref, geo_ref, *refs):
-    far_ref, refs = (None, refs) if sz.near_only else (refs[0], refs[1:])
-    out_refs, (tend_ref, ext) = refs[:-2], refs[-2:]
+def polar_kernel(sz, h_ref, w_ref, near_ref, sides_ref, geo_ref, far_ref, *refs):
+    out_refs, (through_ref, tend_ref, ext) = refs[:-3], refs[-3:]
+    through_ref[...] = far_ref[...]
+    if sz.near_only:
+        far_ref = None
     band = lax.axis_index("lat")
     ring = Tiles(sz)
     lane = ring.lane
@@ -344,8 +346,7 @@
     ref[last] = jnp.where(low, a, b)
 
 
-def weights_kernel(sz, cut_ref, n_ref, inverse_ref, far_ref, after_ref, weights_ref, to_far_ref):
-    to_far_ref[...] = far_ref[...]
+def weights_kernel(sz, cut_ref, n_ref, inverse_ref, after_ref, weights_ref):
     band = lax.axis_index("lat")
     size = PER_TILE * sz.stack
     for i in range(sz.share):
@@ -358,7 +359,7 @@
         weights_ref[size * i : size * (i + 1)] = weights.astype(jnp.bfloat16)
 
 
-def filter_kernel(sz, weights_ref, geo_ref, *refs):
+def filter_kernel(sz, weights_ref, geo_ref, after_ref, *refs):
     n_lon, stack, share = sz.n_lon, sz.stack, sz.share
     in_refs, out_refs, (gathered, results) = refs[:n_lon], refs[n_lon : 2 * n_lon], refs[2 * n_lon :]
     for k, in_ref in enumerate(in_refs):
@@ -502,7 +503,7 @@
             else:
                 far.append((band * n_lon + i, band * n_lon + (i + n_lon // 2) % n_lon))
     from_near = lax.ppermute(to_near, ("lat", "lon"), near)
-    first_far = () if sz.near_only else (lax.ppermute(to_far, ("lat", "lon"), far),)
+    far_rows = to_far if sz.near_only else lax.ppermute(to_far, ("lat", "lon"), far)
 
     order = [sz.turns(False), sz.turns(True)]
 
@@ -514,28 +515,28 @@
         return got
 
     all_pieces = pltpu.VMEM((n_lon, sz.size, LANES), f32)
-    tends = call(
+    *tends, far_rows = call(
         polar_kernel,
         "polar",
-        [vmem] * (5 + len(first_far)),
-        [shaped(sz.size, LANES)] + [shaped(sz.size + EXT_ROWS, LANES)] * (n_lon - 1),
+        [vmem] * 6,
+        [shaped(sz.size, LANES)] + [shaped(sz.size + EXT_ROWS, LANES)] * (n_lon - 1) + [row_pair],
         [pltpu.VMEM((n_lon * sz.size, LANES), f32), pltpu.VMEM((3, EXT_ROWS, sz.tiles * LANES), f32)],
-    )(thickness, winds, from_near, sides, geo, *first_far)
+    )(thickness, winds, from_near, sides, geo, far_rows)
     met = meetings(tends)
-    weights, to_far = call(
+    from_far = lax.ppermute(far_rows, ("lat", "lon"), far) if sz.near_only else far_rows
+    weights = call(
         weights_kernel,
         "weights",
-        [smem, vmem, vmem, vmem, anywhere],
-        (jax.ShapeDtypeStruct((sz.share * PER_TILE * sz.stack, n_lon * sz.stack), jnp.bfloat16), row_pair),
-    )(cutoff, n, inverse, to_far, tends[0])
-    from_far = lax.ppermute(to_far, ("lat", "lon"), far) if sz.near_only else first_far[0]
+        [smem, vmem, vmem, anywhere],
+        jax.ShapeDtypeStruct((sz.share * PER_TILE * sz.stack, n_lon * sz.stack), jnp.bfloat16),
+    )(cutoff, n, inverse, tends[0])
     worked = call(
         filter_kernel,
         "filter",
-        [vmem] * (2 + n_lon),
+        [vmem] * 2 + [anywhere] + [vmem] * n_lon,
         [shaped(sz.size, LANES)] * n_lon,
         [all_pieces, all_pieces],
-    )(weights, geo, *met)
+    )(weights, geo, from_far, *met)
     back = meetings(worked)
 
     plain_w, plain_h, mass = call(

time: 27.5 us -> 25 us (0.909)
  waiting for transfers between devices: 5.98 us -> 3.67 us
  local copies, waits for them, and re-layouts: 2.45 us -> 1.81 us
  starting transfers between devices: 10 us -> 10.5 us
    ppermute x6, waiting for transfers between devices: 2.76 us -> 1.6 us  [meetings(): lax.ppermute(shares[k], ('lat', 'lon'), [(b * n_lon + i, b * n_lon + j) f...]
    ppermute x1, waiting for transfers between devices: 3.08 us -> 1.93 us  [local(): lax.ppermute(far_rows, ('lat', 'lon'), far)]
    unnamed x19, local copies, waits for them, and re-layouts: 2.45 us -> 1.81 us
    ppermute x1, starting transfers between devices: 1.46 us -> 1.92 us  [local(): lax.ppermute(far_rows, ('lat', 'lon'), far)]
  transfers between devices with their start and end apart: 8 -> 8, of which waited for: 4 -> 4; matrix products, arithmetic and copies ran while one was open for 6% -> 7% of each run, Pallas kernels for 11% -> 12%
where the time goes in v8:
time: 25 us; the launch traced here: 24.8 us
  starting transfers between devices  10.5 us (42%)
  Pallas kernels  8.07 us (32%)
  waiting for transfers between devices  3.67 us (15%)
  local copies, waits for them, and re-layouts  1.81 us (7%)
  between operations  0.75 us (3%)
    ppermute x6, starting transfers between devices, meetings(): lax.ppermute(shares[k], ('lat', 'lon'), [(b * n_lon + i, b * n_lon + j) f...  8.06 us
    ppermute x1, waiting for transfers between devices, local(): lax.ppermute(far_rows, ('lat', 'lon'), far)  1.93 us
    ppermute x1, starting transfers between devices, local(): lax.ppermute(far_rows, ('lat', 'lon'), far)  1.92 us
    unnamed x19, local copies, waits for them, and re-layouts  1.81 us
    pallas_call x1, Pallas kernels, local(): call(rows_kernel, 'rows', [hbm] * 3, (row_pair, row_pair, shaped(2 * EXT_...  1.73 us
    pallas_call x1, Pallas kernels, local(): call(rest_kernel, 'rest', [vmem] * 6 + [anywhere] + [vmem] * (n_lon - 1),...  1.71 us
    ppermute x6, waiting for transfers between devices, meetings(): lax.ppermute(shares[k], ('lat', 'lon'), [(b * n_lon + i, b * n_lon + j) f...  1.6 us
    pallas_call x1, Pallas kernels, local(): call(finish_kernel, 'finish', [smem] + [vmem] * (4 + n_lon), (shaped(*win...  1.52 us
  transfers between devices with their start and end apart: 8, of which 4 were waited for; matrix products, arithmetic and copies ran while one was open for 7% of the time, Pallas kernels for 12%

profile of v8, /device:TPU:0, one launch (start us, length us, event | category | flops | bytes accessed | tf_op | source)
XLA Modules:
  0.0 24.8 jit_solution(4343515030110681305)
XLA Ops:
  0.6 1.7 %rows.1 = (f32[120,128]{1,0:T(8,128)}, f32[120,128]{1,0:T(8,128)}, f32[32,128]{1,0:T(8,128)}) custom-call(f32[9,2880]{1,0:T(8,128)} %h_ref.5, f32[9,2,2880]{2,1,0:T(2,128)} %bitcast.3, bf16[9,3,2880]{2,1,0:T(4,128)(2,1)} %bitcast.4), custom_call_target="tpu_custom_call" | custom-call | tf_op jit(solution)/shard_map/rows/pallas_call | solution.py:481
  2.4 0.0 copy-start
  2.4 0.0 copy-start.1
  2.4 0.5 %collective-permute-start = (f32[120,128]{1,0:T(8,128)}, f32[120,128]{1,0:T(8,128)S(1)}, u32[]{:S(2)}, u32[]{:S(2)}) collective-permute-start(f32[120,128]{1,0:T(8,128)} %get-tuple-element.20), channel_id=1, source_target_pairs={{0,4},{1,5},{2,6},{3,7},{4,0},{5,1},{6,2},{7,3},{8,12},{9,13},{10,... | collective-permute-start | bytes 184328 | tf_op jit(solution)/shard_map/ppermute | solution.py:505
  2.9 1.0 %copy.13.w_ref = f32[2,9,2880]{2,1,0:T(8,128)S(1)} copy(f32[2,9,2880]{2,0,1:T(2,128)} %param.7) | data formatting | bytes 414720 | tf_op args[0]
  3.9 0.1 collective-permute-done.near_ref
  4.1 0.0 copy-start.2
  4.1 0.0 copy-start.3
  4.1 0.8 %polar.1 = (f32[168,128]{1,0:T(8,128)S(1)}, f32[184,128]{1,0:T(8,128)S(1)}, f32[184,128]{1,0:T(8,128)S(1)}, f32[184,128]{1,0:T(8,128)S(1)}, f32[120,128]{1,0:T(8,128)S(1)}) custom-call(f32[9,2880]{1,0:T(8,128)S(1)} %copy-done, f32[2,9,2880]{2,1,0:T(8,128)S(1)} %copy.13.w_ref, f32[120,128]{1,0:T(8,128)S(1)} %collective-permute-done.near_ref, ...), custom_call_target="tpu_custom_call" | custom-call | tf_op jit(solution)/shard_map/polar/pallas_call | solution.py:518
  4.9 3.9 %collective-permute-start.2 = (f32[184,128]{1,0:T(8,128)S(1)}, f32[184,128]{1,0:T(8,128)S(1)}, u32[]{:S(2)}, u32[]{:S(2)}) collective-permute-start(f32[184,128]{1,0:T(8,128)S(1)} %get-tuple-element.25), channel_id=1, source_target_pairs={{0,3},{1,2},{2,1},{3,0},{4,7},{5,6},{6,5},{7,4},{8,11},{9,10},{10,... | collective-permute-start | bytes 282632 | tf_op jit(solution)/shard_map/ppermute | solution.py:514
  8.7 0.5 %collective-permute-start.3 = (f32[184,128]{1,0:T(8,128)S(1)}, f32[184,128]{1,0:T(8,128)S(1)}, u32[]{:S(2)}, u32[]{:S(2)}) collective-permute-start(f32[184,128]{1,0:T(8,128)S(1)} %get-tuple-element.26), channel_id=1, source_target_pairs={{0,1},{1,0},{2,3},{3,2},{4,6},{5,7},{6,4},{7,5},{8,9},{9,8},{10,11... | collective-permute-start | bytes 282632 | tf_op jit(solution)/shard_map/ppermute | solution.py:514
  9.3 0.1 collective-permute-start.4
  9.4 1.9 %collective-permute-start.1 = (f32[120,128]{1,0:T(8,128)S(1)}, f32[120,128]{1,0:T(8,128)S(1)}, u32[]{:S(2)}, u32[]{:S(2)}) collective-permute-start(f32[120,128]{1,0:T(8,128)S(1)} %get-tuple-element.23), channel_id=1, source_target_pairs={{0,2},{1,3},{2,0},{3,1},{4,8},{5,9},{6,10},{7,11},{8,4},{9,5},{10,... | collective-permute-start | bytes 184328 | tf_op jit(solution)/shard_map/ppermute | solution.py:526
  11.3 1.2 %weights.1.weights_ref = bf16[1344,96]{1,0:T(8,128)(2,1)S(1)} custom-call(s32[72]{0:T(128)S(1)} %copy-done.6, f32[192,96]{1,0:T(8,128)S(1)} %copy-done.3, f32[192,96]{1,0:T(8,128)S(1)} %copy-done.2, f32[168,128]{1,0:T(8,128)S(1)} %get-tuple-element.24.after_ref.refs_0_), custom_call_target="tpu_custom_call" | custom-call | tf_op jit(solution)/shard_map/weights/pallas_call | solution.py:527
  12.6 1.9 %collective-permute-done.1.after_ref.far_ref = f32[120,128]{1,0:T(8,128)S(1)} collective-permute-done((f32[120,128]{1,0:T(8,128)S(1)}, f32[120,128]{1,0:T(8,128)S(1)}, u32[]{:S(2)}, u32[]{:S(2)}) %collective-permute-start.1) | collective-permute-done | bytes 61472 | tf_op jit(solution)/shard_map/ppermute | solution.py:526
  14.5 1.1 %filter.1 = (f32[168,128]{1,0:T(8,128)S(1)}, f32[168,128]{1,0:T(8,128)S(1)}, f32[168,128]{1,0:T(8,128)S(1)}, f32[168,128]{1,0:T(8,128)S(1)}) custom-call(bf16[1344,96]{1,0:T(8,128)(2,1)S(1)} %weights.1.weights_ref, f32[8,3,16,128]{3,2,1,0:T(8,128)S(1)} %copy-done.1, f32[120,128]{1,0:T(8,128)S(1)} %collective-permute-done.1.after_ref.far_ref, ...), custom_call_target="tpu_custom_call" | custom-call | tf_op jit(solution)/shard_map/filter/pallas_call | solution.py:533
  15.6 2.0 %collective-permute-start.5 = (f32[168,128]{1,0:T(8,128)S(1)}, f32[168,128]{1,0:T(8,128)S(1)}, u32[]{:S(2)}, u32[]{:S(2)}) collective-permute-start(f32[168,128]{1,0:T(8,128)S(1)} %get-tuple-element.31), channel_id=1, source_target_pairs={{0,3},{1,2},{2,1},{3,0},{4,7},{5,6},{6,5},{7,4},{8,11},{9,10},{10,... | collective-permute-start | bytes 258056 | tf_op jit(solution)/shard_map/ppermute | solution.py:514
  17.6 1.2 %collective-permute-start.6 = (f32[168,128]{1,0:T(8,128)S(1)}, f32[168,128]{1,0:T(8,128)S(1)}, u32[]{:S(2)}, u32[]{:S(2)}) collective-permute-start(f32[168,128]{1,0:T(8,128)S(1)} %get-tuple-element.32), channel_id=1, source_target_pairs={{0,1},{1,0},{2,3},{3,2},{4,6},{5,7},{6,4},{7,5},{8,9},{9,8},{10,11... | collective-permute-start | bytes 258056 | tf_op jit(solution)/shard_map/ppermute | solution.py:514
  18.8 0.4 %collective-permute-start.7 = (f32[168,128]{1,0:T(8,128)S(1)}, f32[168,128]{1,0:T(8,128)S(1)}, u32[]{:S(2)}, u32[]{:S(2)}) collective-permute-start(f32[168,128]{1,0:T(8,128)S(1)} %get-tuple-element.33), channel_id=1, source_target_pairs={{0,2},{1,3},{2,0},{3,1},{4,5},{5,4},{6,7},{7,6},{8,10},{9,11},{10,... | collective-permute-start | bytes 258056 | tf_op jit(solution)/shard_map/ppermute | solution.py:514
  19.2 1.7 %rest.1 = (f32[2,9,2880]{2,1,0:T(8,128)S(1)}, f32[9,2880]{1,0:T(8,128)S(1)}, bf16[3,9,2880]{2,1,0:T(8,128)(2,1)S(1)}) custom-call(f32[9,2880]{1,0:T(8,128)S(1)} %copy-done, f32[2,9,2880]{2,1,0:T(8,128)S(1)} %copy.13.w_ref, bf16[3,9,2880]{2,1,0:T(8,128)(2,1)S(1)} %copy.12.q_ref, f32[120,128]{1,0:T(8,128)S(1)} %collective-permute-done.near_ref, ...), custom_call_target="tpu_custom_call" | custom-call | tf_op jit(solution)/shard_map/rest/pallas_call | solution.py:542
  20.9 0.8 %copy.14 = bf16[3,9,2880]{2,0,1:T(4,128)(2,1)} copy(bf16[3,9,2880]{2,1,0:T(8,128)(2,1)S(1)} %get-tuple-element.39) | data formatting | bytes 311040
  21.7 0.9 %collective-permute-done.6.refs_2_ = f32[168,128]{1,0:T(8,128)S(1)} collective-permute-done((f32[168,128]{1,0:T(8,128)S(1)}, f32[168,128]{1,0:T(8,128)S(1)}, u32[]{:S(2)}, u32[]{:S(2)}) %collective-permute-start.6) | collective-permute-done | bytes 86048 | tf_op jit(solution)/shard_map/ppermute | solution.py:514
  22.6 0.7 %collective-permute-done.7.refs_3_ = f32[168,128]{1,0:T(8,128)S(1)} collective-permute-done((f32[168,128]{1,0:T(8,128)S(1)}, f32[168,128]{1,0:T(8,128)S(1)}, u32[]{:S(2)}, u32[]{:S(2)}) %collective-permute-start.7) | collective-permute-done | bytes 86048 | tf_op jit(solution)/shard_map/ppermute | solution.py:514
  23.3 1.5 %finish.1 = (f32[9,2,2880]{2,1,0:T(2,128)}, f32[9,2880]{1,0:T(8,128)}) custom-call(s32[72]{0:T(128)S(1)} %copy-done.6, f32[9,2880]{1,0:T(8,128)S(1)} %copy-done, f32[2,9,2880]{2,1,0:T(8,128)S(1)} %copy.13.w_ref, f32[2,9,2880]{2,1,0:T(8,128)S(1)} %get-tuple-element.29.plain_w_ref, f32[9,2880]{1,0:T(8,128)S(1)} %get-tuple-element.30.plain_h_ref, ...), custom_call_target="tpu_custom_call" | custom-call | tf_op jit(solution)/shard_map/finish/pallas_call | solution.py:550
  (17 shorter events, 0.1 us)
Async XLA Ops:
  2.4 1.7 %copy-start = (f32[9,2880]{1,0:T(8,128)S(1)}, f32[9,2880]{1,0:T(8,128)}, u32[]{:S(2)}) copy-start(f32[9,2880]{1,0:T(8,128)} %h_ref.5) | copy-start | bytes 311044
  2.4 1.7 %copy-start.1 = (f32[8,3,16,128]{3,2,1,0:T(8,128)S(1)}, f32[8,3,16,128]{3,2,1,0:T(8,128)}, u32[]{:S(2)}) copy-start(f32[8,3,16,128]{3,2,1,0:T(8,128)} %constant.6.clone.geo_ref) | copy-start | bytes 589828
  2.4 1.7 %copy-start.4 = (f32[120,128]{1,0:T(8,128)S(1)}, f32[120,128]{1,0:T(8,128)}, u32[]{:S(2)}) copy-start(f32[120,128]{1,0:T(8,128)} %get-tuple-element.22.far_ref) | copy-start | bytes 184324
  2.4 1.6 %copy-start.5 = (f32[32,128]{1,0:T(8,128)S(1)}, f32[32,128]{1,0:T(8,128)}, u32[]{:S(2)}) copy-start(f32[32,128]{1,0:T(8,128)} %get-tuple-element.21.sides_ref) | copy-start | bytes 49156
  2.4 1.6 %collective-permute-start = (f32[120,128]{1,0:T(8,128)}, f32[120,128]{1,0:T(8,128)S(1)}, u32[]{:S(2)}, u32[]{:S(2)}) collective-permute-start(f32[120,128]{1,0:T(8,128)} %get-tuple-element.20), channel_id=1, source_target_pairs={{0,4},{1,5},{2,6},{3,7},{4,0},{5,1},{6,2},{7,3},{8,12},{9,13},{10,... | collective-permute-start | bytes 184328 | tf_op jit(solution)/shard_map/ppermute | solution.py:505
  4.1 7.2 %copy-start.2 = (f32[192,96]{1,0:T(8,128)S(1)}, f32[192,96]{1,0:T(8,128)}, u32[]{:S(2)}) copy-start(f32[192,96]{1,0:T(8,128)} %constant.8.clone.inverse_ref) | copy-start | bytes 221188
  4.1 7.2 %copy-start.3 = (f32[192,96]{1,0:T(8,128)S(1)}, f32[192,96]{1,0:T(8,128)}, u32[]{:S(2)}) copy-start(f32[192,96]{1,0:T(8,128)} %constant.7.clone.n_ref) | copy-start | bytes 221188
  4.9 9.6 %collective-permute-start.2 = (f32[184,128]{1,0:T(8,128)S(1)}, f32[184,128]{1,0:T(8,128)S(1)}, u32[]{:S(2)}, u32[]{:S(2)}) collective-permute-start(f32[184,128]{1,0:T(8,128)S(1)} %get-tuple-element.25), channel_id=1, source_target_pairs={{0,3},{1,2},{2,1},{3,0},{4,7},{5,6},{6,5},{7,4},{8,11},{9,10},{10,... | collective-permute-start | bytes 282632 | tf_op jit(solution)/shard_map/ppermute | solution.py:514
  8.7 5.8 %collective-permute-start.3 = (f32[184,128]{1,0:T(8,128)S(1)}, f32[184,128]{1,0:T(8,128)S(1)}, u32[]{:S(2)}, u32[]{:S(2)}) collective-permute-start(f32[184,128]{1,0:T(8,128)S(1)} %get-tuple-element.26), channel_id=1, source_target_pairs={{0,1},{1,0},{2,3},{3,2},{4,6},{5,7},{6,4},{7,5},{8,9},{9,8},{10,11... | collective-permute-start | bytes 282632 | tf_op jit(solution)/shard_map/ppermute | solution.py:514
  9.3 5.2 %collective-permute-start.4 = (f32[184,128]{1,0:T(8,128)S(1)}, f32[184,128]{1,0:T(8,128)S(1)}, u32[]{:S(2)}, u32[]{:S(2)}) collective-permute-start(f32[184,128]{1,0:T(8,128)S(1)} %get-tuple-element.27), channel_id=1, source_target_pairs={{0,2},{1,3},{2,0},{3,1},{4,5},{5,4},{6,7},{7,6},{8,10},{9,11},{10,... | collective-permute-start | bytes 282632 | tf_op jit(solution)/shard_map/ppermute | solution.py:514
  9.4 1.9 %copy-start.6 = (s32[72]{0:T(128)S(1)}, s32[72]{0:T(128)}, u32[]{:S(2)}) copy-start(s32[72]{0:T(128)} %cut_ref.3) | copy-start | bytes 868
  9.4 5.1 %collective-permute-start.1 = (f32[120,128]{1,0:T(8,128)S(1)}, f32[120,128]{1,0:T(8,128)S(1)}, u32[]{:S(2)}, u32[]{:S(2)}) collective-permute-start(f32[120,128]{1,0:T(8,128)S(1)} %get-tuple-element.23), channel_id=1, source_target_pairs={{0,2},{1,3},{2,0},{3,1},{4,8},{5,9},{6,10},{7,11},{8,4},{9,5},{10,... | collective-permute-start | bytes 184328 | tf_op jit(solution)/shard_map/ppermute | solution.py:526
  12.6 6.6 %copy-start.7 = (bf16[3,9,2880]{2,0,1:T(4,128)(2,1)S(1)}, bf16[3,9,2880]{2,0,1:T(4,128)(2,1)}, u32[]{:S(2)}) copy-start(bf16[3,9,2880]{2,0,1:T(4,128)(2,1)} %param.9) | copy-start | bytes 466564
  15.6 6.1 %collective-permute-start.5 = (f32[168,128]{1,0:T(8,128)S(1)}, f32[168,128]{1,0:T(8,128)S(1)}, u32[]{:S(2)}, u32[]{:S(2)}) collective-permute-start(f32[168,128]{1,0:T(8,128)S(1)} %get-tuple-element.31), channel_id=1, source_target_pairs={{0,3},{1,2},{2,1},{3,0},{4,7},{5,6},{6,5},{7,4},{8,11},{9,10},{10,... | collective-permute-start | bytes 258056 | tf_op jit(solution)/shard_map/ppermute | solution.py:514
  17.6 5.0 %collective-permute-start.6 = (f32[168,128]{1,0:T(8,128)S(1)}, f32[168,128]{1,0:T(8,128)S(1)}, u32[]{:S(2)}, u32[]{:S(2)}) collective-permute-start(f32[168,128]{1,0:T(8,128)S(1)} %get-tuple-element.32), channel_id=1, source_target_pairs={{0,1},{1,0},{2,3},{3,2},{4,6},{5,7},{6,4},{7,5},{8,9},{9,8},{10,11... | collective-permute-start | bytes 258056 | tf_op jit(solution)/shard_map/ppermute | solution.py:514
  18.8 4.5 %collective-permute-start.7 = (f32[168,128]{1,0:T(8,128)S(1)}, f32[168,128]{1,0:T(8,128)S(1)}, u32[]{:S(2)}, u32[]{:S(2)}) collective-permute-start(f32[168,128]{1,0:T(8,128)S(1)} %get-tuple-element.33), channel_id=1, source_target_pairs={{0,2},{1,3},{2,0},{3,1},{4,5},{5,4},{6,7},{7,6},{8,10},{9,11},{10,... | collective-permute-start | bytes 258056 | tf_op jit(solution)/shard_map/ppermute | solution.py:514

commit v9 on v8

--- a/solution.py
+++ b/solution.py
@@ -16,7 +16,7 @@
 PER_TILE = LANES // LEVELS
 EXT_ROWS = 16
 LIMIT = 48 * 1024 * 1024
-ALL_VMEM = 64 * 1024 * 1024 - 256 * 1024
+MOST_VMEM = 64 * 1024 * 1024 - 10500 * 1024
 
 
 class Sizes:
@@ -84,9 +84,10 @@
     return n.astype(np.float32), inverse.astype(np.float32)
 
 
-def rows_kernel(sz, h_hbm, w_hbm, q_hbm, near_ref, far_ref, sides_ref, *scratch):
+def edges_kernel(sz, h_hbm, w_hbm, q_hbm, near_ref, far_ref, sides_ref, *scratch):
     row_refs, first_refs, last_refs, sems = scratch[:3], scratch[3:6], scratch[6:9], scratch[9]
     rows, last = sz.rows, sz.rows - 1
+    even = lax.rem(lax.axis_index("lat"), 2) == 0
     copies = []
     for i, source in enumerate((h_hbm, w_hbm, q_hbm)):
         for k, row in enumerate((0, last)):
@@ -100,7 +101,6 @@
         copy.start()
     for copy in copies:
         copy.wait()
-    even = lax.rem(lax.axis_index("lat"), 2) == 0
     h_rows, w_rows, q_rows = row_refs
     for t in range(sz.tiles):
         wide = sz.span(t)
@@ -113,8 +113,9 @@
                 first, final = w_rows[0, 1:2, lanes], w_rows[1, 1:2, lanes]
             else:
                 first, final = q[0][f - 2 : f - 1], q[1][f - 2 : f - 1]
+                at = sz.stack * (f - 2) + t
+                near_ref[at : at + 1, :wide] = jnp.where(even, final, first)
             at = sz.stack * f + t
-            near_ref[at : at + 1, :wide] = jnp.where(even, final, first)
             far_ref[at : at + 1, :wide] = jnp.where(even, first, final)
     sides_ref[...] = jnp.zeros(sides_ref.shape, jnp.float32)
     for k, (refs, at) in enumerate(((first_refs, 0), (last_refs, sz.tail - LEVELS))):
@@ -129,17 +130,24 @@
             sides_ref[EXT_ROWS * k : EXT_ROWS * k + rows, LEVELS * f : LEVELS * (f + 1)] = value
 
 
-def add_rows(sz, ext, fields, near_ref, far_ref):
+def add_rows(sz, ext, near_h_ref, near_w_ref, near_q_ref, far_ref):
     band = lax.axis_index("lat")
     even = lax.rem(band, 2) == 0
     over_pole = (band == 0) | (band == sz.n_lat - 1)
-    for f in range(fields):
+    last = sz.rows - 1
+    for f in range(2 if near_q_ref is None else 5):
         flip = jnp.where(over_pole, -1.0, 1.0) if f == 1 else 1.0
         for t in range(sz.tiles):
-            at = slice(sz.stack * f + t, sz.stack * f + t + 1)
-            near = near_ref[at]
-            far = jnp.zeros_like(near) if far_ref is None else far_ref[at] * flip
-            lanes = slice(LANES * t, LANES * (t + 1))
+            lanes = slice(LANES * t, LANES * t + sz.span(t))
+            if f == 0:
+                near = jnp.where(even, near_h_ref[0:1, lanes], near_h_ref[last : sz.rows, lanes])
+            elif f == 1:
+                near = jnp.where(even, near_w_ref[0, 1:2, lanes], near_w_ref[last, 1:2, lanes])
+            else:
+                at = sz.stack * (f - 2) + t
+                near = near_q_ref[at : at + 1, : sz.span(t)]
+            at = sz.stack * f + t
+            far = jnp.zeros_like(near) if far_ref is None else far_ref[at : at + 1, : sz.span(t)] * flip
             ext[f, sz.rows : sz.rows + 1, lanes] = jnp.where(even, near, far)
             ext[f, EXT_ROWS - 1 : EXT_ROWS, lanes] = jnp.where(even, far, near)
 
@@ -173,19 +181,20 @@
     return pltpu.roll(value, 1, 0)
 
 
-def polar_kernel(sz, h_ref, w_ref, near_ref, sides_ref, geo_ref, far_ref, *refs):
-    out_refs, (through_ref, tend_ref, ext) = refs[:-3], refs[-3:]
-    through_ref[...] = far_ref[...]
+def polar_kernel(sz, h_ref, w_ref, near_h_ref, near_w_ref, sides_ref, geo_ref, far_ref, near_q_ref, *refs):
+    out_refs, (far_out, near_out, tend_ref, ext) = refs[:-4], refs[-4:]
+    far_out[...] = far_ref[...]
+    near_out[...] = near_q_ref[...]
     if sz.near_only:
         far_ref = None
     band = lax.axis_index("lat")
     ring = Tiles(sz)
     lane = ring.lane
     tiles, stack, rows = sz.tiles, sz.stack, sz.rows
-    for f, value in enumerate((h_ref[...], w_ref[1], w_ref[0])):
+    for f, value in enumerate((h_ref[...], w_ref[:, 1, :], w_ref[:, 0, :])):
         ext[f, :rows, sz.end :] = jnp.zeros((rows, LANES), jnp.float32)
         ext[f, :rows, : sz.merged] = value
-    add_rows(sz, ext, 2, near_ref, far_ref)
+    add_rows(sz, ext, near_h_ref, near_w_ref, None, far_ref)
     inv_cos, sin_centre, cos_face = geo_ref[band, 0], geo_ref[band, 1], geo_ref[band, 2]
     ratio = sz.ratio
 
@@ -245,7 +254,7 @@
             out_ref[sz.size :] = jnp.where(eastward, sides_ref[EXT_ROWS:], sides_ref[:EXT_ROWS])
 
 
-def rest_kernel(sz, h_ref, w_ref, q_ref, near_ref, far_ref, geo_ref, after_ref, *refs):
+def rest_kernel(sz, h_ref, w_ref, q_ref, near_h_ref, near_w_ref, near_q_ref, far_ref, geo_ref, after_ref, *refs):
     met_refs, (new_w_ref, new_h_ref, mass_ref, ext) = refs[: sz.n_lon - 1], refs[sz.n_lon - 1 :]
     band = lax.axis_index("lat")
     ring = Tiles(sz)
@@ -253,11 +262,11 @@
     tiles, rows = sz.tiles, sz.rows
     for f in range(6):
         if f < 2 or f == 5:
-            value = (h_ref[...], w_ref[1], w_ref[0])[min(f, 2)]
+            value = (h_ref[...], w_ref[:, 1, :], w_ref[:, 0, :])[min(f, 2)]
         else:
             value = q_ref[f - 2].astype(jnp.float32)
         ext[f, :rows, : sz.merged] = value
-    add_rows(sz, ext, 5, near_ref, far_ref)
+    add_rows(sz, ext, near_h_ref, near_w_ref, near_q_ref, far_ref)
     lane9 = lane[:rows]
     here = lax.axis_index("lon")
     from_e = from_w = met_refs[0][sz.size :]
@@ -359,7 +368,7 @@
         weights_ref[size * i : size * (i + 1)] = weights.astype(jnp.bfloat16)
 
 
-def filter_kernel(sz, weights_ref, geo_ref, after_ref, *refs):
+def filter_kernel(sz, weights_ref, geo_ref, after_ref, also_after_ref, *refs):
     n_lon, stack, share = sz.n_lon, sz.stack, sz.share
     in_refs, out_refs, (gathered, results) = refs[:n_lon], refs[n_lon : 2 * n_lon], refs[2 * n_lon :]
     for k, in_ref in enumerate(in_refs):
@@ -442,7 +451,7 @@
                 new = h_ref[:, lanes] + TIME_STEP * tend
                 new_h_ref[:, lanes] = jnp.where(active[:, :span], new, plain_h_ref[:, lanes])
             else:
-                new = w_ref[f - 1, :, lanes] + TIME_STEP * tend
+                new = w_ref[:, f - 1, lanes] + TIME_STEP * tend
                 new_w_ref[:, f - 1, lanes] = jnp.where(active[:, :span], new, plain_w_ref[f - 1, :, lanes])
 
 
@@ -476,13 +485,13 @@
 
     wind_rows = jnp.swapaxes(winds, 0, 1)
     tracer_rows = jnp.swapaxes(tracers, 0, 1)
-    row_pair = shaped(5 * sz.stack, LANES)
+    far_row, near_row = shaped(5 * sz.stack, LANES), shaped(3 * sz.stack, LANES)
     kept = [((1,), f32), ((2,), f32), ((3,), jnp.bfloat16)]
-    to_near, to_far, sides = call(
-        rows_kernel,
-        "rows",
+    near_q, far_rows, sides = call(
+        edges_kernel,
+        "edges",
         [hbm] * 3,
-        (row_pair, row_pair, shaped(2 * EXT_ROWS, LANES)),
+        (near_row, far_row, shaped(2 * EXT_ROWS, LANES)),
         [pltpu.VMEM((2,) + count + (merged,), dtype) for count, dtype in kept]
         + [
             pltpu.VMEM((rows,) + (count if count != (1,) else ()) + (lanes,), dtype)
@@ -490,7 +499,7 @@
             for count, dtype in kept
         ]
         + [pltpu.SemaphoreType.DMA((3, 4))],
-        limit=ALL_VMEM,
+        limit=MOST_VMEM,
     )(thickness, wind_rows, tracer_rows)
 
     near = [(band * n_lon + i, (band ^ 1) * n_lon + i) for band in range(n_lat) for i in range(n_lon)]
@@ -502,8 +511,10 @@
                 far.append((band * n_lon + i, other * n_lon + i))
             else:
                 far.append((band * n_lon + i, band * n_lon + (i + n_lon // 2) % n_lon))
-    from_near = lax.ppermute(to_near, ("lat", "lon"), near)
-    far_rows = to_far if sz.near_only else lax.ppermute(to_far, ("lat", "lon"), far)
+    near_h = lax.ppermute(thickness, ("lat", "lon"), near)
+    near_w = lax.ppermute(wind_rows, ("lat", "lon"), near)
+    if not sz.near_only:
+        far_rows = lax.ppermute(far_rows, ("lat", "lon"), far)
 
     order = [sz.turns(False), sz.turns(True)]
 
@@ -515,14 +526,15 @@
         return got
 
     all_pieces = pltpu.VMEM((n_lon, sz.size, LANES), f32)
-    *tends, far_rows = call(
+    *tends, far_rows, near_q = call(
         polar_kernel,
         "polar",
-        [vmem] * 6,
-        [shaped(sz.size, LANES)] + [shaped(sz.size + EXT_ROWS, LANES)] * (n_lon - 1) + [row_pair],
+        [vmem] * 8,
+        [shaped(sz.size, LANES)] + [shaped(sz.size + EXT_ROWS, LANES)] * (n_lon - 1) + [far_row, near_row],
         [pltpu.VMEM((n_lon * sz.size, LANES), f32), pltpu.VMEM((3, EXT_ROWS, sz.tiles * LANES), f32)],
-    )(thickness, winds, from_near, sides, geo, far_rows)
+    )(thickness, wind_rows, near_h, near_w, sides, geo, far_rows, near_q)
     met = meetings(tends)
+    near_q = lax.ppermute(near_q, ("lat", "lon"), near)
     from_far = lax.ppermute(far_rows, ("lat", "lon"), far) if sz.near_only else far_rows
     weights = call(
         weights_kernel,
@@ -533,19 +545,19 @@
     worked = call(
         filter_kernel,
         "filter",
-        [vmem] * 2 + [anywhere] + [vmem] * n_lon,
+        [vmem] * 2 + [anywhere] * 2 + [vmem] * n_lon,
         [shaped(sz.size, LANES)] * n_lon,
         [all_pieces, all_pieces],
-    )(weights, geo, from_far, *met)
+    )(weights, geo, from_far, near_q, *met)
     back = meetings(worked)
 
     plain_w, plain_h, mass = call(
         rest_kernel,
         "rest",
-        [vmem] * 6 + [anywhere] + [vmem] * (n_lon - 1),
+        [vmem] * 8 + [anywhere] + [vmem] * (n_lon - 1),
         (shaped(2, rows, merged), shaped(rows, merged), jax.ShapeDtypeStruct(tracers.shape, jnp.bfloat16)),
         [pltpu.VMEM((6, EXT_ROWS, sz.tiles * LANES), f32)],
-    )(thickness, winds, tracers, from_near, from_far, geo, worked[0], *met[1:])
+    )(thickness, wind_rows, tracers, near_h, near_w, near_q, from_far, geo, worked[0], *met[1:])
 
     new_w, new_h = call(
         finish_kernel,
@@ -553,7 +565,7 @@
         [smem] + [vmem] * (4 + n_lon),
         (shaped(*wind_rows.shape), shaped(rows, merged)),
         [pltpu.VMEM((n_lon * sz.size, LANES), f32)],
-    )(cutoff, thickness, winds, plain_w, plain_h, *back)
+    )(cutoff, thickness, wind_rows, plain_w, plain_h, *back)
     return jnp.swapaxes(new_w, 0, 1), new_h, mass
 
 

time: 25 us -> 23.8 us (0.952)
  Pallas kernels: 8.07 us -> 7.57 us
  local copies, waits for them, and re-layouts: 1.81 us -> 1.31 us
  waiting for transfers between devices: 3.67 us -> 3.3 us
    ppermute x1, waiting for transfers between devices: 1.93 us -> 1.28 us  [local(): lax.ppermute(far_rows, ('lat', 'lon'), far)]
    pallas_call x4, Pallas kernels: 5.3 us -> 4.72 us  [the longest x1 1.72 us: local(): call(rest_kernel, 'rest', [vmem] * 8 + [anywhere] + [vmem] * (n_lon - 1),...]
    unnamed x19 -> x16, local copies, waits for them, and re-layouts: 1.81 us -> 1.31 us
    ppermute x1 -> x3, starting transfers between devices: 0.52 us -> 0.76 us  [the longest x1 0.52 us: local(): near_w = lax.ppermute(wind_rows, ('lat', 'lon'), near)]
  transfers between devices with their start and end apart: 8 -> 10, of which waited for: 4 -> 4; matrix products, arithmetic and copies ran while one was open for 7% -> 3% of each run, Pallas kernels for 12% -> 18%
where the time goes in v9:
time: 23.8 us; the launch traced here: 23.6 us
  starting transfers between devices  10.7 us (45%)
  Pallas kernels  7.57 us (32%)
  waiting for transfers between devices  3.3 us (14%)
  local copies, waits for them, and re-layouts  1.31 us (6%)
  between operations  0.73 us (3%)
    ppermute x6, starting transfers between devices, meetings(): lax.ppermute(shares[k], ('lat', 'lon'), [(b * n_lon + i, b * n_lon + j) f...  8 us
    ppermute x1, starting transfers between devices, local(): lax.ppermute(far_rows, ('lat', 'lon'), far)  1.92 us
    pallas_call x1, Pallas kernels, local(): call(rest_kernel, 'rest', [vmem] * 8 + [anywhere] + [vmem] * (n_lon - 1),...  1.72 us
    ppermute x6, waiting for transfers between devices, meetings(): lax.ppermute(shares[k], ('lat', 'lon'), [(b * n_lon + i, b * n_lon + j) f...  1.64 us
    pallas_call x1, Pallas kernels, local(): call(finish_kernel, 'finish', [smem] + [vmem] * (4 + n_lon), (shaped(*win...  1.61 us
    unnamed x16, local copies, waits for them, and re-layouts  1.31 us
    ppermute x1, waiting for transfers between devices, local(): lax.ppermute(far_rows, ('lat', 'lon'), far)  1.28 us
    pallas_call x1, Pallas kernels, local(): call(weights_kernel, 'weights', [smem, vmem, vmem, anywhere], jax.ShapeDt...  1.24 us
  transfers between devices with their start and end apart: 10, of which 4 were waited for; matrix products, arithmetic and copies ran while one was open for 3% of the time, Pallas kernels for 18%

profile of v9, /device:TPU:0, one launch (start us, length us, event | category | flops | bytes accessed | tf_op | source)
XLA Modules:
  0.0 23.6 jit_solution(137416695007584931)
XLA Ops:
  0.6 0.5 %collective-permute-start.1 = (f32[9,2,2880]{2,1,0:T(2,128)}, f32[9,2,2880]{2,1,0:T(2,128)S(1)}, u32[]{:S(2)}, u32[]{:S(2)}) collective-permute-start(f32[9,2,2880]{2,1,0:T(2,128)} %bitcast.3), channel_id=1, source_target_pairs={{0,4},{1,5},{2,6},{3,7},{4,0},{5,1},{6,2},{7,3},{8,12},{9,13},{10,... | collective-permute-start | bytes 622088 | tf_op jit(solution)/shard_map/ppermute | solution.py:515
  1.1 0.1 collective-permute-start
  1.2 1.2 %edges.1 = (f32[72,128]{1,0:T(8,128)S(1)}, f32[120,128]{1,0:T(8,128)S(1)}, f32[32,128]{1,0:T(8,128)S(1)}) custom-call(f32[9,2880]{1,0:T(8,128)} %h_ref.5, f32[9,2,2880]{2,1,0:T(2,128)} %bitcast.4, bf16[9,3,2880]{2,1,0:T(4,128)(2,1)} %bitcast.8), custom_call_target="tpu_custom_call" | custom-call | tf_op jit(solution)/shard_map/edges/pallas_call | solution.py:490
  2.4 0.4 %collective-permute-done.near_h_ref = f32[9,2880]{1,0:T(8,128)S(1)} collective-permute-done((f32[9,2880]{1,0:T(8,128)}, f32[9,2880]{1,0:T(8,128)S(1)}, u32[]{:S(2)}, u32[]{:S(2)}) %collective-permute-start) | collective-permute-done | bytes 103712 | tf_op jit(solution)/shard_map/ppermute | solution.py:514
  2.8 0.0 copy-start.3
  2.8 0.0 copy-start.4
  2.8 0.7 %polar.1 = (f32[168,128]{1,0:T(8,128)S(1)}, f32[184,128]{1,0:T(8,128)S(1)}, f32[184,128]{1,0:T(8,128)S(1)}, f32[184,128]{1,0:T(8,128)S(1)}, f32[120,128]{1,0:T(8,128)S(1)}, /*index=5*/f32[72,128]{1,0:T(8,128)S(1)}) custom-call(f32[9,2880]{1,0:T(8,128)S(1)} %copy-done.1, f32[9,2,2880]{2,1,0:T(2,128)S(1)} %bitcast.5, ...), custom_call_target="tpu_custom_call" | custom-call | tf_op jit(solution)/shard_map/polar/pallas_call | solution.py:529
  3.6 3.8 %collective-permute-start.4 = (f32[184,128]{1,0:T(8,128)S(1)}, f32[184,128]{1,0:T(8,128)S(1)}, u32[]{:S(2)}, u32[]{:S(2)}) collective-permute-start(f32[184,128]{1,0:T(8,128)S(1)} %get-tuple-element.27), channel_id=1, source_target_pairs={{0,3},{1,2},{2,1},{3,0},{4,7},{5,6},{6,5},{7,4},{8,11},{9,10},{10,... | collective-permute-start | bytes 282632 | tf_op jit(solution)/shard_map/ppermute | solution.py:525
  7.4 0.5 %collective-permute-start.5 = (f32[184,128]{1,0:T(8,128)S(1)}, f32[184,128]{1,0:T(8,128)S(1)}, u32[]{:S(2)}, u32[]{:S(2)}) collective-permute-start(f32[184,128]{1,0:T(8,128)S(1)} %get-tuple-element.28), channel_id=1, source_target_pairs={{0,1},{1,0},{2,3},{3,2},{4,6},{5,7},{6,4},{7,5},{8,9},{9,8},{10,11... | collective-permute-start | bytes 282632 | tf_op jit(solution)/shard_map/ppermute | solution.py:525
  7.9 0.1 collective-permute-start.6
  8.0 1.9 %collective-permute-start.3 = (f32[120,128]{1,0:T(8,128)S(1)}, f32[120,128]{1,0:T(8,128)S(1)}, u32[]{:S(2)}, u32[]{:S(2)}) collective-permute-start(f32[120,128]{1,0:T(8,128)S(1)} %get-tuple-element.25), channel_id=1, source_target_pairs={{0,2},{1,3},{2,0},{3,1},{4,8},{5,9},{6,10},{7,11},{8,4},{9,5},{10,... | collective-permute-start | bytes 184328 | tf_op jit(solution)/shard_map/ppermute | solution.py:538
  10.0 0.2 collective-permute-start.2
  10.1 0.5 %copy-done.5 = s32[72]{0:T(128)S(1)} copy-done((s32[72]{0:T(128)S(1)}, s32[72]{0:T(128)}, u32[]{:S(2)}) %copy-start.5) | copy-done | bytes 312
  10.6 1.2 %weights.1.weights_ref = bf16[1344,96]{1,0:T(8,128)(2,1)S(1)} custom-call(s32[72]{0:T(128)S(1)} %copy-done.5, f32[192,96]{1,0:T(8,128)S(1)} %copy-done.4, f32[192,96]{1,0:T(8,128)S(1)} %copy-done.3, f32[168,128]{1,0:T(8,128)S(1)} %get-tuple-element.26.after_ref.refs_0_), custom_call_target="tpu_custom_call" | custom-call | tf_op jit(solution)/shard_map/weights/pallas_call | solution.py:539
  11.9 1.3 %collective-permute-done.3.after_ref.far_ref = f32[120,128]{1,0:T(8,128)S(1)} collective-permute-done((f32[120,128]{1,0:T(8,128)S(1)}, f32[120,128]{1,0:T(8,128)S(1)}, u32[]{:S(2)}, u32[]{:S(2)}) %collective-permute-start.3) | collective-permute-done | bytes 61472 | tf_op jit(solution)/shard_map/ppermute | solution.py:538
  13.2 1.1 %filter.1 = (f32[168,128]{1,0:T(8,128)S(1)}, f32[168,128]{1,0:T(8,128)S(1)}, f32[168,128]{1,0:T(8,128)S(1)}, f32[168,128]{1,0:T(8,128)S(1)}) custom-call(bf16[1344,96]{1,0:T(8,128)(2,1)S(1)} %weights.1.weights_ref, f32[8,3,16,128]{3,2,1,0:T(8,128)S(1)} %copy-done.2, f32[120,128]{1,0:T(8,128)S(1)} %collective-permute-done.3.after_ref.far_ref, ...), custom_call_target="tpu_custom_call" | custom-call | tf_op jit(solution)/shard_map/filter/pallas_call | solution.py:545
  14.3 2.0 %collective-permute-start.7 = (f32[168,128]{1,0:T(8,128)S(1)}, f32[168,128]{1,0:T(8,128)S(1)}, u32[]{:S(2)}, u32[]{:S(2)}) collective-permute-start(f32[168,128]{1,0:T(8,128)S(1)} %get-tuple-element.33), channel_id=1, source_target_pairs={{0,3},{1,2},{2,1},{3,0},{4,7},{5,6},{6,5},{7,4},{8,11},{9,10},{10,... | collective-permute-start | bytes 258056 | tf_op jit(solution)/shard_map/ppermute | solution.py:525
  16.3 1.2 %collective-permute-start.8 = (f32[168,128]{1,0:T(8,128)S(1)}, f32[168,128]{1,0:T(8,128)S(1)}, u32[]{:S(2)}, u32[]{:S(2)}) collective-permute-start(f32[168,128]{1,0:T(8,128)S(1)} %get-tuple-element.34), channel_id=1, source_target_pairs={{0,1},{1,0},{2,3},{3,2},{4,6},{5,7},{6,4},{7,5},{8,9},{9,8},{10,11... | collective-permute-start | bytes 258056 | tf_op jit(solution)/shard_map/ppermute | solution.py:525
  17.5 0.3 %collective-permute-start.9 = (f32[168,128]{1,0:T(8,128)S(1)}, f32[168,128]{1,0:T(8,128)S(1)}, u32[]{:S(2)}, u32[]{:S(2)}) collective-permute-start(f32[168,128]{1,0:T(8,128)S(1)} %get-tuple-element.35), channel_id=1, source_target_pairs={{0,2},{1,3},{2,0},{3,1},{4,5},{5,4},{6,7},{7,6},{8,10},{9,11},{10,... | collective-permute-start | bytes 258056 | tf_op jit(solution)/shard_map/ppermute | solution.py:525
  17.9 1.7 %rest.1 = (f32[2,9,2880]{2,1,0:T(8,128)S(1)}, f32[9,2880]{1,0:T(8,128)S(1)}, bf16[3,9,2880]{2,1,0:T(8,128)(2,1)S(1)}) custom-call(f32[9,2880]{1,0:T(8,128)S(1)} %copy-done.1, f32[9,2,2880]{2,1,0:T(2,128)S(1)} %bitcast.6, bf16[3,9,2880]{2,1,0:T(8,128)(2,1)S(1)} %copy.10.q_ref, f32[9,2880]{1,0:T(8,128)S(1)} %collective-permute-done.near_h_ref, ...), custom_call_target="tpu_custom_call" | custom-call | tf_op jit(solution)/shard_map/rest/pallas_call | solution.py:554
  19.6 0.8 %copy.11 = bf16[3,9,2880]{2,0,1:T(4,128)(2,1)} copy(bf16[3,9,2880]{2,1,0:T(8,128)(2,1)S(1)} %get-tuple-element.41) | data formatting | bytes 311040
  20.4 0.9 %collective-permute-done.8.refs_2_ = f32[168,128]{1,0:T(8,128)S(1)} collective-permute-done((f32[168,128]{1,0:T(8,128)S(1)}, f32[168,128]{1,0:T(8,128)S(1)}, u32[]{:S(2)}, u32[]{:S(2)}) %collective-permute-start.8) | collective-permute-done | bytes 86048 | tf_op jit(solution)/shard_map/ppermute | solution.py:525
  21.3 0.7 %collective-permute-done.9.refs_3_ = f32[168,128]{1,0:T(8,128)S(1)} collective-permute-done((f32[168,128]{1,0:T(8,128)S(1)}, f32[168,128]{1,0:T(8,128)S(1)}, u32[]{:S(2)}, u32[]{:S(2)}) %collective-permute-start.9) | collective-permute-done | bytes 86048 | tf_op jit(solution)/shard_map/ppermute | solution.py:525
  22.0 1.6 %finish.1 = (f32[9,2,2880]{2,1,0:T(2,128)}, f32[9,2880]{1,0:T(8,128)}) custom-call(s32[72]{0:T(128)S(1)} %copy-done.5, f32[9,2880]{1,0:T(8,128)S(1)} %copy-done.1, f32[9,2,2880]{2,1,0:T(2,128)S(1)} %bitcast.7, f32[2,9,2880]{2,1,0:T(8,128)S(1)} %get-tuple-element.31.plain_w_ref, f32[9,2880]{1,0:T(8,128)S(1)} %get-tuple-element.32.plain_h_ref, ...), custom_call_target="tpu_custom_call" | custom-call | tf_op jit(solution)/shard_map/finish/pallas_call | solution.py:562
  (18 shorter events, 0.1 us)
Async XLA Ops:
  0.6 2.2 %collective-permute-start.1 = (f32[9,2,2880]{2,1,0:T(2,128)}, f32[9,2,2880]{2,1,0:T(2,128)S(1)}, u32[]{:S(2)}, u32[]{:S(2)}) collective-permute-start(f32[9,2,2880]{2,1,0:T(2,128)} %bitcast.3), channel_id=1, source_target_pairs={{0,4},{1,5},{2,6},{3,7},{4,0},{5,1},{6,2},{7,3},{8,12},{9,13},{10,... | collective-permute-start | bytes 622088 | tf_op jit(solution)/shard_map/ppermute | solution.py:515
  1.1 1.6 %collective-permute-start = (f32[9,2880]{1,0:T(8,128)}, f32[9,2880]{1,0:T(8,128)S(1)}, u32[]{:S(2)}, u32[]{:S(2)}) collective-permute-start(f32[9,2880]{1,0:T(8,128)} %h_ref.5), channel_id=1, source_target_pairs={{0,4},{1,5},{2,6},{3,7},{4,0},{5,1},{6,2},{7,3},{8,12},{9,13},{10,... | collective-permute-start | bytes 311048 | tf_op jit(solution)/shard_map/ppermute | solution.py:514
  1.2 1.6 %copy-start = (f32[2,9,2880]{2,0,1:T(2,128)S(1)}, f32[2,9,2880]{2,0,1:T(2,128)}, u32[]{:S(2)}) copy-start(f32[2,9,2880]{2,0,1:T(2,128)} %param.7) | copy-start | bytes 622084
  1.2 1.6 %copy-start.1 = (f32[9,2880]{1,0:T(8,128)S(1)}, f32[9,2880]{1,0:T(8,128)}, u32[]{:S(2)}) copy-start(f32[9,2880]{1,0:T(8,128)} %h_ref.5) | copy-start | bytes 311044
  1.2 1.6 %copy-start.2 = (f32[8,3,16,128]{3,2,1,0:T(8,128)S(1)}, f32[8,3,16,128]{3,2,1,0:T(8,128)}, u32[]{:S(2)}) copy-start(f32[8,3,16,128]{3,2,1,0:T(8,128)} %constant.6.clone.geo_ref) | copy-start | bytes 589828
  2.8 7.3 %copy-start.3 = (f32[192,96]{1,0:T(8,128)S(1)}, f32[192,96]{1,0:T(8,128)}, u32[]{:S(2)}) copy-start(f32[192,96]{1,0:T(8,128)} %constant.8.clone.inverse_ref) | copy-start | bytes 221188
  2.8 7.3 %copy-start.4 = (f32[192,96]{1,0:T(8,128)S(1)}, f32[192,96]{1,0:T(8,128)}, u32[]{:S(2)}) copy-start(f32[192,96]{1,0:T(8,128)} %constant.7.clone.n_ref) | copy-start | bytes 221188
  3.6 9.6 %collective-permute-start.4 = (f32[184,128]{1,0:T(8,128)S(1)}, f32[184,128]{1,0:T(8,128)S(1)}, u32[]{:S(2)}, u32[]{:S(2)}) collective-permute-start(f32[184,128]{1,0:T(8,128)S(1)} %get-tuple-element.27), channel_id=1, source_target_pairs={{0,3},{1,2},{2,1},{3,0},{4,7},{5,6},{6,5},{7,4},{8,11},{9,10},{10,... | collective-permute-start | bytes 282632 | tf_op jit(solution)/shard_map/ppermute | solution.py:525
  7.4 5.8 %collective-permute-start.5 = (f32[184,128]{1,0:T(8,128)S(1)}, f32[184,128]{1,0:T(8,128)S(1)}, u32[]{:S(2)}, u32[]{:S(2)}) collective-permute-start(f32[184,128]{1,0:T(8,128)S(1)} %get-tuple-element.28), channel_id=1, source_target_pairs={{0,1},{1,0},{2,3},{3,2},{4,6},{5,7},{6,4},{7,5},{8,9},{9,8},{10,11... | collective-permute-start | bytes 282632 | tf_op jit(solution)/shard_map/ppermute | solution.py:525
  7.9 5.2 %collective-permute-start.6 = (f32[184,128]{1,0:T(8,128)S(1)}, f32[184,128]{1,0:T(8,128)S(1)}, u32[]{:S(2)}, u32[]{:S(2)}) collective-permute-start(f32[184,128]{1,0:T(8,128)S(1)} %get-tuple-element.29), channel_id=1, source_target_pairs={{0,2},{1,3},{2,0},{3,1},{4,5},{5,4},{6,7},{7,6},{8,10},{9,11},{10,... | collective-permute-start | bytes 282632 | tf_op jit(solution)/shard_map/ppermute | solution.py:525
  8.0 5.1 %collective-permute-start.3 = (f32[120,128]{1,0:T(8,128)S(1)}, f32[120,128]{1,0:T(8,128)S(1)}, u32[]{:S(2)}, u32[]{:S(2)}) collective-permute-start(f32[120,128]{1,0:T(8,128)S(1)} %get-tuple-element.25), channel_id=1, source_target_pairs={{0,2},{1,3},{2,0},{3,1},{4,8},{5,9},{6,10},{7,11},{8,4},{9,5},{10,... | collective-permute-start | bytes 184328 | tf_op jit(solution)/shard_map/ppermute | solution.py:538
  10.0 0.7 %copy-start.5 = (s32[72]{0:T(128)S(1)}, s32[72]{0:T(128)}, u32[]{:S(2)}) copy-start(s32[72]{0:T(128)} %cut_ref.3) | copy-start | bytes 868
  10.0 1.9 %collective-permute-start.2 = (f32[72,128]{1,0:T(8,128)S(1)}, f32[72,128]{1,0:T(8,128)S(1)}, u32[]{:S(2)}, u32[]{:S(2)}) collective-permute-start(f32[72,128]{1,0:T(8,128)S(1)} %get-tuple-element.24), channel_id=1, source_target_pairs={{0,4},{1,5},{2,6},{3,7},{4,0},{5,1},{6,2},{7,3},{8,12},{9,13},{10,... | collective-permute-start | bytes 110600 | tf_op jit(solution)/shard_map/ppermute | solution.py:537
  11.9 6.0 %copy-start.6 = (bf16[3,9,2880]{2,0,1:T(4,128)(2,1)S(1)}, bf16[3,9,2880]{2,0,1:T(4,128)(2,1)}, u32[]{:S(2)}) copy-start(bf16[3,9,2880]{2,0,1:T(4,128)(2,1)} %param.9) | copy-start | bytes 466564
  14.3 6.1 %collective-permute-start.7 = (f32[168,128]{1,0:T(8,128)S(1)}, f32[168,128]{1,0:T(8,128)S(1)}, u32[]{:S(2)}, u32[]{:S(2)}) collective-permute-start(f32[168,128]{1,0:T(8,128)S(1)} %get-tuple-element.33), channel_id=1, source_target_pairs={{0,3},{1,2},{2,1},{3,0},{4,7},{5,6},{6,5},{7,4},{8,11},{9,10},{10,... | collective-permute-start | bytes 258056 | tf_op jit(solution)/shard_map/ppermute | solution.py:525
  16.3 5.0 %collective-permute-start.8 = (f32[168,128]{1,0:T(8,128)S(1)}, f32[168,128]{1,0:T(8,128)S(1)}, u32[]{:S(2)}, u32[]{:S(2)}) collective-permute-start(f32[168,128]{1,0:T(8,128)S(1)} %get-tuple-element.34), channel_id=1, source_target_pairs={{0,1},{1,0},{2,3},{3,2},{4,6},{5,7},{6,4},{7,5},{8,9},{9,8},{10,11... | collective-permute-start | bytes 258056 | tf_op jit(solution)/shard_map/ppermute | solution.py:525
  17.5 4.5 %collective-permute-start.9 = (f32[168,128]{1,0:T(8,128)S(1)}, f32[168,128]{1,0:T(8,128)S(1)}, u32[]{:S(2)}, u32[]{:S(2)}) collective-permute-start(f32[168,128]{1,0:T(8,128)S(1)} %get-tuple-element.35), channel_id=1, source_target_pairs={{0,2},{1,3},{2,0},{3,1},{4,5},{5,4},{6,7},{7,6},{8,10},{9,11},{10,... | collective-permute-start | bytes 258056 | tf_op jit(solution)/shard_map/ppermute | solution.py:525

commit v10 on v9

--- a/solution.py
+++ b/solution.py
@@ -33,16 +33,31 @@
         self.end = (self.tiles - 1) * LANES
         self.tail = merged - self.end
         self.stack = -(-(self.tiles + 1) // 8) * 8
-        self.units = 3 * rows
+        self.near_only = rows <= self.nlat // 6 < 2 * rows
+        self.work = rows - 1 if self.near_only else rows
+        self.units = 3 * self.work
         self.share = -(-self.units // n_lon)
         self.size = self.share * self.stack
-        self.pole = self.units - 1
-        self.near_only = self.nlat // 6 < 2 * rows and self.units % self.share > 0
         assert self.tail <= LANES - 4 * LEVELS and rows + 2 <= EXT_ROWS and n_lat % 2 == 0
         assert n_lon >= 4 and n_lon & (n_lon - 1) == 0
 
     def span(self, tile):
         return self.tail if tile == self.tiles - 1 else LANES
+
+    def first(self):
+        return jnp.where(lax.rem(lax.axis_index("lat"), 2) == 0, 1, 0) if self.near_only else 0
+
+    def at_pole(self, row):
+        band = lax.axis_index("lat")
+        south, north = (row == 0) & (band == 0), (row == self.rows - 1) & (band == self.n_lat - 1)
+        return (south | north) & self.near_only
+
+    def active(self, cut_ref, shape):
+        row = lax.broadcasted_iota(jnp.int32, shape, 0)
+        cuts = jnp.full(shape, self.nlon // 2, jnp.int32)
+        for j in range(self.rows):
+            cuts = jnp.where(row == j, cut_ref[lax.axis_index("lat") * self.rows + j], cuts)
+        return cuts < self.nlon // 2, self.at_pole(row)
 
     def turns(self, odd):
         middle = list(range(1, self.n_lon - 1))
@@ -82,6 +97,12 @@
     with np.errstate(divide="ignore"):
         inverse = np.where(n == 0, 0.0, 1.0 / (sz.nlon * np.sin(np.pi * n / sz.nlon)))
     return n.astype(np.float32), inverse.astype(np.float32)
+
+
+def waves(sz):
+    column = PER_TILE * np.arange(sz.stack)[:, None] + np.arange(LANES)[None, :] // LEVELS
+    angle = 2 * np.pi * column / sz.nlon
+    return np.stack([np.cos(angle), np.sin(angle)]).astype(np.float32)
 
 
 def edges_kernel(sz, h_hbm, w_hbm, q_hbm, near_ref, far_ref, sides_ref, *scratch):
@@ -181,8 +202,8 @@
     return pltpu.roll(value, 1, 0)
 
 
-def polar_kernel(sz, h_ref, w_ref, near_h_ref, near_w_ref, sides_ref, geo_ref, far_ref, near_q_ref, *refs):
-    out_refs, (far_out, near_out, tend_ref, ext) = refs[:-4], refs[-4:]
+def polar_kernel(sz, h_ref, w_ref, near_h_ref, near_w_ref, sides_ref, geo_ref, wave_ref, far_ref, near_q_ref, *refs):
+    out_refs, (far_out, near_out, tend_ref, pole_ref, ext) = refs[:-5], refs[-5:]
     far_out[...] = far_ref[...]
     near_out[...] = near_q_ref[...]
     if sz.near_only:
@@ -190,7 +211,8 @@
     band = lax.axis_index("lat")
     ring = Tiles(sz)
     lane = ring.lane
-    tiles, stack, rows = sz.tiles, sz.stack, sz.rows
+    tiles, stack, rows, work = sz.tiles, sz.stack, sz.rows, sz.work
+    even = lax.rem(band, 2) == 0
     for f, value in enumerate((h_ref[...], w_ref[:, 1, :], w_ref[:, 0, :])):
         ext[f, :rows, sz.end :] = jnp.zeros((rows, LANES), jnp.float32)
         ext[f, :rows, : sz.merged] = value
@@ -230,32 +252,103 @@
             for k, (source, at) in reversed(list(enumerate(columns))):
                 to = sz.tail + LEVELS * k
                 spare = jnp.where(lane < to + LEVELS, pltpu.roll(source, (to - at) % LANES, 1), spare)
-        for f, tend in enumerate((thick_tend, wind_u_tend, wind_v_tend)):
+        for f, tend in enumerate((thick_tend, wind_u_tend, wind_v_tend, thick)):
+            if sz.near_only:
+                alone = jnp.where(band < sz.n_lat // 2, tend[:1], tend[rows - 1 : rows])
+                if t == tiles - 1:
+                    alone = jnp.where(lane[:1] < sz.tail, alone, 0.0)
+                pole_ref[stack * f + t : stack * f + t + 1] = alone
+            if f == 3:
+                continue
             if t == tiles - 1:
                 tend = jnp.where(lane < sz.tail, tend, spare)
-            tend_ref[pl.ds(stack * rows * f + t, rows, stride=stack), :] = tend[:rows]
+            if sz.near_only:
+                tend = jnp.where(even, north(tend), tend)
+            tend_ref[pl.ds(stack * work * f + t, work, stride=stack), :] = tend[:work]
     for f in range(3):
         for t in range(tiles, stack):
-            tend_ref[pl.ds(stack * rows * f + t, rows, stride=stack), :] = jnp.zeros((rows, LANES), jnp.float32)
+            tend_ref[pl.ds(stack * work * f + t, work, stride=stack), :] = jnp.zeros((work, LANES), jnp.float32)
     used = stack * sz.units
     if used < tend_ref.shape[0]:
         tend_ref[used:, :] = jnp.zeros((tend_ref.shape[0] - used, LANES), jnp.float32)
+    sides = [sides_ref[:EXT_ROWS], sides_ref[EXT_ROWS:]]
     if sz.near_only:
-        swap_ends(sz, tend_ref)
-        for t in range(tiles):
-            lanes = slice(LANES * t, LANES * (t + 1))
-            row = jnp.where(band < sz.n_lat // 2, ext[0, 0:1, lanes], ext[0, rows - 1 : rows, lanes])
-            tend_ref[used + t : used + t + 1, :] = row
+        sums = pole_sums(sz, pole_ref, wave_ref, spare, band)
+        row = lax.broadcasted_iota(jnp.int32, (EXT_ROWS, LANES), 0)
+        for k, total in enumerate(sums):
+            sides = [jnp.where(row == rows + k, total, side) for side in sides]
     here = lax.axis_index("lon")
     for k, out_ref in enumerate(out_refs):
         out_ref[: sz.size] = tend_ref[sz.piece(k), :]
-        if k:
-            eastward = sz.partner(k) == lax.rem(here + 1, sz.n_lon)
-            out_ref[sz.size :] = jnp.where(eastward, sides_ref[EXT_ROWS:], sides_ref[:EXT_ROWS])
-
-
-def rest_kernel(sz, h_ref, w_ref, q_ref, near_h_ref, near_w_ref, near_q_ref, far_ref, geo_ref, after_ref, *refs):
-    met_refs, (new_w_ref, new_h_ref, mass_ref, ext) = refs[: sz.n_lon - 1], refs[sz.n_lon - 1 :]
+        eastward = sz.partner(k) == lax.rem(here + 1, sz.n_lon)
+        out_ref[sz.size :] = jnp.where(eastward, sides[1], sides[0])
+
+
+def pole_sums(sz, pole_ref, wave_ref, spare, band):
+    stack, rows = sz.stack, sz.rows
+    lane = lax.broadcasted_iota(jnp.int32, (1, LANES), 1)
+    sides = jnp.where(band < sz.n_lat // 2, spare[:1], spare[rows - 1 : rows])
+    found = [jnp.zeros((1, LANES), jnp.float32), pltpu.roll(sides, (LANES // 2 - sz.tail) % LANES, 1)]
+    for f in range(4):
+        if sz.tiles < stack:
+            pole_ref[stack * f + sz.tiles : stack * (f + 1)] = jnp.zeros((stack - sz.tiles, LANES), jnp.float32)
+        values = pole_ref[stack * f : stack * (f + 1)]
+        for k, terms in enumerate((values, values * wave_ref[0], values * wave_ref[1])):
+            total = jnp.sum(terms, axis=0, keepdims=True)
+            for step in (64, 32, 16):
+                total = total + pltpu.roll(total, step, 1)
+            row, place = divmod(3 * f + k, PER_TILE)
+            inside = (lane >= LEVELS * place) & (lane < LEVELS * (place + 1))
+            found[row] = jnp.where(inside, total, found[row])
+    return found
+
+
+def pole_waves(sz, rows_in, inv_cos, sign):
+    n_lon = sz.n_lon
+    lane = lax.broadcasted_iota(jnp.int32, (1, LANES), 1)
+
+    def value(s, place):
+        row, at = divmod(place, PER_TILE)
+        return pltpu.roll(rows_in[s % n_lon, row : row + 1], (-LEVELS * at) % LANES, 1)
+
+    theta = 2 * math.pi / sz.nlon
+    ends = (1.0, math.cos(theta * (sz.columns - 1)), math.sin(theta * (sz.columns - 1)))
+    sums = [[[value(s, 3 * f + k) for k in range(3)] for f in range(4)] for s in range(n_lon)]
+    for s in range(n_lon):
+        thick_w, thick_e = value(s, 13), value(s + 1, 12)
+        flux = 0.25 * (value(s, 15) + value(s + 1, 14)) * (thick_w + thick_e) * inv_cos
+        slope = 0.5 * inv_cos
+        after = (s + 1) % n_lon
+        for f, (west_of, east_of) in enumerate(((flux, flux), (slope * thick_e, slope * thick_w))):
+            for k in range(3):
+                sums[s][f][k] = sums[s][f][k] - west_of * ends[k]
+            for k in range(2):
+                sums[after][f][k] = sums[after][f][k] + east_of
+    result = []
+    for f in range(3):
+        waves_of = [0.0, 0.0, 0.0]
+        for s in range(n_lon):
+            level, cosine, sine = sums[s][f]
+            if f == 2:
+                level = level + (0.5 * sz.ratio) * sign * sums[s][3][0]
+                cosine = cosine - (0.5 * sz.ratio) * sign * sums[s][3][1]
+                sine = sine - (0.5 * sz.ratio) * sign * sums[s][3][2]
+            c, d = math.cos(2 * math.pi * s / n_lon), math.sin(2 * math.pi * s / n_lon)
+            waves_of[0] = waves_of[0] + level
+            waves_of[1] = waves_of[1] + (c * cosine - d * sine)
+            waves_of[2] = waves_of[2] + (d * cosine + c * sine)
+        spread = []
+        for k, total in enumerate(waves_of):
+            total = jnp.where(lane < LEVELS, total * ((1.0 if k == 0 else 2.0) / sz.nlon), 0.0)
+            for step in (16, 32, 64):
+                total = total + pltpu.roll(total, step, 1)
+            spread.append(total)
+        result.append(spread)
+    return result
+
+
+def rest_kernel(sz, cut_ref, h_ref, w_ref, q_ref, near_h_ref, near_w_ref, near_q_ref, far_ref, geo_ref, wave_ref, after_ref, *refs):
+    met_refs, (new_w_ref, new_h_ref, mass_ref, ext, pole_in) = refs[: sz.n_lon], refs[sz.n_lon :]
     band = lax.axis_index("lat")
     ring = Tiles(sz)
     lane = ring.lane
@@ -270,7 +363,9 @@
     lane9 = lane[:rows]
     here = lax.axis_index("lon")
     from_e = from_w = met_refs[0][sz.size :]
-    for k, met_ref in enumerate(met_refs[1:], 2):
+    for k, met_ref in enumerate(met_refs):
+        eastward = lax.rem(sz.partner(k) - here + sz.n_lon, sz.n_lon)
+        pole_in[eastward] = met_ref[sz.size + 8 :]
         from_e = jnp.where(sz.partner(k) == lax.rem(here + 1, sz.n_lon), met_ref[sz.size :], from_e)
         from_w = jnp.where(sz.partner(k) == lax.rem(here + sz.n_lon - 1, sz.n_lon), met_ref[sz.size :], from_w)
     for place, f in enumerate((0, 5, 2, 3, 4)):
@@ -281,6 +376,21 @@
         ext[f, :rows, sz.end :] = jnp.where(lane9 < sz.tail, own, edge)
     inv_cos, sin_centre, cos_face = geo_ref[band, 0], geo_ref[band, 1], geo_ref[band, 2]
     ratio = sz.ratio
+
+    active, alone = sz.active(cut_ref, (EXT_ROWS, LANES))
+    if sz.near_only:
+        band = lax.axis_index("lat")
+        low = band < sz.n_lat // 2
+        pole_cos = jnp.where(low, inv_cos[:1], inv_cos[rows - 1 : rows])
+        kept_waves = pole_waves(sz, pole_in.at[:, rows - 8 :], pole_cos, jnp.where(low, 1.0, -1.0))
+
+    def stepped(f, t, value, tend):
+        tend = jnp.where(active, 0.0, tend)
+        if sz.near_only:
+            level, cosine, sine = kept_waves[f]
+            wave = level + cosine * wave_ref[0, t : t + 1] + sine * wave_ref[1, t : t + 1]
+            tend = jnp.where(alone, wave, tend)
+        return value + TIME_STEP * tend
 
     def tile(f, t):
         return ext[f, :, LANES * t : LANES * (t + 1)]
@@ -312,9 +422,9 @@
         thick_tend = -((flux - flux_w) + (flux_n - south(flux_n)) * inv_cos)
         wind_u_tend = sin_centre * wind_v - (thick_e - thick_w) * (0.5 * inv_cos)
         wind_v_tend = -sin_centre * wind_u - (0.5 * ratio) * (thick_n - south(thick))
-        new_h_ref[:, lanes] = (thick + TIME_STEP * thick_tend)[:rows, :span]
-        new_w_ref[0, :, lanes] = (wind_u + TIME_STEP * wind_u_tend)[:rows, :span]
-        new_w_ref[1, :, lanes] = (wind_v + TIME_STEP * wind_v_tend)[:rows, :span]
+        new_h_ref[:, lanes] = stepped(0, t, thick, thick_tend)[:rows, :span]
+        new_w_ref[0, :, lanes] = stepped(1, t, wind_u, wind_u_tend)[:rows, :span]
+        new_w_ref[1, :, lanes] = stepped(2, t, wind_v, wind_v_tend)[:rows, :span]
         for k in range(3):
             q = tile(2 + k, t)
             q_n = north(q)
@@ -338,21 +448,7 @@
 
 def share_of(sz, i):
     unit = lax.axis_index("lon") * sz.share + i
-    row = lax.rem(unit, sz.rows)
-    if sz.near_only:
-        low = lax.axis_index("lat") < sz.n_lat // 2
-        row = jnp.where(low & (unit == sz.pole), 0, row)
-        row = jnp.where(low & (unit == 2 * sz.rows), sz.rows - 1, row)
-    return unit // sz.rows, row
-
-
-def swap_ends(sz, ref):
-    low = lax.axis_index("lat") < sz.n_lat // 2
-    first = slice(2 * sz.rows * sz.stack, (2 * sz.rows + 1) * sz.stack)
-    last = slice(sz.pole * sz.stack, sz.units * sz.stack)
-    a, b = ref[first], ref[last]
-    ref[first] = jnp.where(low, b, a)
-    ref[last] = jnp.where(low, a, b)
+    return unit // sz.work, sz.first() + lax.rem(unit, sz.work)
 
 
 def weights_kernel(sz, cut_ref, n_ref, inverse_ref, after_ref, weights_ref):
@@ -399,14 +495,6 @@
         at = pl.ds(0, share, stride=stack)
         after = (s + 1) % n_lon
         gathered[after, at, :] = gathered[after, at, :] + jnp.where(lane < LEVELS, east_of, 0.0)
-
-    if sz.near_only:
-        sign = jnp.where(band == 0, 1.0, jnp.where(band == sz.n_lat - 1, -1.0, 0.0))
-        factor = jnp.where(lax.axis_index("lon") == sz.pole // share, 0.5 * sz.ratio * sign, 0.0)
-        at = sz.pole % share * stack
-        for s in range(n_lon):
-            over = gathered[(s + n_lon // 2) % n_lon, at + stack : at + 2 * stack]
-            gathered[s, at : at + stack] = gathered[s, at : at + stack] + factor * over
 
     wide = lax.broadcasted_iota(jnp.int32, (stack, LANES), 1)
     rows = PER_TILE * stack
@@ -430,29 +518,27 @@
         out_ref[...] = results[sz.partner(k)]
 
 
-def finish_kernel(sz, cut_ref, h_ref, w_ref, plain_w_ref, plain_h_ref, *refs):
+def finish_kernel(sz, cut_ref, base_w_ref, base_h_ref, *refs):
     back_refs, (new_w_ref, new_h_ref, back_ref) = refs[: sz.n_lon], refs[sz.n_lon :]
-    rows = sz.rows
+    rows, work = sz.rows, sz.work
     for k, ref in enumerate(back_refs):
         back_ref[sz.piece(k), :] = ref[...]
-    if sz.near_only:
-        swap_ends(sz, back_ref)
-    row = lax.broadcasted_iota(jnp.int32, (rows, LANES), 0)
-    cuts = jnp.zeros((rows, LANES), jnp.int32)
-    for j in range(rows):
-        cuts = jnp.where(row == j, cut_ref[lax.axis_index("lat") * rows + j], cuts)
-    active = cuts < sz.nlon // 2
+    active, alone = sz.active(cut_ref, (EXT_ROWS, LANES))
+    scale = jnp.where(active & jnp.logical_not(alone), TIME_STEP, 0.0)
+    even = lax.rem(lax.axis_index("lat"), 2) == 0
     for f in range(3):
         for t in range(sz.tiles):
             span = sz.span(t)
             lanes = slice(LANES * t, LANES * t + span)
-            tend = back_ref[pl.ds(sz.stack * rows * f + t, rows, stride=sz.stack), :][:, :span]
+            tend = back_ref[pl.ds(sz.stack * work * f + t, work, stride=sz.stack), :]
+            if sz.near_only:
+                tend = jnp.concatenate([tend, jnp.zeros((EXT_ROWS - work, LANES), jnp.float32)], axis=0)
+                tend = jnp.where(even, south(tend), tend)
+            change = (scale[:rows] * tend[:rows])[:, :span]
             if f == 0:
-                new = h_ref[:, lanes] + TIME_STEP * tend
-                new_h_ref[:, lanes] = jnp.where(active[:, :span], new, plain_h_ref[:, lanes])
+                new_h_ref[:, lanes] = base_h_ref[:, lanes] + change
             else:
-                new = w_ref[:, f - 1, lanes] + TIME_STEP * tend
-                new_w_ref[:, f - 1, lanes] = jnp.where(active[:, :span], new, plain_w_ref[f - 1, :, lanes])
+                new_w_ref[:, f - 1, lanes] = base_w_ref[f - 1, :, lanes] + change
 
 
 def local(winds, thickness, tracers, cutoff):
@@ -481,6 +567,7 @@
         )
 
     geo = jnp.asarray(geometry(sz))
+    wave = jnp.asarray(waves(sz))
     n, inverse = (jnp.asarray(table) for table in offsets(sz))
 
     wind_rows = jnp.swapaxes(winds, 0, 1)
@@ -529,10 +616,14 @@
     *tends, far_rows, near_q = call(
         polar_kernel,
         "polar",
-        [vmem] * 8,
-        [shaped(sz.size, LANES)] + [shaped(sz.size + EXT_ROWS, LANES)] * (n_lon - 1) + [far_row, near_row],
-        [pltpu.VMEM((n_lon * sz.size, LANES), f32), pltpu.VMEM((3, EXT_ROWS, sz.tiles * LANES), f32)],
-    )(thickness, wind_rows, near_h, near_w, sides, geo, far_rows, near_q)
+        [vmem] * 9,
+        [shaped(sz.size + EXT_ROWS, LANES)] * n_lon + [far_row, near_row],
+        [
+            pltpu.VMEM((n_lon * sz.size, LANES), f32),
+            pltpu.VMEM((4 * sz.stack, LANES), f32),
+            pltpu.VMEM((3, EXT_ROWS, sz.tiles * LANES), f32),
+        ],
+    )(thickness, wind_rows, near_h, near_w, sides, geo, wave, far_rows, near_q)
     met = meetings(tends)
     near_q = lax.ppermute(near_q, ("lat", "lon"), near)
     from_far = lax.ppermute(far_rows, ("lat", "lon"), far) if sz.near_only else far_rows
@@ -551,21 +642,21 @@
     )(weights, geo, from_far, near_q, *met)
     back = meetings(worked)
 
-    plain_w, plain_h, mass = call(
+    base_w, base_h, mass = call(
         rest_kernel,
         "rest",
-        [vmem] * 8 + [anywhere] + [vmem] * (n_lon - 1),
+        [smem] + [vmem] * 9 + [anywhere] + [vmem] * n_lon,
         (shaped(2, rows, merged), shaped(rows, merged), jax.ShapeDtypeStruct(tracers.shape, jnp.bfloat16)),
-        [pltpu.VMEM((6, EXT_ROWS, sz.tiles * LANES), f32)],
-    )(thickness, wind_rows, tracers, near_h, near_w, near_q, from_far, geo, worked[0], *met[1:])
+        [pltpu.VMEM((6, EXT_ROWS, sz.tiles * LANES), f32), pltpu.VMEM((n_lon, 8, LANES), f32)],
+    )(cutoff, thickness, wind_rows, tracers, near_h, near_w, near_q, from_far, geo, wave, worked[0], *met)
 
     new_w, new_h = call(
         finish_kernel,
         "finish",
-        [smem] + [vmem] * (4 + n_lon),
+        [smem] + [vmem] * (2 + n_lon),
         (shaped(*wind_rows.shape), shaped(rows, merged)),
         [pltpu.VMEM((n_lon * sz.size, LANES), f32)],
-    )(cutoff, thickness, wind_rows, plain_w, plain_h, *back)
+    )(cutoff, base_w, base_h, *back)
     return jnp.swapaxes(new_w, 0, 1), new_h, mass
 
 

time: 23.8 us -> 22.8 us (0.958)
  waiting for transfers between devices: 3.3 us -> 1.91 us
  Pallas kernels: 7.57 us -> 7.98 us
    ppermute x6, waiting for transfers between devices: 1.64 us -> 0.29 us  [meetings(): lax.ppermute(shares[k], ('lat', 'lon'), [(b * n_lon + i, b * n_lon + j) f...]
    pallas_call x3, Pallas kernels: 4.07 us -> 4.67 us  [the longest x1 2.55 us: local(): call(rest_kernel, 'rest', [smem] + [vmem] * 9 + [anywhere] + [vmem] * n_l...]
    unnamed x16 -> x18, local copies, waits for them, and re-layouts: 1.31 us -> 1.32 us
  transfers between devices with their start and end apart: 10 -> 10, of which waited for: 4 -> 3; matrix products, arithmetic and copies ran while one was open for 3% -> 4% of each run, Pallas kernels for 18% -> 22%
where the time goes in v10:
time: 22.8 us; the launch traced here: 22.6 us
  starting transfers between devices  10.7 us (47%)
  Pallas kernels  7.98 us (35%)
  waiting for transfers between devices  1.91 us (8%)
  local copies, waits for them, and re-layouts  1.32 us (6%)
  between operations  0.75 us (3%)
    ppermute x6, starting transfers between devices, meetings(): lax.ppermute(shares[k], ('lat', 'lon'), [(b * n_lon + i, b * n_lon + j) f...  8.01 us
    pallas_call x1, Pallas kernels, local(): call(rest_kernel, 'rest', [smem] + [vmem] * 9 + [anywhere] + [vmem] * n_l...  2.55 us
    ppermute x1, starting transfers between devices, local(): lax.ppermute(far_rows, ('lat', 'lon'), far)  1.92 us
    pallas_call x1, Pallas kernels, local(): call(finish_kernel, 'finish', [smem] + [vmem] * (2 + n_lon), (shaped(*win...  1.46 us
    unnamed x18, local copies, waits for them, and re-layouts  1.32 us
    ppermute x1, waiting for transfers between devices, local(): lax.ppermute(far_rows, ('lat', 'lon'), far)  1.24 us
    pallas_call x1, Pallas kernels, local(): call(edges_kernel, 'edges', [hbm] * 3, (near_row, far_row, shaped(2 * EXT...  1.17 us
    pallas_call x1, Pallas kernels, local(): call(weights_kernel, 'weights', [smem, vmem, vmem, anywhere], jax.ShapeDt...  1.14 us
  transfers between devices with their start and end apart: 10, of which 3 were waited for; matrix products, arithmetic and copies ran while one was open for 4% of the time, Pallas kernels for 22%

profile of v10, /device:TPU:0, one launch (start us, length us, event | category | flops | bytes accessed | tf_op | source)
XLA Modules:
  0.0 22.6 jit_solution(15471434661355091804)
XLA Ops:
  0.6 0.0 copy-start.3
  0.6 0.5 %collective-permute-start.1 = (f32[9,2,2880]{2,1,0:T(2,128)}, f32[9,2,2880]{2,1,0:T(2,128)S(1)}, u32[]{:S(2)}, u32[]{:S(2)}) collective-permute-start(f32[9,2,2880]{2,1,0:T(2,128)} %bitcast.3), channel_id=1, source_target_pairs={{0,4},{1,5},{2,6},{3,7},{4,0},{5,1},{6,2},{7,3},{8,12},{9,13},{10,... | collective-permute-start | bytes 622088 | tf_op jit(solution)/shard_map/ppermute | solution.py:602
  1.2 0.1 collective-permute-start
  1.2 1.2 %edges.1 = (f32[72,128]{1,0:T(8,128)S(1)}, f32[120,128]{1,0:T(8,128)S(1)}, f32[32,128]{1,0:T(8,128)S(1)}) custom-call(f32[9,2880]{1,0:T(8,128)} %h_ref.3, f32[9,2,2880]{2,1,0:T(2,128)} %bitcast.4, bf16[9,3,2880]{2,1,0:T(4,128)(2,1)} %bitcast.7), custom_call_target="tpu_custom_call" | custom-call | tf_op jit(solution)/shard_map/edges/pallas_call | solution.py:577
  2.4 0.4 %collective-permute-done.near_h_ref = f32[9,2880]{1,0:T(8,128)S(1)} collective-permute-done((f32[9,2880]{1,0:T(8,128)}, f32[9,2880]{1,0:T(8,128)S(1)}, u32[]{:S(2)}, u32[]{:S(2)}) %collective-permute-start) | collective-permute-done | bytes 103712 | tf_op jit(solution)/shard_map/ppermute | solution.py:601
  2.8 0.0 copy-start.4
  2.8 0.0 copy-start.5
  2.9 0.7 %polar.1 = (f32[160,128]{1,0:T(8,128)S(1)}, f32[160,128]{1,0:T(8,128)S(1)}, f32[160,128]{1,0:T(8,128)S(1)}, f32[160,128]{1,0:T(8,128)S(1)}, f32[120,128]{1,0:T(8,128)S(1)}, /*index=5*/f32[72,128]{1,0:T(8,128)S(1)}) custom-call(f32[9,2880]{1,0:T(8,128)S(1)} %copy-done.2, f32[9,2,2880]{2,1,0:T(2,128)S(1)} %bitcast.5, ...), custom_call_target="tpu_custom_call" | custom-call | tf_op jit(solution)/shard_map/polar/pallas_call | solution.py:616
  3.5 3.8 %collective-permute-start.4 = (f32[160,128]{1,0:T(8,128)S(1)}, f32[160,128]{1,0:T(8,128)S(1)}, u32[]{:S(2)}, u32[]{:S(2)}) collective-permute-start(f32[160,128]{1,0:T(8,128)S(1)} %get-tuple-element.27), channel_id=1, source_target_pairs={{0,3},{1,2},{2,1},{3,0},{4,7},{5,6},{6,5},{7,4},{8,11},{9,10},{10,... | collective-permute-start | bytes 245768 | tf_op jit(solution)/shard_map/ppermute | solution.py:612
  7.4 0.5 %collective-permute-start.5 = (f32[160,128]{1,0:T(8,128)S(1)}, f32[160,128]{1,0:T(8,128)S(1)}, u32[]{:S(2)}, u32[]{:S(2)}) collective-permute-start(f32[160,128]{1,0:T(8,128)S(1)} %get-tuple-element.28), channel_id=1, source_target_pairs={{0,1},{1,0},{2,3},{3,2},{4,6},{5,7},{6,4},{7,5},{8,9},{9,8},{10,11... | collective-permute-start | bytes 245768 | tf_op jit(solution)/shard_map/ppermute | solution.py:612
  7.9 0.1 collective-permute-start.6
  8.0 1.9 %collective-permute-start.3 = (f32[120,128]{1,0:T(8,128)S(1)}, f32[120,128]{1,0:T(8,128)S(1)}, u32[]{:S(2)}, u32[]{:S(2)}) collective-permute-start(f32[120,128]{1,0:T(8,128)S(1)} %get-tuple-element.25), channel_id=1, source_target_pairs={{0,2},{1,3},{2,0},{3,1},{4,8},{5,9},{6,10},{7,11},{8,4},{9,5},{10,... | collective-permute-start | bytes 184328 | tf_op jit(solution)/shard_map/ppermute | solution.py:629
  9.9 0.2 collective-permute-start.2
  10.1 0.5 %copy-done.6 = s32[72]{0:T(128)S(1)} copy-done((s32[72]{0:T(128)S(1)}, s32[72]{0:T(128)}, u32[]{:S(2)}) %copy-start.6) | copy-done | bytes 312
  10.6 1.1 %weights.1.weights_ref = bf16[1152,96]{1,0:T(8,128)(2,1)S(1)} custom-call(s32[72]{0:T(128)S(1)} %copy-done.6, f32[192,96]{1,0:T(8,128)S(1)} %copy-done.5, f32[192,96]{1,0:T(8,128)S(1)} %copy-done.4, f32[160,128]{1,0:T(8,128)S(1)} %get-tuple-element.26.after_ref.refs_0_), custom_call_target="tpu_custom_call" | custom-call | tf_op jit(solution)/shard_map/weights/pallas_call | solution.py:630
  11.7 1.2 %collective-permute-done.3.after_ref.far_ref = f32[120,128]{1,0:T(8,128)S(1)} collective-permute-done((f32[120,128]{1,0:T(8,128)S(1)}, f32[120,128]{1,0:T(8,128)S(1)}, u32[]{:S(2)}, u32[]{:S(2)}) %collective-permute-start.3) | collective-permute-done | bytes 61472 | tf_op jit(solution)/shard_map/ppermute | solution.py:629
  13.0 1.0 %filter.1 = (f32[144,128]{1,0:T(8,128)S(1)}, f32[144,128]{1,0:T(8,128)S(1)}, f32[144,128]{1,0:T(8,128)S(1)}, f32[144,128]{1,0:T(8,128)S(1)}) custom-call(bf16[1152,96]{1,0:T(8,128)(2,1)S(1)} %weights.1.weights_ref, f32[8,3,16,128]{3,2,1,0:T(8,128)S(1)} %copy-done.1, f32[120,128]{1,0:T(8,128)S(1)} %collective-permute-done.3.after_ref.far_ref, ...), custom_call_target="tpu_custom_call" | custom-call | tf_op jit(solution)/shard_map/filter/pallas_call | solution.py:636
  14.0 2.2 %collective-permute-start.7 = (f32[144,128]{1,0:T(8,128)S(1)}, f32[144,128]{1,0:T(8,128)S(1)}, u32[]{:S(2)}, u32[]{:S(2)}) collective-permute-start(f32[144,128]{1,0:T(8,128)S(1)} %get-tuple-element.33), channel_id=1, source_target_pairs={{0,3},{1,2},{2,1},{3,0},{4,7},{5,6},{6,5},{7,4},{8,11},{9,10},{10,... | collective-permute-start | bytes 221192 | tf_op jit(solution)/shard_map/ppermute | solution.py:612
  16.1 0.7 %collective-permute-start.8 = (f32[144,128]{1,0:T(8,128)S(1)}, f32[144,128]{1,0:T(8,128)S(1)}, u32[]{:S(2)}, u32[]{:S(2)}) collective-permute-start(f32[144,128]{1,0:T(8,128)S(1)} %get-tuple-element.34), channel_id=1, source_target_pairs={{0,1},{1,0},{2,3},{3,2},{4,6},{5,7},{6,4},{7,5},{8,9},{9,8},{10,11... | collective-permute-start | bytes 221192 | tf_op jit(solution)/shard_map/ppermute | solution.py:612
  16.8 0.7 %collective-permute-start.9 = (f32[144,128]{1,0:T(8,128)S(1)}, f32[144,128]{1,0:T(8,128)S(1)}, u32[]{:S(2)}, u32[]{:S(2)}) collective-permute-start(f32[144,128]{1,0:T(8,128)S(1)} %get-tuple-element.35), channel_id=1, source_target_pairs={{0,2},{1,3},{2,0},{3,1},{4,5},{5,4},{6,7},{7,6},{8,10},{9,11},{10,... | collective-permute-start | bytes 221192 | tf_op jit(solution)/shard_map/ppermute | solution.py:612
  17.6 2.5 %rest.1 = (f32[2,9,2880]{2,1,0:T(8,128)S(1)}, f32[9,2880]{1,0:T(8,128)S(1)}, bf16[3,9,2880]{2,1,0:T(8,128)(2,1)S(1)}) custom-call(s32[72]{0:T(128)S(1)} %copy-done.6, f32[9,2880]{1,0:T(8,128)S(1)} %copy-done.2, f32[9,2,2880]{2,1,0:T(2,128)S(1)} %bitcast.6, bf16[3,9,2880]{2,1,0:T(8,128)(2,1)S(1)} %copy.11.q_ref, ...), custom_call_target="tpu_custom_call" | custom-call | tf_op jit(solution)/shard_map/rest/pallas_call | solution.py:645
  20.1 0.8 %copy.12 = bf16[3,9,2880]{2,0,1:T(4,128)(2,1)} copy(bf16[3,9,2880]{2,1,0:T(8,128)(2,1)S(1)} %get-tuple-element.41) | data formatting | bytes 311040
  20.9 0.3 %collective-permute-done.9.refs_3_ = f32[144,128]{1,0:T(8,128)S(1)} collective-permute-done((f32[144,128]{1,0:T(8,128)S(1)}, f32[144,128]{1,0:T(8,128)S(1)}, u32[]{:S(2)}, u32[]{:S(2)}) %collective-permute-start.9) | collective-permute-done | bytes 73760 | tf_op jit(solution)/shard_map/ppermute | solution.py:612
  21.2 1.5 %finish.1 = (f32[9,2,2880]{2,1,0:T(2,128)}, f32[9,2880]{1,0:T(8,128)}) custom-call(s32[72]{0:T(128)S(1)} %copy-done.6, f32[2,9,2880]{2,1,0:T(8,128)S(1)} %get-tuple-element.31.base_w_ref, f32[9,2880]{1,0:T(8,128)S(1)} %get-tuple-element.32.base_h_ref, f32[144,128]{1,0:T(8,128)S(1)} %get-tuple-element.30.after_ref.refs_0_, ...), custom_call_target="tpu_custom_call" | custom-call | tf_op jit(solution)/shard_map/finish/pallas_call | solution.py:653
  (20 shorter events, 0.1 us)
Async XLA Ops:
  0.6 2.2 %copy-start.3 = (f32[2,24,128]{2,1,0:T(8,128)S(1)}, f32[2,24,128]{2,1,0:T(8,128)}, u32[]{:S(2)}) copy-start(f32[2,24,128]{2,1,0:T(8,128)} %constant.9.clone.wave_ref) | copy-start | bytes 73732
  0.6 2.2 %collective-permute-start.1 = (f32[9,2,2880]{2,1,0:T(2,128)}, f32[9,2,2880]{2,1,0:T(2,128)S(1)}, u32[]{:S(2)}, u32[]{:S(2)}) collective-permute-start(f32[9,2,2880]{2,1,0:T(2,128)} %bitcast.3), channel_id=1, source_target_pairs={{0,4},{1,5},{2,6},{3,7},{4,0},{5,1},{6,2},{7,3},{8,12},{9,13},{10,... | collective-permute-start | bytes 622088 | tf_op jit(solution)/shard_map/ppermute | solution.py:602
  1.2 1.6 %collective-permute-start = (f32[9,2880]{1,0:T(8,128)}, f32[9,2880]{1,0:T(8,128)S(1)}, u32[]{:S(2)}, u32[]{:S(2)}) collective-permute-start(f32[9,2880]{1,0:T(8,128)} %h_ref.3), channel_id=1, source_target_pairs={{0,4},{1,5},{2,6},{3,7},{4,0},{5,1},{6,2},{7,3},{8,12},{9,13},{10,... | collective-permute-start | bytes 311048 | tf_op jit(solution)/shard_map/ppermute | solution.py:601
  1.2 1.6 %copy-start = (f32[2,9,2880]{2,0,1:T(2,128)S(1)}, f32[2,9,2880]{2,0,1:T(2,128)}, u32[]{:S(2)}) copy-start(f32[2,9,2880]{2,0,1:T(2,128)} %param.8) | copy-start | bytes 622084
  1.2 1.6 %copy-start.1 = (f32[8,3,16,128]{3,2,1,0:T(8,128)S(1)}, f32[8,3,16,128]{3,2,1,0:T(8,128)}, u32[]{:S(2)}) copy-start(f32[8,3,16,128]{3,2,1,0:T(8,128)} %constant.8.clone.geo_ref) | copy-start | bytes 589828
  1.2 1.6 %copy-start.2 = (f32[9,2880]{1,0:T(8,128)S(1)}, f32[9,2880]{1,0:T(8,128)}, u32[]{:S(2)}) copy-start(f32[9,2880]{1,0:T(8,128)} %h_ref.3) | copy-start | bytes 311044
  2.8 7.3 %copy-start.4 = (f32[192,96]{1,0:T(8,128)S(1)}, f32[192,96]{1,0:T(8,128)}, u32[]{:S(2)}) copy-start(f32[192,96]{1,0:T(8,128)} %constant.11.clone.inverse_ref) | copy-start | bytes 221188
  2.8 7.2 %copy-start.5 = (f32[192,96]{1,0:T(8,128)S(1)}, f32[192,96]{1,0:T(8,128)}, u32[]{:S(2)}) copy-start(f32[192,96]{1,0:T(8,128)} %constant.10.clone.n_ref) | copy-start | bytes 221188
  3.5 9.5 %collective-permute-start.4 = (f32[160,128]{1,0:T(8,128)S(1)}, f32[160,128]{1,0:T(8,128)S(1)}, u32[]{:S(2)}, u32[]{:S(2)}) collective-permute-start(f32[160,128]{1,0:T(8,128)S(1)} %get-tuple-element.27), channel_id=1, source_target_pairs={{0,3},{1,2},{2,1},{3,0},{4,7},{5,6},{6,5},{7,4},{8,11},{9,10},{10,... | collective-permute-start | bytes 245768 | tf_op jit(solution)/shard_map/ppermute | solution.py:612
  7.4 5.6 %collective-permute-start.5 = (f32[160,128]{1,0:T(8,128)S(1)}, f32[160,128]{1,0:T(8,128)S(1)}, u32[]{:S(2)}, u32[]{:S(2)}) collective-permute-start(f32[160,128]{1,0:T(8,128)S(1)} %get-tuple-element.28), channel_id=1, source_target_pairs={{0,1},{1,0},{2,3},{3,2},{4,6},{5,7},{6,4},{7,5},{8,9},{9,8},{10,11... | collective-permute-start | bytes 245768 | tf_op jit(solution)/shard_map/ppermute | solution.py:612
  7.9 5.1 %collective-permute-start.6 = (f32[160,128]{1,0:T(8,128)S(1)}, f32[160,128]{1,0:T(8,128)S(1)}, u32[]{:S(2)}, u32[]{:S(2)}) collective-permute-start(f32[160,128]{1,0:T(8,128)S(1)} %get-tuple-element.29), channel_id=1, source_target_pairs={{0,2},{1,3},{2,0},{3,1},{4,5},{5,4},{6,7},{7,6},{8,10},{9,11},{10,... | collective-permute-start | bytes 245768 | tf_op jit(solution)/shard_map/ppermute | solution.py:612
  8.0 5.0 %collective-permute-start.3 = (f32[120,128]{1,0:T(8,128)S(1)}, f32[120,128]{1,0:T(8,128)S(1)}, u32[]{:S(2)}, u32[]{:S(2)}) collective-permute-start(f32[120,128]{1,0:T(8,128)S(1)} %get-tuple-element.25), channel_id=1, source_target_pairs={{0,2},{1,3},{2,0},{3,1},{4,8},{5,9},{6,10},{7,11},{8,4},{9,5},{10,... | collective-permute-start | bytes 184328 | tf_op jit(solution)/shard_map/ppermute | solution.py:629
  9.9 0.7 %copy-start.6 = (s32[72]{0:T(128)S(1)}, s32[72]{0:T(128)}, u32[]{:S(2)}) copy-start(s32[72]{0:T(128)} %cut_ref.5) | copy-start | bytes 868
  9.9 1.8 %collective-permute-start.2 = (f32[72,128]{1,0:T(8,128)S(1)}, f32[72,128]{1,0:T(8,128)S(1)}, u32[]{:S(2)}, u32[]{:S(2)}) collective-permute-start(f32[72,128]{1,0:T(8,128)S(1)} %get-tuple-element.24), channel_id=1, source_target_pairs={{0,4},{1,5},{2,6},{3,7},{4,0},{5,1},{6,2},{7,3},{8,12},{9,13},{10,... | collective-permute-start | bytes 110600 | tf_op jit(solution)/shard_map/ppermute | solution.py:628
  11.7 5.8 %copy-start.7 = (bf16[3,9,2880]{2,0,1:T(4,128)(2,1)S(1)}, bf16[3,9,2880]{2,0,1:T(4,128)(2,1)}, u32[]{:S(2)}) copy-start(bf16[3,9,2880]{2,0,1:T(4,128)(2,1)} %param.10) | copy-start | bytes 466564
  14.0 6.9 %collective-permute-start.7 = (f32[144,128]{1,0:T(8,128)S(1)}, f32[144,128]{1,0:T(8,128)S(1)}, u32[]{:S(2)}, u32[]{:S(2)}) collective-permute-start(f32[144,128]{1,0:T(8,128)S(1)} %get-tuple-element.33), channel_id=1, source_target_pairs={{0,3},{1,2},{2,1},{3,0},{4,7},{5,6},{6,5},{7,4},{8,11},{9,10},{10,... | collective-permute-start | bytes 221192 | tf_op jit(solution)/shard_map/ppermute | solution.py:612
  16.1 4.8 %collective-permute-start.8 = (f32[144,128]{1,0:T(8,128)S(1)}, f32[144,128]{1,0:T(8,128)S(1)}, u32[]{:S(2)}, u32[]{:S(2)}) collective-permute-start(f32[144,128]{1,0:T(8,128)S(1)} %get-tuple-element.34), channel_id=1, source_target_pairs={{0,1},{1,0},{2,3},{3,2},{4,6},{5,7},{6,4},{7,5},{8,9},{9,8},{10,11... | collective-permute-start | bytes 221192 | tf_op jit(solution)/shard_map/ppermute | solution.py:612
  16.8 4.4 %collective-permute-start.9 = (f32[144,128]{1,0:T(8,128)S(1)}, f32[144,128]{1,0:T(8,128)S(1)}, u32[]{:S(2)}, u32[]{:S(2)}) collective-permute-start(f32[144,128]{1,0:T(8,128)S(1)} %get-tuple-element.35), channel_id=1, source_target_pairs={{0,2},{1,3},{2,0},{3,1},{4,5},{5,4},{6,7},{7,6},{8,10},{9,11},{10,... | collective-permute-start | bytes 221192 | tf_op jit(solution)/shard_map/ppermute | solution.py:612

commit v11 on v10

--- a/solution.py
+++ b/solution.py
@@ -49,15 +49,8 @@
 
     def at_pole(self, row):
         band = lax.axis_index("lat")
-        south, north = (row == 0) & (band == 0), (row == self.rows - 1) & (band == self.n_lat - 1)
-        return (south | north) & self.near_only
-
-    def active(self, cut_ref, shape):
-        row = lax.broadcasted_iota(jnp.int32, shape, 0)
-        cuts = jnp.full(shape, self.nlon // 2, jnp.int32)
-        for j in range(self.rows):
-            cuts = jnp.where(row == j, cut_ref[lax.axis_index("lat") * self.rows + j], cuts)
-        return cuts < self.nlon // 2, self.at_pole(row)
+        pole = jnp.where(band == 0, 0, jnp.where(band == self.n_lat - 1, self.rows - 1, -1))
+        return row == (pole if self.near_only else -1)
 
     def turns(self, odd):
         middle = list(range(1, self.n_lon - 1))
@@ -347,7 +340,7 @@
     return result
 
 
-def rest_kernel(sz, cut_ref, h_ref, w_ref, q_ref, near_h_ref, near_w_ref, near_q_ref, far_ref, geo_ref, wave_ref, after_ref, *refs):
+def rest_kernel(sz, masks_ref, h_ref, w_ref, q_ref, near_h_ref, near_w_ref, near_q_ref, far_ref, geo_ref, wave_ref, after_ref, *refs):
     met_refs, (new_w_ref, new_h_ref, mass_ref, ext, pole_in) = refs[: sz.n_lon], refs[sz.n_lon :]
     band = lax.axis_index("lat")
     ring = Tiles(sz)
@@ -377,7 +370,7 @@
     inv_cos, sin_centre, cos_face = geo_ref[band, 0], geo_ref[band, 1], geo_ref[band, 2]
     ratio = sz.ratio
 
-    active, alone = sz.active(cut_ref, (EXT_ROWS, LANES))
+    plain, alone = masks_ref[0], masks_ref[1]
     if sz.near_only:
         band = lax.axis_index("lat")
         low = band < sz.n_lat // 2
@@ -385,12 +378,12 @@
         kept_waves = pole_waves(sz, pole_in.at[:, rows - 8 :], pole_cos, jnp.where(low, 1.0, -1.0))
 
     def stepped(f, t, value, tend):
-        tend = jnp.where(active, 0.0, tend)
+        value = value + plain * tend
         if sz.near_only:
             level, cosine, sine = kept_waves[f]
             wave = level + cosine * wave_ref[0, t : t + 1] + sine * wave_ref[1, t : t + 1]
-            tend = jnp.where(alone, wave, tend)
-        return value + TIME_STEP * tend
+            value = value + alone * wave
+        return value
 
     def tile(f, t):
         return ext[f, :, LANES * t : LANES * (t + 1)]
@@ -451,8 +444,16 @@
     return unit // sz.work, sz.first() + lax.rem(unit, sz.work)
 
 
-def weights_kernel(sz, cut_ref, n_ref, inverse_ref, after_ref, weights_ref):
+def weights_kernel(sz, cut_ref, n_ref, inverse_ref, after_ref, weights_ref, masks_ref):
     band = lax.axis_index("lat")
+    row = lax.broadcasted_iota(jnp.int32, (EXT_ROWS, LANES), 0)
+    cuts = jnp.full((EXT_ROWS, LANES), sz.nlon // 2, jnp.int32)
+    for j in range(sz.rows):
+        cuts = jnp.where(row == j, cut_ref[band * sz.rows + j], cuts)
+    plain, alone = cuts >= sz.nlon // 2, sz.at_pole(row)
+    masks_ref[0] = jnp.where(plain, TIME_STEP, 0.0)
+    masks_ref[1] = jnp.where(alone, TIME_STEP, 0.0)
+    masks_ref[2] = jnp.where(plain | alone, 0.0, TIME_STEP)
     size = PER_TILE * sz.stack
     for i in range(sz.share):
         width = (2 * cut_ref[band * sz.rows + share_of(sz, i)[1]] + 1).astype(jnp.float32)
@@ -518,13 +519,12 @@
         out_ref[...] = results[sz.partner(k)]
 
 
-def finish_kernel(sz, cut_ref, base_w_ref, base_h_ref, *refs):
+def finish_kernel(sz, masks_ref, base_w_ref, base_h_ref, *refs):
     back_refs, (new_w_ref, new_h_ref, back_ref) = refs[: sz.n_lon], refs[sz.n_lon :]
     rows, work = sz.rows, sz.work
     for k, ref in enumerate(back_refs):
         back_ref[sz.piece(k), :] = ref[...]
-    active, alone = sz.active(cut_ref, (EXT_ROWS, LANES))
-    scale = jnp.where(active & jnp.logical_not(alone), TIME_STEP, 0.0)
+    scale = masks_ref[2]
     even = lax.rem(lax.axis_index("lat"), 2) == 0
     for f in range(3):
         for t in range(sz.tiles):
@@ -627,11 +627,14 @@
     met = meetings(tends)
     near_q = lax.ppermute(near_q, ("lat", "lon"), near)
     from_far = lax.ppermute(far_rows, ("lat", "lon"), far) if sz.near_only else far_rows
-    weights = call(
+    weights, masks = call(
         weights_kernel,
         "weights",
         [smem, vmem, vmem, anywhere],
-        jax.ShapeDtypeStruct((sz.share * PER_TILE * sz.stack, n_lon * sz.stack), jnp.bfloat16),
+        (
+            jax.ShapeDtypeStruct((sz.share * PER_TILE * sz.stack, n_lon * sz.stack), jnp.bfloat16),
+            shaped(3, EXT_ROWS, LANES),
+        ),
     )(cutoff, n, inverse, tends[0])
     worked = call(
         filter_kernel,
@@ -645,18 +648,18 @@
     base_w, base_h, mass = call(
         rest_kernel,
         "rest",
-        [smem] + [vmem] * 9 + [anywhere] + [vmem] * n_lon,
+        [vmem] * 10 + [anywhere] + [vmem] * n_lon,
         (shaped(2, rows, merged), shaped(rows, merged), jax.ShapeDtypeStruct(tracers.shape, jnp.bfloat16)),
         [pltpu.VMEM((6, EXT_ROWS, sz.tiles * LANES), f32), pltpu.VMEM((n_lon, 8, LANES), f32)],
-    )(cutoff, thickness, wind_rows, tracers, near_h, near_w, near_q, from_far, geo, wave, worked[0], *met)
+    )(masks, thickness, wind_rows, tracers, near_h, near_w, near_q, from_far, geo, wave, worked[0], *met)
 
     new_w, new_h = call(
         finish_kernel,
         "finish",
-        [smem] + [vmem] * (2 + n_lon),
+        [vmem] * (3 + n_lon),
         (shaped(*wind_rows.shape), shaped(rows, merged)),
         [pltpu.VMEM((n_lon * sz.size, LANES), f32)],
-    )(cutoff, base_w, base_h, *back)
+    )(masks, base_w, base_h, *back)
     return jnp.swapaxes(new_w, 0, 1), new_h, mass
 
 

time: 22.8 us -> 22.3 us (0.978)
  Pallas kernels: 7.98 us -> 6.87 us
  waiting for transfers between devices: 1.91 us -> 2.49 us
    pallas_call x3, Pallas kernels: 5.15 us -> 4.05 us  [the longest x1 1.98 us: local(): call(rest_kernel, 'rest', [vmem] * 10 + [anywhere] + [vmem] * n_lon, (sha...]
    ppermute x6, waiting for transfers between devices: 0.29 us -> 0.85 us  [meetings(): lax.ppermute(shares[k], ('lat', 'lon'), [(b * n_lon + i, b * n_lon + j) f...]
  transfers between devices with their start and end apart: 10 -> 10, of which waited for: 3 -> 4; matrix products, arithmetic and copies ran while one was open for 4% -> 4% of each run, Pallas kernels for 22% -> 19%
where the time goes in v11:
time: 22.3 us; the launch traced here: 22.1 us
  starting transfers between devices  10.7 us (48%)
  Pallas kernels  6.87 us (31%)
  waiting for transfers between devices  2.49 us (11%)
  local copies, waits for them, and re-layouts  1.32 us (6%)
  between operations  0.75 us (3%)
    ppermute x6, starting transfers between devices, meetings(): lax.ppermute(shares[k], ('lat', 'lon'), [(b * n_lon + i, b * n_lon + j) f...  8.01 us
    pallas_call x1, Pallas kernels, local(): call(rest_kernel, 'rest', [vmem] * 10 + [anywhere] + [vmem] * n_lon, (sha...  1.98 us
    ppermute x1, starting transfers between devices, local(): lax.ppermute(far_rows, ('lat', 'lon'), far)  1.92 us
    unnamed x18, local copies, waits for them, and re-layouts  1.32 us
    ppermute x1, waiting for transfers between devices, local(): lax.ppermute(far_rows, ('lat', 'lon'), far)  1.25 us
    pallas_call x1, Pallas kernels, local(): call(edges_kernel, 'edges', [hbm] * 3, (near_row, far_row, shaped(2 * EXT...  1.17 us
    pallas_call x1, Pallas kernels, local(): call(weights_kernel, 'weights', [smem, vmem, vmem, anywhere], (jax.ShapeD...  1.15 us
    pallas_call x1, Pallas kernels, local(): call(filter_kernel, 'filter', [vmem] * 2 + [anywhere] * 2 + [vmem] * n_lo...  0.98 us
  transfers between devices with their start and end apart: 10, of which 4 were waited for; matrix products, arithmetic and copies ran while one was open for 4% of the time, Pallas kernels for 19%

profile of v11, /device:TPU:0, one launch (start us, length us, event | category | flops | bytes accessed | tf_op | source)
XLA Modules:
  0.0 22.1 jit_solution(13781587267583732609)
XLA Ops:
  0.6 0.0 copy-start.3
  0.6 0.5 %collective-permute-start.1 = (f32[9,2,2880]{2,1,0:T(2,128)}, f32[9,2,2880]{2,1,0:T(2,128)S(1)}, u32[]{:S(2)}, u32[]{:S(2)}) collective-permute-start(f32[9,2,2880]{2,1,0:T(2,128)} %bitcast.3), channel_id=1, source_target_pairs={{0,4},{1,5},{2,6},{3,7},{4,0},{5,1},{6,2},{7,3},{8,12},{9,13},{10,... | collective-permute-start | bytes 622088 | tf_op jit(solution)/shard_map/ppermute | solution.py:602
  1.2 0.1 collective-permute-start
  1.2 1.2 %edges.1 = (f32[72,128]{1,0:T(8,128)S(1)}, f32[120,128]{1,0:T(8,128)S(1)}, f32[32,128]{1,0:T(8,128)S(1)}) custom-call(f32[9,2880]{1,0:T(8,128)} %h_ref.3, f32[9,2,2880]{2,1,0:T(2,128)} %bitcast.4, bf16[9,3,2880]{2,1,0:T(4,128)(2,1)} %bitcast.7), custom_call_target="tpu_custom_call" | custom-call | tf_op jit(solution)/shard_map/edges/pallas_call | solution.py:577
  2.4 0.4 %collective-permute-done.near_h_ref = f32[9,2880]{1,0:T(8,128)S(1)} collective-permute-done((f32[9,2880]{1,0:T(8,128)}, f32[9,2880]{1,0:T(8,128)S(1)}, u32[]{:S(2)}, u32[]{:S(2)}) %collective-permute-start) | collective-permute-done | bytes 103712 | tf_op jit(solution)/shard_map/ppermute | solution.py:601
  2.8 0.0 copy-start.4
  2.9 0.7 %polar.1 = (f32[160,128]{1,0:T(8,128)S(1)}, f32[160,128]{1,0:T(8,128)S(1)}, f32[160,128]{1,0:T(8,128)S(1)}, f32[160,128]{1,0:T(8,128)S(1)}, f32[120,128]{1,0:T(8,128)S(1)}, /*index=5*/f32[72,128]{1,0:T(8,128)S(1)}) custom-call(f32[9,2880]{1,0:T(8,128)S(1)} %copy-done.2, f32[9,2,2880]{2,1,0:T(2,128)S(1)} %bitcast.5, ...), custom_call_target="tpu_custom_call" | custom-call | tf_op jit(solution)/shard_map/polar/pallas_call | solution.py:616
  3.5 3.8 %collective-permute-start.4 = (f32[160,128]{1,0:T(8,128)S(1)}, f32[160,128]{1,0:T(8,128)S(1)}, u32[]{:S(2)}, u32[]{:S(2)}) collective-permute-start(f32[160,128]{1,0:T(8,128)S(1)} %get-tuple-element.31), channel_id=1, source_target_pairs={{0,3},{1,2},{2,1},{3,0},{4,7},{5,6},{6,5},{7,4},{8,11},{9,10},{10,... | collective-permute-start | bytes 245768 | tf_op jit(solution)/shard_map/ppermute | solution.py:612
  7.4 0.5 %collective-permute-start.5 = (f32[160,128]{1,0:T(8,128)S(1)}, f32[160,128]{1,0:T(8,128)S(1)}, u32[]{:S(2)}, u32[]{:S(2)}) collective-permute-start(f32[160,128]{1,0:T(8,128)S(1)} %get-tuple-element.32), channel_id=1, source_target_pairs={{0,1},{1,0},{2,3},{3,2},{4,6},{5,7},{6,4},{7,5},{8,9},{9,8},{10,11... | collective-permute-start | bytes 245768 | tf_op jit(solution)/shard_map/ppermute | solution.py:612
  7.9 0.1 collective-permute-start.6
  8.0 1.9 %collective-permute-start.3 = (f32[120,128]{1,0:T(8,128)S(1)}, f32[120,128]{1,0:T(8,128)S(1)}, u32[]{:S(2)}, u32[]{:S(2)}) collective-permute-start(f32[120,128]{1,0:T(8,128)S(1)} %get-tuple-element.29), channel_id=1, source_target_pairs={{0,2},{1,3},{2,0},{3,1},{4,8},{5,9},{6,10},{7,11},{8,4},{9,5},{10,... | collective-permute-start | bytes 184328 | tf_op jit(solution)/shard_map/ppermute | solution.py:629
  9.9 0.2 collective-permute-start.2
  10.1 0.5 %copy-done.6 = s32[72]{0:T(128)S(1)} copy-done((s32[72]{0:T(128)S(1)}, s32[72]{0:T(128)}, u32[]{:S(2)}) %copy-start.6) | copy-done | bytes 312
  10.6 1.1 %weights.1 = (bf16[1152,96]{1,0:T(8,128)(2,1)S(1)}, f32[3,16,128]{2,1,0:T(8,128)S(1)}) custom-call(s32[72]{0:T(128)S(1)} %copy-done.6, f32[192,96]{1,0:T(8,128)S(1)} %copy-done.5, f32[192,96]{1,0:T(8,128)S(1)} %copy-done.4, f32[160,128]{1,0:T(8,128)S(1)} %get-tuple-element.26.after_ref.refs_0_), custom_call_target="tpu_custom_call" | custom-call | tf_op jit(solution)/shard_map/weights/pallas_call | solution.py:630
  11.7 1.3 %collective-permute-done.3.after_ref.far_ref = f32[120,128]{1,0:T(8,128)S(1)} collective-permute-done((f32[120,128]{1,0:T(8,128)S(1)}, f32[120,128]{1,0:T(8,128)S(1)}, u32[]{:S(2)}, u32[]{:S(2)}) %collective-permute-start.3) | collective-permute-done | bytes 61472 | tf_op jit(solution)/shard_map/ppermute | solution.py:629
  13.0 1.0 %filter.1 = (f32[144,128]{1,0:T(8,128)S(1)}, f32[144,128]{1,0:T(8,128)S(1)}, f32[144,128]{1,0:T(8,128)S(1)}, f32[144,128]{1,0:T(8,128)S(1)}) custom-call(bf16[1152,96]{1,0:T(8,128)(2,1)S(1)} %get-tuple-element.30.weights_ref, f32[8,3,16,128]{3,2,1,0:T(8,128)S(1)} %copy-done.1, f32[120,128]{1,0:T(8,128)S(1)} %collective-permute-done.3.after_ref.far_ref, ...), custom_call_target="tpu_custom_call" | custom-call | tf_op jit(solution)/shard_map/filter/pallas_call | solution.py:639
  14.0 2.2 %collective-permute-start.7 = (f32[144,128]{1,0:T(8,128)S(1)}, f32[144,128]{1,0:T(8,128)S(1)}, u32[]{:S(2)}, u32[]{:S(2)}) collective-permute-start(f32[144,128]{1,0:T(8,128)S(1)} %get-tuple-element.37), channel_id=1, source_target_pairs={{0,3},{1,2},{2,1},{3,0},{4,7},{5,6},{6,5},{7,4},{8,11},{9,10},{10,... | collective-permute-start | bytes 221192 | tf_op jit(solution)/shard_map/ppermute | solution.py:612
  16.2 0.7 %collective-permute-start.8 = (f32[144,128]{1,0:T(8,128)S(1)}, f32[144,128]{1,0:T(8,128)S(1)}, u32[]{:S(2)}, u32[]{:S(2)}) collective-permute-start(f32[144,128]{1,0:T(8,128)S(1)} %get-tuple-element.38), channel_id=1, source_target_pairs={{0,1},{1,0},{2,3},{3,2},{4,6},{5,7},{6,4},{7,5},{8,9},{9,8},{10,11... | collective-permute-start | bytes 221192 | tf_op jit(solution)/shard_map/ppermute | solution.py:612
  16.8 0.7 %collective-permute-start.9 = (f32[144,128]{1,0:T(8,128)S(1)}, f32[144,128]{1,0:T(8,128)S(1)}, u32[]{:S(2)}, u32[]{:S(2)}) collective-permute-start(f32[144,128]{1,0:T(8,128)S(1)} %get-tuple-element.39), channel_id=1, source_target_pairs={{0,2},{1,3},{2,0},{3,1},{4,5},{5,4},{6,7},{7,6},{8,10},{9,11},{10,... | collective-permute-start | bytes 221192 | tf_op jit(solution)/shard_map/ppermute | solution.py:612
  17.6 2.0 %rest.1 = (f32[2,9,2880]{2,1,0:T(8,128)S(1)}, f32[9,2880]{1,0:T(8,128)S(1)}, bf16[3,9,2880]{2,1,0:T(8,128)(2,1)S(1)}) custom-call(f32[3,16,128]{2,1,0:T(8,128)S(1)} %get-tuple-element.27.masks_ref, f32[9,2880]{1,0:T(8,128)S(1)} %copy-done.2, f32[9,2,2880]{2,1,0:T(2,128)S(1)} %bitcast.6, bf16[3,9,2880]{2,1,0:T(8,128)(2,1)S(1)} %copy.11.q_ref, ...), custom_call_target="tpu_custom_call" | custom-call | tf_op jit(solution)/shard_map/rest/pallas_call | solution.py:648
  19.6 0.8 %copy.12 = bf16[3,9,2880]{2,0,1:T(4,128)(2,1)} copy(bf16[3,9,2880]{2,1,0:T(8,128)(2,1)S(1)} %get-tuple-element.45) | data formatting | bytes 311040
  20.4 0.4 %collective-permute-done.8.refs_2_ = f32[144,128]{1,0:T(8,128)S(1)} collective-permute-done((f32[144,128]{1,0:T(8,128)S(1)}, f32[144,128]{1,0:T(8,128)S(1)}, u32[]{:S(2)}, u32[]{:S(2)}) %collective-permute-start.8) | collective-permute-done | bytes 73760 | tf_op jit(solution)/shard_map/ppermute | solution.py:612
  20.7 0.5 %collective-permute-done.9.refs_3_ = f32[144,128]{1,0:T(8,128)S(1)} collective-permute-done((f32[144,128]{1,0:T(8,128)S(1)}, f32[144,128]{1,0:T(8,128)S(1)}, u32[]{:S(2)}, u32[]{:S(2)}) %collective-permute-start.9) | collective-permute-done | bytes 73760 | tf_op jit(solution)/shard_map/ppermute | solution.py:612
  21.2 0.9 %finish.1 = (f32[9,2,2880]{2,1,0:T(2,128)}, f32[9,2880]{1,0:T(8,128)}) custom-call(f32[3,16,128]{2,1,0:T(8,128)S(1)} %get-tuple-element.27.masks_ref, f32[2,9,2880]{2,1,0:T(8,128)S(1)} %get-tuple-element.35.base_w_ref, f32[9,2880]{1,0:T(8,128)S(1)} %get-tuple-element.36.base_h_ref, f32[144,128]{1,0:T(8,128)S(1)} %get-tuple-element.34.after_ref.refs_0_, ...), custom_call_target="tpu_custom_call" | custom-call | tf_op jit(solution)/shard_map/finish/pallas_call | solution.py:656
  (20 shorter events, 0.1 us)
Async XLA Ops:
  0.6 2.2 %copy-start.3 = (f32[2,24,128]{2,1,0:T(8,128)S(1)}, f32[2,24,128]{2,1,0:T(8,128)}, u32[]{:S(2)}) copy-start(f32[2,24,128]{2,1,0:T(8,128)} %constant.9.clone.wave_ref) | copy-start | bytes 73732
  0.6 2.2 %collective-permute-start.1 = (f32[9,2,2880]{2,1,0:T(2,128)}, f32[9,2,2880]{2,1,0:T(2,128)S(1)}, u32[]{:S(2)}, u32[]{:S(2)}) collective-permute-start(f32[9,2,2880]{2,1,0:T(2,128)} %bitcast.3), channel_id=1, source_target_pairs={{0,4},{1,5},{2,6},{3,7},{4,0},{5,1},{6,2},{7,3},{8,12},{9,13},{10,... | collective-permute-start | bytes 622088 | tf_op jit(solution)/shard_map/ppermute | solution.py:602
  1.2 1.6 %collective-permute-start = (f32[9,2880]{1,0:T(8,128)}, f32[9,2880]{1,0:T(8,128)S(1)}, u32[]{:S(2)}, u32[]{:S(2)}) collective-permute-start(f32[9,2880]{1,0:T(8,128)} %h_ref.3), channel_id=1, source_target_pairs={{0,4},{1,5},{2,6},{3,7},{4,0},{5,1},{6,2},{7,3},{8,12},{9,13},{10,... | collective-permute-start | bytes 311048 | tf_op jit(solution)/shard_map/ppermute | solution.py:601
  1.2 1.6 %copy-start = (f32[2,9,2880]{2,0,1:T(2,128)S(1)}, f32[2,9,2880]{2,0,1:T(2,128)}, u32[]{:S(2)}) copy-start(f32[2,9,2880]{2,0,1:T(2,128)} %param.8) | copy-start | bytes 622084
  1.2 1.6 %copy-start.1 = (f32[8,3,16,128]{3,2,1,0:T(8,128)S(1)}, f32[8,3,16,128]{3,2,1,0:T(8,128)}, u32[]{:S(2)}) copy-start(f32[8,3,16,128]{3,2,1,0:T(8,128)} %constant.8.clone.geo_ref) | copy-start | bytes 589828
  1.2 1.6 %copy-start.2 = (f32[9,2880]{1,0:T(8,128)S(1)}, f32[9,2880]{1,0:T(8,128)}, u32[]{:S(2)}) copy-start(f32[9,2880]{1,0:T(8,128)} %h_ref.3) | copy-start | bytes 311044
  2.8 7.3 %copy-start.4 = (f32[192,96]{1,0:T(8,128)S(1)}, f32[192,96]{1,0:T(8,128)}, u32[]{:S(2)}) copy-start(f32[192,96]{1,0:T(8,128)} %constant.11.clone.inverse_ref) | copy-start | bytes 221188
  2.8 7.2 %copy-start.5 = (f32[192,96]{1,0:T(8,128)S(1)}, f32[192,96]{1,0:T(8,128)}, u32[]{:S(2)}) copy-start(f32[192,96]{1,0:T(8,128)} %constant.10.clone.n_ref) | copy-start | bytes 221188
  3.5 9.5 %collective-permute-start.4 = (f32[160,128]{1,0:T(8,128)S(1)}, f32[160,128]{1,0:T(8,128)S(1)}, u32[]{:S(2)}, u32[]{:S(2)}) collective-permute-start(f32[160,128]{1,0:T(8,128)S(1)} %get-tuple-element.31), channel_id=1, source_target_pairs={{0,3},{1,2},{2,1},{3,0},{4,7},{5,6},{6,5},{7,4},{8,11},{9,10},{10,... | collective-permute-start | bytes 245768 | tf_op jit(solution)/shard_map/ppermute | solution.py:612
  7.4 5.6 %collective-permute-start.5 = (f32[160,128]{1,0:T(8,128)S(1)}, f32[160,128]{1,0:T(8,128)S(1)}, u32[]{:S(2)}, u32[]{:S(2)}) collective-permute-start(f32[160,128]{1,0:T(8,128)S(1)} %get-tuple-element.32), channel_id=1, source_target_pairs={{0,1},{1,0},{2,3},{3,2},{4,6},{5,7},{6,4},{7,5},{8,9},{9,8},{10,11... | collective-permute-start | bytes 245768 | tf_op jit(solution)/shard_map/ppermute | solution.py:612
  7.9 5.1 %collective-permute-start.6 = (f32[160,128]{1,0:T(8,128)S(1)}, f32[160,128]{1,0:T(8,128)S(1)}, u32[]{:S(2)}, u32[]{:S(2)}) collective-permute-start(f32[160,128]{1,0:T(8,128)S(1)} %get-tuple-element.33), channel_id=1, source_target_pairs={{0,2},{1,3},{2,0},{3,1},{4,5},{5,4},{6,7},{7,6},{8,10},{9,11},{10,... | collective-permute-start | bytes 245768 | tf_op jit(solution)/shard_map/ppermute | solution.py:612
  8.0 5.0 %collective-permute-start.3 = (f32[120,128]{1,0:T(8,128)S(1)}, f32[120,128]{1,0:T(8,128)S(1)}, u32[]{:S(2)}, u32[]{:S(2)}) collective-permute-start(f32[120,128]{1,0:T(8,128)S(1)} %get-tuple-element.29), channel_id=1, source_target_pairs={{0,2},{1,3},{2,0},{3,1},{4,8},{5,9},{6,10},{7,11},{8,4},{9,5},{10,... | collective-permute-start | bytes 184328 | tf_op jit(solution)/shard_map/ppermute | solution.py:629
  9.9 0.7 %copy-start.6 = (s32[72]{0:T(128)S(1)}, s32[72]{0:T(128)}, u32[]{:S(2)}) copy-start(s32[72]{0:T(128)} %cut_ref.1) | copy-start | bytes 868
  9.9 1.8 %collective-permute-start.2 = (f32[72,128]{1,0:T(8,128)S(1)}, f32[72,128]{1,0:T(8,128)S(1)}, u32[]{:S(2)}, u32[]{:S(2)}) collective-permute-start(f32[72,128]{1,0:T(8,128)S(1)} %get-tuple-element.28), channel_id=1, source_target_pairs={{0,4},{1,5},{2,6},{3,7},{4,0},{5,1},{6,2},{7,3},{8,12},{9,13},{10,... | collective-permute-start | bytes 110600 | tf_op jit(solution)/shard_map/ppermute | solution.py:628
  13.0 4.6 %copy-start.7 = (bf16[3,9,2880]{2,0,1:T(4,128)(2,1)S(1)}, bf16[3,9,2880]{2,0,1:T(4,128)(2,1)}, u32[]{:S(2)}) copy-start(bf16[3,9,2880]{2,0,1:T(4,128)(2,1)} %param.10) | copy-start | bytes 466564
  14.0 6.4 %collective-permute-start.7 = (f32[144,128]{1,0:T(8,128)S(1)}, f32[144,128]{1,0:T(8,128)S(1)}, u32[]{:S(2)}, u32[]{:S(2)}) collective-permute-start(f32[144,128]{1,0:T(8,128)S(1)} %get-tuple-element.37), channel_id=1, source_target_pairs={{0,3},{1,2},{2,1},{3,0},{4,7},{5,6},{6,5},{7,4},{8,11},{9,10},{10,... | collective-permute-start | bytes 221192 | tf_op jit(solution)/shard_map/ppermute | solution.py:612
  16.2 4.6 %collective-permute-start.8 = (f32[144,128]{1,0:T(8,128)S(1)}, f32[144,128]{1,0:T(8,128)S(1)}, u32[]{:S(2)}, u32[]{:S(2)}) collective-permute-start(f32[144,128]{1,0:T(8,128)S(1)} %get-tuple-element.38), channel_id=1, source_target_pairs={{0,1},{1,0},{2,3},{3,2},{4,6},{5,7},{6,4},{7,5},{8,9},{9,8},{10,11... | collective-permute-start | bytes 221192 | tf_op jit(solution)/shard_map/ppermute | solution.py:612
  16.8 4.4 %collective-permute-start.9 = (f32[144,128]{1,0:T(8,128)S(1)}, f32[144,128]{1,0:T(8,128)S(1)}, u32[]{:S(2)}, u32[]{:S(2)}) collective-permute-start(f32[144,128]{1,0:T(8,128)S(1)} %get-tuple-element.39), channel_id=1, source_target_pairs={{0,2},{1,3},{2,0},{3,1},{4,5},{5,4},{6,7},{7,6},{8,10},{9,11},{10,... | collective-permute-start | bytes 221192 | tf_op jit(solution)/shard_map/ppermute | solution.py:612

commit v12 on v11

--- a/solution.py
+++ b/solution.py
@@ -465,7 +465,11 @@
         weights_ref[size * i : size * (i + 1)] = weights.astype(jnp.bfloat16)
 
 
-def filter_kernel(sz, weights_ref, geo_ref, after_ref, also_after_ref, *refs):
+def pass_kernel(sz, piece_ref, after_ref, also_after_ref, out_ref):
+    out_ref[...] = piece_ref[...]
+
+
+def filter_kernel(sz, weights_ref, geo_ref, *refs):
     n_lon, stack, share = sz.n_lon, sz.stack, sz.share
     in_refs, out_refs, (gathered, results) = refs[:n_lon], refs[n_lon : 2 * n_lon], refs[2 * n_lon :]
     for k, in_ref in enumerate(in_refs):
@@ -639,10 +643,12 @@
     worked = call(
         filter_kernel,
         "filter",
-        [vmem] * 2 + [anywhere] * 2 + [vmem] * n_lon,
+        [vmem] * 2 + [vmem] * n_lon,
         [shaped(sz.size, LANES)] * n_lon,
         [all_pieces, all_pieces],
-    )(weights, geo, from_far, near_q, *met)
+    )(weights, geo, *met)
+    held = call(pass_kernel, "pass", [vmem] + [anywhere] * 2, shaped(sz.size, LANES))(worked[-1], from_far, near_q)
+    worked = [*worked[:-1], held]
     back = meetings(worked)
 
     base_w, base_h, mass = call(

time: 22.3 us -> 21.7 us (0.973)
  waiting for transfers between devices: 2.49 us -> 1.82 us
    ppermute x1, waiting for transfers between devices: 1.25 us -> 0.01 us  [local(): lax.ppermute(far_rows, ('lat', 'lon'), far)]
    ppermute x6, waiting for transfers between devices: 0.85 us -> 1.43 us  [meetings(): lax.ppermute(shares[k], ('lat', 'lon'), [(b * n_lon + i, b * n_lon + j) f...]
    pallas_call x1 -> x2, Pallas kernels: 0.98 us -> 0.99 us  [the longest x1 0.99 us: local(): call(filter_kernel, 'filter', [vmem] * 2 + [vmem] * n_lon, [shaped(sz.siz...]
  transfers between devices with their start and end apart: 10 -> 10, of which waited for: 4 -> 5; matrix products, arithmetic and copies ran while one was open for 4% -> 4% of each run, Pallas kernels for 19% -> 25%
where the time goes in v12:
time: 21.7 us; the launch traced here: 21.5 us
  starting transfers between devices  10.8 us (50%)
  Pallas kernels  6.88 us (32%)
  waiting for transfers between devices  1.82 us (8%)
  local copies, waits for them, and re-layouts  1.32 us (6%)
  between operations  0.75 us (3%)
    ppermute x6, starting transfers between devices, meetings(): lax.ppermute(shares[k], ('lat', 'lon'), [(b * n_lon + i, b * n_lon + j) f...  8.07 us
    pallas_call x1, Pallas kernels, local(): call(rest_kernel, 'rest', [vmem] * 10 + [anywhere] + [vmem] * n_lon, (sha...  1.98 us
    ppermute x1, starting transfers between devices, local(): lax.ppermute(far_rows, ('lat', 'lon'), far)  1.92 us
    ppermute x6, waiting for transfers between devices, meetings(): lax.ppermute(shares[k], ('lat', 'lon'), [(b * n_lon + i, b * n_lon + j) f...  1.43 us
    unnamed x18, local copies, waits for them, and re-layouts  1.32 us
    pallas_call x1, Pallas kernels, local(): call(edges_kernel, 'edges', [hbm] * 3, (near_row, far_row, shaped(2 * EXT...  1.17 us
    pallas_call x1, Pallas kernels, local(): call(weights_kernel, 'weights', [smem, vmem, vmem, anywhere], (jax.ShapeD...  1.15 us
    pallas_call x1, Pallas kernels, local(): call(filter_kernel, 'filter', [vmem] * 2 + [vmem] * n_lon, [shaped(sz.siz...  0.99 us
  transfers between devices with their start and end apart: 10, of which 5 were waited for; matrix products, arithmetic and copies ran while one was open for 4% of the time, Pallas kernels for 25%

profile of v12, /device:TPU:0, one launch (start us, length us, event | category | flops | bytes accessed | tf_op | source)
XLA Modules:
  0.0 21.5 jit_solution(393297196155509857)
XLA Ops:
  0.6 0.5 %collective-permute-start.1 = (f32[9,2,2880]{2,1,0:T(2,128)}, f32[9,2,2880]{2,1,0:T(2,128)S(1)}, u32[]{:S(2)}, u32[]{:S(2)}) collective-permute-start(f32[9,2,2880]{2,1,0:T(2,128)} %bitcast.3), channel_id=1, source_target_pairs={{0,4},{1,5},{2,6},{3,7},{4,0},{5,1},{6,2},{7,3},{8,12},{9,13},{10,... | collective-permute-start | bytes 622088 | tf_op jit(solution)/shard_map/ppermute | solution.py:606
  1.2 0.1 collective-permute-start
  1.2 1.2 %edges.1 = (f32[72,128]{1,0:T(8,128)S(1)}, f32[120,128]{1,0:T(8,128)S(1)}, f32[32,128]{1,0:T(8,128)S(1)}) custom-call(f32[9,2880]{1,0:T(8,128)} %h_ref.3, f32[9,2,2880]{2,1,0:T(2,128)} %bitcast.4, bf16[9,3,2880]{2,1,0:T(4,128)(2,1)} %bitcast.7), custom_call_target="tpu_custom_call" | custom-call | tf_op jit(solution)/shard_map/edges/pallas_call | solution.py:581
  2.4 0.4 %collective-permute-done.near_h_ref = f32[9,2880]{1,0:T(8,128)S(1)} collective-permute-done((f32[9,2880]{1,0:T(8,128)}, f32[9,2880]{1,0:T(8,128)S(1)}, u32[]{:S(2)}, u32[]{:S(2)}) %collective-permute-start) | collective-permute-done | bytes 103712 | tf_op jit(solution)/shard_map/ppermute | solution.py:605
  2.8 0.0 copy-start.4
  2.9 0.7 %polar.1 = (f32[160,128]{1,0:T(8,128)S(1)}, f32[160,128]{1,0:T(8,128)S(1)}, f32[160,128]{1,0:T(8,128)S(1)}, f32[160,128]{1,0:T(8,128)S(1)}, f32[120,128]{1,0:T(8,128)S(1)}, /*index=5*/f32[72,128]{1,0:T(8,128)S(1)}) custom-call(f32[9,2880]{1,0:T(8,128)S(1)} %copy-done.2, f32[9,2,2880]{2,1,0:T(2,128)S(1)} %bitcast.5, ...), custom_call_target="tpu_custom_call" | custom-call | tf_op jit(solution)/shard_map/polar/pallas_call | solution.py:620
  3.5 3.8 %collective-permute-start.4 = (f32[160,128]{1,0:T(8,128)S(1)}, f32[160,128]{1,0:T(8,128)S(1)}, u32[]{:S(2)}, u32[]{:S(2)}) collective-permute-start(f32[160,128]{1,0:T(8,128)S(1)} %get-tuple-element.31), channel_id=1, source_target_pairs={{0,3},{1,2},{2,1},{3,0},{4,7},{5,6},{6,5},{7,4},{8,11},{9,10},{10,... | collective-permute-start | bytes 245768 | tf_op jit(solution)/shard_map/ppermute | solution.py:616
  7.4 0.5 %collective-permute-start.5 = (f32[160,128]{1,0:T(8,128)S(1)}, f32[160,128]{1,0:T(8,128)S(1)}, u32[]{:S(2)}, u32[]{:S(2)}) collective-permute-start(f32[160,128]{1,0:T(8,128)S(1)} %get-tuple-element.32), channel_id=1, source_target_pairs={{0,1},{1,0},{2,3},{3,2},{4,6},{5,7},{6,4},{7,5},{8,9},{9,8},{10,11... | collective-permute-start | bytes 245768 | tf_op jit(solution)/shard_map/ppermute | solution.py:616
  7.9 0.1 collective-permute-start.6
  8.0 1.9 %collective-permute-start.3 = (f32[120,128]{1,0:T(8,128)S(1)}, f32[120,128]{1,0:T(8,128)S(1)}, u32[]{:S(2)}, u32[]{:S(2)}) collective-permute-start(f32[120,128]{1,0:T(8,128)S(1)} %get-tuple-element.29), channel_id=1, source_target_pairs={{0,2},{1,3},{2,0},{3,1},{4,8},{5,9},{6,10},{7,11},{8,4},{9,5},{10,... | collective-permute-start | bytes 184328 | tf_op jit(solution)/shard_map/ppermute | solution.py:633
  9.9 0.2 collective-permute-start.2
  10.1 0.5 %copy-done.6 = s32[72]{0:T(128)S(1)} copy-done((s32[72]{0:T(128)S(1)}, s32[72]{0:T(128)}, u32[]{:S(2)}) %copy-start.6) | copy-done | bytes 312
  10.6 1.1 %weights.1 = (bf16[1152,96]{1,0:T(8,128)(2,1)S(1)}, f32[3,16,128]{2,1,0:T(8,128)S(1)}) custom-call(s32[72]{0:T(128)S(1)} %copy-done.6, f32[192,96]{1,0:T(8,128)S(1)} %copy-done.5, f32[192,96]{1,0:T(8,128)S(1)} %copy-done.4, f32[160,128]{1,0:T(8,128)S(1)} %get-tuple-element.26.after_ref.refs_0_), custom_call_target="tpu_custom_call" | custom-call | tf_op jit(solution)/shard_map/weights/pallas_call | solution.py:634
  11.7 0.4 %collective-permute-done.5.refs_2_ = f32[160,128]{1,0:T(8,128)S(1)} collective-permute-done((f32[160,128]{1,0:T(8,128)S(1)}, f32[160,128]{1,0:T(8,128)S(1)}, u32[]{:S(2)}, u32[]{:S(2)}) %collective-permute-start.5) | collective-permute-done | bytes 81952 | tf_op jit(solution)/shard_map/ppermute | solution.py:616
  12.2 0.2 collective-permute-done.6.refs_3_
  12.3 1.0 %filter.1 = (f32[144,128]{1,0:T(8,128)S(1)}, f32[144,128]{1,0:T(8,128)S(1)}, f32[144,128]{1,0:T(8,128)S(1)}, f32[144,128]{1,0:T(8,128)S(1)}) custom-call(bf16[1152,96]{1,0:T(8,128)(2,1)S(1)} %get-tuple-element.30.weights_ref, f32[8,3,16,128]{3,2,1,0:T(8,128)S(1)} %copy-done.1, f32[160,128]{1,0:T(8,128)S(1)} %get-tuple-element.26.after_ref.refs_0_, ...), custom_call_target="tpu_custom_call" | custom-call | tf_op jit(solution)/shard_map/filter/pallas_call | solution.py:643
  13.3 1.8 %collective-permute-start.7 = (f32[144,128]{1,0:T(8,128)S(1)}, f32[144,128]{1,0:T(8,128)S(1)}, u32[]{:S(2)}, u32[]{:S(2)}) collective-permute-start(f32[144,128]{1,0:T(8,128)S(1)} %get-tuple-element.37), channel_id=1, source_target_pairs={{0,3},{1,2},{2,1},{3,0},{4,7},{5,6},{6,5},{7,4},{8,11},{9,10},{10,... | collective-permute-start | bytes 221192 | tf_op jit(solution)/shard_map/ppermute | solution.py:616
  15.2 1.0 %collective-permute-start.8 = (f32[144,128]{1,0:T(8,128)S(1)}, f32[144,128]{1,0:T(8,128)S(1)}, u32[]{:S(2)}, u32[]{:S(2)}) collective-permute-start(f32[144,128]{1,0:T(8,128)S(1)} %get-tuple-element.38), channel_id=1, source_target_pairs={{0,1},{1,0},{2,3},{3,2},{4,6},{5,7},{6,4},{7,5},{8,9},{9,8},{10,11... | collective-permute-start | bytes 221192 | tf_op jit(solution)/shard_map/ppermute | solution.py:616
  16.2 0.8 %collective-permute-start.9 = (f32[144,128]{1,0:T(8,128)S(1)}, f32[144,128]{1,0:T(8,128)S(1)}, u32[]{:S(2)}, u32[]{:S(2)}) collective-permute-start(f32[144,128]{1,0:T(8,128)S(1)} %pass.1), channel_id=1, source_target_pairs={{0,2},{1,3},{2,0},{3,1},{4,5},{5,4},{6,7},{7,6},{8,10},{9,11},{10,... | collective-permute-start | bytes 221192 | tf_op jit(solution)/shard_map/ppermute | solution.py:616
  17.0 2.0 %rest.1 = (f32[2,9,2880]{2,1,0:T(8,128)S(1)}, f32[9,2880]{1,0:T(8,128)S(1)}, bf16[3,9,2880]{2,1,0:T(8,128)(2,1)S(1)}) custom-call(f32[3,16,128]{2,1,0:T(8,128)S(1)} %get-tuple-element.27.masks_ref, f32[9,2880]{1,0:T(8,128)S(1)} %copy-done.2, f32[9,2,2880]{2,1,0:T(2,128)S(1)} %bitcast.6, bf16[3,9,2880]{2,1,0:T(8,128)(2,1)S(1)} %copy.11.q_ref, ...), custom_call_target="tpu_custom_call" | custom-call | tf_op jit(solution)/shard_map/rest/pallas_call | solution.py:654
  19.0 0.8 %copy.12 = bf16[3,9,2880]{2,0,1:T(4,128)(2,1)} copy(bf16[3,9,2880]{2,1,0:T(8,128)(2,1)S(1)} %get-tuple-element.45) | data formatting | bytes 311040
  19.8 0.3 %collective-permute-done.8.refs_2_ = f32[144,128]{1,0:T(8,128)S(1)} collective-permute-done((f32[144,128]{1,0:T(8,128)S(1)}, f32[144,128]{1,0:T(8,128)S(1)}, u32[]{:S(2)}, u32[]{:S(2)}) %collective-permute-start.8) | collective-permute-done | bytes 73760 | tf_op jit(solution)/shard_map/ppermute | solution.py:616
  20.1 0.5 %collective-permute-done.9.refs_3_ = f32[144,128]{1,0:T(8,128)S(1)} collective-permute-done((f32[144,128]{1,0:T(8,128)S(1)}, f32[144,128]{1,0:T(8,128)S(1)}, u32[]{:S(2)}, u32[]{:S(2)}) %collective-permute-start.9) | collective-permute-done | bytes 73760 | tf_op jit(solution)/shard_map/ppermute | solution.py:616
  20.6 0.9 %finish.1 = (f32[9,2,2880]{2,1,0:T(2,128)}, f32[9,2880]{1,0:T(8,128)}) custom-call(f32[3,16,128]{2,1,0:T(8,128)S(1)} %get-tuple-element.27.masks_ref, f32[2,9,2880]{2,1,0:T(8,128)S(1)} %get-tuple-element.35.base_w_ref, f32[9,2880]{1,0:T(8,128)S(1)} %get-tuple-element.36.base_h_ref, f32[144,128]{1,0:T(8,128)S(1)} %get-tuple-element.34.after_ref.refs_0_, ...), custom_call_target="tpu_custom_call" | custom-call | tf_op jit(solution)/shard_map/finish/pallas_call | solution.py:662
  (21 shorter events, 0.1 us)
Async XLA Ops:
  0.6 2.2 %copy-start.3 = (f32[2,24,128]{2,1,0:T(8,128)S(1)}, f32[2,24,128]{2,1,0:T(8,128)}, u32[]{:S(2)}) copy-start(f32[2,24,128]{2,1,0:T(8,128)} %constant.9.clone.wave_ref) | copy-start | bytes 73732
  0.6 2.2 %collective-permute-start.1 = (f32[9,2,2880]{2,1,0:T(2,128)}, f32[9,2,2880]{2,1,0:T(2,128)S(1)}, u32[]{:S(2)}, u32[]{:S(2)}) collective-permute-start(f32[9,2,2880]{2,1,0:T(2,128)} %bitcast.3), channel_id=1, source_target_pairs={{0,4},{1,5},{2,6},{3,7},{4,0},{5,1},{6,2},{7,3},{8,12},{9,13},{10,... | collective-permute-start | bytes 622088 | tf_op jit(solution)/shard_map/ppermute | solution.py:606
  1.2 1.6 %collective-permute-start = (f32[9,2880]{1,0:T(8,128)}, f32[9,2880]{1,0:T(8,128)S(1)}, u32[]{:S(2)}, u32[]{:S(2)}) collective-permute-start(f32[9,2880]{1,0:T(8,128)} %h_ref.3), channel_id=1, source_target_pairs={{0,4},{1,5},{2,6},{3,7},{4,0},{5,1},{6,2},{7,3},{8,12},{9,13},{10,... | collective-permute-start | bytes 311048 | tf_op jit(solution)/shard_map/ppermute | solution.py:605
  1.2 1.6 %copy-start = (f32[2,9,2880]{2,0,1:T(2,128)S(1)}, f32[2,9,2880]{2,0,1:T(2,128)}, u32[]{:S(2)}) copy-start(f32[2,9,2880]{2,0,1:T(2,128)} %param.8) | copy-start | bytes 622084
  1.2 1.6 %copy-start.1 = (f32[8,3,16,128]{3,2,1,0:T(8,128)S(1)}, f32[8,3,16,128]{3,2,1,0:T(8,128)}, u32[]{:S(2)}) copy-start(f32[8,3,16,128]{3,2,1,0:T(8,128)} %constant.8.clone.geo_ref) | copy-start | bytes 589828
  1.2 1.6 %copy-start.2 = (f32[9,2880]{1,0:T(8,128)S(1)}, f32[9,2880]{1,0:T(8,128)}, u32[]{:S(2)}) copy-start(f32[9,2880]{1,0:T(8,128)} %h_ref.3) | copy-start | bytes 311044
  2.8 7.3 %copy-start.4 = (f32[192,96]{1,0:T(8,128)S(1)}, f32[192,96]{1,0:T(8,128)}, u32[]{:S(2)}) copy-start(f32[192,96]{1,0:T(8,128)} %constant.11.clone.inverse_ref) | copy-start | bytes 221188
  2.8 7.2 %copy-start.5 = (f32[192,96]{1,0:T(8,128)S(1)}, f32[192,96]{1,0:T(8,128)}, u32[]{:S(2)}) copy-start(f32[192,96]{1,0:T(8,128)} %constant.10.clone.n_ref) | copy-start | bytes 221188
  3.5 8.2 %collective-permute-start.4 = (f32[160,128]{1,0:T(8,128)S(1)}, f32[160,128]{1,0:T(8,128)S(1)}, u32[]{:S(2)}, u32[]{:S(2)}) collective-permute-start(f32[160,128]{1,0:T(8,128)S(1)} %get-tuple-element.31), channel_id=1, source_target_pairs={{0,3},{1,2},{2,1},{3,0},{4,7},{5,6},{6,5},{7,4},{8,11},{9,10},{10,... | collective-permute-start | bytes 245768 | tf_op jit(solution)/shard_map/ppermute | solution.py:616
  7.4 4.8 %collective-permute-start.5 = (f32[160,128]{1,0:T(8,128)S(1)}, f32[160,128]{1,0:T(8,128)S(1)}, u32[]{:S(2)}, u32[]{:S(2)}) collective-permute-start(f32[160,128]{1,0:T(8,128)S(1)} %get-tuple-element.32), channel_id=1, source_target_pairs={{0,1},{1,0},{2,3},{3,2},{4,6},{5,7},{6,4},{7,5},{8,9},{9,8},{10,11... | collective-permute-start | bytes 245768 | tf_op jit(solution)/shard_map/ppermute | solution.py:616
  7.9 4.4 %collective-permute-start.6 = (f32[160,128]{1,0:T(8,128)S(1)}, f32[160,128]{1,0:T(8,128)S(1)}, u32[]{:S(2)}, u32[]{:S(2)}) collective-permute-start(f32[160,128]{1,0:T(8,128)S(1)} %get-tuple-element.33), channel_id=1, source_target_pairs={{0,2},{1,3},{2,0},{3,1},{4,5},{5,4},{6,7},{7,6},{8,10},{9,11},{10,... | collective-permute-start | bytes 245768 | tf_op jit(solution)/shard_map/ppermute | solution.py:616
  8.0 8.2 %collective-permute-start.3 = (f32[120,128]{1,0:T(8,128)S(1)}, f32[120,128]{1,0:T(8,128)S(1)}, u32[]{:S(2)}, u32[]{:S(2)}) collective-permute-start(f32[120,128]{1,0:T(8,128)S(1)} %get-tuple-element.29), channel_id=1, source_target_pairs={{0,2},{1,3},{2,0},{3,1},{4,8},{5,9},{6,10},{7,11},{8,4},{9,5},{10,... | collective-permute-start | bytes 184328 | tf_op jit(solution)/shard_map/ppermute | solution.py:633
  9.9 0.7 %copy-start.6 = (s32[72]{0:T(128)S(1)}, s32[72]{0:T(128)}, u32[]{:S(2)}) copy-start(s32[72]{0:T(128)} %cut_ref.1) | copy-start | bytes 868
  9.9 6.3 %collective-permute-start.2 = (f32[72,128]{1,0:T(8,128)S(1)}, f32[72,128]{1,0:T(8,128)S(1)}, u32[]{:S(2)}, u32[]{:S(2)}) collective-permute-start(f32[72,128]{1,0:T(8,128)S(1)} %get-tuple-element.28), channel_id=1, source_target_pairs={{0,4},{1,5},{2,6},{3,7},{4,0},{5,1},{6,2},{7,3},{8,12},{9,13},{10,... | collective-permute-start | bytes 110600 | tf_op jit(solution)/shard_map/ppermute | solution.py:632
  13.3 3.7 %copy-start.7 = (bf16[3,9,2880]{2,0,1:T(4,128)(2,1)S(1)}, bf16[3,9,2880]{2,0,1:T(4,128)(2,1)}, u32[]{:S(2)}) copy-start(bf16[3,9,2880]{2,0,1:T(4,128)(2,1)} %param.10) | copy-start | bytes 466564
  13.3 6.4 %collective-permute-start.7 = (f32[144,128]{1,0:T(8,128)S(1)}, f32[144,128]{1,0:T(8,128)S(1)}, u32[]{:S(2)}, u32[]{:S(2)}) collective-permute-start(f32[144,128]{1,0:T(8,128)S(1)} %get-tuple-element.37), channel_id=1, source_target_pairs={{0,3},{1,2},{2,1},{3,0},{4,7},{5,6},{6,5},{7,4},{8,11},{9,10},{10,... | collective-permute-start | bytes 221192 | tf_op jit(solution)/shard_map/ppermute | solution.py:616
  15.2 4.9 %collective-permute-start.8 = (f32[144,128]{1,0:T(8,128)S(1)}, f32[144,128]{1,0:T(8,128)S(1)}, u32[]{:S(2)}, u32[]{:S(2)}) collective-permute-start(f32[144,128]{1,0:T(8,128)S(1)} %get-tuple-element.38), channel_id=1, source_target_pairs={{0,1},{1,0},{2,3},{3,2},{4,6},{5,7},{6,4},{7,5},{8,9},{9,8},{10,11... | collective-permute-start | bytes 221192 | tf_op jit(solution)/shard_map/ppermute | solution.py:616
  16.2 4.4 %collective-permute-start.9 = (f32[144,128]{1,0:T(8,128)S(1)}, f32[144,128]{1,0:T(8,128)S(1)}, u32[]{:S(2)}, u32[]{:S(2)}) collective-permute-start(f32[144,128]{1,0:T(8,128)S(1)} %pass.1), channel_id=1, source_target_pairs={{0,2},{1,3},{2,0},{3,1},{4,5},{5,4},{6,7},{7,6},{8,10},{9,11},{10,... | collective-permute-start | bytes 221192 | tf_op jit(solution)/shard_map/ppermute | solution.py:616

commit v13 on v12

--- a/solution.py
+++ b/solution.py
@@ -446,17 +446,22 @@
 
 def weights_kernel(sz, cut_ref, n_ref, inverse_ref, after_ref, weights_ref, masks_ref):
     band = lax.axis_index("lat")
+    cuts = cut_ref[...].astype(jnp.float32)
+
+    def cut_of(rows):
+        column = lax.broadcasted_iota(jnp.int32, (rows.shape[0], sz.nlat), 1)
+        return jnp.sum(jnp.where(column == band * sz.rows + rows, cuts, 0.0), axis=1, keepdims=True)
+
     row = lax.broadcasted_iota(jnp.int32, (EXT_ROWS, LANES), 0)
-    cuts = jnp.full((EXT_ROWS, LANES), sz.nlon // 2, jnp.int32)
-    for j in range(sz.rows):
-        cuts = jnp.where(row == j, cut_ref[band * sz.rows + j], cuts)
-    plain, alone = cuts >= sz.nlon // 2, sz.at_pole(row)
+    cut = cut_of(lax.broadcasted_iota(jnp.int32, (EXT_ROWS, sz.nlat), 0))
+    inside = row < sz.rows
+    plain, alone = (cut >= sz.nlon // 2) & inside, sz.at_pole(row)
     masks_ref[0] = jnp.where(plain, TIME_STEP, 0.0)
     masks_ref[1] = jnp.where(alone, TIME_STEP, 0.0)
     masks_ref[2] = jnp.where(plain | alone, 0.0, TIME_STEP)
     size = PER_TILE * sz.stack
     for i in range(sz.share):
-        width = (2 * cut_ref[band * sz.rows + share_of(sz, i)[1]] + 1).astype(jnp.float32)
+        width = 2.0 * cut_of(jnp.full((1, sz.nlat), share_of(sz, i)[1])) + 1.0
         n = n_ref[...]
         turns = n * width
         turns = turns - jnp.round(turns * (0.5 / sz.nlon)) * (2.0 * sz.nlon)
@@ -514,11 +519,10 @@
             for e in range(1, PER_TILE):
                 part = spread[stack * e : stack * (e + 1), LANES * s : LANES * (s + 1)]
                 part = pltpu.roll(part, LEVELS * e, 1)
-                inside = wide >= LEVELS * e
-                same = same + jnp.where(inside, part, 0.0)
-                over = jnp.where(inside, 0.0, part)
+                over = jnp.where(wide < LEVELS * e, part, 0.0)
+                same = same + part
                 carried = over if carried is None else carried + over
-            results[s, here] = pltpu.roll(same, stack - 1, 0) + carried
+            results[s, here] = pltpu.roll(same - carried, stack - 1, 0) + carried
     for k, out_ref in enumerate(out_refs):
         out_ref[...] = results[sz.partner(k)]
 
@@ -552,7 +556,6 @@
     sz = Sizes(rows, merged, n_lat, n_lon)
     f32 = jnp.float32
     vmem = pl.BlockSpec(memory_space=pltpu.VMEM)
-    smem = pl.BlockSpec(memory_space=pltpu.SMEM)
     hbm = pl.BlockSpec(memory_space=pltpu.HBM)
     anywhere = pl.BlockSpec(memory_space=pl.ANY)
 
@@ -634,12 +637,12 @@
     weights, masks = call(
         weights_kernel,
         "weights",
-        [smem, vmem, vmem, anywhere],
+        [vmem, vmem, vmem, anywhere],
         (
             jax.ShapeDtypeStruct((sz.share * PER_TILE * sz.stack, n_lon * sz.stack), jnp.bfloat16),
             shaped(3, EXT_ROWS, LANES),
         ),
-    )(cutoff, n, inverse, tends[0])
+    )(cutoff.reshape(1, -1), n, inverse, tends[0])
     worked = call(
         filter_kernel,
         "filter",

time: 21.7 us -> 21.7 us (level)
  Pallas kernels: 6.88 us -> 6.64 us
    pallas_call x1, Pallas kernels: 1.15 us -> 0.89 us  [local(): call(weights_kernel, 'weights', [vmem, vmem, vmem, anywhere], (jax.ShapeD...]
  transfers between devices with their start and end apart: 10 -> 10, of which waited for: 5 -> 5; matrix products, arithmetic and copies ran while one was open for 4% -> 4% of each run, Pallas kernels for 25% -> 23%
where the time goes in v13:
time: 21.7 us; the launch traced here: 21.5 us
  starting transfers between devices  10.8 us (50%)
  Pallas kernels  6.64 us (31%)
  waiting for transfers between devices  1.91 us (9%)
  local copies, waits for them, and re-layouts  1.49 us (7%)
  between operations  0.75 us (3%)
    ppermute x6, starting transfers between devices, meetings(): lax.ppermute(shares[k], ('lat', 'lon'), [(b * n_lon + i, b * n_lon + j) f...  8.07 us
    pallas_call x1, Pallas kernels, local(): call(rest_kernel, 'rest', [vmem] * 10 + [anywhere] + [vmem] * n_lon, (sha...  1.98 us
    ppermute x1, starting transfers between devices, local(): lax.ppermute(far_rows, ('lat', 'lon'), far)  1.92 us
    ppermute x6, waiting for transfers between devices, meetings(): lax.ppermute(shares[k], ('lat', 'lon'), [(b * n_lon + i, b * n_lon + j) f...  1.52 us
    unnamed x18, local copies, waits for them, and re-layouts  1.49 us
    pallas_call x1, Pallas kernels, local(): call(edges_kernel, 'edges', [hbm] * 3, (near_row, far_row, shaped(2 * EXT...  1.17 us
    pallas_call x1, Pallas kernels, local(): call(filter_kernel, 'filter', [vmem] * 2 + [vmem] * n_lon, [shaped(sz.siz...  1 us
    pallas_call x1, Pallas kernels, local(): call(finish_kernel, 'finish', [vmem] * (3 + n_lon), (shaped(*wind_rows.sh...  0.92 us
  transfers between devices with their start and end apart: 10, of which 5 were waited for; matrix products, arithmetic and copies ran while one was open for 4% of the time, Pallas kernels for 23%

profile of v13, /device:TPU:0, one launch (start us, length us, event | category | flops | bytes accessed | tf_op | source)
XLA Modules:
  0.0 21.5 jit_solution(9661789670196689452)
XLA Ops:
  0.6 0.0 copy-start.3
  0.6 0.5 %collective-permute-start.1 = (f32[9,2,2880]{2,1,0:T(2,128)}, f32[9,2,2880]{2,1,0:T(2,128)S(1)}, u32[]{:S(2)}, u32[]{:S(2)}) collective-permute-start(f32[9,2,2880]{2,1,0:T(2,128)} %bitcast.4), channel_id=1, source_target_pairs={{0,4},{1,5},{2,6},{3,7},{4,0},{5,1},{6,2},{7,3},{8,12},{9,13},{10,... | collective-permute-start | bytes 622088 | tf_op jit(solution)/shard_map/ppermute | solution.py:609
  1.2 0.1 collective-permute-start
  1.2 1.2 %edges.1 = (f32[72,128]{1,0:T(8,128)S(1)}, f32[120,128]{1,0:T(8,128)S(1)}, f32[32,128]{1,0:T(8,128)S(1)}) custom-call(f32[9,2880]{1,0:T(8,128)} %h_ref.3, f32[9,2,2880]{2,1,0:T(2,128)} %bitcast.5, bf16[9,3,2880]{2,1,0:T(4,128)(2,1)} %bitcast.9), custom_call_target="tpu_custom_call" | custom-call | tf_op jit(solution)/shard_map/edges/pallas_call | solution.py:584
  2.4 0.4 %collective-permute-done.near_h_ref = f32[9,2880]{1,0:T(8,128)S(1)} collective-permute-done((f32[9,2880]{1,0:T(8,128)}, f32[9,2880]{1,0:T(8,128)S(1)}, u32[]{:S(2)}, u32[]{:S(2)}) %collective-permute-start) | collective-permute-done | bytes 103712 | tf_op jit(solution)/shard_map/ppermute | solution.py:608
  2.9 0.7 %polar.1 = (f32[160,128]{1,0:T(8,128)S(1)}, f32[160,128]{1,0:T(8,128)S(1)}, f32[160,128]{1,0:T(8,128)S(1)}, f32[160,128]{1,0:T(8,128)S(1)}, f32[120,128]{1,0:T(8,128)S(1)}, /*index=5*/f32[72,128]{1,0:T(8,128)S(1)}) custom-call(f32[9,2880]{1,0:T(8,128)S(1)} %copy-done.2, f32[9,2,2880]{2,1,0:T(2,128)S(1)} %bitcast.6, ...), custom_call_target="tpu_custom_call" | custom-call | tf_op jit(solution)/shard_map/polar/pallas_call | solution.py:623
  3.5 3.8 %collective-permute-start.4 = (f32[160,128]{1,0:T(8,128)S(1)}, f32[160,128]{1,0:T(8,128)S(1)}, u32[]{:S(2)}, u32[]{:S(2)}) collective-permute-start(f32[160,128]{1,0:T(8,128)S(1)} %get-tuple-element.31), channel_id=1, source_target_pairs={{0,3},{1,2},{2,1},{3,0},{4,7},{5,6},{6,5},{7,4},{8,11},{9,10},{10,... | collective-permute-start | bytes 245768 | tf_op jit(solution)/shard_map/ppermute | solution.py:619
  7.4 0.5 %collective-permute-start.5 = (f32[160,128]{1,0:T(8,128)S(1)}, f32[160,128]{1,0:T(8,128)S(1)}, u32[]{:S(2)}, u32[]{:S(2)}) collective-permute-start(f32[160,128]{1,0:T(8,128)S(1)} %get-tuple-element.32), channel_id=1, source_target_pairs={{0,1},{1,0},{2,3},{3,2},{4,6},{5,7},{6,4},{7,5},{8,9},{9,8},{10,11... | collective-permute-start | bytes 245768 | tf_op jit(solution)/shard_map/ppermute | solution.py:619
  7.9 0.1 collective-permute-start.6
  8.0 1.9 %collective-permute-start.3 = (f32[120,128]{1,0:T(8,128)S(1)}, f32[120,128]{1,0:T(8,128)S(1)}, u32[]{:S(2)}, u32[]{:S(2)}) collective-permute-start(f32[120,128]{1,0:T(8,128)S(1)} %get-tuple-element.29), channel_id=1, source_target_pairs={{0,2},{1,3},{2,0},{3,1},{4,8},{5,9},{6,10},{7,11},{8,4},{9,5},{10,... | collective-permute-start | bytes 184328 | tf_op jit(solution)/shard_map/ppermute | solution.py:636
  9.9 0.2 collective-permute-start.2
  10.1 0.6 %copy-done.6 = s32[72]{0:T(128)S(1)} copy-done((s32[72]{0:T(128)S(1)}, s32[72]{0:T(128)}, u32[]{:S(2)}) %copy-start.6) | copy-done | bytes 312
  10.7 0.9 %weights.1 = (bf16[1152,96]{1,0:T(8,128)(2,1)S(1)}, f32[3,16,128]{2,1,0:T(8,128)S(1)}) custom-call(s32[1,72]{1,0:T(1,128)S(1)} %bitcast.8, f32[192,96]{1,0:T(8,128)S(1)} %copy-done.5, f32[192,96]{1,0:T(8,128)S(1)} %copy-done.4, f32[160,128]{1,0:T(8,128)S(1)} %get-tuple-element.26.after_ref.refs_0_), custom_call_target="tpu_custom_call" | custom-call | tf_op jit(solution)/shard_map/weights/pallas_call | solution.py:637
  11.6 0.5 %collective-permute-done.5.refs_2_ = f32[160,128]{1,0:T(8,128)S(1)} collective-permute-done((f32[160,128]{1,0:T(8,128)S(1)}, f32[160,128]{1,0:T(8,128)S(1)}, u32[]{:S(2)}, u32[]{:S(2)}) %collective-permute-start.5) | collective-permute-done | bytes 81952 | tf_op jit(solution)/shard_map/ppermute | solution.py:619
  12.2 0.2 collective-permute-done.6.refs_3_
  12.3 1.0 %filter.1 = (f32[144,128]{1,0:T(8,128)S(1)}, f32[144,128]{1,0:T(8,128)S(1)}, f32[144,128]{1,0:T(8,128)S(1)}, f32[144,128]{1,0:T(8,128)S(1)}) custom-call(bf16[1152,96]{1,0:T(8,128)(2,1)S(1)} %get-tuple-element.30.weights_ref, f32[8,3,16,128]{3,2,1,0:T(8,128)S(1)} %copy-done.1, f32[160,128]{1,0:T(8,128)S(1)} %get-tuple-element.26.after_ref.refs_0_, ...), custom_call_target="tpu_custom_call" | custom-call | tf_op jit(solution)/shard_map/filter/pallas_call | solution.py:646
  13.4 1.9 %collective-permute-start.7 = (f32[144,128]{1,0:T(8,128)S(1)}, f32[144,128]{1,0:T(8,128)S(1)}, u32[]{:S(2)}, u32[]{:S(2)}) collective-permute-start(f32[144,128]{1,0:T(8,128)S(1)} %get-tuple-element.37), channel_id=1, source_target_pairs={{0,3},{1,2},{2,1},{3,0},{4,7},{5,6},{6,5},{7,4},{8,11},{9,10},{10,... | collective-permute-start | bytes 221192 | tf_op jit(solution)/shard_map/ppermute | solution.py:619
  15.2 1.0 %collective-permute-start.8 = (f32[144,128]{1,0:T(8,128)S(1)}, f32[144,128]{1,0:T(8,128)S(1)}, u32[]{:S(2)}, u32[]{:S(2)}) collective-permute-start(f32[144,128]{1,0:T(8,128)S(1)} %get-tuple-element.38), channel_id=1, source_target_pairs={{0,1},{1,0},{2,3},{3,2},{4,6},{5,7},{6,4},{7,5},{8,9},{9,8},{10,11... | collective-permute-start | bytes 221192 | tf_op jit(solution)/shard_map/ppermute | solution.py:619
  16.2 0.8 %collective-permute-start.9 = (f32[144,128]{1,0:T(8,128)S(1)}, f32[144,128]{1,0:T(8,128)S(1)}, u32[]{:S(2)}, u32[]{:S(2)}) collective-permute-start(f32[144,128]{1,0:T(8,128)S(1)} %pass.1), channel_id=1, source_target_pairs={{0,2},{1,3},{2,0},{3,1},{4,5},{5,4},{6,7},{7,6},{8,10},{9,11},{10,... | collective-permute-start | bytes 221192 | tf_op jit(solution)/shard_map/ppermute | solution.py:619
  17.0 2.0 %rest.1 = (f32[2,9,2880]{2,1,0:T(8,128)S(1)}, f32[9,2880]{1,0:T(8,128)S(1)}, bf16[3,9,2880]{2,1,0:T(8,128)(2,1)S(1)}) custom-call(f32[3,16,128]{2,1,0:T(8,128)S(1)} %get-tuple-element.27.masks_ref, f32[9,2880]{1,0:T(8,128)S(1)} %copy-done.2, f32[9,2,2880]{2,1,0:T(2,128)S(1)} %bitcast.7, bf16[3,9,2880]{2,1,0:T(8,128)(2,1)S(1)} %copy.11.q_ref, ...), custom_call_target="tpu_custom_call" | custom-call | tf_op jit(solution)/shard_map/rest/pallas_call | solution.py:657
  19.0 0.8 %copy.12 = bf16[3,9,2880]{2,0,1:T(4,128)(2,1)} copy(bf16[3,9,2880]{2,1,0:T(8,128)(2,1)S(1)} %get-tuple-element.45) | data formatting | bytes 311040
  19.8 0.3 %collective-permute-done.8.refs_2_ = f32[144,128]{1,0:T(8,128)S(1)} collective-permute-done((f32[144,128]{1,0:T(8,128)S(1)}, f32[144,128]{1,0:T(8,128)S(1)}, u32[]{:S(2)}, u32[]{:S(2)}) %collective-permute-start.8) | collective-permute-done | bytes 73760 | tf_op jit(solution)/shard_map/ppermute | solution.py:619
  20.1 0.5 %collective-permute-done.9.refs_3_ = f32[144,128]{1,0:T(8,128)S(1)} collective-permute-done((f32[144,128]{1,0:T(8,128)S(1)}, f32[144,128]{1,0:T(8,128)S(1)}, u32[]{:S(2)}, u32[]{:S(2)}) %collective-permute-start.9) | collective-permute-done | bytes 73760 | tf_op jit(solution)/shard_map/ppermute | solution.py:619
  20.6 0.9 %finish.1 = (f32[9,2,2880]{2,1,0:T(2,128)}, f32[9,2880]{1,0:T(8,128)}) custom-call(f32[3,16,128]{2,1,0:T(8,128)S(1)} %get-tuple-element.27.masks_ref, f32[2,9,2880]{2,1,0:T(8,128)S(1)} %get-tuple-element.35.base_w_ref, f32[9,2880]{1,0:T(8,128)S(1)} %get-tuple-element.36.base_h_ref, f32[144,128]{1,0:T(8,128)S(1)} %get-tuple-element.34.after_ref.refs_0_, ...), custom_call_target="tpu_custom_call" | custom-call | tf_op jit(solution)/shard_map/finish/pallas_call | solution.py:665
  (21 shorter events, 0.1 us)
Async XLA Ops:
  0.6 2.2 %copy-start.3 = (f32[2,24,128]{2,1,0:T(8,128)S(1)}, f32[2,24,128]{2,1,0:T(8,128)}, u32[]{:S(2)}) copy-start(f32[2,24,128]{2,1,0:T(8,128)} %constant.9.clone.wave_ref) | copy-start | bytes 73732
  0.6 2.2 %collective-permute-start.1 = (f32[9,2,2880]{2,1,0:T(2,128)}, f32[9,2,2880]{2,1,0:T(2,128)S(1)}, u32[]{:S(2)}, u32[]{:S(2)}) collective-permute-start(f32[9,2,2880]{2,1,0:T(2,128)} %bitcast.4), channel_id=1, source_target_pairs={{0,4},{1,5},{2,6},{3,7},{4,0},{5,1},{6,2},{7,3},{8,12},{9,13},{10,... | collective-permute-start | bytes 622088 | tf_op jit(solution)/shard_map/ppermute | solution.py:609
  1.2 1.6 %collective-permute-start = (f32[9,2880]{1,0:T(8,128)}, f32[9,2880]{1,0:T(8,128)S(1)}, u32[]{:S(2)}, u32[]{:S(2)}) collective-permute-start(f32[9,2880]{1,0:T(8,128)} %h_ref.3), channel_id=1, source_target_pairs={{0,4},{1,5},{2,6},{3,7},{4,0},{5,1},{6,2},{7,3},{8,12},{9,13},{10,... | collective-permute-start | bytes 311048 | tf_op jit(solution)/shard_map/ppermute | solution.py:608
  1.2 1.6 %copy-start = (f32[2,9,2880]{2,0,1:T(2,128)S(1)}, f32[2,9,2880]{2,0,1:T(2,128)}, u32[]{:S(2)}) copy-start(f32[2,9,2880]{2,0,1:T(2,128)} %param.8) | copy-start | bytes 622084
  1.2 1.6 %copy-start.1 = (f32[8,3,16,128]{3,2,1,0:T(8,128)S(1)}, f32[8,3,16,128]{3,2,1,0:T(8,128)}, u32[]{:S(2)}) copy-start(f32[8,3,16,128]{3,2,1,0:T(8,128)} %constant.8.clone.geo_ref) | copy-start | bytes 589828
  1.2 1.6 %copy-start.2 = (f32[9,2880]{1,0:T(8,128)S(1)}, f32[9,2880]{1,0:T(8,128)}, u32[]{:S(2)}) copy-start(f32[9,2880]{1,0:T(8,128)} %h_ref.3) | copy-start | bytes 311044
  2.8 7.3 %copy-start.4 = (f32[192,96]{1,0:T(8,128)S(1)}, f32[192,96]{1,0:T(8,128)}, u32[]{:S(2)}) copy-start(f32[192,96]{1,0:T(8,128)} %constant.11.clone.inverse_ref) | copy-start | bytes 221188
  2.8 7.2 %copy-start.5 = (f32[192,96]{1,0:T(8,128)S(1)}, f32[192,96]{1,0:T(8,128)}, u32[]{:S(2)}) copy-start(f32[192,96]{1,0:T(8,128)} %constant.10.clone.n_ref) | copy-start | bytes 221188
  3.5 8.1 %collective-permute-start.4 = (f32[160,128]{1,0:T(8,128)S(1)}, f32[160,128]{1,0:T(8,128)S(1)}, u32[]{:S(2)}, u32[]{:S(2)}) collective-permute-start(f32[160,128]{1,0:T(8,128)S(1)} %get-tuple-element.31), channel_id=1, source_target_pairs={{0,3},{1,2},{2,1},{3,0},{4,7},{5,6},{6,5},{7,4},{8,11},{9,10},{10,... | collective-permute-start | bytes 245768 | tf_op jit(solution)/shard_map/ppermute | solution.py:619
  7.4 4.8 %collective-permute-start.5 = (f32[160,128]{1,0:T(8,128)S(1)}, f32[160,128]{1,0:T(8,128)S(1)}, u32[]{:S(2)}, u32[]{:S(2)}) collective-permute-start(f32[160,128]{1,0:T(8,128)S(1)} %get-tuple-element.32), channel_id=1, source_target_pairs={{0,1},{1,0},{2,3},{3,2},{4,6},{5,7},{6,4},{7,5},{8,9},{9,8},{10,11... | collective-permute-start | bytes 245768 | tf_op jit(solution)/shard_map/ppermute | solution.py:619
  7.9 4.4 %collective-permute-start.6 = (f32[160,128]{1,0:T(8,128)S(1)}, f32[160,128]{1,0:T(8,128)S(1)}, u32[]{:S(2)}, u32[]{:S(2)}) collective-permute-start(f32[160,128]{1,0:T(8,128)S(1)} %get-tuple-element.33), channel_id=1, source_target_pairs={{0,2},{1,3},{2,0},{3,1},{4,5},{5,4},{6,7},{7,6},{8,10},{9,11},{10,... | collective-permute-start | bytes 245768 | tf_op jit(solution)/shard_map/ppermute | solution.py:619
  8.0 8.2 %collective-permute-start.3 = (f32[120,128]{1,0:T(8,128)S(1)}, f32[120,128]{1,0:T(8,128)S(1)}, u32[]{:S(2)}, u32[]{:S(2)}) collective-permute-start(f32[120,128]{1,0:T(8,128)S(1)} %get-tuple-element.29), channel_id=1, source_target_pairs={{0,2},{1,3},{2,0},{3,1},{4,8},{5,9},{6,10},{7,11},{8,4},{9,5},{10,... | collective-permute-start | bytes 184328 | tf_op jit(solution)/shard_map/ppermute | solution.py:636
  9.9 6.3 %collective-permute-start.2 = (f32[72,128]{1,0:T(8,128)S(1)}, f32[72,128]{1,0:T(8,128)S(1)}, u32[]{:S(2)}, u32[]{:S(2)}) collective-permute-start(f32[72,128]{1,0:T(8,128)S(1)} %get-tuple-element.28), channel_id=1, source_target_pairs={{0,4},{1,5},{2,6},{3,7},{4,0},{5,1},{6,2},{7,3},{8,12},{9,13},{10,... | collective-permute-start | bytes 110600 | tf_op jit(solution)/shard_map/ppermute | solution.py:635
  10.1 0.7 %copy-start.6 = (s32[72]{0:T(128)S(1)}, s32[72]{0:T(128)}, u32[]{:S(2)}) copy-start(s32[72]{0:T(128)} %param.11) | copy-start | bytes 868
  13.3 3.7 %copy-start.7 = (bf16[3,9,2880]{2,0,1:T(4,128)(2,1)S(1)}, bf16[3,9,2880]{2,0,1:T(4,128)(2,1)}, u32[]{:S(2)}) copy-start(bf16[3,9,2880]{2,0,1:T(4,128)(2,1)} %param.10) | copy-start | bytes 466564
  13.4 6.4 %collective-permute-start.7 = (f32[144,128]{1,0:T(8,128)S(1)}, f32[144,128]{1,0:T(8,128)S(1)}, u32[]{:S(2)}, u32[]{:S(2)}) collective-permute-start(f32[144,128]{1,0:T(8,128)S(1)} %get-tuple-element.37), channel_id=1, source_target_pairs={{0,3},{1,2},{2,1},{3,0},{4,7},{5,6},{6,5},{7,4},{8,11},{9,10},{10,... | collective-permute-start | bytes 221192 | tf_op jit(solution)/shard_map/ppermute | solution.py:619
  15.2 4.9 %collective-permute-start.8 = (f32[144,128]{1,0:T(8,128)S(1)}, f32[144,128]{1,0:T(8,128)S(1)}, u32[]{:S(2)}, u32[]{:S(2)}) collective-permute-start(f32[144,128]{1,0:T(8,128)S(1)} %get-tuple-element.38), channel_id=1, source_target_pairs={{0,1},{1,0},{2,3},{3,2},{4,6},{5,7},{6,4},{7,5},{8,9},{9,8},{10,11... | collective-permute-start | bytes 221192 | tf_op jit(solution)/shard_map/ppermute | solution.py:619
  16.2 4.4 %collective-permute-start.9 = (f32[144,128]{1,0:T(8,128)S(1)}, f32[144,128]{1,0:T(8,128)S(1)}, u32[]{:S(2)}, u32[]{:S(2)}) collective-permute-start(f32[144,128]{1,0:T(8,128)S(1)} %pass.1), channel_id=1, source_target_pairs={{0,2},{1,3},{2,0},{3,1},{4,5},{5,4},{6,7},{7,6},{8,10},{9,11},{10,... | collective-permute-start | bytes 221192 | tf_op jit(solution)/shard_map/ppermute | solution.py:619

commit v14 on v12

--- a/solution.py
+++ b/solution.py
@@ -505,8 +505,9 @@
     rows = PER_TILE * stack
     for i in range(share):
         here = slice(stack * i, stack * (i + 1))
-        pieces = [gathered[s, here].astype(jnp.bfloat16) for s in range(n_lon)]
+        pieces = [gathered[s, here] for s in range(n_lon)]
         circle = jnp.concatenate([jnp.concatenate(pieces[s:] + pieces[:s], axis=0) for s in range(n_lon)], axis=1)
+        circle = circle.astype(jnp.bfloat16)
         spread = jnp.dot(weights_ref[rows * i : rows * (i + 1)], circle, preferred_element_type=jnp.float32)
         for s in range(n_lon):
             same = spread[:stack, LANES * s : LANES * (s + 1)]
@@ -524,21 +525,24 @@
 
 
 def finish_kernel(sz, masks_ref, base_w_ref, base_h_ref, *refs):
-    back_refs, (new_w_ref, new_h_ref, back_ref) = refs[: sz.n_lon], refs[sz.n_lon :]
-    rows, work = sz.rows, sz.work
+    back_refs, (new_w_ref, new_h_ref, back_ref, placed) = refs[: sz.n_lon], refs[sz.n_lon :]
+    rows, stack = sz.rows, sz.stack
     for k, ref in enumerate(back_refs):
         back_ref[sz.piece(k), :] = ref[...]
-    scale = masks_ref[2]
-    even = lax.rem(lax.axis_index("lat"), 2) == 0
+    size = sz.work * stack
+    for f in range(3):
+        start = rows * stack * f
+        if sz.near_only:
+            for row in (0, rows - 1):
+                placed[start + stack * row : start + stack * (row + 1)] = jnp.zeros((stack, LANES), jnp.float32)
+        to = pl.multiple_of(start + sz.first() * stack, 8)
+        placed[pl.ds(to, size), :] = back_ref[size * f : size * (f + 1)]
+    scale = masks_ref[2][:rows]
     for f in range(3):
         for t in range(sz.tiles):
             span = sz.span(t)
             lanes = slice(LANES * t, LANES * t + span)
-            tend = back_ref[pl.ds(sz.stack * work * f + t, work, stride=sz.stack), :]
-            if sz.near_only:
-                tend = jnp.concatenate([tend, jnp.zeros((EXT_ROWS - work, LANES), jnp.float32)], axis=0)
-                tend = jnp.where(even, south(tend), tend)
-            change = (scale[:rows] * tend[:rows])[:, :span]
+            change = (scale * placed[pl.ds(rows * stack * f + t, rows, stride=stack), :])[:, :span]
             if f == 0:
                 new_h_ref[:, lanes] = base_h_ref[:, lanes] + change
             else:
@@ -664,7 +668,7 @@
         "finish",
         [vmem] * (3 + n_lon),
         (shaped(*wind_rows.shape), shaped(rows, merged)),
-        [pltpu.VMEM((n_lon * sz.size, LANES), f32)],
+        [pltpu.VMEM((n_lon * sz.size, LANES), f32), pltpu.VMEM((3 * rows * sz.stack, LANES), f32)],
     )(masks, base_w, base_h, *back)
     return jnp.swapaxes(new_w, 0, 1), new_h, mass
 

time: 21.7 us -> 21.7 us (level)
  no operation moved by 1% of the time
where the time goes in v14:
time: 21.7 us; the launch traced here: 21.5 us
  starting transfers between devices  10.8 us (50%)
  Pallas kernels  6.89 us (32%)
  waiting for transfers between devices  1.82 us (8%)
  local copies, waits for them, and re-layouts  1.32 us (6%)
  between operations  0.75 us (3%)
    ppermute x6, starting transfers between devices, meetings(): lax.ppermute(shares[k], ('lat', 'lon'), [(b * n_lon + i, b * n_lon + j) f...  8.07 us
    pallas_call x1, Pallas kernels, local(): call(rest_kernel, 'rest', [vmem] * 10 + [anywhere] + [vmem] * n_lon, (sha...  1.98 us
    ppermute x1, starting transfers between devices, local(): lax.ppermute(far_rows, ('lat', 'lon'), far)  1.92 us
    ppermute x6, waiting for transfers between devices, meetings(): lax.ppermute(shares[k], ('lat', 'lon'), [(b * n_lon + i, b * n_lon + j) f...  1.43 us
    unnamed x18, local copies, waits for them, and re-layouts  1.32 us
    pallas_call x1, Pallas kernels, local(): call(edges_kernel, 'edges', [hbm] * 3, (near_row, far_row, shaped(2 * EXT...  1.17 us
    pallas_call x1, Pallas kernels, local(): call(weights_kernel, 'weights', [smem, vmem, vmem, anywhere], (jax.ShapeD...  1.15 us
    pallas_call x1, Pallas kernels, local(): call(filter_kernel, 'filter', [vmem] * 2 + [vmem] * n_lon, [shaped(sz.siz...  0.98 us
  transfers between devices with their start and end apart: 10, of which 5 were waited for; matrix products, arithmetic and copies ran while one was open for 4% of the time, Pallas kernels for 25%

profile of v14, /device:TPU:0, one launch (start us, length us, event | category | flops | bytes accessed | tf_op | source)
XLA Modules:
  0.0 21.5 jit_solution(12767018465856730054)
XLA Ops:
  0.6 0.5 %collective-permute-start.1 = (f32[9,2,2880]{2,1,0:T(2,128)}, f32[9,2,2880]{2,1,0:T(2,128)S(1)}, u32[]{:S(2)}, u32[]{:S(2)}) collective-permute-start(f32[9,2,2880]{2,1,0:T(2,128)} %bitcast.3), channel_id=1, source_target_pairs={{0,4},{1,5},{2,6},{3,7},{4,0},{5,1},{6,2},{7,3},{8,12},{9,13},{10,... | collective-permute-start | bytes 622088 | tf_op jit(solution)/shard_map/ppermute | solution.py:610
  1.2 0.1 collective-permute-start
  1.2 1.2 %edges.1 = (f32[72,128]{1,0:T(8,128)S(1)}, f32[120,128]{1,0:T(8,128)S(1)}, f32[32,128]{1,0:T(8,128)S(1)}) custom-call(f32[9,2880]{1,0:T(8,128)} %h_ref.3, f32[9,2,2880]{2,1,0:T(2,128)} %bitcast.4, bf16[9,3,2880]{2,1,0:T(4,128)(2,1)} %bitcast.7), custom_call_target="tpu_custom_call" | custom-call | tf_op jit(solution)/shard_map/edges/pallas_call | solution.py:585
  2.4 0.4 %collective-permute-done.near_h_ref = f32[9,2880]{1,0:T(8,128)S(1)} collective-permute-done((f32[9,2880]{1,0:T(8,128)}, f32[9,2880]{1,0:T(8,128)S(1)}, u32[]{:S(2)}, u32[]{:S(2)}) %collective-permute-start) | collective-permute-done | bytes 103712 | tf_op jit(solution)/shard_map/ppermute | solution.py:609
  2.8 0.0 copy-start.4
  2.9 0.7 %polar.1 = (f32[160,128]{1,0:T(8,128)S(1)}, f32[160,128]{1,0:T(8,128)S(1)}, f32[160,128]{1,0:T(8,128)S(1)}, f32[160,128]{1,0:T(8,128)S(1)}, f32[120,128]{1,0:T(8,128)S(1)}, /*index=5*/f32[72,128]{1,0:T(8,128)S(1)}) custom-call(f32[9,2880]{1,0:T(8,128)S(1)} %copy-done.2, f32[9,2,2880]{2,1,0:T(2,128)S(1)} %bitcast.5, ...), custom_call_target="tpu_custom_call" | custom-call | tf_op jit(solution)/shard_map/polar/pallas_call | solution.py:624
  3.5 3.8 %collective-permute-start.4 = (f32[160,128]{1,0:T(8,128)S(1)}, f32[160,128]{1,0:T(8,128)S(1)}, u32[]{:S(2)}, u32[]{:S(2)}) collective-permute-start(f32[160,128]{1,0:T(8,128)S(1)} %get-tuple-element.31), channel_id=1, source_target_pairs={{0,3},{1,2},{2,1},{3,0},{4,7},{5,6},{6,5},{7,4},{8,11},{9,10},{10,... | collective-permute-start | bytes 245768 | tf_op jit(solution)/shard_map/ppermute | solution.py:620
  7.4 0.5 %collective-permute-start.5 = (f32[160,128]{1,0:T(8,128)S(1)}, f32[160,128]{1,0:T(8,128)S(1)}, u32[]{:S(2)}, u32[]{:S(2)}) collective-permute-start(f32[160,128]{1,0:T(8,128)S(1)} %get-tuple-element.32), channel_id=1, source_target_pairs={{0,1},{1,0},{2,3},{3,2},{4,6},{5,7},{6,4},{7,5},{8,9},{9,8},{10,11... | collective-permute-start | bytes 245768 | tf_op jit(solution)/shard_map/ppermute | solution.py:620
  7.9 0.1 collective-permute-start.6
  8.0 1.9 %collective-permute-start.3 = (f32[120,128]{1,0:T(8,128)S(1)}, f32[120,128]{1,0:T(8,128)S(1)}, u32[]{:S(2)}, u32[]{:S(2)}) collective-permute-start(f32[120,128]{1,0:T(8,128)S(1)} %get-tuple-element.29), channel_id=1, source_target_pairs={{0,2},{1,3},{2,0},{3,1},{4,8},{5,9},{6,10},{7,11},{8,4},{9,5},{10,... | collective-permute-start | bytes 184328 | tf_op jit(solution)/shard_map/ppermute | solution.py:637
  9.9 0.2 collective-permute-start.2
  10.1 0.5 %copy-done.6 = s32[72]{0:T(128)S(1)} copy-done((s32[72]{0:T(128)S(1)}, s32[72]{0:T(128)}, u32[]{:S(2)}) %copy-start.6) | copy-done | bytes 312
  10.6 1.1 %weights.1 = (bf16[1152,96]{1,0:T(8,128)(2,1)S(1)}, f32[3,16,128]{2,1,0:T(8,128)S(1)}) custom-call(s32[72]{0:T(128)S(1)} %copy-done.6, f32[192,96]{1,0:T(8,128)S(1)} %copy-done.5, f32[192,96]{1,0:T(8,128)S(1)} %copy-done.4, f32[160,128]{1,0:T(8,128)S(1)} %get-tuple-element.26.after_ref.refs_0_), custom_call_target="tpu_custom_call" | custom-call | tf_op jit(solution)/shard_map/weights/pallas_call | solution.py:638
  11.7 0.4 %collective-permute-done.5.refs_2_ = f32[160,128]{1,0:T(8,128)S(1)} collective-permute-done((f32[160,128]{1,0:T(8,128)S(1)}, f32[160,128]{1,0:T(8,128)S(1)}, u32[]{:S(2)}, u32[]{:S(2)}) %collective-permute-start.5) | collective-permute-done | bytes 81952 | tf_op jit(solution)/shard_map/ppermute | solution.py:620
  12.2 0.2 collective-permute-done.6.refs_3_
  12.3 1.0 %filter.1 = (f32[144,128]{1,0:T(8,128)S(1)}, f32[144,128]{1,0:T(8,128)S(1)}, f32[144,128]{1,0:T(8,128)S(1)}, f32[144,128]{1,0:T(8,128)S(1)}) custom-call(bf16[1152,96]{1,0:T(8,128)(2,1)S(1)} %get-tuple-element.30.weights_ref, f32[8,3,16,128]{3,2,1,0:T(8,128)S(1)} %copy-done.1, f32[160,128]{1,0:T(8,128)S(1)} %get-tuple-element.26.after_ref.refs_0_, ...), custom_call_target="tpu_custom_call" | custom-call | tf_op jit(solution)/shard_map/filter/pallas_call | solution.py:647
  13.3 1.8 %collective-permute-start.7 = (f32[144,128]{1,0:T(8,128)S(1)}, f32[144,128]{1,0:T(8,128)S(1)}, u32[]{:S(2)}, u32[]{:S(2)}) collective-permute-start(f32[144,128]{1,0:T(8,128)S(1)} %get-tuple-element.37), channel_id=1, source_target_pairs={{0,3},{1,2},{2,1},{3,0},{4,7},{5,6},{6,5},{7,4},{8,11},{9,10},{10,... | collective-permute-start | bytes 221192 | tf_op jit(solution)/shard_map/ppermute | solution.py:620
  15.2 1.0 %collective-permute-start.8 = (f32[144,128]{1,0:T(8,128)S(1)}, f32[144,128]{1,0:T(8,128)S(1)}, u32[]{:S(2)}, u32[]{:S(2)}) collective-permute-start(f32[144,128]{1,0:T(8,128)S(1)} %get-tuple-element.38), channel_id=1, source_target_pairs={{0,1},{1,0},{2,3},{3,2},{4,6},{5,7},{6,4},{7,5},{8,9},{9,8},{10,11... | collective-permute-start | bytes 221192 | tf_op jit(solution)/shard_map/ppermute | solution.py:620
  16.2 0.8 %collective-permute-start.9 = (f32[144,128]{1,0:T(8,128)S(1)}, f32[144,128]{1,0:T(8,128)S(1)}, u32[]{:S(2)}, u32[]{:S(2)}) collective-permute-start(f32[144,128]{1,0:T(8,128)S(1)} %pass.1), channel_id=1, source_target_pairs={{0,2},{1,3},{2,0},{3,1},{4,5},{5,4},{6,7},{7,6},{8,10},{9,11},{10,... | collective-permute-start | bytes 221192 | tf_op jit(solution)/shard_map/ppermute | solution.py:620
  17.0 2.0 %rest.1 = (f32[2,9,2880]{2,1,0:T(8,128)S(1)}, f32[9,2880]{1,0:T(8,128)S(1)}, bf16[3,9,2880]{2,1,0:T(8,128)(2,1)S(1)}) custom-call(f32[3,16,128]{2,1,0:T(8,128)S(1)} %get-tuple-element.27.masks_ref, f32[9,2880]{1,0:T(8,128)S(1)} %copy-done.2, f32[9,2,2880]{2,1,0:T(2,128)S(1)} %bitcast.6, bf16[3,9,2880]{2,1,0:T(8,128)(2,1)S(1)} %copy.11.q_ref, ...), custom_call_target="tpu_custom_call" | custom-call | tf_op jit(solution)/shard_map/rest/pallas_call | solution.py:658
  19.0 0.8 %copy.12 = bf16[3,9,2880]{2,0,1:T(4,128)(2,1)} copy(bf16[3,9,2880]{2,1,0:T(8,128)(2,1)S(1)} %get-tuple-element.45) | data formatting | bytes 311040
  19.8 0.3 %collective-permute-done.8.refs_2_ = f32[144,128]{1,0:T(8,128)S(1)} collective-permute-done((f32[144,128]{1,0:T(8,128)S(1)}, f32[144,128]{1,0:T(8,128)S(1)}, u32[]{:S(2)}, u32[]{:S(2)}) %collective-permute-start.8) | collective-permute-done | bytes 73760 | tf_op jit(solution)/shard_map/ppermute | solution.py:620
  20.1 0.5 %collective-permute-done.9.refs_3_ = f32[144,128]{1,0:T(8,128)S(1)} collective-permute-done((f32[144,128]{1,0:T(8,128)S(1)}, f32[144,128]{1,0:T(8,128)S(1)}, u32[]{:S(2)}, u32[]{:S(2)}) %collective-permute-start.9) | collective-permute-done | bytes 73760 | tf_op jit(solution)/shard_map/ppermute | solution.py:620
  20.6 0.9 %finish.1 = (f32[9,2,2880]{2,1,0:T(2,128)}, f32[9,2880]{1,0:T(8,128)}) custom-call(f32[3,16,128]{2,1,0:T(8,128)S(1)} %get-tuple-element.27.masks_ref, f32[2,9,2880]{2,1,0:T(8,128)S(1)} %get-tuple-element.35.base_w_ref, f32[9,2880]{1,0:T(8,128)S(1)} %get-tuple-element.36.base_h_ref, f32[144,128]{1,0:T(8,128)S(1)} %get-tuple-element.34.after_ref.refs_0_, ...), custom_call_target="tpu_custom_call" | custom-call | tf_op jit(solution)/shard_map/finish/pallas_call | solution.py:666
  (21 shorter events, 0.1 us)
Async XLA Ops:
  0.6 2.2 %copy-start.3 = (f32[2,24,128]{2,1,0:T(8,128)S(1)}, f32[2,24,128]{2,1,0:T(8,128)}, u32[]{:S(2)}) copy-start(f32[2,24,128]{2,1,0:T(8,128)} %constant.9.clone.wave_ref) | copy-start | bytes 73732
  0.6 2.2 %collective-permute-start.1 = (f32[9,2,2880]{2,1,0:T(2,128)}, f32[9,2,2880]{2,1,0:T(2,128)S(1)}, u32[]{:S(2)}, u32[]{:S(2)}) collective-permute-start(f32[9,2,2880]{2,1,0:T(2,128)} %bitcast.3), channel_id=1, source_target_pairs={{0,4},{1,5},{2,6},{3,7},{4,0},{5,1},{6,2},{7,3},{8,12},{9,13},{10,... | collective-permute-start | bytes 622088 | tf_op jit(solution)/shard_map/ppermute | solution.py:610
  1.2 1.6 %collective-permute-start = (f32[9,2880]{1,0:T(8,128)}, f32[9,2880]{1,0:T(8,128)S(1)}, u32[]{:S(2)}, u32[]{:S(2)}) collective-permute-start(f32[9,2880]{1,0:T(8,128)} %h_ref.3), channel_id=1, source_target_pairs={{0,4},{1,5},{2,6},{3,7},{4,0},{5,1},{6,2},{7,3},{8,12},{9,13},{10,... | collective-permute-start | bytes 311048 | tf_op jit(solution)/shard_map/ppermute | solution.py:609
  1.2 1.6 %copy-start = (f32[2,9,2880]{2,0,1:T(2,128)S(1)}, f32[2,9,2880]{2,0,1:T(2,128)}, u32[]{:S(2)}) copy-start(f32[2,9,2880]{2,0,1:T(2,128)} %param.8) | copy-start | bytes 622084
  1.2 1.6 %copy-start.1 = (f32[8,3,16,128]{3,2,1,0:T(8,128)S(1)}, f32[8,3,16,128]{3,2,1,0:T(8,128)}, u32[]{:S(2)}) copy-start(f32[8,3,16,128]{3,2,1,0:T(8,128)} %constant.8.clone.geo_ref) | copy-start | bytes 589828
  1.2 1.6 %copy-start.2 = (f32[9,2880]{1,0:T(8,128)S(1)}, f32[9,2880]{1,0:T(8,128)}, u32[]{:S(2)}) copy-start(f32[9,2880]{1,0:T(8,128)} %h_ref.3) | copy-start | bytes 311044
  2.8 7.3 %copy-start.4 = (f32[192,96]{1,0:T(8,128)S(1)}, f32[192,96]{1,0:T(8,128)}, u32[]{:S(2)}) copy-start(f32[192,96]{1,0:T(8,128)} %constant.11.clone.inverse_ref) | copy-start | bytes 221188
  2.8 7.2 %copy-start.5 = (f32[192,96]{1,0:T(8,128)S(1)}, f32[192,96]{1,0:T(8,128)}, u32[]{:S(2)}) copy-start(f32[192,96]{1,0:T(8,128)} %constant.10.clone.n_ref) | copy-start | bytes 221188
  3.5 8.2 %collective-permute-start.4 = (f32[160,128]{1,0:T(8,128)S(1)}, f32[160,128]{1,0:T(8,128)S(1)}, u32[]{:S(2)}, u32[]{:S(2)}) collective-permute-start(f32[160,128]{1,0:T(8,128)S(1)} %get-tuple-element.31), channel_id=1, source_target_pairs={{0,3},{1,2},{2,1},{3,0},{4,7},{5,6},{6,5},{7,4},{8,11},{9,10},{10,... | collective-permute-start | bytes 245768 | tf_op jit(solution)/shard_map/ppermute | solution.py:620
  7.4 4.8 %collective-permute-start.5 = (f32[160,128]{1,0:T(8,128)S(1)}, f32[160,128]{1,0:T(8,128)S(1)}, u32[]{:S(2)}, u32[]{:S(2)}) collective-permute-start(f32[160,128]{1,0:T(8,128)S(1)} %get-tuple-element.32), channel_id=1, source_target_pairs={{0,1},{1,0},{2,3},{3,2},{4,6},{5,7},{6,4},{7,5},{8,9},{9,8},{10,11... | collective-permute-start | bytes 245768 | tf_op jit(solution)/shard_map/ppermute | solution.py:620
  7.9 4.4 %collective-permute-start.6 = (f32[160,128]{1,0:T(8,128)S(1)}, f32[160,128]{1,0:T(8,128)S(1)}, u32[]{:S(2)}, u32[]{:S(2)}) collective-permute-start(f32[160,128]{1,0:T(8,128)S(1)} %get-tuple-element.33), channel_id=1, source_target_pairs={{0,2},{1,3},{2,0},{3,1},{4,5},{5,4},{6,7},{7,6},{8,10},{9,11},{10,... | collective-permute-start | bytes 245768 | tf_op jit(solution)/shard_map/ppermute | solution.py:620
  8.0 8.2 %collective-permute-start.3 = (f32[120,128]{1,0:T(8,128)S(1)}, f32[120,128]{1,0:T(8,128)S(1)}, u32[]{:S(2)}, u32[]{:S(2)}) collective-permute-start(f32[120,128]{1,0:T(8,128)S(1)} %get-tuple-element.29), channel_id=1, source_target_pairs={{0,2},{1,3},{2,0},{3,1},{4,8},{5,9},{6,10},{7,11},{8,4},{9,5},{10,... | collective-permute-start | bytes 184328 | tf_op jit(solution)/shard_map/ppermute | solution.py:637
  9.9 0.7 %copy-start.6 = (s32[72]{0:T(128)S(1)}, s32[72]{0:T(128)}, u32[]{:S(2)}) copy-start(s32[72]{0:T(128)} %cut_ref.1) | copy-start | bytes 868
  9.9 6.3 %collective-permute-start.2 = (f32[72,128]{1,0:T(8,128)S(1)}, f32[72,128]{1,0:T(8,128)S(1)}, u32[]{:S(2)}, u32[]{:S(2)}) collective-permute-start(f32[72,128]{1,0:T(8,128)S(1)} %get-tuple-element.28), channel_id=1, source_target_pairs={{0,4},{1,5},{2,6},{3,7},{4,0},{5,1},{6,2},{7,3},{8,12},{9,13},{10,... | collective-permute-start | bytes 110600 | tf_op jit(solution)/shard_map/ppermute | solution.py:636
  13.3 3.7 %copy-start.7 = (bf16[3,9,2880]{2,0,1:T(4,128)(2,1)S(1)}, bf16[3,9,2880]{2,0,1:T(4,128)(2,1)}, u32[]{:S(2)}) copy-start(bf16[3,9,2880]{2,0,1:T(4,128)(2,1)} %param.10) | copy-start | bytes 466564
  13.3 6.4 %collective-permute-start.7 = (f32[144,128]{1,0:T(8,128)S(1)}, f32[144,128]{1,0:T(8,128)S(1)}, u32[]{:S(2)}, u32[]{:S(2)}) collective-permute-start(f32[144,128]{1,0:T(8,128)S(1)} %get-tuple-element.37), channel_id=1, source_target_pairs={{0,3},{1,2},{2,1},{3,0},{4,7},{5,6},{6,5},{7,4},{8,11},{9,10},{10,... | collective-permute-start | bytes 221192 | tf_op jit(solution)/shard_map/ppermute | solution.py:620
  15.2 4.9 %collective-permute-start.8 = (f32[144,128]{1,0:T(8,128)S(1)}, f32[144,128]{1,0:T(8,128)S(1)}, u32[]{:S(2)}, u32[]{:S(2)}) collective-permute-start(f32[144,128]{1,0:T(8,128)S(1)} %get-tuple-element.38), channel_id=1, source_target_pairs={{0,1},{1,0},{2,3},{3,2},{4,6},{5,7},{6,4},{7,5},{8,9},{9,8},{10,11... | collective-permute-start | bytes 221192 | tf_op jit(solution)/shard_map/ppermute | solution.py:620
  16.2 4.4 %collective-permute-start.9 = (f32[144,128]{1,0:T(8,128)S(1)}, f32[144,128]{1,0:T(8,128)S(1)}, u32[]{:S(2)}, u32[]{:S(2)}) collective-permute-start(f32[144,128]{1,0:T(8,128)S(1)} %pass.1), channel_id=1, source_target_pairs={{0,2},{1,3},{2,0},{3,1},{4,5},{5,4},{6,7},{7,6},{8,10},{9,11},{10,... | collective-permute-start | bytes 221192 | tf_op jit(solution)/shard_map/ppermute | solution.py:620

commit v15 on v12

--- a/solution.py
+++ b/solution.py
@@ -53,8 +53,8 @@
         return row == (pole if self.near_only else -1)
 
     def turns(self, odd):
-        middle = list(range(1, self.n_lon - 1))
-        return [0, self.n_lon - 1] + (middle[::-1] if odd else middle)
+        middle, last = list(range(1, self.n_lon - 1)), self.n_lon - 1
+        return [0, middle[-1], last] + middle[-2::-1] if odd else [0, last] + middle
 
     def partner(self, k):
         odd = lax.rem(lax.axis_index("lat"), 2) == 1

time: 21.7 us -> 21.2 us (0.977)
  waiting for transfers between devices: 1.82 us -> 1.32 us
    ppermute x6, waiting for transfers between devices: 1.43 us -> 0.93 us  [meetings(): lax.ppermute(shares[k], ('lat', 'lon'), [(b * n_lon + i, b * n_lon + j) f...]
where the time goes in v15:
time: 21.2 us; the launch traced here: 21 us
  starting transfers between devices  10.8 us (51%)
  Pallas kernels  6.89 us (32%)
  local copies, waits for them, and re-layouts  1.32 us (6%)
  waiting for transfers between devices  1.32 us (6%)
  between operations  0.75 us (4%)
    ppermute x6, starting transfers between devices, meetings(): lax.ppermute(shares[k], ('lat', 'lon'), [(b * n_lon + i, b * n_lon + j) f...  8.07 us
    pallas_call x1, Pallas kernels, local(): call(rest_kernel, 'rest', [vmem] * 10 + [anywhere] + [vmem] * n_lon, (sha...  1.99 us
    ppermute x1, starting transfers between devices, local(): lax.ppermute(far_rows, ('lat', 'lon'), far)  1.92 us
    unnamed x18, local copies, waits for them, and re-layouts  1.32 us
    pallas_call x1, Pallas kernels, local(): call(edges_kernel, 'edges', [hbm] * 3, (near_row, far_row, shaped(2 * EXT...  1.17 us
    pallas_call x1, Pallas kernels, local(): call(weights_kernel, 'weights', [smem, vmem, vmem, anywhere], (jax.ShapeD...  1.15 us
    pallas_call x1, Pallas kernels, local(): call(filter_kernel, 'filter', [vmem] * 2 + [vmem] * n_lon, [shaped(sz.siz...  0.98 us
    ppermute x6, waiting for transfers between devices, meetings(): lax.ppermute(shares[k], ('lat', 'lon'), [(b * n_lon + i, b * n_lon + j) f...  0.93 us
  transfers between devices with their start and end apart: 10, of which 5 were waited for; matrix products, arithmetic and copies ran while one was open for 4% of the time, Pallas kernels for 25%

profile of v15, /device:TPU:0, one launch (start us, length us, event | category | flops | bytes accessed | tf_op | source)
XLA Modules:
  0.0 21.0 jit_solution(11924366587783624923)
XLA Ops:
  0.6 0.0 copy-start.3
  0.6 0.5 %collective-permute-start.1 = (f32[9,2,2880]{2,1,0:T(2,128)}, f32[9,2,2880]{2,1,0:T(2,128)S(1)}, u32[]{:S(2)}, u32[]{:S(2)}) collective-permute-start(f32[9,2,2880]{2,1,0:T(2,128)} %bitcast.3), channel_id=1, source_target_pairs={{0,4},{1,5},{2,6},{3,7},{4,0},{5,1},{6,2},{7,3},{8,12},{9,13},{10,... | collective-permute-start | bytes 622088 | tf_op jit(solution)/shard_map/ppermute | solution.py:606
  1.2 0.1 collective-permute-start
  1.2 1.2 %edges.1 = (f32[72,128]{1,0:T(8,128)S(1)}, f32[120,128]{1,0:T(8,128)S(1)}, f32[32,128]{1,0:T(8,128)S(1)}) custom-call(f32[9,2880]{1,0:T(8,128)} %h_ref.3, f32[9,2,2880]{2,1,0:T(2,128)} %bitcast.4, bf16[9,3,2880]{2,1,0:T(4,128)(2,1)} %bitcast.7), custom_call_target="tpu_custom_call" | custom-call | tf_op jit(solution)/shard_map/edges/pallas_call | solution.py:581
  2.4 0.4 %collective-permute-done.near_h_ref = f32[9,2880]{1,0:T(8,128)S(1)} collective-permute-done((f32[9,2880]{1,0:T(8,128)}, f32[9,2880]{1,0:T(8,128)S(1)}, u32[]{:S(2)}, u32[]{:S(2)}) %collective-permute-start) | collective-permute-done | bytes 103712 | tf_op jit(solution)/shard_map/ppermute | solution.py:605
  2.9 0.7 %polar.1 = (f32[160,128]{1,0:T(8,128)S(1)}, f32[160,128]{1,0:T(8,128)S(1)}, f32[160,128]{1,0:T(8,128)S(1)}, f32[160,128]{1,0:T(8,128)S(1)}, f32[120,128]{1,0:T(8,128)S(1)}, /*index=5*/f32[72,128]{1,0:T(8,128)S(1)}) custom-call(f32[9,2880]{1,0:T(8,128)S(1)} %copy-done.2, f32[9,2,2880]{2,1,0:T(2,128)S(1)} %bitcast.5, ...), custom_call_target="tpu_custom_call" | custom-call | tf_op jit(solution)/shard_map/polar/pallas_call | solution.py:620
  3.5 3.8 %collective-permute-start.4 = (f32[160,128]{1,0:T(8,128)S(1)}, f32[160,128]{1,0:T(8,128)S(1)}, u32[]{:S(2)}, u32[]{:S(2)}) collective-permute-start(f32[160,128]{1,0:T(8,128)S(1)} %get-tuple-element.31), channel_id=1, source_target_pairs={{0,3},{1,2},{2,1},{3,0},{4,6},{5,7},{6,4},{7,5},{8,11},{9,10},{10,... | collective-permute-start | bytes 245768 | tf_op jit(solution)/shard_map/ppermute | solution.py:616
  7.4 0.5 %collective-permute-start.5 = (f32[160,128]{1,0:T(8,128)S(1)}, f32[160,128]{1,0:T(8,128)S(1)}, u32[]{:S(2)}, u32[]{:S(2)}) collective-permute-start(f32[160,128]{1,0:T(8,128)S(1)} %get-tuple-element.32), channel_id=1, source_target_pairs={{0,1},{1,0},{2,3},{3,2},{4,7},{5,6},{6,5},{7,4},{8,9},{9,8},{10,11... | collective-permute-start | bytes 245768 | tf_op jit(solution)/shard_map/ppermute | solution.py:616
  7.9 0.1 collective-permute-start.6
  8.0 1.9 %collective-permute-start.3 = (f32[120,128]{1,0:T(8,128)S(1)}, f32[120,128]{1,0:T(8,128)S(1)}, u32[]{:S(2)}, u32[]{:S(2)}) collective-permute-start(f32[120,128]{1,0:T(8,128)S(1)} %get-tuple-element.29), channel_id=1, source_target_pairs={{0,2},{1,3},{2,0},{3,1},{4,8},{5,9},{6,10},{7,11},{8,4},{9,5},{10,... | collective-permute-start | bytes 184328 | tf_op jit(solution)/shard_map/ppermute | solution.py:633
  9.9 0.2 collective-permute-start.2
  10.1 0.5 %copy-done.6 = s32[72]{0:T(128)S(1)} copy-done((s32[72]{0:T(128)S(1)}, s32[72]{0:T(128)}, u32[]{:S(2)}) %copy-start.6) | copy-done | bytes 312
  10.6 1.1 %weights.1 = (bf16[1152,96]{1,0:T(8,128)(2,1)S(1)}, f32[3,16,128]{2,1,0:T(8,128)S(1)}) custom-call(s32[72]{0:T(128)S(1)} %copy-done.6, f32[192,96]{1,0:T(8,128)S(1)} %copy-done.5, f32[192,96]{1,0:T(8,128)S(1)} %copy-done.4, f32[160,128]{1,0:T(8,128)S(1)} %get-tuple-element.26.after_ref.refs_0_), custom_call_target="tpu_custom_call" | custom-call | tf_op jit(solution)/shard_map/weights/pallas_call | solution.py:634
  11.7 0.5 %collective-permute-done.5.refs_2_ = f32[160,128]{1,0:T(8,128)S(1)} collective-permute-done((f32[160,128]{1,0:T(8,128)S(1)}, f32[160,128]{1,0:T(8,128)S(1)}, u32[]{:S(2)}, u32[]{:S(2)}) %collective-permute-start.5) | collective-permute-done | bytes 81952 | tf_op jit(solution)/shard_map/ppermute | solution.py:616
  12.3 0.1 collective-permute-done.6.refs_3_
  12.3 1.0 %filter.1 = (f32[144,128]{1,0:T(8,128)S(1)}, f32[144,128]{1,0:T(8,128)S(1)}, f32[144,128]{1,0:T(8,128)S(1)}, f32[144,128]{1,0:T(8,128)S(1)}) custom-call(bf16[1152,96]{1,0:T(8,128)(2,1)S(1)} %get-tuple-element.30.weights_ref, f32[8,3,16,128]{3,2,1,0:T(8,128)S(1)} %copy-done.1, f32[160,128]{1,0:T(8,128)S(1)} %get-tuple-element.26.after_ref.refs_0_, ...), custom_call_target="tpu_custom_call" | custom-call | tf_op jit(solution)/shard_map/filter/pallas_call | solution.py:643
  13.3 1.8 %collective-permute-start.7 = (f32[144,128]{1,0:T(8,128)S(1)}, f32[144,128]{1,0:T(8,128)S(1)}, u32[]{:S(2)}, u32[]{:S(2)}) collective-permute-start(f32[144,128]{1,0:T(8,128)S(1)} %get-tuple-element.37), channel_id=1, source_target_pairs={{0,3},{1,2},{2,1},{3,0},{4,6},{5,7},{6,4},{7,5},{8,11},{9,10},{10,... | collective-permute-start | bytes 221192 | tf_op jit(solution)/shard_map/ppermute | solution.py:616
  15.2 0.4 %collective-permute-start.8 = (f32[144,128]{1,0:T(8,128)S(1)}, f32[144,128]{1,0:T(8,128)S(1)}, u32[]{:S(2)}, u32[]{:S(2)}) collective-permute-start(f32[144,128]{1,0:T(8,128)S(1)} %get-tuple-element.38), channel_id=1, source_target_pairs={{0,1},{1,0},{2,3},{3,2},{4,7},{5,6},{6,5},{7,4},{8,9},{9,8},{10,11... | collective-permute-start | bytes 221192 | tf_op jit(solution)/shard_map/ppermute | solution.py:616
  15.5 1.4 %collective-permute-start.9 = (f32[144,128]{1,0:T(8,128)S(1)}, f32[144,128]{1,0:T(8,128)S(1)}, u32[]{:S(2)}, u32[]{:S(2)}) collective-permute-start(f32[144,128]{1,0:T(8,128)S(1)} %pass.1), channel_id=1, source_target_pairs={{0,2},{1,3},{2,0},{3,1},{4,5},{5,4},{6,7},{7,6},{8,10},{9,11},{10,... | collective-permute-start | bytes 221192 | tf_op jit(solution)/shard_map/ppermute | solution.py:616
  17.0 2.0 %rest.1 = (f32[2,9,2880]{2,1,0:T(8,128)S(1)}, f32[9,2880]{1,0:T(8,128)S(1)}, bf16[3,9,2880]{2,1,0:T(8,128)(2,1)S(1)}) custom-call(f32[3,16,128]{2,1,0:T(8,128)S(1)} %get-tuple-element.27.masks_ref, f32[9,2880]{1,0:T(8,128)S(1)} %copy-done.2, f32[9,2,2880]{2,1,0:T(2,128)S(1)} %bitcast.6, bf16[3,9,2880]{2,1,0:T(8,128)(2,1)S(1)} %copy.11.q_ref, ...), custom_call_target="tpu_custom_call" | custom-call | tf_op jit(solution)/shard_map/rest/pallas_call | solution.py:654
  19.0 0.8 %copy.12 = bf16[3,9,2880]{2,0,1:T(4,128)(2,1)} copy(bf16[3,9,2880]{2,1,0:T(8,128)(2,1)S(1)} %get-tuple-element.45) | data formatting | bytes 311040
  19.8 0.2 collective-permute-done.8.refs_2_
  19.9 0.2 collective-permute-done.9.refs_3_
  20.1 0.9 %finish.1 = (f32[9,2,2880]{2,1,0:T(2,128)}, f32[9,2880]{1,0:T(8,128)}) custom-call(f32[3,16,128]{2,1,0:T(8,128)S(1)} %get-tuple-element.27.masks_ref, f32[2,9,2880]{2,1,0:T(8,128)S(1)} %get-tuple-element.35.base_w_ref, f32[9,2880]{1,0:T(8,128)S(1)} %get-tuple-element.36.base_h_ref, f32[144,128]{1,0:T(8,128)S(1)} %get-tuple-element.34.after_ref.refs_0_, ...), custom_call_target="tpu_custom_call" | custom-call | tf_op jit(solution)/shard_map/finish/pallas_call | solution.py:662
  (21 shorter events, 0.1 us)
Async XLA Ops:
  0.6 2.2 %copy-start.3 = (f32[2,24,128]{2,1,0:T(8,128)S(1)}, f32[2,24,128]{2,1,0:T(8,128)}, u32[]{:S(2)}) copy-start(f32[2,24,128]{2,1,0:T(8,128)} %constant.9.clone.wave_ref) | copy-start | bytes 73732
  0.6 2.2 %collective-permute-start.1 = (f32[9,2,2880]{2,1,0:T(2,128)}, f32[9,2,2880]{2,1,0:T(2,128)S(1)}, u32[]{:S(2)}, u32[]{:S(2)}) collective-permute-start(f32[9,2,2880]{2,1,0:T(2,128)} %bitcast.3), channel_id=1, source_target_pairs={{0,4},{1,5},{2,6},{3,7},{4,0},{5,1},{6,2},{7,3},{8,12},{9,13},{10,... | collective-permute-start | bytes 622088 | tf_op jit(solution)/shard_map/ppermute | solution.py:606
  1.2 1.6 %collective-permute-start = (f32[9,2880]{1,0:T(8,128)}, f32[9,2880]{1,0:T(8,128)S(1)}, u32[]{:S(2)}, u32[]{:S(2)}) collective-permute-start(f32[9,2880]{1,0:T(8,128)} %h_ref.3), channel_id=1, source_target_pairs={{0,4},{1,5},{2,6},{3,7},{4,0},{5,1},{6,2},{7,3},{8,12},{9,13},{10,... | collective-permute-start | bytes 311048 | tf_op jit(solution)/shard_map/ppermute | solution.py:605
  1.2 1.6 %copy-start = (f32[2,9,2880]{2,0,1:T(2,128)S(1)}, f32[2,9,2880]{2,0,1:T(2,128)}, u32[]{:S(2)}) copy-start(f32[2,9,2880]{2,0,1:T(2,128)} %param.8) | copy-start | bytes 622084
  1.2 1.6 %copy-start.1 = (f32[8,3,16,128]{3,2,1,0:T(8,128)S(1)}, f32[8,3,16,128]{3,2,1,0:T(8,128)}, u32[]{:S(2)}) copy-start(f32[8,3,16,128]{3,2,1,0:T(8,128)} %constant.8.clone.geo_ref) | copy-start | bytes 589828
  1.2 1.6 %copy-start.2 = (f32[9,2880]{1,0:T(8,128)S(1)}, f32[9,2880]{1,0:T(8,128)}, u32[]{:S(2)}) copy-start(f32[9,2880]{1,0:T(8,128)} %h_ref.3) | copy-start | bytes 311044
  2.8 7.3 %copy-start.4 = (f32[192,96]{1,0:T(8,128)S(1)}, f32[192,96]{1,0:T(8,128)}, u32[]{:S(2)}) copy-start(f32[192,96]{1,0:T(8,128)} %constant.11.clone.inverse_ref) | copy-start | bytes 221188
  2.8 7.2 %copy-start.5 = (f32[192,96]{1,0:T(8,128)S(1)}, f32[192,96]{1,0:T(8,128)}, u32[]{:S(2)}) copy-start(f32[192,96]{1,0:T(8,128)} %constant.10.clone.n_ref) | copy-start | bytes 221188
  3.5 8.2 %collective-permute-start.4 = (f32[160,128]{1,0:T(8,128)S(1)}, f32[160,128]{1,0:T(8,128)S(1)}, u32[]{:S(2)}, u32[]{:S(2)}) collective-permute-start(f32[160,128]{1,0:T(8,128)S(1)} %get-tuple-element.31), channel_id=1, source_target_pairs={{0,3},{1,2},{2,1},{3,0},{4,6},{5,7},{6,4},{7,5},{8,11},{9,10},{10,... | collective-permute-start | bytes 245768 | tf_op jit(solution)/shard_map/ppermute | solution.py:616
  7.4 4.9 %collective-permute-start.5 = (f32[160,128]{1,0:T(8,128)S(1)}, f32[160,128]{1,0:T(8,128)S(1)}, u32[]{:S(2)}, u32[]{:S(2)}) collective-permute-start(f32[160,128]{1,0:T(8,128)S(1)} %get-tuple-element.32), channel_id=1, source_target_pairs={{0,1},{1,0},{2,3},{3,2},{4,7},{5,6},{6,5},{7,4},{8,9},{9,8},{10,11... | collective-permute-start | bytes 245768 | tf_op jit(solution)/shard_map/ppermute | solution.py:616
  7.9 4.4 %collective-permute-start.6 = (f32[160,128]{1,0:T(8,128)S(1)}, f32[160,128]{1,0:T(8,128)S(1)}, u32[]{:S(2)}, u32[]{:S(2)}) collective-permute-start(f32[160,128]{1,0:T(8,128)S(1)} %get-tuple-element.33), channel_id=1, source_target_pairs={{0,2},{1,3},{2,0},{3,1},{4,5},{5,4},{6,7},{7,6},{8,10},{9,11},{10,... | collective-permute-start | bytes 245768 | tf_op jit(solution)/shard_map/ppermute | solution.py:616
  8.0 7.5 %collective-permute-start.3 = (f32[120,128]{1,0:T(8,128)S(1)}, f32[120,128]{1,0:T(8,128)S(1)}, u32[]{:S(2)}, u32[]{:S(2)}) collective-permute-start(f32[120,128]{1,0:T(8,128)S(1)} %get-tuple-element.29), channel_id=1, source_target_pairs={{0,2},{1,3},{2,0},{3,1},{4,8},{5,9},{6,10},{7,11},{8,4},{9,5},{10,... | collective-permute-start | bytes 184328 | tf_op jit(solution)/shard_map/ppermute | solution.py:633
  9.9 0.7 %copy-start.6 = (s32[72]{0:T(128)S(1)}, s32[72]{0:T(128)}, u32[]{:S(2)}) copy-start(s32[72]{0:T(128)} %cut_ref.1) | copy-start | bytes 868
  9.9 5.6 %collective-permute-start.2 = (f32[72,128]{1,0:T(8,128)S(1)}, f32[72,128]{1,0:T(8,128)S(1)}, u32[]{:S(2)}, u32[]{:S(2)}) collective-permute-start(f32[72,128]{1,0:T(8,128)S(1)} %get-tuple-element.28), channel_id=1, source_target_pairs={{0,4},{1,5},{2,6},{3,7},{4,0},{5,1},{6,2},{7,3},{8,12},{9,13},{10,... | collective-permute-start | bytes 110600 | tf_op jit(solution)/shard_map/ppermute | solution.py:632
  13.3 3.7 %copy-start.7 = (bf16[3,9,2880]{2,0,1:T(4,128)(2,1)S(1)}, bf16[3,9,2880]{2,0,1:T(4,128)(2,1)}, u32[]{:S(2)}) copy-start(bf16[3,9,2880]{2,0,1:T(4,128)(2,1)} %param.10) | copy-start | bytes 466564
  13.3 6.4 %collective-permute-start.7 = (f32[144,128]{1,0:T(8,128)S(1)}, f32[144,128]{1,0:T(8,128)S(1)}, u32[]{:S(2)}, u32[]{:S(2)}) collective-permute-start(f32[144,128]{1,0:T(8,128)S(1)} %get-tuple-element.37), channel_id=1, source_target_pairs={{0,3},{1,2},{2,1},{3,0},{4,6},{5,7},{6,4},{7,5},{8,11},{9,10},{10,... | collective-permute-start | bytes 221192 | tf_op jit(solution)/shard_map/ppermute | solution.py:616
  15.2 4.8 %collective-permute-start.8 = (f32[144,128]{1,0:T(8,128)S(1)}, f32[144,128]{1,0:T(8,128)S(1)}, u32[]{:S(2)}, u32[]{:S(2)}) collective-permute-start(f32[144,128]{1,0:T(8,128)S(1)} %get-tuple-element.38), channel_id=1, source_target_pairs={{0,1},{1,0},{2,3},{3,2},{4,7},{5,6},{6,5},{7,4},{8,9},{9,8},{10,11... | collective-permute-start | bytes 221192 | tf_op jit(solution)/shard_map/ppermute | solution.py:616
  15.5 4.6 %collective-permute-start.9 = (f32[144,128]{1,0:T(8,128)S(1)}, f32[144,128]{1,0:T(8,128)S(1)}, u32[]{:S(2)}, u32[]{:S(2)}) collective-permute-start(f32[144,128]{1,0:T(8,128)S(1)} %pass.1), channel_id=1, source_target_pairs={{0,2},{1,3},{2,0},{3,1},{4,5},{5,4},{6,7},{7,6},{8,10},{9,11},{10,... | collective-permute-start | bytes 221192 | tf_op jit(solution)/shard_map/ppermute | solution.py:616

commit v16 on v15

--- a/solution.py
+++ b/solution.py
@@ -52,17 +52,19 @@
         pole = jnp.where(band == 0, 0, jnp.where(band == self.n_lat - 1, self.rows - 1, -1))
         return row == (pole if self.near_only else -1)
 
-    def turns(self, odd):
+    def turns(self, odd, back):
         middle, last = list(range(1, self.n_lon - 1)), self.n_lon - 1
-        return [0, middle[-1], last] + middle[-2::-1] if odd else [0, last] + middle
-
-    def partner(self, k):
+        if odd and back:
+            return [0, middle[-1], last] + middle[-2::-1]
+        return [0, last] + (middle[::-1] if odd else middle)
+
+    def partner(self, k, back=False):
         odd = lax.rem(lax.axis_index("lat"), 2) == 1
-        turn = jnp.where(odd, self.turns(True)[k], self.turns(False)[k])
+        turn = jnp.where(odd, self.turns(True, back)[k], self.turns(False, back)[k])
         return jnp.bitwise_xor(lax.axis_index("lon"), turn)
 
-    def piece(self, k):
-        return pl.ds(pl.multiple_of(self.partner(k) * self.size, 8), self.size)
+    def piece(self, k, back=False):
+        return pl.ds(pl.multiple_of(self.partner(k, back) * self.size, 8), self.size)
 
 
 def geometry(sz):
@@ -520,14 +522,14 @@
                 carried = over if carried is None else carried + over
             results[s, here] = pltpu.roll(same, stack - 1, 0) + carried
     for k, out_ref in enumerate(out_refs):
-        out_ref[...] = results[sz.partner(k)]
+        out_ref[...] = results[sz.partner(k, True)]
 
 
 def finish_kernel(sz, masks_ref, base_w_ref, base_h_ref, *refs):
     back_refs, (new_w_ref, new_h_ref, back_ref) = refs[: sz.n_lon], refs[sz.n_lon :]
     rows, work = sz.rows, sz.work
     for k, ref in enumerate(back_refs):
-        back_ref[sz.piece(k), :] = ref[...]
+        back_ref[sz.piece(k, True), :] = ref[...]
     scale = masks_ref[2]
     even = lax.rem(lax.axis_index("lat"), 2) == 0
     for f in range(3):
@@ -607,9 +609,8 @@
     if not sz.near_only:
         far_rows = lax.ppermute(far_rows, ("lat", "lon"), far)
 
-    order = [sz.turns(False), sz.turns(True)]
-
-    def meetings(shares):
+    def meetings(shares, back):
+        order = [sz.turns(False, back), sz.turns(True, back)]
         got = [shares[0]]
         for k in range(1, n_lon):
             sectors = [(band, i, i ^ order[band % 2][k]) for band in range(n_lat) for i in range(n_lon)]
@@ -628,7 +629,7 @@
             pltpu.VMEM((3, EXT_ROWS, sz.tiles * LANES), f32),
         ],
     )(thickness, wind_rows, near_h, near_w, sides, geo, wave, far_rows, near_q)
-    met = meetings(tends)
+    met = meetings(tends, False)
     near_q = lax.ppermute(near_q, ("lat", "lon"), near)
     from_far = lax.ppermute(far_rows, ("lat", "lon"), far) if sz.near_only else far_rows
     weights, masks = call(
@@ -649,7 +650,7 @@
     )(weights, geo, *met)
     held = call(pass_kernel, "pass", [vmem] + [anywhere] * 2, shaped(sz.size, LANES))(worked[-1], from_far, near_q)
     worked = [*worked[:-1], held]
-    back = meetings(worked)
+    back = meetings(worked, True)
 
     base_w, base_h, mass = call(
         rest_kernel,

time: 21.2 us -> 21.7 us (1.024)
  waiting for transfers between devices: 1.32 us -> 1.82 us
    ppermute x6, waiting for transfers between devices: 0.93 us -> 1.44 us  [meetings(): lax.ppermute(shares[k], ('lat', 'lon'), [(b * n_lon + i, b * n_lon + j) f...]
where the time goes in v16:
time: 21.7 us; the launch traced here: 21.5 us
  starting transfers between devices  10.8 us (50%)
  Pallas kernels  6.88 us (32%)
  waiting for transfers between devices  1.82 us (8%)
  local copies, waits for them, and re-layouts  1.32 us (6%)
  between operations  0.75 us (3%)
    ppermute x6, starting transfers between devices, meetings(): lax.ppermute(shares[k], ('lat', 'lon'), [(b * n_lon + i, b * n_lon + j) f...  8.07 us
    pallas_call x1, Pallas kernels, local(): call(rest_kernel, 'rest', [vmem] * 10 + [anywhere] + [vmem] * n_lon, (sha...  1.98 us
    ppermute x1, starting transfers between devices, local(): lax.ppermute(far_rows, ('lat', 'lon'), far)  1.92 us
    ppermute x6, waiting for transfers between devices, meetings(): lax.ppermute(shares[k], ('lat', 'lon'), [(b * n_lon + i, b * n_lon + j) f...  1.44 us
    unnamed x18, local copies, waits for them, and re-layouts  1.32 us
    pallas_call x1, Pallas kernels, local(): call(edges_kernel, 'edges', [hbm] * 3, (near_row, far_row, shaped(2 * EXT...  1.17 us
    pallas_call x1, Pallas kernels, local(): call(weights_kernel, 'weights', [smem, vmem, vmem, anywhere], (jax.ShapeD...  1.15 us
    pallas_call x1, Pallas kernels, local(): call(filter_kernel, 'filter', [vmem] * 2 + [vmem] * n_lon, [shaped(sz.siz...  0.98 us
  transfers between devices with their start and end apart: 10, of which 5 were waited for; matrix products, arithmetic and copies ran while one was open for 4% of the time, Pallas kernels for 25%

profile of v16, /device:TPU:0, one launch (start us, length us, event | category | flops | bytes accessed | tf_op | source)
XLA Modules:
  0.0 21.5 jit_solution(3712150040587092934)
XLA Ops:
  0.6 0.0 copy-start.3
  0.6 0.5 %collective-permute-start.1 = (f32[9,2,2880]{2,1,0:T(2,128)}, f32[9,2,2880]{2,1,0:T(2,128)S(1)}, u32[]{:S(2)}, u32[]{:S(2)}) collective-permute-start(f32[9,2,2880]{2,1,0:T(2,128)} %bitcast.3), channel_id=1, source_target_pairs={{0,4},{1,5},{2,6},{3,7},{4,0},{5,1},{6,2},{7,3},{8,12},{9,13},{10,... | collective-permute-start | bytes 622088 | tf_op jit(solution)/shard_map/ppermute | solution.py:608
  1.2 0.1 collective-permute-start
  1.2 1.2 %edges.1 = (f32[72,128]{1,0:T(8,128)S(1)}, f32[120,128]{1,0:T(8,128)S(1)}, f32[32,128]{1,0:T(8,128)S(1)}) custom-call(f32[9,2880]{1,0:T(8,128)} %h_ref.3, f32[9,2,2880]{2,1,0:T(2,128)} %bitcast.4, bf16[9,3,2880]{2,1,0:T(4,128)(2,1)} %bitcast.7), custom_call_target="tpu_custom_call" | custom-call | tf_op jit(solution)/shard_map/edges/pallas_call | solution.py:583
  2.4 0.4 %collective-permute-done.near_h_ref = f32[9,2880]{1,0:T(8,128)S(1)} collective-permute-done((f32[9,2880]{1,0:T(8,128)}, f32[9,2880]{1,0:T(8,128)S(1)}, u32[]{:S(2)}, u32[]{:S(2)}) %collective-permute-start) | collective-permute-done | bytes 103712 | tf_op jit(solution)/shard_map/ppermute | solution.py:607
  2.9 0.7 %polar.1 = (f32[160,128]{1,0:T(8,128)S(1)}, f32[160,128]{1,0:T(8,128)S(1)}, f32[160,128]{1,0:T(8,128)S(1)}, f32[160,128]{1,0:T(8,128)S(1)}, f32[120,128]{1,0:T(8,128)S(1)}, /*index=5*/f32[72,128]{1,0:T(8,128)S(1)}) custom-call(f32[9,2880]{1,0:T(8,128)S(1)} %copy-done.2, f32[9,2,2880]{2,1,0:T(2,128)S(1)} %bitcast.5, ...), custom_call_target="tpu_custom_call" | custom-call | tf_op jit(solution)/shard_map/polar/pallas_call | solution.py:621
  3.5 3.8 %collective-permute-start.4 = (f32[160,128]{1,0:T(8,128)S(1)}, f32[160,128]{1,0:T(8,128)S(1)}, u32[]{:S(2)}, u32[]{:S(2)}) collective-permute-start(f32[160,128]{1,0:T(8,128)S(1)} %get-tuple-element.31), channel_id=1, source_target_pairs={{0,3},{1,2},{2,1},{3,0},{4,7},{5,6},{6,5},{7,4},{8,11},{9,10},{10,... | collective-permute-start | bytes 245768 | tf_op jit(solution)/shard_map/ppermute | solution.py:617
  7.4 0.5 %collective-permute-start.5 = (f32[160,128]{1,0:T(8,128)S(1)}, f32[160,128]{1,0:T(8,128)S(1)}, u32[]{:S(2)}, u32[]{:S(2)}) collective-permute-start(f32[160,128]{1,0:T(8,128)S(1)} %get-tuple-element.32), channel_id=1, source_target_pairs={{0,1},{1,0},{2,3},{3,2},{4,6},{5,7},{6,4},{7,5},{8,9},{9,8},{10,11... | collective-permute-start | bytes 245768 | tf_op jit(solution)/shard_map/ppermute | solution.py:617
  7.9 0.1 collective-permute-start.6
  8.0 1.9 %collective-permute-start.3 = (f32[120,128]{1,0:T(8,128)S(1)}, f32[120,128]{1,0:T(8,128)S(1)}, u32[]{:S(2)}, u32[]{:S(2)}) collective-permute-start(f32[120,128]{1,0:T(8,128)S(1)} %get-tuple-element.29), channel_id=1, source_target_pairs={{0,2},{1,3},{2,0},{3,1},{4,8},{5,9},{6,10},{7,11},{8,4},{9,5},{10,... | collective-permute-start | bytes 184328 | tf_op jit(solution)/shard_map/ppermute | solution.py:634
  9.9 0.2 collective-permute-start.2
  10.1 0.5 %copy-done.6 = s32[72]{0:T(128)S(1)} copy-done((s32[72]{0:T(128)S(1)}, s32[72]{0:T(128)}, u32[]{:S(2)}) %copy-start.6) | copy-done | bytes 312
  10.6 1.1 %weights.1 = (bf16[1152,96]{1,0:T(8,128)(2,1)S(1)}, f32[3,16,128]{2,1,0:T(8,128)S(1)}) custom-call(s32[72]{0:T(128)S(1)} %copy-done.6, f32[192,96]{1,0:T(8,128)S(1)} %copy-done.5, f32[192,96]{1,0:T(8,128)S(1)} %copy-done.4, f32[160,128]{1,0:T(8,128)S(1)} %get-tuple-element.26.after_ref.refs_0_), custom_call_target="tpu_custom_call" | custom-call | tf_op jit(solution)/shard_map/weights/pallas_call | solution.py:635
  11.7 0.4 %collective-permute-done.5.refs_2_ = f32[160,128]{1,0:T(8,128)S(1)} collective-permute-done((f32[160,128]{1,0:T(8,128)S(1)}, f32[160,128]{1,0:T(8,128)S(1)}, u32[]{:S(2)}, u32[]{:S(2)}) %collective-permute-start.5) | collective-permute-done | bytes 81952 | tf_op jit(solution)/shard_map/ppermute | solution.py:617
  12.2 0.2 collective-permute-done.6.refs_3_
  12.3 1.0 %filter.1 = (f32[144,128]{1,0:T(8,128)S(1)}, f32[144,128]{1,0:T(8,128)S(1)}, f32[144,128]{1,0:T(8,128)S(1)}, f32[144,128]{1,0:T(8,128)S(1)}) custom-call(bf16[1152,96]{1,0:T(8,128)(2,1)S(1)} %get-tuple-element.30.weights_ref, f32[8,3,16,128]{3,2,1,0:T(8,128)S(1)} %copy-done.1, f32[160,128]{1,0:T(8,128)S(1)} %get-tuple-element.26.after_ref.refs_0_, ...), custom_call_target="tpu_custom_call" | custom-call | tf_op jit(solution)/shard_map/filter/pallas_call | solution.py:644
  13.3 1.8 %collective-permute-start.7 = (f32[144,128]{1,0:T(8,128)S(1)}, f32[144,128]{1,0:T(8,128)S(1)}, u32[]{:S(2)}, u32[]{:S(2)}) collective-permute-start(f32[144,128]{1,0:T(8,128)S(1)} %get-tuple-element.37), channel_id=1, source_target_pairs={{0,3},{1,2},{2,1},{3,0},{4,6},{5,7},{6,4},{7,5},{8,11},{9,10},{10,... | collective-permute-start | bytes 221192 | tf_op jit(solution)/shard_map/ppermute | solution.py:617
  15.2 1.0 %collective-permute-start.8 = (f32[144,128]{1,0:T(8,128)S(1)}, f32[144,128]{1,0:T(8,128)S(1)}, u32[]{:S(2)}, u32[]{:S(2)}) collective-permute-start(f32[144,128]{1,0:T(8,128)S(1)} %get-tuple-element.38), channel_id=1, source_target_pairs={{0,1},{1,0},{2,3},{3,2},{4,7},{5,6},{6,5},{7,4},{8,9},{9,8},{10,11... | collective-permute-start | bytes 221192 | tf_op jit(solution)/shard_map/ppermute | solution.py:617
  16.2 0.8 %collective-permute-start.9 = (f32[144,128]{1,0:T(8,128)S(1)}, f32[144,128]{1,0:T(8,128)S(1)}, u32[]{:S(2)}, u32[]{:S(2)}) collective-permute-start(f32[144,128]{1,0:T(8,128)S(1)} %pass.1), channel_id=1, source_target_pairs={{0,2},{1,3},{2,0},{3,1},{4,5},{5,4},{6,7},{7,6},{8,10},{9,11},{10,... | collective-permute-start | bytes 221192 | tf_op jit(solution)/shard_map/ppermute | solution.py:617
  17.0 2.0 %rest.1 = (f32[2,9,2880]{2,1,0:T(8,128)S(1)}, f32[9,2880]{1,0:T(8,128)S(1)}, bf16[3,9,2880]{2,1,0:T(8,128)(2,1)S(1)}) custom-call(f32[3,16,128]{2,1,0:T(8,128)S(1)} %get-tuple-element.27.masks_ref, f32[9,2880]{1,0:T(8,128)S(1)} %copy-done.2, f32[9,2,2880]{2,1,0:T(2,128)S(1)} %bitcast.6, bf16[3,9,2880]{2,1,0:T(8,128)(2,1)S(1)} %copy.11.q_ref, ...), custom_call_target="tpu_custom_call" | custom-call | tf_op jit(solution)/shard_map/rest/pallas_call | solution.py:655
  19.0 0.8 %copy.12 = bf16[3,9,2880]{2,0,1:T(4,128)(2,1)} copy(bf16[3,9,2880]{2,1,0:T(8,128)(2,1)S(1)} %get-tuple-element.45) | data formatting | bytes 311040
  19.8 0.3 %collective-permute-done.8.refs_2_ = f32[144,128]{1,0:T(8,128)S(1)} collective-permute-done((f32[144,128]{1,0:T(8,128)S(1)}, f32[144,128]{1,0:T(8,128)S(1)}, u32[]{:S(2)}, u32[]{:S(2)}) %collective-permute-start.8) | collective-permute-done | bytes 73760 | tf_op jit(solution)/shard_map/ppermute | solution.py:617
  20.1 0.5 %collective-permute-done.9.refs_3_ = f32[144,128]{1,0:T(8,128)S(1)} collective-permute-done((f32[144,128]{1,0:T(8,128)S(1)}, f32[144,128]{1,0:T(8,128)S(1)}, u32[]{:S(2)}, u32[]{:S(2)}) %collective-permute-start.9) | collective-permute-done | bytes 73760 | tf_op jit(solution)/shard_map/ppermute | solution.py:617
  20.6 0.9 %finish.1 = (f32[9,2,2880]{2,1,0:T(2,128)}, f32[9,2880]{1,0:T(8,128)}) custom-call(f32[3,16,128]{2,1,0:T(8,128)S(1)} %get-tuple-element.27.masks_ref, f32[2,9,2880]{2,1,0:T(8,128)S(1)} %get-tuple-element.35.base_w_ref, f32[9,2880]{1,0:T(8,128)S(1)} %get-tuple-element.36.base_h_ref, f32[144,128]{1,0:T(8,128)S(1)} %get-tuple-element.34.after_ref.refs_0_, ...), custom_call_target="tpu_custom_call" | custom-call | tf_op jit(solution)/shard_map/finish/pallas_call | solution.py:663
  (21 shorter events, 0.1 us)
Async XLA Ops:
  0.6 2.2 %copy-start.3 = (f32[2,24,128]{2,1,0:T(8,128)S(1)}, f32[2,24,128]{2,1,0:T(8,128)}, u32[]{:S(2)}) copy-start(f32[2,24,128]{2,1,0:T(8,128)} %constant.9.clone.wave_ref) | copy-start | bytes 73732
  0.6 2.2 %collective-permute-start.1 = (f32[9,2,2880]{2,1,0:T(2,128)}, f32[9,2,2880]{2,1,0:T(2,128)S(1)}, u32[]{:S(2)}, u32[]{:S(2)}) collective-permute-start(f32[9,2,2880]{2,1,0:T(2,128)} %bitcast.3), channel_id=1, source_target_pairs={{0,4},{1,5},{2,6},{3,7},{4,0},{5,1},{6,2},{7,3},{8,12},{9,13},{10,... | collective-permute-start | bytes 622088 | tf_op jit(solution)/shard_map/ppermute | solution.py:608
  1.2 1.6 %collective-permute-start = (f32[9,2880]{1,0:T(8,128)}, f32[9,2880]{1,0:T(8,128)S(1)}, u32[]{:S(2)}, u32[]{:S(2)}) collective-permute-start(f32[9,2880]{1,0:T(8,128)} %h_ref.3), channel_id=1, source_target_pairs={{0,4},{1,5},{2,6},{3,7},{4,0},{5,1},{6,2},{7,3},{8,12},{9,13},{10,... | collective-permute-start | bytes 311048 | tf_op jit(solution)/shard_map/ppermute | solution.py:607
  1.2 1.6 %copy-start = (f32[2,9,2880]{2,0,1:T(2,128)S(1)}, f32[2,9,2880]{2,0,1:T(2,128)}, u32[]{:S(2)}) copy-start(f32[2,9,2880]{2,0,1:T(2,128)} %param.8) | copy-start | bytes 622084
  1.2 1.6 %copy-start.1 = (f32[8,3,16,128]{3,2,1,0:T(8,128)S(1)}, f32[8,3,16,128]{3,2,1,0:T(8,128)}, u32[]{:S(2)}) copy-start(f32[8,3,16,128]{3,2,1,0:T(8,128)} %constant.8.clone.geo_ref) | copy-start | bytes 589828
  1.2 1.6 %copy-start.2 = (f32[9,2880]{1,0:T(8,128)S(1)}, f32[9,2880]{1,0:T(8,128)}, u32[]{:S(2)}) copy-start(f32[9,2880]{1,0:T(8,128)} %h_ref.3) | copy-start | bytes 311044
  2.8 7.3 %copy-start.4 = (f32[192,96]{1,0:T(8,128)S(1)}, f32[192,96]{1,0:T(8,128)}, u32[]{:S(2)}) copy-start(f32[192,96]{1,0:T(8,128)} %constant.11.clone.inverse_ref) | copy-start | bytes 221188
  2.8 7.2 %copy-start.5 = (f32[192,96]{1,0:T(8,128)S(1)}, f32[192,96]{1,0:T(8,128)}, u32[]{:S(2)}) copy-start(f32[192,96]{1,0:T(8,128)} %constant.10.clone.n_ref) | copy-start | bytes 221188
  3.5 8.2 %collective-permute-start.4 = (f32[160,128]{1,0:T(8,128)S(1)}, f32[160,128]{1,0:T(8,128)S(1)}, u32[]{:S(2)}, u32[]{:S(2)}) collective-permute-start(f32[160,128]{1,0:T(8,128)S(1)} %get-tuple-element.31), channel_id=1, source_target_pairs={{0,3},{1,2},{2,1},{3,0},{4,7},{5,6},{6,5},{7,4},{8,11},{9,10},{10,... | collective-permute-start | bytes 245768 | tf_op jit(solution)/shard_map/ppermute | solution.py:617
  7.4 4.8 %collective-permute-start.5 = (f32[160,128]{1,0:T(8,128)S(1)}, f32[160,128]{1,0:T(8,128)S(1)}, u32[]{:S(2)}, u32[]{:S(2)}) collective-permute-start(f32[160,128]{1,0:T(8,128)S(1)} %get-tuple-element.32), channel_id=1, source_target_pairs={{0,1},{1,0},{2,3},{3,2},{4,6},{5,7},{6,4},{7,5},{8,9},{9,8},{10,11... | collective-permute-start | bytes 245768 | tf_op jit(solution)/shard_map/ppermute | solution.py:617
  7.9 4.4 %collective-permute-start.6 = (f32[160,128]{1,0:T(8,128)S(1)}, f32[160,128]{1,0:T(8,128)S(1)}, u32[]{:S(2)}, u32[]{:S(2)}) collective-permute-start(f32[160,128]{1,0:T(8,128)S(1)} %get-tuple-element.33), channel_id=1, source_target_pairs={{0,2},{1,3},{2,0},{3,1},{4,5},{5,4},{6,7},{7,6},{8,10},{9,11},{10,... | collective-permute-start | bytes 245768 | tf_op jit(solution)/shard_map/ppermute | solution.py:617
  8.0 8.2 %collective-permute-start.3 = (f32[120,128]{1,0:T(8,128)S(1)}, f32[120,128]{1,0:T(8,128)S(1)}, u32[]{:S(2)}, u32[]{:S(2)}) collective-permute-start(f32[120,128]{1,0:T(8,128)S(1)} %get-tuple-element.29), channel_id=1, source_target_pairs={{0,2},{1,3},{2,0},{3,1},{4,8},{5,9},{6,10},{7,11},{8,4},{9,5},{10,... | collective-permute-start | bytes 184328 | tf_op jit(solution)/shard_map/ppermute | solution.py:634
  9.9 0.7 %copy-start.6 = (s32[72]{0:T(128)S(1)}, s32[72]{0:T(128)}, u32[]{:S(2)}) copy-start(s32[72]{0:T(128)} %cut_ref.1) | copy-start | bytes 868
  9.9 6.3 %collective-permute-start.2 = (f32[72,128]{1,0:T(8,128)S(1)}, f32[72,128]{1,0:T(8,128)S(1)}, u32[]{:S(2)}, u32[]{:S(2)}) collective-permute-start(f32[72,128]{1,0:T(8,128)S(1)} %get-tuple-element.28), channel_id=1, source_target_pairs={{0,4},{1,5},{2,6},{3,7},{4,0},{5,1},{6,2},{7,3},{8,12},{9,13},{10,... | collective-permute-start | bytes 110600 | tf_op jit(solution)/shard_map/ppermute | solution.py:633
  13.3 3.7 %copy-start.7 = (bf16[3,9,2880]{2,0,1:T(4,128)(2,1)S(1)}, bf16[3,9,2880]{2,0,1:T(4,128)(2,1)}, u32[]{:S(2)}) copy-start(bf16[3,9,2880]{2,0,1:T(4,128)(2,1)} %param.10) | copy-start | bytes 466564
  13.3 6.4 %collective-permute-start.7 = (f32[144,128]{1,0:T(8,128)S(1)}, f32[144,128]{1,0:T(8,128)S(1)}, u32[]{:S(2)}, u32[]{:S(2)}) collective-permute-start(f32[144,128]{1,0:T(8,128)S(1)} %get-tuple-element.37), channel_id=1, source_target_pairs={{0,3},{1,2},{2,1},{3,0},{4,6},{5,7},{6,4},{7,5},{8,11},{9,10},{10,... | collective-permute-start | bytes 221192 | tf_op jit(solution)/shard_map/ppermute | solution.py:617
  15.2 4.9 %collective-permute-start.8 = (f32[144,128]{1,0:T(8,128)S(1)}, f32[144,128]{1,0:T(8,128)S(1)}, u32[]{:S(2)}, u32[]{:S(2)}) collective-permute-start(f32[144,128]{1,0:T(8,128)S(1)} %get-tuple-element.38), channel_id=1, source_target_pairs={{0,1},{1,0},{2,3},{3,2},{4,7},{5,6},{6,5},{7,4},{8,9},{9,8},{10,11... | collective-permute-start | bytes 221192 | tf_op jit(solution)/shard_map/ppermute | solution.py:617
  16.2 4.4 %collective-permute-start.9 = (f32[144,128]{1,0:T(8,128)S(1)}, f32[144,128]{1,0:T(8,128)S(1)}, u32[]{:S(2)}, u32[]{:S(2)}) collective-permute-start(f32[144,128]{1,0:T(8,128)S(1)} %pass.1), channel_id=1, source_target_pairs={{0,2},{1,3},{2,0},{3,1},{4,5},{5,4},{6,7},{7,6},{8,10},{9,11},{10,... | collective-permute-start | bytes 221192 | tf_op jit(solution)/shard_map/ppermute | solution.py:617

commit v17 on v16

--- a/solution.py
+++ b/solution.py
@@ -54,7 +54,7 @@
 
     def turns(self, odd, back):
         middle, last = list(range(1, self.n_lon - 1)), self.n_lon - 1
-        if odd and back:
+        if odd and not back:
             return [0, middle[-1], last] + middle[-2::-1]
         return [0, last] + (middle[::-1] if odd else middle)
 

time: 21.7 us -> 21.2 us (0.977)
  waiting for transfers between devices: 1.82 us -> 1.35 us
    ppermute x6, waiting for transfers between devices: 1.44 us -> 0.97 us  [meetings(): lax.ppermute(shares[k], ('lat', 'lon'), [(b * n_lon + i, b * n_lon + j) f...]
  transfers between devices with their start and end apart: 10 -> 10, of which waited for: 5 -> 4; matrix products, arithmetic and copies ran while one was open for 4% -> 4% of each run, Pallas kernels for 25% -> 25%
where the time goes in v17:
time: 21.2 us; the launch traced here: 21.1 us
  starting transfers between devices  10.8 us (51%)
  Pallas kernels  6.89 us (32%)
  waiting for transfers between devices  1.35 us (6%)
  local copies, waits for them, and re-layouts  1.32 us (6%)
  between operations  0.75 us (4%)
    ppermute x6, starting transfers between devices, meetings(): lax.ppermute(shares[k], ('lat', 'lon'), [(b * n_lon + i, b * n_lon + j) f...  8.07 us
    pallas_call x1, Pallas kernels, local(): call(rest_kernel, 'rest', [vmem] * 10 + [anywhere] + [vmem] * n_lon, (sha...  1.99 us
    ppermute x1, starting transfers between devices, local(): lax.ppermute(far_rows, ('lat', 'lon'), far)  1.92 us
    unnamed x18, local copies, waits for them, and re-layouts  1.32 us
    pallas_call x1, Pallas kernels, local(): call(edges_kernel, 'edges', [hbm] * 3, (near_row, far_row, shaped(2 * EXT...  1.17 us
    pallas_call x1, Pallas kernels, local(): call(weights_kernel, 'weights', [smem, vmem, vmem, anywhere], (jax.ShapeD...  1.15 us
    pallas_call x1, Pallas kernels, local(): call(filter_kernel, 'filter', [vmem] * 2 + [vmem] * n_lon, [shaped(sz.siz...  0.98 us
    ppermute x6, waiting for transfers between devices, meetings(): lax.ppermute(shares[k], ('lat', 'lon'), [(b * n_lon + i, b * n_lon + j) f...  0.97 us
  transfers between devices with their start and end apart: 10, of which 4 were waited for; matrix products, arithmetic and copies ran while one was open for 4% of the time, Pallas kernels for 25%

profile of v17, /device:TPU:0, one launch (start us, length us, event | category | flops | bytes accessed | tf_op | source)
XLA Modules:
  0.0 21.1 jit_solution(18386625402741637387)
XLA Ops:
  0.6 0.0 copy-start.3
  0.6 0.5 %collective-permute-start.1 = (f32[9,2,2880]{2,1,0:T(2,128)}, f32[9,2,2880]{2,1,0:T(2,128)S(1)}, u32[]{:S(2)}, u32[]{:S(2)}) collective-permute-start(f32[9,2,2880]{2,1,0:T(2,128)} %bitcast.3), channel_id=1, source_target_pairs={{0,4},{1,5},{2,6},{3,7},{4,0},{5,1},{6,2},{7,3},{8,12},{9,13},{10,... | collective-permute-start | bytes 622088 | tf_op jit(solution)/shard_map/ppermute | solution.py:608
  1.2 0.1 collective-permute-start
  1.2 1.2 %edges.1 = (f32[72,128]{1,0:T(8,128)S(1)}, f32[120,128]{1,0:T(8,128)S(1)}, f32[32,128]{1,0:T(8,128)S(1)}) custom-call(f32[9,2880]{1,0:T(8,128)} %h_ref.3, f32[9,2,2880]{2,1,0:T(2,128)} %bitcast.4, bf16[9,3,2880]{2,1,0:T(4,128)(2,1)} %bitcast.7), custom_call_target="tpu_custom_call" | custom-call | tf_op jit(solution)/shard_map/edges/pallas_call | solution.py:583
  2.4 0.4 %collective-permute-done.near_h_ref = f32[9,2880]{1,0:T(8,128)S(1)} collective-permute-done((f32[9,2880]{1,0:T(8,128)}, f32[9,2880]{1,0:T(8,128)S(1)}, u32[]{:S(2)}, u32[]{:S(2)}) %collective-permute-start) | collective-permute-done | bytes 103712 | tf_op jit(solution)/shard_map/ppermute | solution.py:607
  2.8 0.0 copy-start.5
  2.9 0.7 %polar.1 = (f32[160,128]{1,0:T(8,128)S(1)}, f32[160,128]{1,0:T(8,128)S(1)}, f32[160,128]{1,0:T(8,128)S(1)}, f32[160,128]{1,0:T(8,128)S(1)}, f32[120,128]{1,0:T(8,128)S(1)}, /*index=5*/f32[72,128]{1,0:T(8,128)S(1)}) custom-call(f32[9,2880]{1,0:T(8,128)S(1)} %copy-done.2, f32[9,2,2880]{2,1,0:T(2,128)S(1)} %bitcast.5, ...), custom_call_target="tpu_custom_call" | custom-call | tf_op jit(solution)/shard_map/polar/pallas_call | solution.py:621
  3.5 3.8 %collective-permute-start.4 = (f32[160,128]{1,0:T(8,128)S(1)}, f32[160,128]{1,0:T(8,128)S(1)}, u32[]{:S(2)}, u32[]{:S(2)}) collective-permute-start(f32[160,128]{1,0:T(8,128)S(1)} %get-tuple-element.31), channel_id=1, source_target_pairs={{0,3},{1,2},{2,1},{3,0},{4,6},{5,7},{6,4},{7,5},{8,11},{9,10},{10,... | collective-permute-start | bytes 245768 | tf_op jit(solution)/shard_map/ppermute | solution.py:617
  7.4 0.5 %collective-permute-start.5 = (f32[160,128]{1,0:T(8,128)S(1)}, f32[160,128]{1,0:T(8,128)S(1)}, u32[]{:S(2)}, u32[]{:S(2)}) collective-permute-start(f32[160,128]{1,0:T(8,128)S(1)} %get-tuple-element.32), channel_id=1, source_target_pairs={{0,1},{1,0},{2,3},{3,2},{4,7},{5,6},{6,5},{7,4},{8,9},{9,8},{10,11... | collective-permute-start | bytes 245768 | tf_op jit(solution)/shard_map/ppermute | solution.py:617
  7.9 0.1 collective-permute-start.6
  8.0 1.9 %collective-permute-start.3 = (f32[120,128]{1,0:T(8,128)S(1)}, f32[120,128]{1,0:T(8,128)S(1)}, u32[]{:S(2)}, u32[]{:S(2)}) collective-permute-start(f32[120,128]{1,0:T(8,128)S(1)} %get-tuple-element.29), channel_id=1, source_target_pairs={{0,2},{1,3},{2,0},{3,1},{4,8},{5,9},{6,10},{7,11},{8,4},{9,5},{10,... | collective-permute-start | bytes 184328 | tf_op jit(solution)/shard_map/ppermute | solution.py:634
  9.9 0.2 collective-permute-start.2
  10.1 0.5 %copy-done.6 = s32[72]{0:T(128)S(1)} copy-done((s32[72]{0:T(128)S(1)}, s32[72]{0:T(128)}, u32[]{:S(2)}) %copy-start.6) | copy-done | bytes 312
  10.6 1.1 %weights.1 = (bf16[1152,96]{1,0:T(8,128)(2,1)S(1)}, f32[3,16,128]{2,1,0:T(8,128)S(1)}) custom-call(s32[72]{0:T(128)S(1)} %copy-done.6, f32[192,96]{1,0:T(8,128)S(1)} %copy-done.5, f32[192,96]{1,0:T(8,128)S(1)} %copy-done.4, f32[160,128]{1,0:T(8,128)S(1)} %get-tuple-element.26.after_ref.refs_0_), custom_call_target="tpu_custom_call" | custom-call | tf_op jit(solution)/shard_map/weights/pallas_call | solution.py:635
  11.7 0.5 %collective-permute-done.5.refs_2_ = f32[160,128]{1,0:T(8,128)S(1)} collective-permute-done((f32[160,128]{1,0:T(8,128)S(1)}, f32[160,128]{1,0:T(8,128)S(1)}, u32[]{:S(2)}, u32[]{:S(2)}) %collective-permute-start.5) | collective-permute-done | bytes 81952 | tf_op jit(solution)/shard_map/ppermute | solution.py:617
  12.3 0.1 collective-permute-done.6.refs_3_
  12.3 1.0 %filter.1 = (f32[144,128]{1,0:T(8,128)S(1)}, f32[144,128]{1,0:T(8,128)S(1)}, f32[144,128]{1,0:T(8,128)S(1)}, f32[144,128]{1,0:T(8,128)S(1)}) custom-call(bf16[1152,96]{1,0:T(8,128)(2,1)S(1)} %get-tuple-element.30.weights_ref, f32[8,3,16,128]{3,2,1,0:T(8,128)S(1)} %copy-done.1, f32[160,128]{1,0:T(8,128)S(1)} %get-tuple-element.26.after_ref.refs_0_, ...), custom_call_target="tpu_custom_call" | custom-call | tf_op jit(solution)/shard_map/filter/pallas_call | solution.py:644
  13.3 1.8 %collective-permute-start.7 = (f32[144,128]{1,0:T(8,128)S(1)}, f32[144,128]{1,0:T(8,128)S(1)}, u32[]{:S(2)}, u32[]{:S(2)}) collective-permute-start(f32[144,128]{1,0:T(8,128)S(1)} %get-tuple-element.37), channel_id=1, source_target_pairs={{0,3},{1,2},{2,1},{3,0},{4,7},{5,6},{6,5},{7,4},{8,11},{9,10},{10,... | collective-permute-start | bytes 221192 | tf_op jit(solution)/shard_map/ppermute | solution.py:617
  15.2 0.4 %collective-permute-start.8 = (f32[144,128]{1,0:T(8,128)S(1)}, f32[144,128]{1,0:T(8,128)S(1)}, u32[]{:S(2)}, u32[]{:S(2)}) collective-permute-start(f32[144,128]{1,0:T(8,128)S(1)} %get-tuple-element.38), channel_id=1, source_target_pairs={{0,1},{1,0},{2,3},{3,2},{4,6},{5,7},{6,4},{7,5},{8,9},{9,8},{10,11... | collective-permute-start | bytes 221192 | tf_op jit(solution)/shard_map/ppermute | solution.py:617
  15.5 1.4 %collective-permute-start.9 = (f32[144,128]{1,0:T(8,128)S(1)}, f32[144,128]{1,0:T(8,128)S(1)}, u32[]{:S(2)}, u32[]{:S(2)}) collective-permute-start(f32[144,128]{1,0:T(8,128)S(1)} %pass.1), channel_id=1, source_target_pairs={{0,2},{1,3},{2,0},{3,1},{4,5},{5,4},{6,7},{7,6},{8,10},{9,11},{10,... | collective-permute-start | bytes 221192 | tf_op jit(solution)/shard_map/ppermute | solution.py:617
  17.0 2.0 %rest.1 = (f32[2,9,2880]{2,1,0:T(8,128)S(1)}, f32[9,2880]{1,0:T(8,128)S(1)}, bf16[3,9,2880]{2,1,0:T(8,128)(2,1)S(1)}) custom-call(f32[3,16,128]{2,1,0:T(8,128)S(1)} %get-tuple-element.27.masks_ref, f32[9,2880]{1,0:T(8,128)S(1)} %copy-done.2, f32[9,2,2880]{2,1,0:T(2,128)S(1)} %bitcast.6, bf16[3,9,2880]{2,1,0:T(8,128)(2,1)S(1)} %copy.11.q_ref, ...), custom_call_target="tpu_custom_call" | custom-call | tf_op jit(solution)/shard_map/rest/pallas_call | solution.py:655
  19.0 0.8 %copy.12 = bf16[3,9,2880]{2,0,1:T(4,128)(2,1)} copy(bf16[3,9,2880]{2,1,0:T(8,128)(2,1)S(1)} %get-tuple-element.45) | data formatting | bytes 311040
  19.8 0.4 %collective-permute-done.9.refs_3_ = f32[144,128]{1,0:T(8,128)S(1)} collective-permute-done((f32[144,128]{1,0:T(8,128)S(1)}, f32[144,128]{1,0:T(8,128)S(1)}, u32[]{:S(2)}, u32[]{:S(2)}) %collective-permute-start.9) | collective-permute-done | bytes 73760 | tf_op jit(solution)/shard_map/ppermute | solution.py:617
  20.1 0.9 %finish.1 = (f32[9,2,2880]{2,1,0:T(2,128)}, f32[9,2880]{1,0:T(8,128)}) custom-call(f32[3,16,128]{2,1,0:T(8,128)S(1)} %get-tuple-element.27.masks_ref, f32[2,9,2880]{2,1,0:T(8,128)S(1)} %get-tuple-element.35.base_w_ref, f32[9,2880]{1,0:T(8,128)S(1)} %get-tuple-element.36.base_h_ref, f32[144,128]{1,0:T(8,128)S(1)} %get-tuple-element.34.after_ref.refs_0_, ...), custom_call_target="tpu_custom_call" | custom-call | tf_op jit(solution)/shard_map/finish/pallas_call | solution.py:663
  (21 shorter events, 0.1 us)
Async XLA Ops:
  0.6 2.2 %copy-start.3 = (f32[2,24,128]{2,1,0:T(8,128)S(1)}, f32[2,24,128]{2,1,0:T(8,128)}, u32[]{:S(2)}) copy-start(f32[2,24,128]{2,1,0:T(8,128)} %constant.9.clone.wave_ref) | copy-start | bytes 73732
  0.6 2.2 %collective-permute-start.1 = (f32[9,2,2880]{2,1,0:T(2,128)}, f32[9,2,2880]{2,1,0:T(2,128)S(1)}, u32[]{:S(2)}, u32[]{:S(2)}) collective-permute-start(f32[9,2,2880]{2,1,0:T(2,128)} %bitcast.3), channel_id=1, source_target_pairs={{0,4},{1,5},{2,6},{3,7},{4,0},{5,1},{6,2},{7,3},{8,12},{9,13},{10,... | collective-permute-start | bytes 622088 | tf_op jit(solution)/shard_map/ppermute | solution.py:608
  1.2 1.6 %collective-permute-start = (f32[9,2880]{1,0:T(8,128)}, f32[9,2880]{1,0:T(8,128)S(1)}, u32[]{:S(2)}, u32[]{:S(2)}) collective-permute-start(f32[9,2880]{1,0:T(8,128)} %h_ref.3), channel_id=1, source_target_pairs={{0,4},{1,5},{2,6},{3,7},{4,0},{5,1},{6,2},{7,3},{8,12},{9,13},{10,... | collective-permute-start | bytes 311048 | tf_op jit(solution)/shard_map/ppermute | solution.py:607
  1.2 1.6 %copy-start = (f32[2,9,2880]{2,0,1:T(2,128)S(1)}, f32[2,9,2880]{2,0,1:T(2,128)}, u32[]{:S(2)}) copy-start(f32[2,9,2880]{2,0,1:T(2,128)} %param.8) | copy-start | bytes 622084
  1.2 1.6 %copy-start.1 = (f32[8,3,16,128]{3,2,1,0:T(8,128)S(1)}, f32[8,3,16,128]{3,2,1,0:T(8,128)}, u32[]{:S(2)}) copy-start(f32[8,3,16,128]{3,2,1,0:T(8,128)} %constant.8.clone.geo_ref) | copy-start | bytes 589828
  1.2 1.6 %copy-start.2 = (f32[9,2880]{1,0:T(8,128)S(1)}, f32[9,2880]{1,0:T(8,128)}, u32[]{:S(2)}) copy-start(f32[9,2880]{1,0:T(8,128)} %h_ref.3) | copy-start | bytes 311044
  2.8 7.3 %copy-start.4 = (f32[192,96]{1,0:T(8,128)S(1)}, f32[192,96]{1,0:T(8,128)}, u32[]{:S(2)}) copy-start(f32[192,96]{1,0:T(8,128)} %constant.11.clone.inverse_ref) | copy-start | bytes 221188
  2.8 7.2 %copy-start.5 = (f32[192,96]{1,0:T(8,128)S(1)}, f32[192,96]{1,0:T(8,128)}, u32[]{:S(2)}) copy-start(f32[192,96]{1,0:T(8,128)} %constant.10.clone.n_ref) | copy-start | bytes 221188
  3.5 8.2 %collective-permute-start.4 = (f32[160,128]{1,0:T(8,128)S(1)}, f32[160,128]{1,0:T(8,128)S(1)}, u32[]{:S(2)}, u32[]{:S(2)}) collective-permute-start(f32[160,128]{1,0:T(8,128)S(1)} %get-tuple-element.31), channel_id=1, source_target_pairs={{0,3},{1,2},{2,1},{3,0},{4,6},{5,7},{6,4},{7,5},{8,11},{9,10},{10,... | collective-permute-start | bytes 245768 | tf_op jit(solution)/shard_map/ppermute | solution.py:617
  7.4 4.9 %collective-permute-start.5 = (f32[160,128]{1,0:T(8,128)S(1)}, f32[160,128]{1,0:T(8,128)S(1)}, u32[]{:S(2)}, u32[]{:S(2)}) collective-permute-start(f32[160,128]{1,0:T(8,128)S(1)} %get-tuple-element.32), channel_id=1, source_target_pairs={{0,1},{1,0},{2,3},{3,2},{4,7},{5,6},{6,5},{7,4},{8,9},{9,8},{10,11... | collective-permute-start | bytes 245768 | tf_op jit(solution)/shard_map/ppermute | solution.py:617
  7.9 4.4 %collective-permute-start.6 = (f32[160,128]{1,0:T(8,128)S(1)}, f32[160,128]{1,0:T(8,128)S(1)}, u32[]{:S(2)}, u32[]{:S(2)}) collective-permute-start(f32[160,128]{1,0:T(8,128)S(1)} %get-tuple-element.33), channel_id=1, source_target_pairs={{0,2},{1,3},{2,0},{3,1},{4,5},{5,4},{6,7},{7,6},{8,10},{9,11},{10,... | collective-permute-start | bytes 245768 | tf_op jit(solution)/shard_map/ppermute | solution.py:617
  8.0 7.5 %collective-permute-start.3 = (f32[120,128]{1,0:T(8,128)S(1)}, f32[120,128]{1,0:T(8,128)S(1)}, u32[]{:S(2)}, u32[]{:S(2)}) collective-permute-start(f32[120,128]{1,0:T(8,128)S(1)} %get-tuple-element.29), channel_id=1, source_target_pairs={{0,2},{1,3},{2,0},{3,1},{4,8},{5,9},{6,10},{7,11},{8,4},{9,5},{10,... | collective-permute-start | bytes 184328 | tf_op jit(solution)/shard_map/ppermute | solution.py:634
  9.9 0.7 %copy-start.6 = (s32[72]{0:T(128)S(1)}, s32[72]{0:T(128)}, u32[]{:S(2)}) copy-start(s32[72]{0:T(128)} %cut_ref.1) | copy-start | bytes 868
  9.9 5.6 %collective-permute-start.2 = (f32[72,128]{1,0:T(8,128)S(1)}, f32[72,128]{1,0:T(8,128)S(1)}, u32[]{:S(2)}, u32[]{:S(2)}) collective-permute-start(f32[72,128]{1,0:T(8,128)S(1)} %get-tuple-element.28), channel_id=1, source_target_pairs={{0,4},{1,5},{2,6},{3,7},{4,0},{5,1},{6,2},{7,3},{8,12},{9,13},{10,... | collective-permute-start | bytes 110600 | tf_op jit(solution)/shard_map/ppermute | solution.py:633
  13.3 3.7 %copy-start.7 = (bf16[3,9,2880]{2,0,1:T(4,128)(2,1)S(1)}, bf16[3,9,2880]{2,0,1:T(4,128)(2,1)}, u32[]{:S(2)}) copy-start(bf16[3,9,2880]{2,0,1:T(4,128)(2,1)} %param.10) | copy-start | bytes 466564
  13.3 6.4 %collective-permute-start.7 = (f32[144,128]{1,0:T(8,128)S(1)}, f32[144,128]{1,0:T(8,128)S(1)}, u32[]{:S(2)}, u32[]{:S(2)}) collective-permute-start(f32[144,128]{1,0:T(8,128)S(1)} %get-tuple-element.37), channel_id=1, source_target_pairs={{0,3},{1,2},{2,1},{3,0},{4,7},{5,6},{6,5},{7,4},{8,11},{9,10},{10,... | collective-permute-start | bytes 221192 | tf_op jit(solution)/shard_map/ppermute | solution.py:617
  15.2 4.6 %collective-permute-start.8 = (f32[144,128]{1,0:T(8,128)S(1)}, f32[144,128]{1,0:T(8,128)S(1)}, u32[]{:S(2)}, u32[]{:S(2)}) collective-permute-start(f32[144,128]{1,0:T(8,128)S(1)} %get-tuple-element.38), channel_id=1, source_target_pairs={{0,1},{1,0},{2,3},{3,2},{4,6},{5,7},{6,4},{7,5},{8,9},{9,8},{10,11... | collective-permute-start | bytes 221192 | tf_op jit(solution)/shard_map/ppermute | solution.py:617
  15.5 4.6 %collective-permute-start.9 = (f32[144,128]{1,0:T(8,128)S(1)}, f32[144,128]{1,0:T(8,128)S(1)}, u32[]{:S(2)}, u32[]{:S(2)}) collective-permute-start(f32[144,128]{1,0:T(8,128)S(1)} %pass.1), channel_id=1, source_target_pairs={{0,2},{1,3},{2,0},{3,1},{4,5},{5,4},{6,7},{7,6},{8,10},{9,11},{10,... | collective-permute-start | bytes 221192 | tf_op jit(solution)/shard_map/ppermute | solution.py:617

commit v18 on v15

--- a/solution.py
+++ b/solution.py
@@ -54,7 +54,7 @@
 
     def turns(self, odd):
         middle, last = list(range(1, self.n_lon - 1)), self.n_lon - 1
-        return [0, middle[-1], last] + middle[-2::-1] if odd else [0, last] + middle
+        return [0, last] + middle if odd else [0, middle[-1], last] + middle[-2::-1]
 
     def partner(self, k):
         odd = lax.rem(lax.axis_index("lat"), 2) == 1
@@ -261,9 +261,9 @@
     for f in range(3):
         for t in range(tiles, stack):
             tend_ref[pl.ds(stack * work * f + t, work, stride=stack), :] = jnp.zeros((work, LANES), jnp.float32)
-    used = stack * sz.units
-    if used < tend_ref.shape[0]:
-        tend_ref[used:, :] = jnp.zeros((tend_ref.shape[0] - used, LANES), jnp.float32)
+    used, sent = stack * sz.units, sz.n_lon * sz.size
+    if used < sent:
+        tend_ref[used:sent, :] = jnp.zeros((sent - used, LANES), jnp.float32)
     sides = [sides_ref[:EXT_ROWS], sides_ref[EXT_ROWS:]]
     if sz.near_only:
         sums = pole_sums(sz, pole_ref, wave_ref, spare, band)
@@ -473,7 +473,7 @@
     n_lon, stack, share = sz.n_lon, sz.stack, sz.share
     in_refs, out_refs, (gathered, results) = refs[:n_lon], refs[n_lon : 2 * n_lon], refs[2 * n_lon :]
     for k, in_ref in enumerate(in_refs):
-        gathered[sz.partner(k)] = in_ref[: sz.size]
+        gathered[sz.partner(k), : sz.size] = in_ref[: sz.size]
 
     band = lax.axis_index("lat")
     lane = lax.broadcasted_iota(jnp.int32, (share, LANES), 1)
@@ -520,7 +520,7 @@
                 carried = over if carried is None else carried + over
             results[s, here] = pltpu.roll(same, stack - 1, 0) + carried
     for k, out_ref in enumerate(out_refs):
-        out_ref[...] = results[sz.partner(k)]
+        out_ref[...] = results[sz.partner(k), : sz.size]
 
 
 def finish_kernel(sz, masks_ref, base_w_ref, base_h_ref, *refs):
@@ -616,14 +616,15 @@
             got.append(lax.ppermute(shares[k], ("lat", "lon"), [(b * n_lon + i, b * n_lon + j) for b, i, j in sectors]))
         return got
 
-    all_pieces = pltpu.VMEM((n_lon, sz.size, LANES), f32)
+    all_pieces = pltpu.VMEM((n_lon, sz.size + 8 * sz.stack, LANES), f32)
+    all_units = pltpu.VMEM((n_lon * sz.size + 8 * sz.stack, LANES), f32)
     *tends, far_rows, near_q = call(
         polar_kernel,
         "polar",
         [vmem] * 9,
         [shaped(sz.size + EXT_ROWS, LANES)] * n_lon + [far_row, near_row],
         [
-            pltpu.VMEM((n_lon * sz.size, LANES), f32),
+            all_units,
             pltpu.VMEM((4 * sz.stack, LANES), f32),
             pltpu.VMEM((3, EXT_ROWS, sz.tiles * LANES), f32),
         ],
@@ -664,7 +665,7 @@
         "finish",
         [vmem] * (3 + n_lon),
         (shaped(*wind_rows.shape), shaped(rows, merged)),
-        [pltpu.VMEM((n_lon * sz.size, LANES), f32)],
+        [all_units],
     )(masks, base_w, base_h, *back)
     return jnp.swapaxes(new_w, 0, 1), new_h, mass
 

time: 21.2 us -> 21.7 us (1.024)
  waiting for transfers between devices: 1.32 us -> 1.84 us
    ppermute x6, waiting for transfers between devices: 0.93 us -> 1.46 us  [meetings(): lax.ppermute(shares[k], ('lat', 'lon'), [(b * n_lon + i, b * n_lon + j) f...]
where the time goes in v18:
time: 21.7 us; the launch traced here: 21.6 us
  starting transfers between devices  10.8 us (50%)
  Pallas kernels  6.89 us (32%)
  waiting for transfers between devices  1.84 us (8%)
  local copies, waits for them, and re-layouts  1.32 us (6%)
  between operations  0.75 us (3%)
    ppermute x6, starting transfers between devices, meetings(): lax.ppermute(shares[k], ('lat', 'lon'), [(b * n_lon + i, b * n_lon + j) f...  8.04 us
    pallas_call x1, Pallas kernels, local(): call(rest_kernel, 'rest', [vmem] * 10 + [anywhere] + [vmem] * n_lon, (sha...  1.99 us
    ppermute x1, starting transfers between devices, local(): lax.ppermute(far_rows, ('lat', 'lon'), far)  1.95 us
    ppermute x6, waiting for transfers between devices, meetings(): lax.ppermute(shares[k], ('lat', 'lon'), [(b * n_lon + i, b * n_lon + j) f...  1.46 us
    unnamed x18, local copies, waits for them, and re-layouts  1.32 us
    pallas_call x1, Pallas kernels, local(): call(edges_kernel, 'edges', [hbm] * 3, (near_row, far_row, shaped(2 * EXT...  1.17 us
    pallas_call x1, Pallas kernels, local(): call(weights_kernel, 'weights', [smem, vmem, vmem, anywhere], (jax.ShapeD...  1.15 us
    pallas_call x1, Pallas kernels, local(): call(filter_kernel, 'filter', [vmem] * 2 + [vmem] * n_lon, [shaped(sz.siz...  0.98 us
  transfers between devices with their start and end apart: 10, of which 5 were waited for; matrix products, arithmetic and copies ran while one was open for 4% of the time, Pallas kernels for 25%

profile of v18, /device:TPU:0, one launch (start us, length us, event | category | flops | bytes accessed | tf_op | source)
XLA Modules:
  0.0 21.6 jit_solution(11180723127055189994)
XLA Ops:
  0.6 0.5 %collective-permute-start.1 = (f32[9,2,2880]{2,1,0:T(2,128)}, f32[9,2,2880]{2,1,0:T(2,128)S(1)}, u32[]{:S(2)}, u32[]{:S(2)}) collective-permute-start(f32[9,2,2880]{2,1,0:T(2,128)} %bitcast.3), channel_id=1, source_target_pairs={{0,4},{1,5},{2,6},{3,7},{4,0},{5,1},{6,2},{7,3},{8,12},{9,13},{10,... | collective-permute-start | bytes 622088 | tf_op jit(solution)/shard_map/ppermute | solution.py:606
  1.2 0.1 collective-permute-start
  1.2 1.2 %edges.1 = (f32[72,128]{1,0:T(8,128)S(1)}, f32[120,128]{1,0:T(8,128)S(1)}, f32[32,128]{1,0:T(8,128)S(1)}) custom-call(f32[9,2880]{1,0:T(8,128)} %h_ref.3, f32[9,2,2880]{2,1,0:T(2,128)} %bitcast.4, bf16[9,3,2880]{2,1,0:T(4,128)(2,1)} %bitcast.7), custom_call_target="tpu_custom_call" | custom-call | tf_op jit(solution)/shard_map/edges/pallas_call | solution.py:581
  2.4 0.4 %collective-permute-done.near_h_ref = f32[9,2880]{1,0:T(8,128)S(1)} collective-permute-done((f32[9,2880]{1,0:T(8,128)}, f32[9,2880]{1,0:T(8,128)S(1)}, u32[]{:S(2)}, u32[]{:S(2)}) %collective-permute-start) | collective-permute-done | bytes 103712 | tf_op jit(solution)/shard_map/ppermute | solution.py:605
  2.8 0.0 copy-start.4
  2.9 0.7 %polar.1 = (f32[160,128]{1,0:T(8,128)S(1)}, f32[160,128]{1,0:T(8,128)S(1)}, f32[160,128]{1,0:T(8,128)S(1)}, f32[160,128]{1,0:T(8,128)S(1)}, f32[120,128]{1,0:T(8,128)S(1)}, /*index=5*/f32[72,128]{1,0:T(8,128)S(1)}) custom-call(f32[9,2880]{1,0:T(8,128)S(1)} %copy-done.2, f32[9,2,2880]{2,1,0:T(2,128)S(1)} %bitcast.5, ...), custom_call_target="tpu_custom_call" | custom-call | tf_op jit(solution)/shard_map/polar/pallas_call | solution.py:621
  3.5 2.9 %collective-permute-start.4 = (f32[160,128]{1,0:T(8,128)S(1)}, f32[160,128]{1,0:T(8,128)S(1)}, u32[]{:S(2)}, u32[]{:S(2)}) collective-permute-start(f32[160,128]{1,0:T(8,128)S(1)} %get-tuple-element.31), channel_id=1, source_target_pairs={{0,2},{1,3},{2,0},{3,1},{4,7},{5,6},{6,5},{7,4},{8,10},{9,11},{10,... | collective-permute-start | bytes 245768 | tf_op jit(solution)/shard_map/ppermute | solution.py:616
  6.4 1.4 %collective-permute-start.5 = (f32[160,128]{1,0:T(8,128)S(1)}, f32[160,128]{1,0:T(8,128)S(1)}, u32[]{:S(2)}, u32[]{:S(2)}) collective-permute-start(f32[160,128]{1,0:T(8,128)S(1)} %get-tuple-element.32), channel_id=1, source_target_pairs={{0,3},{1,2},{2,1},{3,0},{4,5},{5,4},{6,7},{7,6},{8,11},{9,10},{10,... | collective-permute-start | bytes 245768 | tf_op jit(solution)/shard_map/ppermute | solution.py:616
  7.9 0.1 collective-permute-start.6
  8.0 1.9 %collective-permute-start.3 = (f32[120,128]{1,0:T(8,128)S(1)}, f32[120,128]{1,0:T(8,128)S(1)}, u32[]{:S(2)}, u32[]{:S(2)}) collective-permute-start(f32[120,128]{1,0:T(8,128)S(1)} %get-tuple-element.29), channel_id=1, source_target_pairs={{0,2},{1,3},{2,0},{3,1},{4,8},{5,9},{6,10},{7,11},{8,4},{9,5},{10,... | collective-permute-start | bytes 184328 | tf_op jit(solution)/shard_map/ppermute | solution.py:634
  9.9 0.2 collective-permute-start.2
  10.1 0.5 %copy-done.6 = s32[72]{0:T(128)S(1)} copy-done((s32[72]{0:T(128)S(1)}, s32[72]{0:T(128)}, u32[]{:S(2)}) %copy-start.6) | copy-done | bytes 312
  10.6 1.1 %weights.1 = (bf16[1152,96]{1,0:T(8,128)(2,1)S(1)}, f32[3,16,128]{2,1,0:T(8,128)S(1)}) custom-call(s32[72]{0:T(128)S(1)} %copy-done.6, f32[192,96]{1,0:T(8,128)S(1)} %copy-done.5, f32[192,96]{1,0:T(8,128)S(1)} %copy-done.4, f32[160,128]{1,0:T(8,128)S(1)} %get-tuple-element.26.after_ref.refs_0_), custom_call_target="tpu_custom_call" | custom-call | tf_op jit(solution)/shard_map/weights/pallas_call | solution.py:635
  11.7 0.1 collective-permute-done.5.refs_2_
  11.9 0.4 %collective-permute-done.6.refs_3_ = f32[160,128]{1,0:T(8,128)S(1)} collective-permute-done((f32[160,128]{1,0:T(8,128)S(1)}, f32[160,128]{1,0:T(8,128)S(1)}, u32[]{:S(2)}, u32[]{:S(2)}) %collective-permute-start.6) | collective-permute-done | bytes 81952 | tf_op jit(solution)/shard_map/ppermute | solution.py:616
  12.3 1.0 %filter.1 = (f32[144,128]{1,0:T(8,128)S(1)}, f32[144,128]{1,0:T(8,128)S(1)}, f32[144,128]{1,0:T(8,128)S(1)}, f32[144,128]{1,0:T(8,128)S(1)}) custom-call(bf16[1152,96]{1,0:T(8,128)(2,1)S(1)} %get-tuple-element.30.weights_ref, f32[8,3,16,128]{3,2,1,0:T(8,128)S(1)} %copy-done.1, f32[160,128]{1,0:T(8,128)S(1)} %get-tuple-element.26.after_ref.refs_0_, ...), custom_call_target="tpu_custom_call" | custom-call | tf_op jit(solution)/shard_map/filter/pallas_call | solution.py:644
  13.3 1.6 %collective-permute-start.7 = (f32[144,128]{1,0:T(8,128)S(1)}, f32[144,128]{1,0:T(8,128)S(1)}, u32[]{:S(2)}, u32[]{:S(2)}) collective-permute-start(f32[144,128]{1,0:T(8,128)S(1)} %get-tuple-element.37), channel_id=1, source_target_pairs={{0,2},{1,3},{2,0},{3,1},{4,7},{5,6},{6,5},{7,4},{8,10},{9,11},{10,... | collective-permute-start | bytes 221192 | tf_op jit(solution)/shard_map/ppermute | solution.py:616
  14.9 1.3 %collective-permute-start.8 = (f32[144,128]{1,0:T(8,128)S(1)}, f32[144,128]{1,0:T(8,128)S(1)}, u32[]{:S(2)}, u32[]{:S(2)}) collective-permute-start(f32[144,128]{1,0:T(8,128)S(1)} %get-tuple-element.38), channel_id=1, source_target_pairs={{0,3},{1,2},{2,1},{3,0},{4,5},{5,4},{6,7},{7,6},{8,11},{9,10},{10,... | collective-permute-start | bytes 221192 | tf_op jit(solution)/shard_map/ppermute | solution.py:616
  16.2 0.7 %collective-permute-start.9 = (f32[144,128]{1,0:T(8,128)S(1)}, f32[144,128]{1,0:T(8,128)S(1)}, u32[]{:S(2)}, u32[]{:S(2)}) collective-permute-start(f32[144,128]{1,0:T(8,128)S(1)} %pass.1), channel_id=1, source_target_pairs={{0,1},{1,0},{2,3},{3,2},{4,6},{5,7},{6,4},{7,5},{8,9},{9,8},{10,11... | collective-permute-start | bytes 221192 | tf_op jit(solution)/shard_map/ppermute | solution.py:616
  17.0 2.0 %rest.1 = (f32[2,9,2880]{2,1,0:T(8,128)S(1)}, f32[9,2880]{1,0:T(8,128)S(1)}, bf16[3,9,2880]{2,1,0:T(8,128)(2,1)S(1)}) custom-call(f32[3,16,128]{2,1,0:T(8,128)S(1)} %get-tuple-element.27.masks_ref, f32[9,2880]{1,0:T(8,128)S(1)} %copy-done.2, f32[9,2,2880]{2,1,0:T(2,128)S(1)} %bitcast.6, bf16[3,9,2880]{2,1,0:T(8,128)(2,1)S(1)} %copy.11.q_ref, ...), custom_call_target="tpu_custom_call" | custom-call | tf_op jit(solution)/shard_map/rest/pallas_call | solution.py:655
  19.0 0.8 %copy.12 = bf16[3,9,2880]{2,0,1:T(4,128)(2,1)} copy(bf16[3,9,2880]{2,1,0:T(8,128)(2,1)S(1)} %get-tuple-element.45) | data formatting | bytes 311040
  19.7 0.4 %collective-permute-done.8.refs_2_ = f32[144,128]{1,0:T(8,128)S(1)} collective-permute-done((f32[144,128]{1,0:T(8,128)S(1)}, f32[144,128]{1,0:T(8,128)S(1)}, u32[]{:S(2)}, u32[]{:S(2)}) %collective-permute-start.8) | collective-permute-done | bytes 73760 | tf_op jit(solution)/shard_map/ppermute | solution.py:616
  20.1 0.5 %collective-permute-done.9.refs_3_ = f32[144,128]{1,0:T(8,128)S(1)} collective-permute-done((f32[144,128]{1,0:T(8,128)S(1)}, f32[144,128]{1,0:T(8,128)S(1)}, u32[]{:S(2)}, u32[]{:S(2)}) %collective-permute-start.9) | collective-permute-done | bytes 73760 | tf_op jit(solution)/shard_map/ppermute | solution.py:616
  20.6 0.9 %finish.1 = (f32[9,2,2880]{2,1,0:T(2,128)}, f32[9,2880]{1,0:T(8,128)}) custom-call(f32[3,16,128]{2,1,0:T(8,128)S(1)} %get-tuple-element.27.masks_ref, f32[2,9,2880]{2,1,0:T(8,128)S(1)} %get-tuple-element.35.base_w_ref, f32[9,2880]{1,0:T(8,128)S(1)} %get-tuple-element.36.base_h_ref, f32[144,128]{1,0:T(8,128)S(1)} %get-tuple-element.34.after_ref.refs_0_, ...), custom_call_target="tpu_custom_call" | custom-call | tf_op jit(solution)/shard_map/finish/pallas_call | solution.py:663
  (21 shorter events, 0.1 us)
Async XLA Ops:
  0.6 2.2 %copy-start.3 = (f32[2,24,128]{2,1,0:T(8,128)S(1)}, f32[2,24,128]{2,1,0:T(8,128)}, u32[]{:S(2)}) copy-start(f32[2,24,128]{2,1,0:T(8,128)} %constant.9.clone.wave_ref) | copy-start | bytes 73732
  0.6 2.2 %collective-permute-start.1 = (f32[9,2,2880]{2,1,0:T(2,128)}, f32[9,2,2880]{2,1,0:T(2,128)S(1)}, u32[]{:S(2)}, u32[]{:S(2)}) collective-permute-start(f32[9,2,2880]{2,1,0:T(2,128)} %bitcast.3), channel_id=1, source_target_pairs={{0,4},{1,5},{2,6},{3,7},{4,0},{5,1},{6,2},{7,3},{8,12},{9,13},{10,... | collective-permute-start | bytes 622088 | tf_op jit(solution)/shard_map/ppermute | solution.py:606
  1.2 1.6 %collective-permute-start = (f32[9,2880]{1,0:T(8,128)}, f32[9,2880]{1,0:T(8,128)S(1)}, u32[]{:S(2)}, u32[]{:S(2)}) collective-permute-start(f32[9,2880]{1,0:T(8,128)} %h_ref.3), channel_id=1, source_target_pairs={{0,4},{1,5},{2,6},{3,7},{4,0},{5,1},{6,2},{7,3},{8,12},{9,13},{10,... | collective-permute-start | bytes 311048 | tf_op jit(solution)/shard_map/ppermute | solution.py:605
  1.2 1.6 %copy-start = (f32[2,9,2880]{2,0,1:T(2,128)S(1)}, f32[2,9,2880]{2,0,1:T(2,128)}, u32[]{:S(2)}) copy-start(f32[2,9,2880]{2,0,1:T(2,128)} %param.8) | copy-start | bytes 622084
  1.2 1.6 %copy-start.1 = (f32[8,3,16,128]{3,2,1,0:T(8,128)S(1)}, f32[8,3,16,128]{3,2,1,0:T(8,128)}, u32[]{:S(2)}) copy-start(f32[8,3,16,128]{3,2,1,0:T(8,128)} %constant.8.clone.geo_ref) | copy-start | bytes 589828
  1.2 1.6 %copy-start.2 = (f32[9,2880]{1,0:T(8,128)S(1)}, f32[9,2880]{1,0:T(8,128)}, u32[]{:S(2)}) copy-start(f32[9,2880]{1,0:T(8,128)} %h_ref.3) | copy-start | bytes 311044
  2.8 7.3 %copy-start.4 = (f32[192,96]{1,0:T(8,128)S(1)}, f32[192,96]{1,0:T(8,128)}, u32[]{:S(2)}) copy-start(f32[192,96]{1,0:T(8,128)} %constant.11.clone.inverse_ref) | copy-start | bytes 221188
  2.8 7.2 %copy-start.5 = (f32[192,96]{1,0:T(8,128)S(1)}, f32[192,96]{1,0:T(8,128)}, u32[]{:S(2)}) copy-start(f32[192,96]{1,0:T(8,128)} %constant.10.clone.n_ref) | copy-start | bytes 221188
  3.5 8.2 %collective-permute-start.4 = (f32[160,128]{1,0:T(8,128)S(1)}, f32[160,128]{1,0:T(8,128)S(1)}, u32[]{:S(2)}, u32[]{:S(2)}) collective-permute-start(f32[160,128]{1,0:T(8,128)S(1)} %get-tuple-element.31), channel_id=1, source_target_pairs={{0,2},{1,3},{2,0},{3,1},{4,7},{5,6},{6,5},{7,4},{8,10},{9,11},{10,... | collective-permute-start | bytes 245768 | tf_op jit(solution)/shard_map/ppermute | solution.py:616
  6.4 5.4 %collective-permute-start.5 = (f32[160,128]{1,0:T(8,128)S(1)}, f32[160,128]{1,0:T(8,128)S(1)}, u32[]{:S(2)}, u32[]{:S(2)}) collective-permute-start(f32[160,128]{1,0:T(8,128)S(1)} %get-tuple-element.32), channel_id=1, source_target_pairs={{0,3},{1,2},{2,1},{3,0},{4,5},{5,4},{6,7},{7,6},{8,11},{9,10},{10,... | collective-permute-start | bytes 245768 | tf_op jit(solution)/shard_map/ppermute | solution.py:616
  7.9 4.4 %collective-permute-start.6 = (f32[160,128]{1,0:T(8,128)S(1)}, f32[160,128]{1,0:T(8,128)S(1)}, u32[]{:S(2)}, u32[]{:S(2)}) collective-permute-start(f32[160,128]{1,0:T(8,128)S(1)} %get-tuple-element.33), channel_id=1, source_target_pairs={{0,1},{1,0},{2,3},{3,2},{4,6},{5,7},{6,4},{7,5},{8,9},{9,8},{10,11... | collective-permute-start | bytes 245768 | tf_op jit(solution)/shard_map/ppermute | solution.py:616
  8.0 8.2 %collective-permute-start.3 = (f32[120,128]{1,0:T(8,128)S(1)}, f32[120,128]{1,0:T(8,128)S(1)}, u32[]{:S(2)}, u32[]{:S(2)}) collective-permute-start(f32[120,128]{1,0:T(8,128)S(1)} %get-tuple-element.29), channel_id=1, source_target_pairs={{0,2},{1,3},{2,0},{3,1},{4,8},{5,9},{6,10},{7,11},{8,4},{9,5},{10,... | collective-permute-start | bytes 184328 | tf_op jit(solution)/shard_map/ppermute | solution.py:634
  9.9 0.7 %copy-start.6 = (s32[72]{0:T(128)S(1)}, s32[72]{0:T(128)}, u32[]{:S(2)}) copy-start(s32[72]{0:T(128)} %cut_ref.1) | copy-start | bytes 868
  9.9 6.3 %collective-permute-start.2 = (f32[72,128]{1,0:T(8,128)S(1)}, f32[72,128]{1,0:T(8,128)S(1)}, u32[]{:S(2)}, u32[]{:S(2)}) collective-permute-start(f32[72,128]{1,0:T(8,128)S(1)} %get-tuple-element.28), channel_id=1, source_target_pairs={{0,4},{1,5},{2,6},{3,7},{4,0},{5,1},{6,2},{7,3},{8,12},{9,13},{10,... | collective-permute-start | bytes 110600 | tf_op jit(solution)/shard_map/ppermute | solution.py:633
  13.3 3.6 %copy-start.7 = (bf16[3,9,2880]{2,0,1:T(4,128)(2,1)S(1)}, bf16[3,9,2880]{2,0,1:T(4,128)(2,1)}, u32[]{:S(2)}) copy-start(bf16[3,9,2880]{2,0,1:T(4,128)(2,1)} %param.10) | copy-start | bytes 466564
  13.3 6.4 %collective-permute-start.7 = (f32[144,128]{1,0:T(8,128)S(1)}, f32[144,128]{1,0:T(8,128)S(1)}, u32[]{:S(2)}, u32[]{:S(2)}) collective-permute-start(f32[144,128]{1,0:T(8,128)S(1)} %get-tuple-element.37), channel_id=1, source_target_pairs={{0,2},{1,3},{2,0},{3,1},{4,7},{5,6},{6,5},{7,4},{8,10},{9,11},{10,... | collective-permute-start | bytes 221192 | tf_op jit(solution)/shard_map/ppermute | solution.py:616
  14.9 5.3 %collective-permute-start.8 = (f32[144,128]{1,0:T(8,128)S(1)}, f32[144,128]{1,0:T(8,128)S(1)}, u32[]{:S(2)}, u32[]{:S(2)}) collective-permute-start(f32[144,128]{1,0:T(8,128)S(1)} %get-tuple-element.38), channel_id=1, source_target_pairs={{0,3},{1,2},{2,1},{3,0},{4,5},{5,4},{6,7},{7,6},{8,11},{9,10},{10,... | collective-permute-start | bytes 221192 | tf_op jit(solution)/shard_map/ppermute | solution.py:616
  16.2 4.4 %collective-permute-start.9 = (f32[144,128]{1,0:T(8,128)S(1)}, f32[144,128]{1,0:T(8,128)S(1)}, u32[]{:S(2)}, u32[]{:S(2)}) collective-permute-start(f32[144,128]{1,0:T(8,128)S(1)} %pass.1), channel_id=1, source_target_pairs={{0,1},{1,0},{2,3},{3,2},{4,6},{5,7},{6,4},{7,5},{8,9},{9,8},{10,11... | collective-permute-start | bytes 221192 | tf_op jit(solution)/shard_map/ppermute | solution.py:616

commit v19 on v18

--- a/solution.py
+++ b/solution.py
@@ -54,7 +54,7 @@
 
     def turns(self, odd):
         middle, last = list(range(1, self.n_lon - 1)), self.n_lon - 1
-        return [0, last] + middle if odd else [0, middle[-1], last] + middle[-2::-1]
+        return [0, middle[0], last] + middle[1:] if odd else [0, last] + middle[::-1]
 
     def partner(self, k):
         odd = lax.rem(lax.axis_index("lat"), 2) == 1

time: 21.7 us -> 22.6 us (1.041)
  waiting for transfers between devices: 1.84 us -> 2.71 us
    ppermute x6, waiting for transfers between devices: 1.46 us -> 2.32 us  [meetings(): lax.ppermute(shares[k], ('lat', 'lon'), [(b * n_lon + i, b * n_lon + j) f...]
  transfers between devices with their start and end apart: 10 -> 10, of which waited for: 5 -> 4; matrix products, arithmetic and copies ran while one was open for 4% -> 4% of each run, Pallas kernels for 25% -> 24%
where the time goes in v19:
time: 22.6 us; the launch traced here: 22.4 us
  starting transfers between devices  10.8 us (48%)
  Pallas kernels  6.89 us (30%)
  waiting for transfers between devices  2.71 us (12%)
  local copies, waits for them, and re-layouts  1.32 us (6%)
  between operations  0.75 us (3%)
    ppermute x6, starting transfers between devices, meetings(): lax.ppermute(shares[k], ('lat', 'lon'), [(b * n_lon + i, b * n_lon + j) f...  8.07 us
    ppermute x6, waiting for transfers between devices, meetings(): lax.ppermute(shares[k], ('lat', 'lon'), [(b * n_lon + i, b * n_lon + j) f...  2.32 us
    pallas_call x1, Pallas kernels, local(): call(rest_kernel, 'rest', [vmem] * 10 + [anywhere] + [vmem] * n_lon, (sha...  1.99 us
    ppermute x1, starting transfers between devices, local(): lax.ppermute(far_rows, ('lat', 'lon'), far)  1.92 us
    unnamed x18, local copies, waits for them, and re-layouts  1.32 us
    pallas_call x1, Pallas kernels, local(): call(edges_kernel, 'edges', [hbm] * 3, (near_row, far_row, shaped(2 * EXT...  1.17 us
    pallas_call x1, Pallas kernels, local(): call(weights_kernel, 'weights', [smem, vmem, vmem, anywhere], (jax.ShapeD...  1.15 us
    pallas_call x1, Pallas kernels, local(): call(filter_kernel, 'filter', [vmem] * 2 + [vmem] * n_lon, [shaped(sz.siz...  0.99 us
  transfers between devices with their start and end apart: 10, of which 4 were waited for; matrix products, arithmetic and copies ran while one was open for 4% of the time, Pallas kernels for 24%

profile of v19, /device:TPU:0, one launch (start us, length us, event | category | flops | bytes accessed | tf_op | source)
XLA Modules:
  0.0 22.4 jit_solution(3108129549252421526)
XLA Ops:
  0.6 0.0 copy-start.3
  0.6 0.5 %collective-permute-start.1 = (f32[9,2,2880]{2,1,0:T(2,128)}, f32[9,2,2880]{2,1,0:T(2,128)S(1)}, u32[]{:S(2)}, u32[]{:S(2)}) collective-permute-start(f32[9,2,2880]{2,1,0:T(2,128)} %bitcast.3), channel_id=1, source_target_pairs={{0,4},{1,5},{2,6},{3,7},{4,0},{5,1},{6,2},{7,3},{8,12},{9,13},{10,... | collective-permute-start | bytes 622088 | tf_op jit(solution)/shard_map/ppermute | solution.py:606
  1.2 0.1 collective-permute-start
  1.2 1.2 %edges.1 = (f32[72,128]{1,0:T(8,128)S(1)}, f32[120,128]{1,0:T(8,128)S(1)}, f32[32,128]{1,0:T(8,128)S(1)}) custom-call(f32[9,2880]{1,0:T(8,128)} %h_ref.3, f32[9,2,2880]{2,1,0:T(2,128)} %bitcast.4, bf16[9,3,2880]{2,1,0:T(4,128)(2,1)} %bitcast.7), custom_call_target="tpu_custom_call" | custom-call | tf_op jit(solution)/shard_map/edges/pallas_call | solution.py:581
  2.4 0.4 %collective-permute-done.near_h_ref = f32[9,2880]{1,0:T(8,128)S(1)} collective-permute-done((f32[9,2880]{1,0:T(8,128)}, f32[9,2880]{1,0:T(8,128)S(1)}, u32[]{:S(2)}, u32[]{:S(2)}) %collective-permute-start) | collective-permute-done | bytes 103712 | tf_op jit(solution)/shard_map/ppermute | solution.py:605
  2.8 0.0 copy-start.4
  2.9 0.7 %polar.1 = (f32[160,128]{1,0:T(8,128)S(1)}, f32[160,128]{1,0:T(8,128)S(1)}, f32[160,128]{1,0:T(8,128)S(1)}, f32[160,128]{1,0:T(8,128)S(1)}, f32[120,128]{1,0:T(8,128)S(1)}, /*index=5*/f32[72,128]{1,0:T(8,128)S(1)}) custom-call(f32[9,2880]{1,0:T(8,128)S(1)} %copy-done.2, f32[9,2,2880]{2,1,0:T(2,128)S(1)} %bitcast.5, ...), custom_call_target="tpu_custom_call" | custom-call | tf_op jit(solution)/shard_map/polar/pallas_call | solution.py:621
  3.5 3.8 %collective-permute-start.4 = (f32[160,128]{1,0:T(8,128)S(1)}, f32[160,128]{1,0:T(8,128)S(1)}, u32[]{:S(2)}, u32[]{:S(2)}) collective-permute-start(f32[160,128]{1,0:T(8,128)S(1)} %get-tuple-element.31), channel_id=1, source_target_pairs={{0,3},{1,2},{2,1},{3,0},{4,5},{5,4},{6,7},{7,6},{8,11},{9,10},{10,... | collective-permute-start | bytes 245768 | tf_op jit(solution)/shard_map/ppermute | solution.py:616
  7.4 0.5 %collective-permute-start.5 = (f32[160,128]{1,0:T(8,128)S(1)}, f32[160,128]{1,0:T(8,128)S(1)}, u32[]{:S(2)}, u32[]{:S(2)}) collective-permute-start(f32[160,128]{1,0:T(8,128)S(1)} %get-tuple-element.32), channel_id=1, source_target_pairs={{0,2},{1,3},{2,0},{3,1},{4,7},{5,6},{6,5},{7,4},{8,10},{9,11},{10,... | collective-permute-start | bytes 245768 | tf_op jit(solution)/shard_map/ppermute | solution.py:616
  7.9 0.1 collective-permute-start.6
  8.0 1.9 %collective-permute-start.3 = (f32[120,128]{1,0:T(8,128)S(1)}, f32[120,128]{1,0:T(8,128)S(1)}, u32[]{:S(2)}, u32[]{:S(2)}) collective-permute-start(f32[120,128]{1,0:T(8,128)S(1)} %get-tuple-element.29), channel_id=1, source_target_pairs={{0,2},{1,3},{2,0},{3,1},{4,8},{5,9},{6,10},{7,11},{8,4},{9,5},{10,... | collective-permute-start | bytes 184328 | tf_op jit(solution)/shard_map/ppermute | solution.py:634
  9.9 0.2 collective-permute-start.2
  10.1 0.5 %copy-done.6 = s32[72]{0:T(128)S(1)} copy-done((s32[72]{0:T(128)S(1)}, s32[72]{0:T(128)}, u32[]{:S(2)}) %copy-start.6) | copy-done | bytes 312
  10.6 1.1 %weights.1 = (bf16[1152,96]{1,0:T(8,128)(2,1)S(1)}, f32[3,16,128]{2,1,0:T(8,128)S(1)}) custom-call(s32[72]{0:T(128)S(1)} %copy-done.6, f32[192,96]{1,0:T(8,128)S(1)} %copy-done.5, f32[192,96]{1,0:T(8,128)S(1)} %copy-done.4, f32[160,128]{1,0:T(8,128)S(1)} %get-tuple-element.26.after_ref.refs_0_), custom_call_target="tpu_custom_call" | custom-call | tf_op jit(solution)/shard_map/weights/pallas_call | solution.py:635
  11.7 1.3 %collective-permute-done.5.refs_2_ = f32[160,128]{1,0:T(8,128)S(1)} collective-permute-done((f32[160,128]{1,0:T(8,128)S(1)}, f32[160,128]{1,0:T(8,128)S(1)}, u32[]{:S(2)}, u32[]{:S(2)}) %collective-permute-start.5) | collective-permute-done | bytes 81952 | tf_op jit(solution)/shard_map/ppermute | solution.py:616
  13.0 1.0 %filter.1 = (f32[144,128]{1,0:T(8,128)S(1)}, f32[144,128]{1,0:T(8,128)S(1)}, f32[144,128]{1,0:T(8,128)S(1)}, f32[144,128]{1,0:T(8,128)S(1)}) custom-call(bf16[1152,96]{1,0:T(8,128)(2,1)S(1)} %get-tuple-element.30.weights_ref, f32[8,3,16,128]{3,2,1,0:T(8,128)S(1)} %copy-done.1, f32[160,128]{1,0:T(8,128)S(1)} %get-tuple-element.26.after_ref.refs_0_, ...), custom_call_target="tpu_custom_call" | custom-call | tf_op jit(solution)/shard_map/filter/pallas_call | solution.py:644
  14.0 1.2 %collective-permute-start.7 = (f32[144,128]{1,0:T(8,128)S(1)}, f32[144,128]{1,0:T(8,128)S(1)}, u32[]{:S(2)}, u32[]{:S(2)}) collective-permute-start(f32[144,128]{1,0:T(8,128)S(1)} %get-tuple-element.37), channel_id=1, source_target_pairs={{0,3},{1,2},{2,1},{3,0},{4,5},{5,4},{6,7},{7,6},{8,11},{9,10},{10,... | collective-permute-start | bytes 221192 | tf_op jit(solution)/shard_map/ppermute | solution.py:616
  15.2 1.8 %collective-permute-start.8 = (f32[144,128]{1,0:T(8,128)S(1)}, f32[144,128]{1,0:T(8,128)S(1)}, u32[]{:S(2)}, u32[]{:S(2)}) collective-permute-start(f32[144,128]{1,0:T(8,128)S(1)} %get-tuple-element.38), channel_id=1, source_target_pairs={{0,2},{1,3},{2,0},{3,1},{4,7},{5,6},{6,5},{7,4},{8,10},{9,11},{10,... | collective-permute-start | bytes 221192 | tf_op jit(solution)/shard_map/ppermute | solution.py:616
  17.1 0.6 %collective-permute-start.9 = (f32[144,128]{1,0:T(8,128)S(1)}, f32[144,128]{1,0:T(8,128)S(1)}, u32[]{:S(2)}, u32[]{:S(2)}) collective-permute-start(f32[144,128]{1,0:T(8,128)S(1)} %pass.1), channel_id=1, source_target_pairs={{0,1},{1,0},{2,3},{3,2},{4,6},{5,7},{6,4},{7,5},{8,9},{9,8},{10,11... | collective-permute-start | bytes 221192 | tf_op jit(solution)/shard_map/ppermute | solution.py:616
  17.7 2.0 %rest.1 = (f32[2,9,2880]{2,1,0:T(8,128)S(1)}, f32[9,2880]{1,0:T(8,128)S(1)}, bf16[3,9,2880]{2,1,0:T(8,128)(2,1)S(1)}) custom-call(f32[3,16,128]{2,1,0:T(8,128)S(1)} %get-tuple-element.27.masks_ref, f32[9,2880]{1,0:T(8,128)S(1)} %copy-done.2, f32[9,2,2880]{2,1,0:T(2,128)S(1)} %bitcast.6, bf16[3,9,2880]{2,1,0:T(8,128)(2,1)S(1)} %copy.11.q_ref, ...), custom_call_target="tpu_custom_call" | custom-call | tf_op jit(solution)/shard_map/rest/pallas_call | solution.py:655
  19.7 0.8 %copy.12 = bf16[3,9,2880]{2,0,1:T(4,128)(2,1)} copy(bf16[3,9,2880]{2,1,0:T(8,128)(2,1)S(1)} %get-tuple-element.45) | data formatting | bytes 311040
  20.5 0.9 %collective-permute-done.8.refs_2_ = f32[144,128]{1,0:T(8,128)S(1)} collective-permute-done((f32[144,128]{1,0:T(8,128)S(1)}, f32[144,128]{1,0:T(8,128)S(1)}, u32[]{:S(2)}, u32[]{:S(2)}) %collective-permute-start.8) | collective-permute-done | bytes 73760 | tf_op jit(solution)/shard_map/ppermute | solution.py:616
  21.4 0.1 collective-permute-done.9.refs_3_
  21.5 0.9 %finish.1 = (f32[9,2,2880]{2,1,0:T(2,128)}, f32[9,2880]{1,0:T(8,128)}) custom-call(f32[3,16,128]{2,1,0:T(8,128)S(1)} %get-tuple-element.27.masks_ref, f32[2,9,2880]{2,1,0:T(8,128)S(1)} %get-tuple-element.35.base_w_ref, f32[9,2880]{1,0:T(8,128)S(1)} %get-tuple-element.36.base_h_ref, f32[144,128]{1,0:T(8,128)S(1)} %get-tuple-element.34.after_ref.refs_0_, ...), custom_call_target="tpu_custom_call" | custom-call | tf_op jit(solution)/shard_map/finish/pallas_call | solution.py:663
  (21 shorter events, 0.1 us)
Async XLA Ops:
  0.6 2.2 %copy-start.3 = (f32[2,24,128]{2,1,0:T(8,128)S(1)}, f32[2,24,128]{2,1,0:T(8,128)}, u32[]{:S(2)}) copy-start(f32[2,24,128]{2,1,0:T(8,128)} %constant.9.clone.wave_ref) | copy-start | bytes 73732
  0.6 2.2 %collective-permute-start.1 = (f32[9,2,2880]{2,1,0:T(2,128)}, f32[9,2,2880]{2,1,0:T(2,128)S(1)}, u32[]{:S(2)}, u32[]{:S(2)}) collective-permute-start(f32[9,2,2880]{2,1,0:T(2,128)} %bitcast.3), channel_id=1, source_target_pairs={{0,4},{1,5},{2,6},{3,7},{4,0},{5,1},{6,2},{7,3},{8,12},{9,13},{10,... | collective-permute-start | bytes 622088 | tf_op jit(solution)/shard_map/ppermute | solution.py:606
  1.2 1.6 %collective-permute-start = (f32[9,2880]{1,0:T(8,128)}, f32[9,2880]{1,0:T(8,128)S(1)}, u32[]{:S(2)}, u32[]{:S(2)}) collective-permute-start(f32[9,2880]{1,0:T(8,128)} %h_ref.3), channel_id=1, source_target_pairs={{0,4},{1,5},{2,6},{3,7},{4,0},{5,1},{6,2},{7,3},{8,12},{9,13},{10,... | collective-permute-start | bytes 311048 | tf_op jit(solution)/shard_map/ppermute | solution.py:605
  1.2 1.6 %copy-start = (f32[2,9,2880]{2,0,1:T(2,128)S(1)}, f32[2,9,2880]{2,0,1:T(2,128)}, u32[]{:S(2)}) copy-start(f32[2,9,2880]{2,0,1:T(2,128)} %param.8) | copy-start | bytes 622084
  1.2 1.6 %copy-start.1 = (f32[8,3,16,128]{3,2,1,0:T(8,128)S(1)}, f32[8,3,16,128]{3,2,1,0:T(8,128)}, u32[]{:S(2)}) copy-start(f32[8,3,16,128]{3,2,1,0:T(8,128)} %constant.8.clone.geo_ref) | copy-start | bytes 589828
  1.2 1.6 %copy-start.2 = (f32[9,2880]{1,0:T(8,128)S(1)}, f32[9,2880]{1,0:T(8,128)}, u32[]{:S(2)}) copy-start(f32[9,2880]{1,0:T(8,128)} %h_ref.3) | copy-start | bytes 311044
  2.8 7.3 %copy-start.4 = (f32[192,96]{1,0:T(8,128)S(1)}, f32[192,96]{1,0:T(8,128)}, u32[]{:S(2)}) copy-start(f32[192,96]{1,0:T(8,128)} %constant.11.clone.inverse_ref) | copy-start | bytes 221188
  2.8 7.2 %copy-start.5 = (f32[192,96]{1,0:T(8,128)S(1)}, f32[192,96]{1,0:T(8,128)}, u32[]{:S(2)}) copy-start(f32[192,96]{1,0:T(8,128)} %constant.10.clone.n_ref) | copy-start | bytes 221188
  3.5 8.2 %collective-permute-start.4 = (f32[160,128]{1,0:T(8,128)S(1)}, f32[160,128]{1,0:T(8,128)S(1)}, u32[]{:S(2)}, u32[]{:S(2)}) collective-permute-start(f32[160,128]{1,0:T(8,128)S(1)} %get-tuple-element.31), channel_id=1, source_target_pairs={{0,3},{1,2},{2,1},{3,0},{4,5},{5,4},{6,7},{7,6},{8,11},{9,10},{10,... | collective-permute-start | bytes 245768 | tf_op jit(solution)/shard_map/ppermute | solution.py:616
  7.4 5.7 %collective-permute-start.5 = (f32[160,128]{1,0:T(8,128)S(1)}, f32[160,128]{1,0:T(8,128)S(1)}, u32[]{:S(2)}, u32[]{:S(2)}) collective-permute-start(f32[160,128]{1,0:T(8,128)S(1)} %get-tuple-element.32), channel_id=1, source_target_pairs={{0,2},{1,3},{2,0},{3,1},{4,7},{5,6},{6,5},{7,4},{8,10},{9,11},{10,... | collective-permute-start | bytes 245768 | tf_op jit(solution)/shard_map/ppermute | solution.py:616
  7.9 5.2 %collective-permute-start.6 = (f32[160,128]{1,0:T(8,128)S(1)}, f32[160,128]{1,0:T(8,128)S(1)}, u32[]{:S(2)}, u32[]{:S(2)}) collective-permute-start(f32[160,128]{1,0:T(8,128)S(1)} %get-tuple-element.33), channel_id=1, source_target_pairs={{0,1},{1,0},{2,3},{3,2},{4,6},{5,7},{6,4},{7,5},{8,9},{9,8},{10,11... | collective-permute-start | bytes 245768 | tf_op jit(solution)/shard_map/ppermute | solution.py:616
  8.0 9.1 %collective-permute-start.3 = (f32[120,128]{1,0:T(8,128)S(1)}, f32[120,128]{1,0:T(8,128)S(1)}, u32[]{:S(2)}, u32[]{:S(2)}) collective-permute-start(f32[120,128]{1,0:T(8,128)S(1)} %get-tuple-element.29), channel_id=1, source_target_pairs={{0,2},{1,3},{2,0},{3,1},{4,8},{5,9},{6,10},{7,11},{8,4},{9,5},{10,... | collective-permute-start | bytes 184328 | tf_op jit(solution)/shard_map/ppermute | solution.py:634
  9.9 0.7 %copy-start.6 = (s32[72]{0:T(128)S(1)}, s32[72]{0:T(128)}, u32[]{:S(2)}) copy-start(s32[72]{0:T(128)} %cut_ref.1) | copy-start | bytes 868
  9.9 7.2 %collective-permute-start.2 = (f32[72,128]{1,0:T(8,128)S(1)}, f32[72,128]{1,0:T(8,128)S(1)}, u32[]{:S(2)}, u32[]{:S(2)}) collective-permute-start(f32[72,128]{1,0:T(8,128)S(1)} %get-tuple-element.28), channel_id=1, source_target_pairs={{0,4},{1,5},{2,6},{3,7},{4,0},{5,1},{6,2},{7,3},{8,12},{9,13},{10,... | collective-permute-start | bytes 110600 | tf_op jit(solution)/shard_map/ppermute | solution.py:633
  14.0 3.7 %copy-start.7 = (bf16[3,9,2880]{2,0,1:T(4,128)(2,1)S(1)}, bf16[3,9,2880]{2,0,1:T(4,128)(2,1)}, u32[]{:S(2)}) copy-start(bf16[3,9,2880]{2,0,1:T(4,128)(2,1)} %param.10) | copy-start | bytes 466564
  14.0 6.4 %collective-permute-start.7 = (f32[144,128]{1,0:T(8,128)S(1)}, f32[144,128]{1,0:T(8,128)S(1)}, u32[]{:S(2)}, u32[]{:S(2)}) collective-permute-start(f32[144,128]{1,0:T(8,128)S(1)} %get-tuple-element.37), channel_id=1, source_target_pairs={{0,3},{1,2},{2,1},{3,0},{4,5},{5,4},{6,7},{7,6},{8,11},{9,10},{10,... | collective-permute-start | bytes 221192 | tf_op jit(solution)/shard_map/ppermute | solution.py:616
  15.2 6.1 %collective-permute-start.8 = (f32[144,128]{1,0:T(8,128)S(1)}, f32[144,128]{1,0:T(8,128)S(1)}, u32[]{:S(2)}, u32[]{:S(2)}) collective-permute-start(f32[144,128]{1,0:T(8,128)S(1)} %get-tuple-element.38), channel_id=1, source_target_pairs={{0,2},{1,3},{2,0},{3,1},{4,7},{5,6},{6,5},{7,4},{8,10},{9,11},{10,... | collective-permute-start | bytes 221192 | tf_op jit(solution)/shard_map/ppermute | solution.py:616
  17.1 4.4 %collective-permute-start.9 = (f32[144,128]{1,0:T(8,128)S(1)}, f32[144,128]{1,0:T(8,128)S(1)}, u32[]{:S(2)}, u32[]{:S(2)}) collective-permute-start(f32[144,128]{1,0:T(8,128)S(1)} %pass.1), channel_id=1, source_target_pairs={{0,1},{1,0},{2,3},{3,2},{4,6},{5,7},{6,4},{7,5},{8,9},{9,8},{10,11... | collective-permute-start | bytes 221192 | tf_op jit(solution)/shard_map/ppermute | solution.py:616

commit v20 on v19

--- a/solution.py
+++ b/solution.py
@@ -54,7 +54,7 @@
 
     def turns(self, odd):
         middle, last = list(range(1, self.n_lon - 1)), self.n_lon - 1
-        return [0, middle[0], last] + middle[1:] if odd else [0, last] + middle[::-1]
+        return [0, middle[-1], last] + middle[-2::-1] if odd else [0, last] + middle[::-1]
 
     def partner(self, k):
         odd = lax.rem(lax.axis_index("lat"), 2) == 1

time: 22.6 us -> 22 us (0.973)
  waiting for transfers between devices: 2.71 us -> 2.12 us
    ppermute x6, waiting for transfers between devices: 2.32 us -> 1.73 us  [meetings(): lax.ppermute(shares[k], ('lat', 'lon'), [(b * n_lon + i, b * n_lon + j) f...]
  transfers between devices with their start and end apart: 10 -> 10, of which waited for: 4 -> 5; matrix products, arithmetic and copies ran while one was open for 4% -> 4% of each run, Pallas kernels for 24% -> 24%
where the time goes in v20:
time: 22 us; the launch traced here: 21.8 us
  starting transfers between devices  10.8 us (49%)
  Pallas kernels  6.89 us (31%)
  waiting for transfers between devices  2.12 us (10%)
  local copies, waits for them, and re-layouts  1.32 us (6%)
  between operations  0.75 us (3%)
    ppermute x6, starting transfers between devices, meetings(): lax.ppermute(shares[k], ('lat', 'lon'), [(b * n_lon + i, b * n_lon + j) f...  8.07 us
    pallas_call x1, Pallas kernels, local(): call(rest_kernel, 'rest', [vmem] * 10 + [anywhere] + [vmem] * n_lon, (sha...  1.99 us
    ppermute x1, starting transfers between devices, local(): lax.ppermute(far_rows, ('lat', 'lon'), far)  1.92 us
    ppermute x6, waiting for transfers between devices, meetings(): lax.ppermute(shares[k], ('lat', 'lon'), [(b * n_lon + i, b * n_lon + j) f...  1.73 us
    unnamed x18, local copies, waits for them, and re-layouts  1.32 us
    pallas_call x1, Pallas kernels, local(): call(edges_kernel, 'edges', [hbm] * 3, (near_row, far_row, shaped(2 * EXT...  1.17 us
    pallas_call x1, Pallas kernels, local(): call(weights_kernel, 'weights', [smem, vmem, vmem, anywhere], (jax.ShapeD...  1.15 us
    pallas_call x1, Pallas kernels, local(): call(filter_kernel, 'filter', [vmem] * 2 + [vmem] * n_lon, [shaped(sz.siz...  0.98 us
  transfers between devices with their start and end apart: 10, of which 5 were waited for; matrix products, arithmetic and copies ran while one was open for 4% of the time, Pallas kernels for 24%

profile of v20, /device:TPU:0, one launch (start us, length us, event | category | flops | bytes accessed | tf_op | source)
XLA Modules:
  0.0 21.8 jit_solution(1995784619951550900)
XLA Ops:
  0.6 0.0 copy-start.3
  0.6 0.5 %collective-permute-start.1 = (f32[9,2,2880]{2,1,0:T(2,128)}, f32[9,2,2880]{2,1,0:T(2,128)S(1)}, u32[]{:S(2)}, u32[]{:S(2)}) collective-permute-start(f32[9,2,2880]{2,1,0:T(2,128)} %bitcast.3), channel_id=1, source_target_pairs={{0,4},{1,5},{2,6},{3,7},{4,0},{5,1},{6,2},{7,3},{8,12},{9,13},{10,... | collective-permute-start | bytes 622088 | tf_op jit(solution)/shard_map/ppermute | solution.py:606
  1.2 0.1 collective-permute-start
  1.2 1.2 %edges.1 = (f32[72,128]{1,0:T(8,128)S(1)}, f32[120,128]{1,0:T(8,128)S(1)}, f32[32,128]{1,0:T(8,128)S(1)}) custom-call(f32[9,2880]{1,0:T(8,128)} %h_ref.3, f32[9,2,2880]{2,1,0:T(2,128)} %bitcast.4, bf16[9,3,2880]{2,1,0:T(4,128)(2,1)} %bitcast.7), custom_call_target="tpu_custom_call" | custom-call | tf_op jit(solution)/shard_map/edges/pallas_call | solution.py:581
  2.4 0.4 %collective-permute-done.near_h_ref = f32[9,2880]{1,0:T(8,128)S(1)} collective-permute-done((f32[9,2880]{1,0:T(8,128)}, f32[9,2880]{1,0:T(8,128)S(1)}, u32[]{:S(2)}, u32[]{:S(2)}) %collective-permute-start) | collective-permute-done | bytes 103712 | tf_op jit(solution)/shard_map/ppermute | solution.py:605
  2.9 0.7 %polar.1 = (f32[160,128]{1,0:T(8,128)S(1)}, f32[160,128]{1,0:T(8,128)S(1)}, f32[160,128]{1,0:T(8,128)S(1)}, f32[160,128]{1,0:T(8,128)S(1)}, f32[120,128]{1,0:T(8,128)S(1)}, /*index=5*/f32[72,128]{1,0:T(8,128)S(1)}) custom-call(f32[9,2880]{1,0:T(8,128)S(1)} %copy-done.2, f32[9,2,2880]{2,1,0:T(2,128)S(1)} %bitcast.5, ...), custom_call_target="tpu_custom_call" | custom-call | tf_op jit(solution)/shard_map/polar/pallas_call | solution.py:621
  3.5 3.8 %collective-permute-start.4 = (f32[160,128]{1,0:T(8,128)S(1)}, f32[160,128]{1,0:T(8,128)S(1)}, u32[]{:S(2)}, u32[]{:S(2)}) collective-permute-start(f32[160,128]{1,0:T(8,128)S(1)} %get-tuple-element.31), channel_id=1, source_target_pairs={{0,3},{1,2},{2,1},{3,0},{4,6},{5,7},{6,4},{7,5},{8,11},{9,10},{10,... | collective-permute-start | bytes 245768 | tf_op jit(solution)/shard_map/ppermute | solution.py:616
  7.4 0.5 %collective-permute-start.5 = (f32[160,128]{1,0:T(8,128)S(1)}, f32[160,128]{1,0:T(8,128)S(1)}, u32[]{:S(2)}, u32[]{:S(2)}) collective-permute-start(f32[160,128]{1,0:T(8,128)S(1)} %get-tuple-element.32), channel_id=1, source_target_pairs={{0,2},{1,3},{2,0},{3,1},{4,7},{5,6},{6,5},{7,4},{8,10},{9,11},{10,... | collective-permute-start | bytes 245768 | tf_op jit(solution)/shard_map/ppermute | solution.py:616
  7.9 0.1 collective-permute-start.6
  8.0 1.9 %collective-permute-start.3 = (f32[120,128]{1,0:T(8,128)S(1)}, f32[120,128]{1,0:T(8,128)S(1)}, u32[]{:S(2)}, u32[]{:S(2)}) collective-permute-start(f32[120,128]{1,0:T(8,128)S(1)} %get-tuple-element.29), channel_id=1, source_target_pairs={{0,2},{1,3},{2,0},{3,1},{4,8},{5,9},{6,10},{7,11},{8,4},{9,5},{10,... | collective-permute-start | bytes 184328 | tf_op jit(solution)/shard_map/ppermute | solution.py:634
  9.9 0.2 collective-permute-start.2
  10.1 0.5 %copy-done.6 = s32[72]{0:T(128)S(1)} copy-done((s32[72]{0:T(128)S(1)}, s32[72]{0:T(128)}, u32[]{:S(2)}) %copy-start.6) | copy-done | bytes 312
  10.6 1.1 %weights.1 = (bf16[1152,96]{1,0:T(8,128)(2,1)S(1)}, f32[3,16,128]{2,1,0:T(8,128)S(1)}) custom-call(s32[72]{0:T(128)S(1)} %copy-done.6, f32[192,96]{1,0:T(8,128)S(1)} %copy-done.5, f32[192,96]{1,0:T(8,128)S(1)} %copy-done.4, f32[160,128]{1,0:T(8,128)S(1)} %get-tuple-element.26.after_ref.refs_0_), custom_call_target="tpu_custom_call" | custom-call | tf_op jit(solution)/shard_map/weights/pallas_call | solution.py:635
  11.7 0.1 collective-permute-done.5.refs_2_
  11.8 0.5 %collective-permute-done.6.refs_3_ = f32[160,128]{1,0:T(8,128)S(1)} collective-permute-done((f32[160,128]{1,0:T(8,128)S(1)}, f32[160,128]{1,0:T(8,128)S(1)}, u32[]{:S(2)}, u32[]{:S(2)}) %collective-permute-start.6) | collective-permute-done | bytes 81952 | tf_op jit(solution)/shard_map/ppermute | solution.py:616
  12.3 1.0 %filter.1 = (f32[144,128]{1,0:T(8,128)S(1)}, f32[144,128]{1,0:T(8,128)S(1)}, f32[144,128]{1,0:T(8,128)S(1)}, f32[144,128]{1,0:T(8,128)S(1)}) custom-call(bf16[1152,96]{1,0:T(8,128)(2,1)S(1)} %get-tuple-element.30.weights_ref, f32[8,3,16,128]{3,2,1,0:T(8,128)S(1)} %copy-done.1, f32[160,128]{1,0:T(8,128)S(1)} %get-tuple-element.26.after_ref.refs_0_, ...), custom_call_target="tpu_custom_call" | custom-call | tf_op jit(solution)/shard_map/filter/pallas_call | solution.py:644
  13.3 2.2 %collective-permute-start.7 = (f32[144,128]{1,0:T(8,128)S(1)}, f32[144,128]{1,0:T(8,128)S(1)}, u32[]{:S(2)}, u32[]{:S(2)}) collective-permute-start(f32[144,128]{1,0:T(8,128)S(1)} %get-tuple-element.37), channel_id=1, source_target_pairs={{0,3},{1,2},{2,1},{3,0},{4,6},{5,7},{6,4},{7,5},{8,11},{9,10},{10,... | collective-permute-start | bytes 221192 | tf_op jit(solution)/shard_map/ppermute | solution.py:616
  15.5 1.0 %collective-permute-start.8 = (f32[144,128]{1,0:T(8,128)S(1)}, f32[144,128]{1,0:T(8,128)S(1)}, u32[]{:S(2)}, u32[]{:S(2)}) collective-permute-start(f32[144,128]{1,0:T(8,128)S(1)} %get-tuple-element.38), channel_id=1, source_target_pairs={{0,2},{1,3},{2,0},{3,1},{4,7},{5,6},{6,5},{7,4},{8,10},{9,11},{10,... | collective-permute-start | bytes 221192 | tf_op jit(solution)/shard_map/ppermute | solution.py:616
  16.5 0.4 %collective-permute-start.9 = (f32[144,128]{1,0:T(8,128)S(1)}, f32[144,128]{1,0:T(8,128)S(1)}, u32[]{:S(2)}, u32[]{:S(2)}) collective-permute-start(f32[144,128]{1,0:T(8,128)S(1)} %pass.1), channel_id=1, source_target_pairs={{0,1},{1,0},{2,3},{3,2},{4,5},{5,4},{6,7},{7,6},{8,9},{9,8},{10,11... | collective-permute-start | bytes 221192 | tf_op jit(solution)/shard_map/ppermute | solution.py:616
  17.0 2.0 %rest.1 = (f32[2,9,2880]{2,1,0:T(8,128)S(1)}, f32[9,2880]{1,0:T(8,128)S(1)}, bf16[3,9,2880]{2,1,0:T(8,128)(2,1)S(1)}) custom-call(f32[3,16,128]{2,1,0:T(8,128)S(1)} %get-tuple-element.27.masks_ref, f32[9,2880]{1,0:T(8,128)S(1)} %copy-done.2, f32[9,2,2880]{2,1,0:T(2,128)S(1)} %bitcast.6, bf16[3,9,2880]{2,1,0:T(8,128)(2,1)S(1)} %copy.11.q_ref, ...), custom_call_target="tpu_custom_call" | custom-call | tf_op jit(solution)/shard_map/rest/pallas_call | solution.py:655
  19.0 0.8 %copy.12 = bf16[3,9,2880]{2,0,1:T(4,128)(2,1)} copy(bf16[3,9,2880]{2,1,0:T(8,128)(2,1)S(1)} %get-tuple-element.45) | data formatting | bytes 311040
  19.7 0.4 %collective-permute-done.8.refs_2_ = f32[144,128]{1,0:T(8,128)S(1)} collective-permute-done((f32[144,128]{1,0:T(8,128)S(1)}, f32[144,128]{1,0:T(8,128)S(1)}, u32[]{:S(2)}, u32[]{:S(2)}) %collective-permute-start.8) | collective-permute-done | bytes 73760 | tf_op jit(solution)/shard_map/ppermute | solution.py:616
  20.1 0.8 %collective-permute-done.9.refs_3_ = f32[144,128]{1,0:T(8,128)S(1)} collective-permute-done((f32[144,128]{1,0:T(8,128)S(1)}, f32[144,128]{1,0:T(8,128)S(1)}, u32[]{:S(2)}, u32[]{:S(2)}) %collective-permute-start.9) | collective-permute-done | bytes 73760 | tf_op jit(solution)/shard_map/ppermute | solution.py:616
  20.9 0.9 %finish.1 = (f32[9,2,2880]{2,1,0:T(2,128)}, f32[9,2880]{1,0:T(8,128)}) custom-call(f32[3,16,128]{2,1,0:T(8,128)S(1)} %get-tuple-element.27.masks_ref, f32[2,9,2880]{2,1,0:T(8,128)S(1)} %get-tuple-element.35.base_w_ref, f32[9,2880]{1,0:T(8,128)S(1)} %get-tuple-element.36.base_h_ref, f32[144,128]{1,0:T(8,128)S(1)} %get-tuple-element.34.after_ref.refs_0_, ...), custom_call_target="tpu_custom_call" | custom-call | tf_op jit(solution)/shard_map/finish/pallas_call | solution.py:663
  (21 shorter events, 0.1 us)
Async XLA Ops:
  0.6 2.2 %copy-start.3 = (f32[2,24,128]{2,1,0:T(8,128)S(1)}, f32[2,24,128]{2,1,0:T(8,128)}, u32[]{:S(2)}) copy-start(f32[2,24,128]{2,1,0:T(8,128)} %constant.9.clone.wave_ref) | copy-start | bytes 73732
  0.6 2.2 %collective-permute-start.1 = (f32[9,2,2880]{2,1,0:T(2,128)}, f32[9,2,2880]{2,1,0:T(2,128)S(1)}, u32[]{:S(2)}, u32[]{:S(2)}) collective-permute-start(f32[9,2,2880]{2,1,0:T(2,128)} %bitcast.3), channel_id=1, source_target_pairs={{0,4},{1,5},{2,6},{3,7},{4,0},{5,1},{6,2},{7,3},{8,12},{9,13},{10,... | collective-permute-start | bytes 622088 | tf_op jit(solution)/shard_map/ppermute | solution.py:606
  1.2 1.6 %collective-permute-start = (f32[9,2880]{1,0:T(8,128)}, f32[9,2880]{1,0:T(8,128)S(1)}, u32[]{:S(2)}, u32[]{:S(2)}) collective-permute-start(f32[9,2880]{1,0:T(8,128)} %h_ref.3), channel_id=1, source_target_pairs={{0,4},{1,5},{2,6},{3,7},{4,0},{5,1},{6,2},{7,3},{8,12},{9,13},{10,... | collective-permute-start | bytes 311048 | tf_op jit(solution)/shard_map/ppermute | solution.py:605
  1.2 1.6 %copy-start = (f32[2,9,2880]{2,0,1:T(2,128)S(1)}, f32[2,9,2880]{2,0,1:T(2,128)}, u32[]{:S(2)}) copy-start(f32[2,9,2880]{2,0,1:T(2,128)} %param.8) | copy-start | bytes 622084
  1.2 1.6 %copy-start.1 = (f32[8,3,16,128]{3,2,1,0:T(8,128)S(1)}, f32[8,3,16,128]{3,2,1,0:T(8,128)}, u32[]{:S(2)}) copy-start(f32[8,3,16,128]{3,2,1,0:T(8,128)} %constant.8.clone.geo_ref) | copy-start | bytes 589828
  1.2 1.6 %copy-start.2 = (f32[9,2880]{1,0:T(8,128)S(1)}, f32[9,2880]{1,0:T(8,128)}, u32[]{:S(2)}) copy-start(f32[9,2880]{1,0:T(8,128)} %h_ref.3) | copy-start | bytes 311044
  2.8 7.3 %copy-start.4 = (f32[192,96]{1,0:T(8,128)S(1)}, f32[192,96]{1,0:T(8,128)}, u32[]{:S(2)}) copy-start(f32[192,96]{1,0:T(8,128)} %constant.11.clone.inverse_ref) | copy-start | bytes 221188
  2.8 7.2 %copy-start.5 = (f32[192,96]{1,0:T(8,128)S(1)}, f32[192,96]{1,0:T(8,128)}, u32[]{:S(2)}) copy-start(f32[192,96]{1,0:T(8,128)} %constant.10.clone.n_ref) | copy-start | bytes 221188
  3.5 8.2 %collective-permute-start.4 = (f32[160,128]{1,0:T(8,128)S(1)}, f32[160,128]{1,0:T(8,128)S(1)}, u32[]{:S(2)}, u32[]{:S(2)}) collective-permute-start(f32[160,128]{1,0:T(8,128)S(1)} %get-tuple-element.31), channel_id=1, source_target_pairs={{0,3},{1,2},{2,1},{3,0},{4,6},{5,7},{6,4},{7,5},{8,11},{9,10},{10,... | collective-permute-start | bytes 245768 | tf_op jit(solution)/shard_map/ppermute | solution.py:616
  7.4 4.4 %collective-permute-start.5 = (f32[160,128]{1,0:T(8,128)S(1)}, f32[160,128]{1,0:T(8,128)S(1)}, u32[]{:S(2)}, u32[]{:S(2)}) collective-permute-start(f32[160,128]{1,0:T(8,128)S(1)} %get-tuple-element.32), channel_id=1, source_target_pairs={{0,2},{1,3},{2,0},{3,1},{4,7},{5,6},{6,5},{7,4},{8,10},{9,11},{10,... | collective-permute-start | bytes 245768 | tf_op jit(solution)/shard_map/ppermute | solution.py:616
  7.9 4.4 %collective-permute-start.6 = (f32[160,128]{1,0:T(8,128)S(1)}, f32[160,128]{1,0:T(8,128)S(1)}, u32[]{:S(2)}, u32[]{:S(2)}) collective-permute-start(f32[160,128]{1,0:T(8,128)S(1)} %get-tuple-element.33), channel_id=1, source_target_pairs={{0,1},{1,0},{2,3},{3,2},{4,5},{5,4},{6,7},{7,6},{8,9},{9,8},{10,11... | collective-permute-start | bytes 245768 | tf_op jit(solution)/shard_map/ppermute | solution.py:616
  8.0 8.5 %collective-permute-start.3 = (f32[120,128]{1,0:T(8,128)S(1)}, f32[120,128]{1,0:T(8,128)S(1)}, u32[]{:S(2)}, u32[]{:S(2)}) collective-permute-start(f32[120,128]{1,0:T(8,128)S(1)} %get-tuple-element.29), channel_id=1, source_target_pairs={{0,2},{1,3},{2,0},{3,1},{4,8},{5,9},{6,10},{7,11},{8,4},{9,5},{10,... | collective-permute-start | bytes 184328 | tf_op jit(solution)/shard_map/ppermute | solution.py:634
  9.9 0.7 %copy-start.6 = (s32[72]{0:T(128)S(1)}, s32[72]{0:T(128)}, u32[]{:S(2)}) copy-start(s32[72]{0:T(128)} %cut_ref.1) | copy-start | bytes 868
  9.9 6.6 %collective-permute-start.2 = (f32[72,128]{1,0:T(8,128)S(1)}, f32[72,128]{1,0:T(8,128)S(1)}, u32[]{:S(2)}, u32[]{:S(2)}) collective-permute-start(f32[72,128]{1,0:T(8,128)S(1)} %get-tuple-element.28), channel_id=1, source_target_pairs={{0,4},{1,5},{2,6},{3,7},{4,0},{5,1},{6,2},{7,3},{8,12},{9,13},{10,... | collective-permute-start | bytes 110600 | tf_op jit(solution)/shard_map/ppermute | solution.py:633
  13.3 3.7 %copy-start.7 = (bf16[3,9,2880]{2,0,1:T(4,128)(2,1)S(1)}, bf16[3,9,2880]{2,0,1:T(4,128)(2,1)}, u32[]{:S(2)}) copy-start(bf16[3,9,2880]{2,0,1:T(4,128)(2,1)} %param.10) | copy-start | bytes 466564
  13.3 6.4 %collective-permute-start.7 = (f32[144,128]{1,0:T(8,128)S(1)}, f32[144,128]{1,0:T(8,128)S(1)}, u32[]{:S(2)}, u32[]{:S(2)}) collective-permute-start(f32[144,128]{1,0:T(8,128)S(1)} %get-tuple-element.37), channel_id=1, source_target_pairs={{0,3},{1,2},{2,1},{3,0},{4,6},{5,7},{6,4},{7,5},{8,11},{9,10},{10,... | collective-permute-start | bytes 221192 | tf_op jit(solution)/shard_map/ppermute | solution.py:616
  15.5 4.6 %collective-permute-start.8 = (f32[144,128]{1,0:T(8,128)S(1)}, f32[144,128]{1,0:T(8,128)S(1)}, u32[]{:S(2)}, u32[]{:S(2)}) collective-permute-start(f32[144,128]{1,0:T(8,128)S(1)} %get-tuple-element.38), channel_id=1, source_target_pairs={{0,2},{1,3},{2,0},{3,1},{4,7},{5,6},{6,5},{7,4},{8,10},{9,11},{10,... | collective-permute-start | bytes 221192 | tf_op jit(solution)/shard_map/ppermute | solution.py:616
  16.5 4.4 %collective-permute-start.9 = (f32[144,128]{1,0:T(8,128)S(1)}, f32[144,128]{1,0:T(8,128)S(1)}, u32[]{:S(2)}, u32[]{:S(2)}) collective-permute-start(f32[144,128]{1,0:T(8,128)S(1)} %pass.1), channel_id=1, source_target_pairs={{0,1},{1,0},{2,3},{3,2},{4,5},{5,4},{6,7},{7,6},{8,9},{9,8},{10,11... | collective-permute-start | bytes 221192 | tf_op jit(solution)/shard_map/ppermute | solution.py:616

commit v21 on v20

--- a/solution.py
+++ b/solution.py
@@ -54,7 +54,7 @@
 
     def turns(self, odd):
         middle, last = list(range(1, self.n_lon - 1)), self.n_lon - 1
-        return [0, middle[-1], last] + middle[-2::-1] if odd else [0, last] + middle[::-1]
+        return [0, middle[-1], last] + middle[-2::-1] if odd else [0, last] + middle
 
     def partner(self, k):
         odd = lax.rem(lax.axis_index("lat"), 2) == 1

time: 22 us -> 21.2 us (0.964)
  waiting for transfers between devices: 2.12 us -> 1.32 us
    ppermute x6, waiting for transfers between devices: 1.73 us -> 0.93 us  [meetings(): lax.ppermute(shares[k], ('lat', 'lon'), [(b * n_lon + i, b * n_lon + j) f...]
  transfers between devices with their start and end apart: 10 -> 10, of which waited for: 5 -> 5; matrix products, arithmetic and copies ran while one was open for 4% -> 4% of each run, Pallas kernels for 24% -> 25%
where the time goes in v21:
time: 21.2 us; the launch traced here: 21 us
  starting transfers between devices  10.8 us (51%)
  Pallas kernels  6.89 us (32%)
  local copies, waits for them, and re-layouts  1.32 us (6%)
  waiting for transfers between devices  1.32 us (6%)
  between operations  0.75 us (4%)
    ppermute x6, starting transfers between devices, meetings(): lax.ppermute(shares[k], ('lat', 'lon'), [(b * n_lon + i, b * n_lon + j) f...  8.07 us
    pallas_call x1, Pallas kernels, local(): call(rest_kernel, 'rest', [vmem] * 10 + [anywhere] + [vmem] * n_lon, (sha...  1.99 us
    ppermute x1, starting transfers between devices, local(): lax.ppermute(far_rows, ('lat', 'lon'), far)  1.92 us
    unnamed x18, local copies, waits for them, and re-layouts  1.32 us
    pallas_call x1, Pallas kernels, local(): call(edges_kernel, 'edges', [hbm] * 3, (near_row, far_row, shaped(2 * EXT...  1.17 us
    pallas_call x1, Pallas kernels, local(): call(weights_kernel, 'weights', [smem, vmem, vmem, anywhere], (jax.ShapeD...  1.15 us
    pallas_call x1, Pallas kernels, local(): call(filter_kernel, 'filter', [vmem] * 2 + [vmem] * n_lon, [shaped(sz.siz...  0.98 us
    ppermute x6, waiting for transfers between devices, meetings(): lax.ppermute(shares[k], ('lat', 'lon'), [(b * n_lon + i, b * n_lon + j) f...  0.93 us
  transfers between devices with their start and end apart: 10, of which 5 were waited for; matrix products, arithmetic and copies ran while one was open for 4% of the time, Pallas kernels for 25%

profile of v21, /device:TPU:0, one launch (start us, length us, event | category | flops | bytes accessed | tf_op | source)
XLA Modules:
  0.0 21.0 jit_solution(7207010221431072441)
XLA Ops:
  0.6 0.0 copy-start.3
  0.6 0.5 %collective-permute-start.1 = (f32[9,2,2880]{2,1,0:T(2,128)}, f32[9,2,2880]{2,1,0:T(2,128)S(1)}, u32[]{:S(2)}, u32[]{:S(2)}) collective-permute-start(f32[9,2,2880]{2,1,0:T(2,128)} %bitcast.3), channel_id=1, source_target_pairs={{0,4},{1,5},{2,6},{3,7},{4,0},{5,1},{6,2},{7,3},{8,12},{9,13},{10,... | collective-permute-start | bytes 622088 | tf_op jit(solution)/shard_map/ppermute | solution.py:606
  1.2 0.1 collective-permute-start
  1.2 1.2 %edges.1 = (f32[72,128]{1,0:T(8,128)S(1)}, f32[120,128]{1,0:T(8,128)S(1)}, f32[32,128]{1,0:T(8,128)S(1)}) custom-call(f32[9,2880]{1,0:T(8,128)} %h_ref.3, f32[9,2,2880]{2,1,0:T(2,128)} %bitcast.4, bf16[9,3,2880]{2,1,0:T(4,128)(2,1)} %bitcast.7), custom_call_target="tpu_custom_call" | custom-call | tf_op jit(solution)/shard_map/edges/pallas_call | solution.py:581
  2.4 0.4 %collective-permute-done.near_h_ref = f32[9,2880]{1,0:T(8,128)S(1)} collective-permute-done((f32[9,2880]{1,0:T(8,128)}, f32[9,2880]{1,0:T(8,128)S(1)}, u32[]{:S(2)}, u32[]{:S(2)}) %collective-permute-start) | collective-permute-done | bytes 103712 | tf_op jit(solution)/shard_map/ppermute | solution.py:605
  2.9 0.7 %polar.1 = (f32[160,128]{1,0:T(8,128)S(1)}, f32[160,128]{1,0:T(8,128)S(1)}, f32[160,128]{1,0:T(8,128)S(1)}, f32[160,128]{1,0:T(8,128)S(1)}, f32[120,128]{1,0:T(8,128)S(1)}, /*index=5*/f32[72,128]{1,0:T(8,128)S(1)}) custom-call(f32[9,2880]{1,0:T(8,128)S(1)} %copy-done.2, f32[9,2,2880]{2,1,0:T(2,128)S(1)} %bitcast.5, ...), custom_call_target="tpu_custom_call" | custom-call | tf_op jit(solution)/shard_map/polar/pallas_call | solution.py:621
  3.5 3.8 %collective-permute-start.4 = (f32[160,128]{1,0:T(8,128)S(1)}, f32[160,128]{1,0:T(8,128)S(1)}, u32[]{:S(2)}, u32[]{:S(2)}) collective-permute-start(f32[160,128]{1,0:T(8,128)S(1)} %get-tuple-element.31), channel_id=1, source_target_pairs={{0,3},{1,2},{2,1},{3,0},{4,6},{5,7},{6,4},{7,5},{8,11},{9,10},{10,... | collective-permute-start | bytes 245768 | tf_op jit(solution)/shard_map/ppermute | solution.py:616
  7.4 0.5 %collective-permute-start.5 = (f32[160,128]{1,0:T(8,128)S(1)}, f32[160,128]{1,0:T(8,128)S(1)}, u32[]{:S(2)}, u32[]{:S(2)}) collective-permute-start(f32[160,128]{1,0:T(8,128)S(1)} %get-tuple-element.32), channel_id=1, source_target_pairs={{0,1},{1,0},{2,3},{3,2},{4,7},{5,6},{6,5},{7,4},{8,9},{9,8},{10,11... | collective-permute-start | bytes 245768 | tf_op jit(solution)/shard_map/ppermute | solution.py:616
  7.9 0.1 collective-permute-start.6
  8.0 1.9 %collective-permute-start.3 = (f32[120,128]{1,0:T(8,128)S(1)}, f32[120,128]{1,0:T(8,128)S(1)}, u32[]{:S(2)}, u32[]{:S(2)}) collective-permute-start(f32[120,128]{1,0:T(8,128)S(1)} %get-tuple-element.29), channel_id=1, source_target_pairs={{0,2},{1,3},{2,0},{3,1},{4,8},{5,9},{6,10},{7,11},{8,4},{9,5},{10,... | collective-permute-start | bytes 184328 | tf_op jit(solution)/shard_map/ppermute | solution.py:634
  9.9 0.2 collective-permute-start.2
  10.1 0.5 %copy-done.6 = s32[72]{0:T(128)S(1)} copy-done((s32[72]{0:T(128)S(1)}, s32[72]{0:T(128)}, u32[]{:S(2)}) %copy-start.6) | copy-done | bytes 312
  10.6 1.1 %weights.1 = (bf16[1152,96]{1,0:T(8,128)(2,1)S(1)}, f32[3,16,128]{2,1,0:T(8,128)S(1)}) custom-call(s32[72]{0:T(128)S(1)} %copy-done.6, f32[192,96]{1,0:T(8,128)S(1)} %copy-done.5, f32[192,96]{1,0:T(8,128)S(1)} %copy-done.4, f32[160,128]{1,0:T(8,128)S(1)} %get-tuple-element.26.after_ref.refs_0_), custom_call_target="tpu_custom_call" | custom-call | tf_op jit(solution)/shard_map/weights/pallas_call | solution.py:635
  11.7 0.5 %collective-permute-done.5.refs_2_ = f32[160,128]{1,0:T(8,128)S(1)} collective-permute-done((f32[160,128]{1,0:T(8,128)S(1)}, f32[160,128]{1,0:T(8,128)S(1)}, u32[]{:S(2)}, u32[]{:S(2)}) %collective-permute-start.5) | collective-permute-done | bytes 81952 | tf_op jit(solution)/shard_map/ppermute | solution.py:616
  12.3 0.1 collective-permute-done.6.refs_3_
  12.3 1.0 %filter.1 = (f32[144,128]{1,0:T(8,128)S(1)}, f32[144,128]{1,0:T(8,128)S(1)}, f32[144,128]{1,0:T(8,128)S(1)}, f32[144,128]{1,0:T(8,128)S(1)}) custom-call(bf16[1152,96]{1,0:T(8,128)(2,1)S(1)} %get-tuple-element.30.weights_ref, f32[8,3,16,128]{3,2,1,0:T(8,128)S(1)} %copy-done.1, f32[160,128]{1,0:T(8,128)S(1)} %get-tuple-element.26.after_ref.refs_0_, ...), custom_call_target="tpu_custom_call" | custom-call | tf_op jit(solution)/shard_map/filter/pallas_call | solution.py:644
  13.3 1.8 %collective-permute-start.7 = (f32[144,128]{1,0:T(8,128)S(1)}, f32[144,128]{1,0:T(8,128)S(1)}, u32[]{:S(2)}, u32[]{:S(2)}) collective-permute-start(f32[144,128]{1,0:T(8,128)S(1)} %get-tuple-element.37), channel_id=1, source_target_pairs={{0,3},{1,2},{2,1},{3,0},{4,6},{5,7},{6,4},{7,5},{8,11},{9,10},{10,... | collective-permute-start | bytes 221192 | tf_op jit(solution)/shard_map/ppermute | solution.py:616
  15.2 0.4 %collective-permute-start.8 = (f32[144,128]{1,0:T(8,128)S(1)}, f32[144,128]{1,0:T(8,128)S(1)}, u32[]{:S(2)}, u32[]{:S(2)}) collective-permute-start(f32[144,128]{1,0:T(8,128)S(1)} %get-tuple-element.38), channel_id=1, source_target_pairs={{0,1},{1,0},{2,3},{3,2},{4,7},{5,6},{6,5},{7,4},{8,9},{9,8},{10,11... | collective-permute-start | bytes 221192 | tf_op jit(solution)/shard_map/ppermute | solution.py:616
  15.5 1.4 %collective-permute-start.9 = (f32[144,128]{1,0:T(8,128)S(1)}, f32[144,128]{1,0:T(8,128)S(1)}, u32[]{:S(2)}, u32[]{:S(2)}) collective-permute-start(f32[144,128]{1,0:T(8,128)S(1)} %pass.1), channel_id=1, source_target_pairs={{0,2},{1,3},{2,0},{3,1},{4,5},{5,4},{6,7},{7,6},{8,10},{9,11},{10,... | collective-permute-start | bytes 221192 | tf_op jit(solution)/shard_map/ppermute | solution.py:616
  17.0 2.0 %rest.1 = (f32[2,9,2880]{2,1,0:T(8,128)S(1)}, f32[9,2880]{1,0:T(8,128)S(1)}, bf16[3,9,2880]{2,1,0:T(8,128)(2,1)S(1)}) custom-call(f32[3,16,128]{2,1,0:T(8,128)S(1)} %get-tuple-element.27.masks_ref, f32[9,2880]{1,0:T(8,128)S(1)} %copy-done.2, f32[9,2,2880]{2,1,0:T(2,128)S(1)} %bitcast.6, bf16[3,9,2880]{2,1,0:T(8,128)(2,1)S(1)} %copy.11.q_ref, ...), custom_call_target="tpu_custom_call" | custom-call | tf_op jit(solution)/shard_map/rest/pallas_call | solution.py:655
  19.0 0.8 %copy.12 = bf16[3,9,2880]{2,0,1:T(4,128)(2,1)} copy(bf16[3,9,2880]{2,1,0:T(8,128)(2,1)S(1)} %get-tuple-element.45) | data formatting | bytes 311040
  19.8 0.2 collective-permute-done.8.refs_2_
  19.9 0.2 collective-permute-done.9.refs_3_
  20.1 0.9 %finish.1 = (f32[9,2,2880]{2,1,0:T(2,128)}, f32[9,2880]{1,0:T(8,128)}) custom-call(f32[3,16,128]{2,1,0:T(8,128)S(1)} %get-tuple-element.27.masks_ref, f32[2,9,2880]{2,1,0:T(8,128)S(1)} %get-tuple-element.35.base_w_ref, f32[9,2880]{1,0:T(8,128)S(1)} %get-tuple-element.36.base_h_ref, f32[144,128]{1,0:T(8,128)S(1)} %get-tuple-element.34.after_ref.refs_0_, ...), custom_call_target="tpu_custom_call" | custom-call | tf_op jit(solution)/shard_map/finish/pallas_call | solution.py:663
  (21 shorter events, 0.1 us)
Async XLA Ops:
  0.6 2.2 %copy-start.3 = (f32[2,24,128]{2,1,0:T(8,128)S(1)}, f32[2,24,128]{2,1,0:T(8,128)}, u32[]{:S(2)}) copy-start(f32[2,24,128]{2,1,0:T(8,128)} %constant.9.clone.wave_ref) | copy-start | bytes 73732
  0.6 2.2 %collective-permute-start.1 = (f32[9,2,2880]{2,1,0:T(2,128)}, f32[9,2,2880]{2,1,0:T(2,128)S(1)}, u32[]{:S(2)}, u32[]{:S(2)}) collective-permute-start(f32[9,2,2880]{2,1,0:T(2,128)} %bitcast.3), channel_id=1, source_target_pairs={{0,4},{1,5},{2,6},{3,7},{4,0},{5,1},{6,2},{7,3},{8,12},{9,13},{10,... | collective-permute-start | bytes 622088 | tf_op jit(solution)/shard_map/ppermute | solution.py:606
  1.2 1.6 %collective-permute-start = (f32[9,2880]{1,0:T(8,128)}, f32[9,2880]{1,0:T(8,128)S(1)}, u32[]{:S(2)}, u32[]{:S(2)}) collective-permute-start(f32[9,2880]{1,0:T(8,128)} %h_ref.3), channel_id=1, source_target_pairs={{0,4},{1,5},{2,6},{3,7},{4,0},{5,1},{6,2},{7,3},{8,12},{9,13},{10,... | collective-permute-start | bytes 311048 | tf_op jit(solution)/shard_map/ppermute | solution.py:605
  1.2 1.6 %copy-start = (f32[2,9,2880]{2,0,1:T(2,128)S(1)}, f32[2,9,2880]{2,0,1:T(2,128)}, u32[]{:S(2)}) copy-start(f32[2,9,2880]{2,0,1:T(2,128)} %param.8) | copy-start | bytes 622084
  1.2 1.6 %copy-start.1 = (f32[8,3,16,128]{3,2,1,0:T(8,128)S(1)}, f32[8,3,16,128]{3,2,1,0:T(8,128)}, u32[]{:S(2)}) copy-start(f32[8,3,16,128]{3,2,1,0:T(8,128)} %constant.8.clone.geo_ref) | copy-start | bytes 589828
  1.2 1.6 %copy-start.2 = (f32[9,2880]{1,0:T(8,128)S(1)}, f32[9,2880]{1,0:T(8,128)}, u32[]{:S(2)}) copy-start(f32[9,2880]{1,0:T(8,128)} %h_ref.3) | copy-start | bytes 311044
  2.8 7.3 %copy-start.4 = (f32[192,96]{1,0:T(8,128)S(1)}, f32[192,96]{1,0:T(8,128)}, u32[]{:S(2)}) copy-start(f32[192,96]{1,0:T(8,128)} %constant.11.clone.inverse_ref) | copy-start | bytes 221188
  2.8 7.2 %copy-start.5 = (f32[192,96]{1,0:T(8,128)S(1)}, f32[192,96]{1,0:T(8,128)}, u32[]{:S(2)}) copy-start(f32[192,96]{1,0:T(8,128)} %constant.10.clone.n_ref) | copy-start | bytes 221188
  3.5 8.2 %collective-permute-start.4 = (f32[160,128]{1,0:T(8,128)S(1)}, f32[160,128]{1,0:T(8,128)S(1)}, u32[]{:S(2)}, u32[]{:S(2)}) collective-permute-start(f32[160,128]{1,0:T(8,128)S(1)} %get-tuple-element.31), channel_id=1, source_target_pairs={{0,3},{1,2},{2,1},{3,0},{4,6},{5,7},{6,4},{7,5},{8,11},{9,10},{10,... | collective-permute-start | bytes 245768 | tf_op jit(solution)/shard_map/ppermute | solution.py:616
  7.4 4.9 %collective-permute-start.5 = (f32[160,128]{1,0:T(8,128)S(1)}, f32[160,128]{1,0:T(8,128)S(1)}, u32[]{:S(2)}, u32[]{:S(2)}) collective-permute-start(f32[160,128]{1,0:T(8,128)S(1)} %get-tuple-element.32), channel_id=1, source_target_pairs={{0,1},{1,0},{2,3},{3,2},{4,7},{5,6},{6,5},{7,4},{8,9},{9,8},{10,11... | collective-permute-start | bytes 245768 | tf_op jit(solution)/shard_map/ppermute | solution.py:616
  7.9 4.4 %collective-permute-start.6 = (f32[160,128]{1,0:T(8,128)S(1)}, f32[160,128]{1,0:T(8,128)S(1)}, u32[]{:S(2)}, u32[]{:S(2)}) collective-permute-start(f32[160,128]{1,0:T(8,128)S(1)} %get-tuple-element.33), channel_id=1, source_target_pairs={{0,2},{1,3},{2,0},{3,1},{4,5},{5,4},{6,7},{7,6},{8,10},{9,11},{10,... | collective-permute-start | bytes 245768 | tf_op jit(solution)/shard_map/ppermute | solution.py:616
  8.0 7.5 %collective-permute-start.3 = (f32[120,128]{1,0:T(8,128)S(1)}, f32[120,128]{1,0:T(8,128)S(1)}, u32[]{:S(2)}, u32[]{:S(2)}) collective-permute-start(f32[120,128]{1,0:T(8,128)S(1)} %get-tuple-element.29), channel_id=1, source_target_pairs={{0,2},{1,3},{2,0},{3,1},{4,8},{5,9},{6,10},{7,11},{8,4},{9,5},{10,... | collective-permute-start | bytes 184328 | tf_op jit(solution)/shard_map/ppermute | solution.py:634
  9.9 0.7 %copy-start.6 = (s32[72]{0:T(128)S(1)}, s32[72]{0:T(128)}, u32[]{:S(2)}) copy-start(s32[72]{0:T(128)} %cut_ref.1) | copy-start | bytes 868
  9.9 5.6 %collective-permute-start.2 = (f32[72,128]{1,0:T(8,128)S(1)}, f32[72,128]{1,0:T(8,128)S(1)}, u32[]{:S(2)}, u32[]{:S(2)}) collective-permute-start(f32[72,128]{1,0:T(8,128)S(1)} %get-tuple-element.28), channel_id=1, source_target_pairs={{0,4},{1,5},{2,6},{3,7},{4,0},{5,1},{6,2},{7,3},{8,12},{9,13},{10,... | collective-permute-start | bytes 110600 | tf_op jit(solution)/shard_map/ppermute | solution.py:633
  13.3 3.7 %copy-start.7 = (bf16[3,9,2880]{2,0,1:T(4,128)(2,1)S(1)}, bf16[3,9,2880]{2,0,1:T(4,128)(2,1)}, u32[]{:S(2)}) copy-start(bf16[3,9,2880]{2,0,1:T(4,128)(2,1)} %param.10) | copy-start | bytes 466564
  13.3 6.4 %collective-permute-start.7 = (f32[144,128]{1,0:T(8,128)S(1)}, f32[144,128]{1,0:T(8,128)S(1)}, u32[]{:S(2)}, u32[]{:S(2)}) collective-permute-start(f32[144,128]{1,0:T(8,128)S(1)} %get-tuple-element.37), channel_id=1, source_target_pairs={{0,3},{1,2},{2,1},{3,0},{4,6},{5,7},{6,4},{7,5},{8,11},{9,10},{10,... | collective-permute-start | bytes 221192 | tf_op jit(solution)/shard_map/ppermute | solution.py:616
  15.2 4.8 %collective-permute-start.8 = (f32[144,128]{1,0:T(8,128)S(1)}, f32[144,128]{1,0:T(8,128)S(1)}, u32[]{:S(2)}, u32[]{:S(2)}) collective-permute-start(f32[144,128]{1,0:T(8,128)S(1)} %get-tuple-element.38), channel_id=1, source_target_pairs={{0,1},{1,0},{2,3},{3,2},{4,7},{5,6},{6,5},{7,4},{8,9},{9,8},{10,11... | collective-permute-start | bytes 221192 | tf_op jit(solution)/shard_map/ppermute | solution.py:616
  15.5 4.6 %collective-permute-start.9 = (f32[144,128]{1,0:T(8,128)S(1)}, f32[144,128]{1,0:T(8,128)S(1)}, u32[]{:S(2)}, u32[]{:S(2)}) collective-permute-start(f32[144,128]{1,0:T(8,128)S(1)} %pass.1), channel_id=1, source_target_pairs={{0,2},{1,3},{2,0},{3,1},{4,5},{5,4},{6,7},{7,6},{8,10},{9,11},{10,... | collective-permute-start | bytes 221192 | tf_op jit(solution)/shard_map/ppermute | solution.py:616

commit v22 on v21

--- a/solution.py
+++ b/solution.py
@@ -14,6 +14,7 @@
 DIFFUSION = 0.5
 LANES = 128
 PER_TILE = LANES // LEVELS
+SIDE_ROWS = 8
 EXT_ROWS = 16
 LIMIT = 48 * 1024 * 1024
 MOST_VMEM = 64 * 1024 * 1024 - 10500 * 1024
@@ -39,7 +40,7 @@
         self.share = -(-self.units // n_lon)
         self.size = self.share * self.stack
         assert self.tail <= LANES - 4 * LEVELS and rows + 2 <= EXT_ROWS and n_lat % 2 == 0
-        assert n_lon >= 4 and n_lon & (n_lon - 1) == 0
+        assert n_lon >= 4 and n_lon & (n_lon - 1) == 0 and rows == SIDE_ROWS + 1
 
     def span(self, tile):
         return self.tail if tile == self.tiles - 1 else LANES
@@ -96,6 +97,11 @@
     column = PER_TILE * np.arange(sz.stack)[:, None] + np.arange(LANES)[None, :] // LEVELS
     angle = 2 * np.pi * column / sz.nlon
     return np.stack([np.cos(angle), np.sin(angle)]).astype(np.float32)
+
+
+def spare(place):
+    row, group = divmod(place, 3)
+    return row, LEVELS * (5 + group)
 
 
 def edges_kernel(sz, h_hbm, w_hbm, q_hbm, near_ref, far_ref, sides_ref, *scratch):
@@ -141,7 +147,10 @@
                 value = refs[1][:, 0, columns]
             else:
                 value = refs[2][:, f - 2, columns].astype(jnp.float32)
-            sides_ref[EXT_ROWS * k : EXT_ROWS * k + rows, LEVELS * f : LEVELS * (f + 1)] = value
+            start = SIDE_ROWS * k
+            sides_ref[start : start + SIDE_ROWS, LEVELS * f : LEVELS * (f + 1)] = value[:SIDE_ROWS]
+            row, lane = spare(f)
+            sides_ref[start + row : start + row + 1, lane : lane + LEVELS] = value[SIDE_ROWS:]
 
 
 def add_rows(sz, ext, near_h_ref, near_w_ref, near_q_ref, far_ref):
@@ -238,13 +247,13 @@
         thick_tend = -((flux - flux_w) + (flux_n - south(flux_n)) * inv_cos)
         wind_u_tend = sin_centre * wind_v - (thick_e - thick_w) * (0.5 * inv_cos)
         wind_v_tend = -sin_centre * wind_u - (0.5 * ratio) * (thick_n - south(thick))
-        spare = 0.0
+        extra = 0.0
         if t == tiles - 1:
             last = sz.tail - LEVELS
             columns = [(tile(0, 0), 0), (thick, last), (tile(2, 0), 0), (wind_u, last)]
             for k, (source, at) in reversed(list(enumerate(columns))):
                 to = sz.tail + LEVELS * k
-                spare = jnp.where(lane < to + LEVELS, pltpu.roll(source, (to - at) % LANES, 1), spare)
+                extra = jnp.where(lane < to + LEVELS, pltpu.roll(source, (to - at) % LANES, 1), extra)
         for f, tend in enumerate((thick_tend, wind_u_tend, wind_v_tend, thick)):
             if sz.near_only:
                 alone = jnp.where(band < sz.n_lat // 2, tend[:1], tend[rows - 1 : rows])
@@ -254,7 +263,7 @@
             if f == 3:
                 continue
             if t == tiles - 1:
-                tend = jnp.where(lane < sz.tail, tend, spare)
+                tend = jnp.where(lane < sz.tail, tend, extra)
             if sz.near_only:
                 tend = jnp.where(even, north(tend), tend)
             tend_ref[pl.ds(stack * work * f + t, work, stride=stack), :] = tend[:work]
@@ -264,12 +273,10 @@
     used, sent = stack * sz.units, sz.n_lon * sz.size
     if used < sent:
         tend_ref[used:sent, :] = jnp.zeros((sent - used, LANES), jnp.float32)
-    sides = [sides_ref[:EXT_ROWS], sides_ref[EXT_ROWS:]]
+    sides = [sides_ref[:SIDE_ROWS], sides_ref[SIDE_ROWS:]]
     if sz.near_only:
-        sums = pole_sums(sz, pole_ref, wave_ref, spare, band)
-        row = lax.broadcasted_iota(jnp.int32, (EXT_ROWS, LANES), 0)
-        for k, total in enumerate(sums):
-            sides = [jnp.where(row == rows + k, total, side) for side in sides]
+        sums = pole_sums(sz, pole_ref, wave_ref, extra, band)
+        sides = [side + sums for side in sides]
     here = lax.axis_index("lon")
     for k, out_ref in enumerate(out_refs):
         out_ref[: sz.size] = tend_ref[sz.piece(k), :]
@@ -277,11 +284,16 @@
         out_ref[sz.size :] = jnp.where(eastward, sides[1], sides[0])
 
 
-def pole_sums(sz, pole_ref, wave_ref, spare, band):
+def pole_sums(sz, pole_ref, wave_ref, extra, band):
     stack, rows = sz.stack, sz.rows
-    lane = lax.broadcasted_iota(jnp.int32, (1, LANES), 1)
-    sides = jnp.where(band < sz.n_lat // 2, spare[:1], spare[rows - 1 : rows])
-    found = [jnp.zeros((1, LANES), jnp.float32), pltpu.roll(sides, (LANES // 2 - sz.tail) % LANES, 1)]
+    lane = lax.broadcasted_iota(jnp.int32, (SIDE_ROWS, LANES), 1)
+    row = lax.broadcasted_iota(jnp.int32, (SIDE_ROWS, LANES), 0)
+    found = jnp.zeros((SIDE_ROWS, LANES), jnp.float32)
+
+    def put(place, value):
+        at_row, at = spare(6 + place)
+        return jnp.where((row == at_row) & (lane >= at) & (lane < at + LEVELS), value, found)
+
     for f in range(4):
         if sz.tiles < stack:
             pole_ref[stack * f + sz.tiles : stack * (f + 1)] = jnp.zeros((stack - sz.tiles, LANES), jnp.float32)
@@ -290,9 +302,10 @@
             total = jnp.sum(terms, axis=0, keepdims=True)
             for step in (64, 32, 16):
                 total = total + pltpu.roll(total, step, 1)
-            row, place = divmod(3 * f + k, PER_TILE)
-            inside = (lane >= LEVELS * place) & (lane < LEVELS * (place + 1))
-            found[row] = jnp.where(inside, total, found[row])
+            found = put(3 * f + k, total)
+    beside = jnp.where(band < sz.n_lat // 2, extra[:1], extra[rows - 1 : rows])
+    for k in range(4):
+        found = put(12 + k, pltpu.roll(beside, (spare(18 + k)[1] - sz.tail - LEVELS * k) % LANES, 1))
     return found
 
 
@@ -301,8 +314,8 @@
     lane = lax.broadcasted_iota(jnp.int32, (1, LANES), 1)
 
     def value(s, place):
-        row, at = divmod(place, PER_TILE)
-        return pltpu.roll(rows_in[s % n_lon, row : row + 1], (-LEVELS * at) % LANES, 1)
+        row, at = spare(6 + place)
+        return pltpu.roll(rows_in[s % n_lon, row : row + 1], -at % LANES, 1)
 
     theta = 2 * math.pi / sz.nlon
     ends = (1.0, math.cos(theta * (sz.columns - 1)), math.sin(theta * (sz.columns - 1)))
@@ -340,6 +353,17 @@
     return result
 
 
+def unfolded(sides):
+    lane = lax.broadcasted_iota(jnp.int32, (1, LANES), 1)
+    start, width = spare(0)[1], 3 * LEVELS
+    ninth = jnp.where(
+        lane < width,
+        pltpu.roll(sides[0:1], -start % LANES, 1),
+        pltpu.roll(sides[1:2], (width - start) % LANES, 1),
+    )
+    return jnp.concatenate([sides, jnp.broadcast_to(ninth, sides.shape)], axis=0)
+
+
 def rest_kernel(sz, masks_ref, h_ref, w_ref, q_ref, near_h_ref, near_w_ref, near_q_ref, far_ref, geo_ref, wave_ref, after_ref, *refs):
     met_refs, (new_w_ref, new_h_ref, mass_ref, ext, pole_in) = refs[: sz.n_lon], refs[sz.n_lon :]
     band = lax.axis_index("lat")
@@ -358,9 +382,10 @@
     from_e = from_w = met_refs[0][sz.size :]
     for k, met_ref in enumerate(met_refs):
         eastward = lax.rem(sz.partner(k) - here + sz.n_lon, sz.n_lon)
-        pole_in[eastward] = met_ref[sz.size + 8 :]
+        pole_in[eastward] = met_ref[sz.size :]
         from_e = jnp.where(sz.partner(k) == lax.rem(here + 1, sz.n_lon), met_ref[sz.size :], from_e)
         from_w = jnp.where(sz.partner(k) == lax.rem(here + sz.n_lon - 1, sz.n_lon), met_ref[sz.size :], from_w)
+    from_e, from_w = unfolded(from_e), unfolded(from_w)
     for place, f in enumerate((0, 5, 2, 3, 4)):
         after = pltpu.roll(from_e, (sz.tail - LEVELS * place) % LANES, 1)[:rows]
         before = pltpu.roll(from_w, (LANES - LEVELS - LEVELS * place) % LANES, 1)[:rows]
@@ -375,7 +400,7 @@
         band = lax.axis_index("lat")
         low = band < sz.n_lat // 2
         pole_cos = jnp.where(low, inv_cos[:1], inv_cos[rows - 1 : rows])
-        kept_waves = pole_waves(sz, pole_in.at[:, rows - 8 :], pole_cos, jnp.where(low, 1.0, -1.0))
+        kept_waves = pole_waves(sz, pole_in, pole_cos, jnp.where(low, 1.0, -1.0))
 
     def stepped(f, t, value, tend):
         value = value + plain * tend
@@ -582,7 +607,7 @@
         edges_kernel,
         "edges",
         [hbm] * 3,
-        (near_row, far_row, shaped(2 * EXT_ROWS, LANES)),
+        (near_row, far_row, shaped(2 * SIDE_ROWS, LANES)),
         [pltpu.VMEM((2,) + count + (merged,), dtype) for count, dtype in kept]
         + [
             pltpu.VMEM((rows,) + (count if count != (1,) else ()) + (lanes,), dtype)
@@ -622,7 +647,7 @@
         polar_kernel,
         "polar",
         [vmem] * 9,
-        [shaped(sz.size + EXT_ROWS, LANES)] * n_lon + [far_row, near_row],
+        [shaped(sz.size + SIDE_ROWS, LANES)] * n_lon + [far_row, near_row],
         [
             all_units,
             pltpu.VMEM((4 * sz.stack, LANES), f32),

time: 21.2 us -> 21.2 us (level)
  transfers between devices with their start and end apart: 10 -> 10, of which waited for: 5 -> 5; matrix products, arithmetic and copies ran while one was open for 4% -> 4% of each run, Pallas kernels for 25% -> 26%
where the time goes in v22:
time: 21.2 us; the launch traced here: 21 us
  starting transfers between devices  10.8 us (51%)
  Pallas kernels  6.96 us (33%)
  local copies, waits for them, and re-layouts  1.32 us (6%)
  waiting for transfers between devices  1.24 us (6%)
  between operations  0.74 us (3%)
    ppermute x6, starting transfers between devices, meetings(): lax.ppermute(shares[k], ('lat', 'lon'), [(b * n_lon + i, b * n_lon + j) f...  8.07 us
    pallas_call x1, Pallas kernels, local(): call(rest_kernel, 'rest', [vmem] * 10 + [anywhere] + [vmem] * n_lon, (sha...  2.07 us
    ppermute x1, starting transfers between devices, local(): lax.ppermute(far_rows, ('lat', 'lon'), far)  1.92 us
    unnamed x18, local copies, waits for them, and re-layouts  1.32 us
    pallas_call x1, Pallas kernels, local(): call(edges_kernel, 'edges', [hbm] * 3, (near_row, far_row, shaped(2 * SID...  1.17 us
    pallas_call x1, Pallas kernels, local(): call(weights_kernel, 'weights', [smem, vmem, vmem, anywhere], (jax.ShapeD...  1.15 us
    pallas_call x1, Pallas kernels, local(): call(filter_kernel, 'filter', [vmem] * 2 + [vmem] * n_lon, [shaped(sz.siz...  0.98 us
    pallas_call x1, Pallas kernels, local(): call(finish_kernel, 'finish', [vmem] * (3 + n_lon), (shaped(*wind_rows.sh...  0.92 us
  transfers between devices with their start and end apart: 10, of which 5 were waited for; matrix products, arithmetic and copies ran while one was open for 4% of the time, Pallas kernels for 26%

profile of v22, /device:TPU:0, one launch (start us, length us, event | category | flops | bytes accessed | tf_op | source)
XLA Modules:
  0.0 21.0 jit_solution(7219964741892407891)
XLA Ops:
  0.6 0.5 %collective-permute-start.1 = (f32[9,2,2880]{2,1,0:T(2,128)}, f32[9,2,2880]{2,1,0:T(2,128)S(1)}, u32[]{:S(2)}, u32[]{:S(2)}) collective-permute-start(f32[9,2,2880]{2,1,0:T(2,128)} %bitcast.3), channel_id=1, source_target_pairs={{0,4},{1,5},{2,6},{3,7},{4,0},{5,1},{6,2},{7,3},{8,12},{9,13},{10,... | collective-permute-start | bytes 622088 | tf_op jit(solution)/shard_map/ppermute | solution.py:631
  1.2 0.1 collective-permute-start
  1.2 1.2 %edges.1 = (f32[72,128]{1,0:T(8,128)S(1)}, f32[120,128]{1,0:T(8,128)S(1)}, f32[16,128]{1,0:T(8,128)S(1)}) custom-call(f32[9,2880]{1,0:T(8,128)} %h_ref.3, f32[9,2,2880]{2,1,0:T(2,128)} %bitcast.4, bf16[9,3,2880]{2,1,0:T(4,128)(2,1)} %bitcast.7), custom_call_target="tpu_custom_call" | custom-call | tf_op jit(solution)/shard_map/edges/pallas_call | solution.py:606
  2.4 0.4 %collective-permute-done.near_h_ref = f32[9,2880]{1,0:T(8,128)S(1)} collective-permute-done((f32[9,2880]{1,0:T(8,128)}, f32[9,2880]{1,0:T(8,128)S(1)}, u32[]{:S(2)}, u32[]{:S(2)}) %collective-permute-start) | collective-permute-done | bytes 103712 | tf_op jit(solution)/shard_map/ppermute | solution.py:630
  2.8 0.0 copy-start.5
  2.9 0.7 %polar.1 = (f32[152,128]{1,0:T(8,128)S(1)}, f32[152,128]{1,0:T(8,128)S(1)}, f32[152,128]{1,0:T(8,128)S(1)}, f32[152,128]{1,0:T(8,128)S(1)}, f32[120,128]{1,0:T(8,128)S(1)}, /*index=5*/f32[72,128]{1,0:T(8,128)S(1)}) custom-call(f32[9,2880]{1,0:T(8,128)S(1)} %copy-done.2, f32[9,2,2880]{2,1,0:T(2,128)S(1)} %bitcast.5, ...), custom_call_target="tpu_custom_call" | custom-call | tf_op jit(solution)/shard_map/polar/pallas_call | solution.py:646
  3.5 3.8 %collective-permute-start.4 = (f32[152,128]{1,0:T(8,128)S(1)}, f32[152,128]{1,0:T(8,128)S(1)}, u32[]{:S(2)}, u32[]{:S(2)}) collective-permute-start(f32[152,128]{1,0:T(8,128)S(1)} %get-tuple-element.31), channel_id=1, source_target_pairs={{0,3},{1,2},{2,1},{3,0},{4,6},{5,7},{6,4},{7,5},{8,11},{9,10},{10,... | collective-permute-start | bytes 233480 | tf_op jit(solution)/shard_map/ppermute | solution.py:641
  7.3 0.5 %collective-permute-start.5 = (f32[152,128]{1,0:T(8,128)S(1)}, f32[152,128]{1,0:T(8,128)S(1)}, u32[]{:S(2)}, u32[]{:S(2)}) collective-permute-start(f32[152,128]{1,0:T(8,128)S(1)} %get-tuple-element.32), channel_id=1, source_target_pairs={{0,1},{1,0},{2,3},{3,2},{4,7},{5,6},{6,5},{7,4},{8,9},{9,8},{10,11... | collective-permute-start | bytes 233480 | tf_op jit(solution)/shard_map/ppermute | solution.py:641
  7.9 0.1 collective-permute-start.6
  8.0 1.9 %collective-permute-start.3 = (f32[120,128]{1,0:T(8,128)S(1)}, f32[120,128]{1,0:T(8,128)S(1)}, u32[]{:S(2)}, u32[]{:S(2)}) collective-permute-start(f32[120,128]{1,0:T(8,128)S(1)} %get-tuple-element.29), channel_id=1, source_target_pairs={{0,2},{1,3},{2,0},{3,1},{4,8},{5,9},{6,10},{7,11},{8,4},{9,5},{10,... | collective-permute-start | bytes 184328 | tf_op jit(solution)/shard_map/ppermute | solution.py:659
  9.9 0.2 collective-permute-start.2
  10.1 0.5 %copy-done.6 = s32[72]{0:T(128)S(1)} copy-done((s32[72]{0:T(128)S(1)}, s32[72]{0:T(128)}, u32[]{:S(2)}) %copy-start.6) | copy-done | bytes 312
  10.6 1.1 %weights.1 = (bf16[1152,96]{1,0:T(8,128)(2,1)S(1)}, f32[3,16,128]{2,1,0:T(8,128)S(1)}) custom-call(s32[72]{0:T(128)S(1)} %copy-done.6, f32[192,96]{1,0:T(8,128)S(1)} %copy-done.5, f32[192,96]{1,0:T(8,128)S(1)} %copy-done.4, f32[152,128]{1,0:T(8,128)S(1)} %get-tuple-element.26.after_ref.refs_0_), custom_call_target="tpu_custom_call" | custom-call | tf_op jit(solution)/shard_map/weights/pallas_call | solution.py:660
  11.7 0.3 %collective-permute-done.5.refs_2_ = f32[152,128]{1,0:T(8,128)S(1)} collective-permute-done((f32[152,128]{1,0:T(8,128)S(1)}, f32[152,128]{1,0:T(8,128)S(1)}, u32[]{:S(2)}, u32[]{:S(2)}) %collective-permute-start.5) | collective-permute-done | bytes 77856 | tf_op jit(solution)/shard_map/ppermute | solution.py:641
  12.1 0.2 %collective-permute-done.6.refs_3_ = f32[152,128]{1,0:T(8,128)S(1)} collective-permute-done((f32[152,128]{1,0:T(8,128)S(1)}, f32[152,128]{1,0:T(8,128)S(1)}, u32[]{:S(2)}, u32[]{:S(2)}) %collective-permute-start.6) | collective-permute-done | bytes 77856 | tf_op jit(solution)/shard_map/ppermute | solution.py:641
  12.3 1.0 %filter.1 = (f32[144,128]{1,0:T(8,128)S(1)}, f32[144,128]{1,0:T(8,128)S(1)}, f32[144,128]{1,0:T(8,128)S(1)}, f32[144,128]{1,0:T(8,128)S(1)}) custom-call(bf16[1152,96]{1,0:T(8,128)(2,1)S(1)} %get-tuple-element.30.weights_ref, f32[8,3,16,128]{3,2,1,0:T(8,128)S(1)} %copy-done.1, f32[152,128]{1,0:T(8,128)S(1)} %get-tuple-element.26.after_ref.refs_0_, ...), custom_call_target="tpu_custom_call" | custom-call | tf_op jit(solution)/shard_map/filter/pallas_call | solution.py:669
  13.3 1.8 %collective-permute-start.7 = (f32[144,128]{1,0:T(8,128)S(1)}, f32[144,128]{1,0:T(8,128)S(1)}, u32[]{:S(2)}, u32[]{:S(2)}) collective-permute-start(f32[144,128]{1,0:T(8,128)S(1)} %get-tuple-element.37), channel_id=1, source_target_pairs={{0,3},{1,2},{2,1},{3,0},{4,6},{5,7},{6,4},{7,5},{8,11},{9,10},{10,... | collective-permute-start | bytes 221192 | tf_op jit(solution)/shard_map/ppermute | solution.py:641
  15.1 0.4 %collective-permute-start.8 = (f32[144,128]{1,0:T(8,128)S(1)}, f32[144,128]{1,0:T(8,128)S(1)}, u32[]{:S(2)}, u32[]{:S(2)}) collective-permute-start(f32[144,128]{1,0:T(8,128)S(1)} %get-tuple-element.38), channel_id=1, source_target_pairs={{0,1},{1,0},{2,3},{3,2},{4,7},{5,6},{6,5},{7,4},{8,9},{9,8},{10,11... | collective-permute-start | bytes 221192 | tf_op jit(solution)/shard_map/ppermute | solution.py:641
  15.4 1.5 %collective-permute-start.9 = (f32[144,128]{1,0:T(8,128)S(1)}, f32[144,128]{1,0:T(8,128)S(1)}, u32[]{:S(2)}, u32[]{:S(2)}) collective-permute-start(f32[144,128]{1,0:T(8,128)S(1)} %pass.1), channel_id=1, source_target_pairs={{0,2},{1,3},{2,0},{3,1},{4,5},{5,4},{6,7},{7,6},{8,10},{9,11},{10,... | collective-permute-start | bytes 221192 | tf_op jit(solution)/shard_map/ppermute | solution.py:641
  16.9 2.1 %rest.1 = (f32[2,9,2880]{2,1,0:T(8,128)S(1)}, f32[9,2880]{1,0:T(8,128)S(1)}, bf16[3,9,2880]{2,1,0:T(8,128)(2,1)S(1)}) custom-call(f32[3,16,128]{2,1,0:T(8,128)S(1)} %get-tuple-element.27.masks_ref, f32[9,2880]{1,0:T(8,128)S(1)} %copy-done.2, f32[9,2,2880]{2,1,0:T(2,128)S(1)} %bitcast.6, bf16[3,9,2880]{2,1,0:T(8,128)(2,1)S(1)} %copy.11.q_ref, ...), custom_call_target="tpu_custom_call" | custom-call | tf_op jit(solution)/shard_map/rest/pallas_call | solution.py:680
  19.0 0.8 %copy.12 = bf16[3,9,2880]{2,0,1:T(4,128)(2,1)} copy(bf16[3,9,2880]{2,1,0:T(8,128)(2,1)S(1)} %get-tuple-element.45) | data formatting | bytes 311040
  19.8 0.1 collective-permute-done.8.refs_2_
  19.9 0.2 collective-permute-done.9.refs_3_
  20.1 0.9 %finish.1 = (f32[9,2,2880]{2,1,0:T(2,128)}, f32[9,2880]{1,0:T(8,128)}) custom-call(f32[3,16,128]{2,1,0:T(8,128)S(1)} %get-tuple-element.27.masks_ref, f32[2,9,2880]{2,1,0:T(8,128)S(1)} %get-tuple-element.35.base_w_ref, f32[9,2880]{1,0:T(8,128)S(1)} %get-tuple-element.36.base_h_ref, f32[144,128]{1,0:T(8,128)S(1)} %get-tuple-element.34.after_ref.refs_0_, ...), custom_call_target="tpu_custom_call" | custom-call | tf_op jit(solution)/shard_map/finish/pallas_call | solution.py:688
  (21 shorter events, 0.1 us)
Async XLA Ops:
  0.6 2.2 %copy-start.3 = (f32[2,24,128]{2,1,0:T(8,128)S(1)}, f32[2,24,128]{2,1,0:T(8,128)}, u32[]{:S(2)}) copy-start(f32[2,24,128]{2,1,0:T(8,128)} %constant.9.clone.wave_ref) | copy-start | bytes 73732
  0.6 2.2 %collective-permute-start.1 = (f32[9,2,2880]{2,1,0:T(2,128)}, f32[9,2,2880]{2,1,0:T(2,128)S(1)}, u32[]{:S(2)}, u32[]{:S(2)}) collective-permute-start(f32[9,2,2880]{2,1,0:T(2,128)} %bitcast.3), channel_id=1, source_target_pairs={{0,4},{1,5},{2,6},{3,7},{4,0},{5,1},{6,2},{7,3},{8,12},{9,13},{10,... | collective-permute-start | bytes 622088 | tf_op jit(solution)/shard_map/ppermute | solution.py:631
  1.2 1.6 %collective-permute-start = (f32[9,2880]{1,0:T(8,128)}, f32[9,2880]{1,0:T(8,128)S(1)}, u32[]{:S(2)}, u32[]{:S(2)}) collective-permute-start(f32[9,2880]{1,0:T(8,128)} %h_ref.3), channel_id=1, source_target_pairs={{0,4},{1,5},{2,6},{3,7},{4,0},{5,1},{6,2},{7,3},{8,12},{9,13},{10,... | collective-permute-start | bytes 311048 | tf_op jit(solution)/shard_map/ppermute | solution.py:630
  1.2 1.6 %copy-start = (f32[2,9,2880]{2,0,1:T(2,128)S(1)}, f32[2,9,2880]{2,0,1:T(2,128)}, u32[]{:S(2)}) copy-start(f32[2,9,2880]{2,0,1:T(2,128)} %param.8) | copy-start | bytes 622084
  1.2 1.6 %copy-start.1 = (f32[8,3,16,128]{3,2,1,0:T(8,128)S(1)}, f32[8,3,16,128]{3,2,1,0:T(8,128)}, u32[]{:S(2)}) copy-start(f32[8,3,16,128]{3,2,1,0:T(8,128)} %constant.8.clone.geo_ref) | copy-start | bytes 589828
  1.2 1.6 %copy-start.2 = (f32[9,2880]{1,0:T(8,128)S(1)}, f32[9,2880]{1,0:T(8,128)}, u32[]{:S(2)}) copy-start(f32[9,2880]{1,0:T(8,128)} %h_ref.3) | copy-start | bytes 311044
  2.8 7.2 %copy-start.4 = (f32[192,96]{1,0:T(8,128)S(1)}, f32[192,96]{1,0:T(8,128)}, u32[]{:S(2)}) copy-start(f32[192,96]{1,0:T(8,128)} %constant.11.clone.inverse_ref) | copy-start | bytes 221188
  2.8 7.2 %copy-start.5 = (f32[192,96]{1,0:T(8,128)S(1)}, f32[192,96]{1,0:T(8,128)}, u32[]{:S(2)}) copy-start(f32[192,96]{1,0:T(8,128)} %constant.10.clone.n_ref) | copy-start | bytes 221188
  3.5 8.2 %collective-permute-start.4 = (f32[152,128]{1,0:T(8,128)S(1)}, f32[152,128]{1,0:T(8,128)S(1)}, u32[]{:S(2)}, u32[]{:S(2)}) collective-permute-start(f32[152,128]{1,0:T(8,128)S(1)} %get-tuple-element.31), channel_id=1, source_target_pairs={{0,3},{1,2},{2,1},{3,0},{4,6},{5,7},{6,4},{7,5},{8,11},{9,10},{10,... | collective-permute-start | bytes 233480 | tf_op jit(solution)/shard_map/ppermute | solution.py:641
  7.3 4.7 %collective-permute-start.5 = (f32[152,128]{1,0:T(8,128)S(1)}, f32[152,128]{1,0:T(8,128)S(1)}, u32[]{:S(2)}, u32[]{:S(2)}) collective-permute-start(f32[152,128]{1,0:T(8,128)S(1)} %get-tuple-element.32), channel_id=1, source_target_pairs={{0,1},{1,0},{2,3},{3,2},{4,7},{5,6},{6,5},{7,4},{8,9},{9,8},{10,11... | collective-permute-start | bytes 233480 | tf_op jit(solution)/shard_map/ppermute | solution.py:641
  7.9 4.4 %collective-permute-start.6 = (f32[152,128]{1,0:T(8,128)S(1)}, f32[152,128]{1,0:T(8,128)S(1)}, u32[]{:S(2)}, u32[]{:S(2)}) collective-permute-start(f32[152,128]{1,0:T(8,128)S(1)} %get-tuple-element.33), channel_id=1, source_target_pairs={{0,2},{1,3},{2,0},{3,1},{4,5},{5,4},{6,7},{7,6},{8,10},{9,11},{10,... | collective-permute-start | bytes 233480 | tf_op jit(solution)/shard_map/ppermute | solution.py:641
  8.0 7.5 %collective-permute-start.3 = (f32[120,128]{1,0:T(8,128)S(1)}, f32[120,128]{1,0:T(8,128)S(1)}, u32[]{:S(2)}, u32[]{:S(2)}) collective-permute-start(f32[120,128]{1,0:T(8,128)S(1)} %get-tuple-element.29), channel_id=1, source_target_pairs={{0,2},{1,3},{2,0},{3,1},{4,8},{5,9},{6,10},{7,11},{8,4},{9,5},{10,... | collective-permute-start | bytes 184328 | tf_op jit(solution)/shard_map/ppermute | solution.py:659
  9.9 0.7 %copy-start.6 = (s32[72]{0:T(128)S(1)}, s32[72]{0:T(128)}, u32[]{:S(2)}) copy-start(s32[72]{0:T(128)} %cut_ref.1) | copy-start | bytes 868
  9.9 5.5 %collective-permute-start.2 = (f32[72,128]{1,0:T(8,128)S(1)}, f32[72,128]{1,0:T(8,128)S(1)}, u32[]{:S(2)}, u32[]{:S(2)}) collective-permute-start(f32[72,128]{1,0:T(8,128)S(1)} %get-tuple-element.28), channel_id=1, source_target_pairs={{0,4},{1,5},{2,6},{3,7},{4,0},{5,1},{6,2},{7,3},{8,12},{9,13},{10,... | collective-permute-start | bytes 110600 | tf_op jit(solution)/shard_map/ppermute | solution.py:658
  13.3 3.7 %copy-start.7 = (bf16[3,9,2880]{2,0,1:T(4,128)(2,1)S(1)}, bf16[3,9,2880]{2,0,1:T(4,128)(2,1)}, u32[]{:S(2)}) copy-start(bf16[3,9,2880]{2,0,1:T(4,128)(2,1)} %param.10) | copy-start | bytes 466564
  13.3 6.5 %collective-permute-start.7 = (f32[144,128]{1,0:T(8,128)S(1)}, f32[144,128]{1,0:T(8,128)S(1)}, u32[]{:S(2)}, u32[]{:S(2)}) collective-permute-start(f32[144,128]{1,0:T(8,128)S(1)} %get-tuple-element.37), channel_id=1, source_target_pairs={{0,3},{1,2},{2,1},{3,0},{4,6},{5,7},{6,4},{7,5},{8,11},{9,10},{10,... | collective-permute-start | bytes 221192 | tf_op jit(solution)/shard_map/ppermute | solution.py:641
  15.1 4.9 %collective-permute-start.8 = (f32[144,128]{1,0:T(8,128)S(1)}, f32[144,128]{1,0:T(8,128)S(1)}, u32[]{:S(2)}, u32[]{:S(2)}) collective-permute-start(f32[144,128]{1,0:T(8,128)S(1)} %get-tuple-element.38), channel_id=1, source_target_pairs={{0,1},{1,0},{2,3},{3,2},{4,7},{5,6},{6,5},{7,4},{8,9},{9,8},{10,11... | collective-permute-start | bytes 221192 | tf_op jit(solution)/shard_map/ppermute | solution.py:641
  15.4 4.7 %collective-permute-start.9 = (f32[144,128]{1,0:T(8,128)S(1)}, f32[144,128]{1,0:T(8,128)S(1)}, u32[]{:S(2)}, u32[]{:S(2)}) collective-permute-start(f32[144,128]{1,0:T(8,128)S(1)} %pass.1), channel_id=1, source_target_pairs={{0,2},{1,3},{2,0},{3,1},{4,5},{5,4},{6,7},{7,6},{8,10},{9,11},{10,... | collective-permute-start | bytes 221192 | tf_op jit(solution)/shard_map/ppermute | solution.py:641

commit v23 on v22

--- a/solution.py
+++ b/solution.py
@@ -53,17 +53,19 @@
         pole = jnp.where(band == 0, 0, jnp.where(band == self.n_lat - 1, self.rows - 1, -1))
         return row == (pole if self.near_only else -1)
 
-    def turns(self, odd):
+    def turns(self, odd, back):
         middle, last = list(range(1, self.n_lon - 1)), self.n_lon - 1
-        return [0, middle[-1], last] + middle[-2::-1] if odd else [0, last] + middle
-
-    def partner(self, k):
+        if odd and not back:
+            return [0, middle[-1], last] + middle[-2::-1]
+        return [0, last] + (middle[::-1] if odd else middle)
+
+    def partner(self, k, back=False):
         odd = lax.rem(lax.axis_index("lat"), 2) == 1
-        turn = jnp.where(odd, self.turns(True)[k], self.turns(False)[k])
+        turn = jnp.where(odd, self.turns(True, back)[k], self.turns(False, back)[k])
         return jnp.bitwise_xor(lax.axis_index("lon"), turn)
 
-    def piece(self, k):
-        return pl.ds(pl.multiple_of(self.partner(k) * self.size, 8), self.size)
+    def piece(self, k, back=False):
+        return pl.ds(pl.multiple_of(self.partner(k, back) * self.size, 8), self.size)
 
 
 def geometry(sz):
@@ -455,9 +457,9 @@
 
 
 def sin_pi(y):
-    y = jnp.where(y > 0.5, 1.0 - y, jnp.where(y < -0.5, -1.0 - y, y))
+    y = jnp.maximum(jnp.minimum(y, 1.0 - y), -1.0 - y)
     s = y * y
-    series = [(-1) ** i * math.pi ** (2 * i + 1) / math.factorial(2 * i + 1) for i in range(7)]
+    series = [(-1) ** i * math.pi ** (2 * i + 1) / math.factorial(2 * i + 1) for i in range(6)]
     total = series[-1]
     for factor in reversed(series[:-1]):
         total = total * s + factor
@@ -545,14 +547,14 @@
                 carried = over if carried is None else carried + over
             results[s, here] = pltpu.roll(same, stack - 1, 0) + carried
     for k, out_ref in enumerate(out_refs):
-        out_ref[...] = results[sz.partner(k), : sz.size]
+        out_ref[...] = results[sz.partner(k, True), : sz.size]
 
 
 def finish_kernel(sz, masks_ref, base_w_ref, base_h_ref, *refs):
     back_refs, (new_w_ref, new_h_ref, back_ref) = refs[: sz.n_lon], refs[sz.n_lon :]
     rows, work = sz.rows, sz.work
     for k, ref in enumerate(back_refs):
-        back_ref[sz.piece(k), :] = ref[...]
+        back_ref[sz.piece(k, True), :] = ref[...]
     scale = masks_ref[2]
     even = lax.rem(lax.axis_index("lat"), 2) == 0
     for f in range(3):
@@ -632,9 +634,8 @@
     if not sz.near_only:
         far_rows = lax.ppermute(far_rows, ("lat", "lon"), far)
 
-    order = [sz.turns(False), sz.turns(True)]
-
-    def meetings(shares):
+    def meetings(shares, back):
+        order = [sz.turns(False, back), sz.turns(True, back)]
         got = [shares[0]]
         for k in range(1, n_lon):
             sectors = [(band, i, i ^ order[band % 2][k]) for band in range(n_lat) for i in range(n_lon)]
@@ -654,7 +655,7 @@
             pltpu.VMEM((3, EXT_ROWS, sz.tiles * LANES), f32),
         ],
     )(thickness, wind_rows, near_h, near_w, sides, geo, wave, far_rows, near_q)
-    met = meetings(tends)
+    met = meetings(tends, False)
     near_q = lax.ppermute(near_q, ("lat", "lon"), near)
     from_far = lax.ppermute(far_rows, ("lat", "lon"), far) if sz.near_only else far_rows
     weights, masks = call(
@@ -675,7 +676,7 @@
     )(weights, geo, *met)
     held = call(pass_kernel, "pass", [vmem] + [anywhere] * 2, shaped(sz.size, LANES))(worked[-1], from_far, near_q)
     worked = [*worked[:-1], held]
-    back = meetings(worked)
+    back = meetings(worked, True)
 
     base_w, base_h, mass = call(
         rest_kernel,

time: 21.2 us -> 21.1 us (level)
  transfers between devices with their start and end apart: 10 -> 10, of which waited for: 5 -> 4; matrix products, arithmetic and copies ran while one was open for 4% -> 4% of each run, Pallas kernels for 26% -> 25%
where the time goes in v23:
time: 21.1 us; the launch traced here: 21 us
  starting transfers between devices  10.8 us (51%)
  Pallas kernels  6.88 us (33%)
  local copies, waits for them, and re-layouts  1.32 us (6%)
  waiting for transfers between devices  1.28 us (6%)
  between operations  0.74 us (4%)
    ppermute x6, starting transfers between devices, meetings(): lax.ppermute(shares[k], ('lat', 'lon'), [(b * n_lon + i, b * n_lon + j) f...  8.07 us
    pallas_call x1, Pallas kernels, local(): call(rest_kernel, 'rest', [vmem] * 10 + [anywhere] + [vmem] * n_lon, (sha...  2.07 us
    ppermute x1, starting transfers between devices, local(): lax.ppermute(far_rows, ('lat', 'lon'), far)  1.92 us
    unnamed x18, local copies, waits for them, and re-layouts  1.32 us
    pallas_call x1, Pallas kernels, local(): call(edges_kernel, 'edges', [hbm] * 3, (near_row, far_row, shaped(2 * SID...  1.17 us
    pallas_call x1, Pallas kernels, local(): call(weights_kernel, 'weights', [smem, vmem, vmem, anywhere], (jax.ShapeD...  1.07 us
    pallas_call x1, Pallas kernels, local(): call(filter_kernel, 'filter', [vmem] * 2 + [vmem] * n_lon, [shaped(sz.siz...  0.98 us
    pallas_call x1, Pallas kernels, local(): call(finish_kernel, 'finish', [vmem] * (3 + n_lon), (shaped(*wind_rows.sh...  0.92 us
  transfers between devices with their start and end apart: 10, of which 4 were waited for; matrix products, arithmetic and copies ran while one was open for 4% of the time, Pallas kernels for 25%

profile of v23, /device:TPU:0, one launch (start us, length us, event | category | flops | bytes accessed | tf_op | source)
XLA Modules:
  0.0 21.0 jit_solution(944566022590850724)
XLA Ops:
  0.6 0.0 copy-start.3
  0.6 0.5 %collective-permute-start.1 = (f32[9,2,2880]{2,1,0:T(2,128)}, f32[9,2,2880]{2,1,0:T(2,128)S(1)}, u32[]{:S(2)}, u32[]{:S(2)}) collective-permute-start(f32[9,2,2880]{2,1,0:T(2,128)} %bitcast.3), channel_id=1, source_target_pairs={{0,4},{1,5},{2,6},{3,7},{4,0},{5,1},{6,2},{7,3},{8,12},{9,13},{10,... | collective-permute-start | bytes 622088 | tf_op jit(solution)/shard_map/ppermute | solution.py:633
  1.2 0.1 collective-permute-start
  1.2 1.2 %edges.1 = (f32[72,128]{1,0:T(8,128)S(1)}, f32[120,128]{1,0:T(8,128)S(1)}, f32[16,128]{1,0:T(8,128)S(1)}) custom-call(f32[9,2880]{1,0:T(8,128)} %h_ref.3, f32[9,2,2880]{2,1,0:T(2,128)} %bitcast.4, bf16[9,3,2880]{2,1,0:T(4,128)(2,1)} %bitcast.7), custom_call_target="tpu_custom_call" | custom-call | tf_op jit(solution)/shard_map/edges/pallas_call | solution.py:608
  2.4 0.4 %collective-permute-done.near_h_ref = f32[9,2880]{1,0:T(8,128)S(1)} collective-permute-done((f32[9,2880]{1,0:T(8,128)}, f32[9,2880]{1,0:T(8,128)S(1)}, u32[]{:S(2)}, u32[]{:S(2)}) %collective-permute-start) | collective-permute-done | bytes 103712 | tf_op jit(solution)/shard_map/ppermute | solution.py:632
  2.8 0.0 copy-start.5
  2.9 0.7 %polar.1 = (f32[152,128]{1,0:T(8,128)S(1)}, f32[152,128]{1,0:T(8,128)S(1)}, f32[152,128]{1,0:T(8,128)S(1)}, f32[152,128]{1,0:T(8,128)S(1)}, f32[120,128]{1,0:T(8,128)S(1)}, /*index=5*/f32[72,128]{1,0:T(8,128)S(1)}) custom-call(f32[9,2880]{1,0:T(8,128)S(1)} %copy-done.2, f32[9,2,2880]{2,1,0:T(2,128)S(1)} %bitcast.5, ...), custom_call_target="tpu_custom_call" | custom-call | tf_op jit(solution)/shard_map/polar/pallas_call | solution.py:647
  3.5 3.8 %collective-permute-start.4 = (f32[152,128]{1,0:T(8,128)S(1)}, f32[152,128]{1,0:T(8,128)S(1)}, u32[]{:S(2)}, u32[]{:S(2)}) collective-permute-start(f32[152,128]{1,0:T(8,128)S(1)} %get-tuple-element.31), channel_id=1, source_target_pairs={{0,3},{1,2},{2,1},{3,0},{4,6},{5,7},{6,4},{7,5},{8,11},{9,10},{10,... | collective-permute-start | bytes 233480 | tf_op jit(solution)/shard_map/ppermute | solution.py:642
  7.3 0.5 %collective-permute-start.5 = (f32[152,128]{1,0:T(8,128)S(1)}, f32[152,128]{1,0:T(8,128)S(1)}, u32[]{:S(2)}, u32[]{:S(2)}) collective-permute-start(f32[152,128]{1,0:T(8,128)S(1)} %get-tuple-element.32), channel_id=1, source_target_pairs={{0,1},{1,0},{2,3},{3,2},{4,7},{5,6},{6,5},{7,4},{8,9},{9,8},{10,11... | collective-permute-start | bytes 233480 | tf_op jit(solution)/shard_map/ppermute | solution.py:642
  7.9 0.1 collective-permute-start.6
  8.0 1.9 %collective-permute-start.3 = (f32[120,128]{1,0:T(8,128)S(1)}, f32[120,128]{1,0:T(8,128)S(1)}, u32[]{:S(2)}, u32[]{:S(2)}) collective-permute-start(f32[120,128]{1,0:T(8,128)S(1)} %get-tuple-element.29), channel_id=1, source_target_pairs={{0,2},{1,3},{2,0},{3,1},{4,8},{5,9},{6,10},{7,11},{8,4},{9,5},{10,... | collective-permute-start | bytes 184328 | tf_op jit(solution)/shard_map/ppermute | solution.py:660
  9.9 0.2 collective-permute-start.2
  10.1 0.5 %copy-done.6 = s32[72]{0:T(128)S(1)} copy-done((s32[72]{0:T(128)S(1)}, s32[72]{0:T(128)}, u32[]{:S(2)}) %copy-start.6) | copy-done | bytes 312
  10.6 1.1 %weights.1 = (bf16[1152,96]{1,0:T(8,128)(2,1)S(1)}, f32[3,16,128]{2,1,0:T(8,128)S(1)}) custom-call(s32[72]{0:T(128)S(1)} %copy-done.6, f32[192,96]{1,0:T(8,128)S(1)} %copy-done.5, f32[192,96]{1,0:T(8,128)S(1)} %copy-done.4, f32[152,128]{1,0:T(8,128)S(1)} %get-tuple-element.26.after_ref.refs_0_), custom_call_target="tpu_custom_call" | custom-call | tf_op jit(solution)/shard_map/weights/pallas_call | solution.py:661
  11.6 0.4 %collective-permute-done.5.refs_2_ = f32[152,128]{1,0:T(8,128)S(1)} collective-permute-done((f32[152,128]{1,0:T(8,128)S(1)}, f32[152,128]{1,0:T(8,128)S(1)}, u32[]{:S(2)}, u32[]{:S(2)}) %collective-permute-start.5) | collective-permute-done | bytes 77856 | tf_op jit(solution)/shard_map/ppermute | solution.py:642
  12.1 0.2 %collective-permute-done.6.refs_3_ = f32[152,128]{1,0:T(8,128)S(1)} collective-permute-done((f32[152,128]{1,0:T(8,128)S(1)}, f32[152,128]{1,0:T(8,128)S(1)}, u32[]{:S(2)}, u32[]{:S(2)}) %collective-permute-start.6) | collective-permute-done | bytes 77856 | tf_op jit(solution)/shard_map/ppermute | solution.py:642
  12.3 1.0 %filter.1 = (f32[144,128]{1,0:T(8,128)S(1)}, f32[144,128]{1,0:T(8,128)S(1)}, f32[144,128]{1,0:T(8,128)S(1)}, f32[144,128]{1,0:T(8,128)S(1)}) custom-call(bf16[1152,96]{1,0:T(8,128)(2,1)S(1)} %get-tuple-element.30.weights_ref, f32[8,3,16,128]{3,2,1,0:T(8,128)S(1)} %copy-done.1, f32[152,128]{1,0:T(8,128)S(1)} %get-tuple-element.26.after_ref.refs_0_, ...), custom_call_target="tpu_custom_call" | custom-call | tf_op jit(solution)/shard_map/filter/pallas_call | solution.py:670
  13.3 1.8 %collective-permute-start.7 = (f32[144,128]{1,0:T(8,128)S(1)}, f32[144,128]{1,0:T(8,128)S(1)}, u32[]{:S(2)}, u32[]{:S(2)}) collective-permute-start(f32[144,128]{1,0:T(8,128)S(1)} %get-tuple-element.37), channel_id=1, source_target_pairs={{0,3},{1,2},{2,1},{3,0},{4,7},{5,6},{6,5},{7,4},{8,11},{9,10},{10,... | collective-permute-start | bytes 221192 | tf_op jit(solution)/shard_map/ppermute | solution.py:642
  15.1 0.4 %collective-permute-start.8 = (f32[144,128]{1,0:T(8,128)S(1)}, f32[144,128]{1,0:T(8,128)S(1)}, u32[]{:S(2)}, u32[]{:S(2)}) collective-permute-start(f32[144,128]{1,0:T(8,128)S(1)} %get-tuple-element.38), channel_id=1, source_target_pairs={{0,1},{1,0},{2,3},{3,2},{4,6},{5,7},{6,4},{7,5},{8,9},{9,8},{10,11... | collective-permute-start | bytes 221192 | tf_op jit(solution)/shard_map/ppermute | solution.py:642
  15.4 1.5 %collective-permute-start.9 = (f32[144,128]{1,0:T(8,128)S(1)}, f32[144,128]{1,0:T(8,128)S(1)}, u32[]{:S(2)}, u32[]{:S(2)}) collective-permute-start(f32[144,128]{1,0:T(8,128)S(1)} %pass.1), channel_id=1, source_target_pairs={{0,2},{1,3},{2,0},{3,1},{4,5},{5,4},{6,7},{7,6},{8,10},{9,11},{10,... | collective-permute-start | bytes 221192 | tf_op jit(solution)/shard_map/ppermute | solution.py:642
  16.9 2.1 %rest.1 = (f32[2,9,2880]{2,1,0:T(8,128)S(1)}, f32[9,2880]{1,0:T(8,128)S(1)}, bf16[3,9,2880]{2,1,0:T(8,128)(2,1)S(1)}) custom-call(f32[3,16,128]{2,1,0:T(8,128)S(1)} %get-tuple-element.27.masks_ref, f32[9,2880]{1,0:T(8,128)S(1)} %copy-done.2, f32[9,2,2880]{2,1,0:T(2,128)S(1)} %bitcast.6, bf16[3,9,2880]{2,1,0:T(8,128)(2,1)S(1)} %copy.11.q_ref, ...), custom_call_target="tpu_custom_call" | custom-call | tf_op jit(solution)/shard_map/rest/pallas_call | solution.py:681
  19.0 0.8 %copy.12 = bf16[3,9,2880]{2,0,1:T(4,128)(2,1)} copy(bf16[3,9,2880]{2,1,0:T(8,128)(2,1)S(1)} %get-tuple-element.45) | data formatting | bytes 311040
  19.8 0.3 %collective-permute-done.9.refs_3_ = f32[144,128]{1,0:T(8,128)S(1)} collective-permute-done((f32[144,128]{1,0:T(8,128)S(1)}, f32[144,128]{1,0:T(8,128)S(1)}, u32[]{:S(2)}, u32[]{:S(2)}) %collective-permute-start.9) | collective-permute-done | bytes 73760 | tf_op jit(solution)/shard_map/ppermute | solution.py:642
  20.1 0.9 %finish.1 = (f32[9,2,2880]{2,1,0:T(2,128)}, f32[9,2880]{1,0:T(8,128)}) custom-call(f32[3,16,128]{2,1,0:T(8,128)S(1)} %get-tuple-element.27.masks_ref, f32[2,9,2880]{2,1,0:T(8,128)S(1)} %get-tuple-element.35.base_w_ref, f32[9,2880]{1,0:T(8,128)S(1)} %get-tuple-element.36.base_h_ref, f32[144,128]{1,0:T(8,128)S(1)} %get-tuple-element.34.after_ref.refs_0_, ...), custom_call_target="tpu_custom_call" | custom-call | tf_op jit(solution)/shard_map/finish/pallas_call | solution.py:689
  (21 shorter events, 0.1 us)
Async XLA Ops:
  0.6 2.2 %copy-start.3 = (f32[2,24,128]{2,1,0:T(8,128)S(1)}, f32[2,24,128]{2,1,0:T(8,128)}, u32[]{:S(2)}) copy-start(f32[2,24,128]{2,1,0:T(8,128)} %constant.9.clone.wave_ref) | copy-start | bytes 73732
  0.6 2.2 %collective-permute-start.1 = (f32[9,2,2880]{2,1,0:T(2,128)}, f32[9,2,2880]{2,1,0:T(2,128)S(1)}, u32[]{:S(2)}, u32[]{:S(2)}) collective-permute-start(f32[9,2,2880]{2,1,0:T(2,128)} %bitcast.3), channel_id=1, source_target_pairs={{0,4},{1,5},{2,6},{3,7},{4,0},{5,1},{6,2},{7,3},{8,12},{9,13},{10,... | collective-permute-start | bytes 622088 | tf_op jit(solution)/shard_map/ppermute | solution.py:633
  1.2 1.6 %collective-permute-start = (f32[9,2880]{1,0:T(8,128)}, f32[9,2880]{1,0:T(8,128)S(1)}, u32[]{:S(2)}, u32[]{:S(2)}) collective-permute-start(f32[9,2880]{1,0:T(8,128)} %h_ref.3), channel_id=1, source_target_pairs={{0,4},{1,5},{2,6},{3,7},{4,0},{5,1},{6,2},{7,3},{8,12},{9,13},{10,... | collective-permute-start | bytes 311048 | tf_op jit(solution)/shard_map/ppermute | solution.py:632
  1.2 1.6 %copy-start = (f32[2,9,2880]{2,0,1:T(2,128)S(1)}, f32[2,9,2880]{2,0,1:T(2,128)}, u32[]{:S(2)}) copy-start(f32[2,9,2880]{2,0,1:T(2,128)} %param.8) | copy-start | bytes 622084
  1.2 1.6 %copy-start.1 = (f32[8,3,16,128]{3,2,1,0:T(8,128)S(1)}, f32[8,3,16,128]{3,2,1,0:T(8,128)}, u32[]{:S(2)}) copy-start(f32[8,3,16,128]{3,2,1,0:T(8,128)} %constant.8.clone.geo_ref) | copy-start | bytes 589828
  1.2 1.6 %copy-start.2 = (f32[9,2880]{1,0:T(8,128)S(1)}, f32[9,2880]{1,0:T(8,128)}, u32[]{:S(2)}) copy-start(f32[9,2880]{1,0:T(8,128)} %h_ref.3) | copy-start | bytes 311044
  2.8 7.2 %copy-start.4 = (f32[192,96]{1,0:T(8,128)S(1)}, f32[192,96]{1,0:T(8,128)}, u32[]{:S(2)}) copy-start(f32[192,96]{1,0:T(8,128)} %constant.11.clone.inverse_ref) | copy-start | bytes 221188
  2.8 7.2 %copy-start.5 = (f32[192,96]{1,0:T(8,128)S(1)}, f32[192,96]{1,0:T(8,128)}, u32[]{:S(2)}) copy-start(f32[192,96]{1,0:T(8,128)} %constant.10.clone.n_ref) | copy-start | bytes 221188
  3.5 8.1 %collective-permute-start.4 = (f32[152,128]{1,0:T(8,128)S(1)}, f32[152,128]{1,0:T(8,128)S(1)}, u32[]{:S(2)}, u32[]{:S(2)}) collective-permute-start(f32[152,128]{1,0:T(8,128)S(1)} %get-tuple-element.31), channel_id=1, source_target_pairs={{0,3},{1,2},{2,1},{3,0},{4,6},{5,7},{6,4},{7,5},{8,11},{9,10},{10,... | collective-permute-start | bytes 233480 | tf_op jit(solution)/shard_map/ppermute | solution.py:642
  7.3 4.7 %collective-permute-start.5 = (f32[152,128]{1,0:T(8,128)S(1)}, f32[152,128]{1,0:T(8,128)S(1)}, u32[]{:S(2)}, u32[]{:S(2)}) collective-permute-start(f32[152,128]{1,0:T(8,128)S(1)} %get-tuple-element.32), channel_id=1, source_target_pairs={{0,1},{1,0},{2,3},{3,2},{4,7},{5,6},{6,5},{7,4},{8,9},{9,8},{10,11... | collective-permute-start | bytes 233480 | tf_op jit(solution)/shard_map/ppermute | solution.py:642
  7.9 4.4 %collective-permute-start.6 = (f32[152,128]{1,0:T(8,128)S(1)}, f32[152,128]{1,0:T(8,128)S(1)}, u32[]{:S(2)}, u32[]{:S(2)}) collective-permute-start(f32[152,128]{1,0:T(8,128)S(1)} %get-tuple-element.33), channel_id=1, source_target_pairs={{0,2},{1,3},{2,0},{3,1},{4,5},{5,4},{6,7},{7,6},{8,10},{9,11},{10,... | collective-permute-start | bytes 233480 | tf_op jit(solution)/shard_map/ppermute | solution.py:642
  8.0 7.4 %collective-permute-start.3 = (f32[120,128]{1,0:T(8,128)S(1)}, f32[120,128]{1,0:T(8,128)S(1)}, u32[]{:S(2)}, u32[]{:S(2)}) collective-permute-start(f32[120,128]{1,0:T(8,128)S(1)} %get-tuple-element.29), channel_id=1, source_target_pairs={{0,2},{1,3},{2,0},{3,1},{4,8},{5,9},{6,10},{7,11},{8,4},{9,5},{10,... | collective-permute-start | bytes 184328 | tf_op jit(solution)/shard_map/ppermute | solution.py:660
  9.9 0.7 %copy-start.6 = (s32[72]{0:T(128)S(1)}, s32[72]{0:T(128)}, u32[]{:S(2)}) copy-start(s32[72]{0:T(128)} %cut_ref.1) | copy-start | bytes 868
  9.9 5.5 %collective-permute-start.2 = (f32[72,128]{1,0:T(8,128)S(1)}, f32[72,128]{1,0:T(8,128)S(1)}, u32[]{:S(2)}, u32[]{:S(2)}) collective-permute-start(f32[72,128]{1,0:T(8,128)S(1)} %get-tuple-element.28), channel_id=1, source_target_pairs={{0,4},{1,5},{2,6},{3,7},{4,0},{5,1},{6,2},{7,3},{8,12},{9,13},{10,... | collective-permute-start | bytes 110600 | tf_op jit(solution)/shard_map/ppermute | solution.py:659
  13.3 3.7 %copy-start.7 = (bf16[3,9,2880]{2,0,1:T(4,128)(2,1)S(1)}, bf16[3,9,2880]{2,0,1:T(4,128)(2,1)}, u32[]{:S(2)}) copy-start(bf16[3,9,2880]{2,0,1:T(4,128)(2,1)} %param.10) | copy-start | bytes 466564
  13.3 6.5 %collective-permute-start.7 = (f32[144,128]{1,0:T(8,128)S(1)}, f32[144,128]{1,0:T(8,128)S(1)}, u32[]{:S(2)}, u32[]{:S(2)}) collective-permute-start(f32[144,128]{1,0:T(8,128)S(1)} %get-tuple-element.37), channel_id=1, source_target_pairs={{0,3},{1,2},{2,1},{3,0},{4,7},{5,6},{6,5},{7,4},{8,11},{9,10},{10,... | collective-permute-start | bytes 221192 | tf_op jit(solution)/shard_map/ppermute | solution.py:642
  15.1 4.7 %collective-permute-start.8 = (f32[144,128]{1,0:T(8,128)S(1)}, f32[144,128]{1,0:T(8,128)S(1)}, u32[]{:S(2)}, u32[]{:S(2)}) collective-permute-start(f32[144,128]{1,0:T(8,128)S(1)} %get-tuple-element.38), channel_id=1, source_target_pairs={{0,1},{1,0},{2,3},{3,2},{4,6},{5,7},{6,4},{7,5},{8,9},{9,8},{10,11... | collective-permute-start | bytes 221192 | tf_op jit(solution)/shard_map/ppermute | solution.py:642
  15.4 4.6 %collective-permute-start.9 = (f32[144,128]{1,0:T(8,128)S(1)}, f32[144,128]{1,0:T(8,128)S(1)}, u32[]{:S(2)}, u32[]{:S(2)}) collective-permute-start(f32[144,128]{1,0:T(8,128)S(1)} %pass.1), channel_id=1, source_target_pairs={{0,2},{1,3},{2,0},{3,1},{4,5},{5,4},{6,7},{7,6},{8,10},{9,11},{10,... | collective-permute-start | bytes 221192 | tf_op jit(solution)/shard_map/ppermute | solution.py:642

commit v24 on v22

--- a/solution.py
+++ b/solution.py
@@ -204,12 +204,9 @@
     return pltpu.roll(value, 1, 0)
 
 
-def polar_kernel(sz, h_ref, w_ref, near_h_ref, near_w_ref, sides_ref, geo_ref, wave_ref, far_ref, near_q_ref, *refs):
-    out_refs, (far_out, near_out, tend_ref, pole_ref, ext) = refs[:-5], refs[-5:]
-    far_out[...] = far_ref[...]
-    near_out[...] = near_q_ref[...]
-    if sz.near_only:
-        far_ref = None
+def polar_kernel(sz, h_ref, w_ref, near_h_ref, near_w_ref, sides_ref, geo_ref, wave_ref, *refs):
+    far_ref, refs = (None, refs) if sz.near_only else (refs[0], refs[1:])
+    out_refs, (tend_ref, pole_ref, ext) = refs[:-3], refs[-3:]
     band = lax.axis_index("lat")
     ring = Tiles(sz)
     lane = ring.lane
@@ -643,17 +640,17 @@
 
     all_pieces = pltpu.VMEM((n_lon, sz.size + 8 * sz.stack, LANES), f32)
     all_units = pltpu.VMEM((n_lon * sz.size + 8 * sz.stack, LANES), f32)
-    *tends, far_rows, near_q = call(
+    tends = call(
         polar_kernel,
         "polar",
-        [vmem] * 9,
-        [shaped(sz.size + SIDE_ROWS, LANES)] * n_lon + [far_row, near_row],
+        [vmem] * (7 if sz.near_only else 8),
+        [shaped(sz.size + SIDE_ROWS, LANES)] * n_lon,
         [
             all_units,
             pltpu.VMEM((4 * sz.stack, LANES), f32),
             pltpu.VMEM((3, EXT_ROWS, sz.tiles * LANES), f32),
         ],
-    )(thickness, wind_rows, near_h, near_w, sides, geo, wave, far_rows, near_q)
+    )(thickness, wind_rows, near_h, near_w, sides, geo, wave, *(() if sz.near_only else (far_rows,)))
     met = meetings(tends)
     near_q = lax.ppermute(near_q, ("lat", "lon"), near)
     from_far = lax.ppermute(far_rows, ("lat", "lon"), far) if sz.near_only else far_rows

time: 21.2 us -> 21.2 us (level)
  no operation moved by 1% of the time
where the time goes in v24:
time: 21.2 us; the launch traced here: 21 us
  starting transfers between devices  10.8 us (51%)
  Pallas kernels  6.96 us (33%)
  local copies, waits for them, and re-layouts  1.32 us (6%)
  waiting for transfers between devices  1.24 us (6%)
  between operations  0.75 us (4%)
    ppermute x6, starting transfers between devices, meetings(): lax.ppermute(shares[k], ('lat', 'lon'), [(b * n_lon + i, b * n_lon + j) f...  8.07 us
    pallas_call x1, Pallas kernels, local(): call(rest_kernel, 'rest', [vmem] * 10 + [anywhere] + [vmem] * n_lon, (sha...  2.07 us
    ppermute x1, starting transfers between devices, local(): lax.ppermute(far_rows, ('lat', 'lon'), far)  1.92 us
    unnamed x18, local copies, waits for them, and re-layouts  1.32 us
    pallas_call x1, Pallas kernels, local(): call(edges_kernel, 'edges', [hbm] * 3, (near_row, far_row, shaped(2 * SID...  1.17 us
    pallas_call x1, Pallas kernels, local(): call(weights_kernel, 'weights', [smem, vmem, vmem, anywhere], (jax.ShapeD...  1.15 us
    pallas_call x1, Pallas kernels, local(): call(filter_kernel, 'filter', [vmem] * 2 + [vmem] * n_lon, [shaped(sz.siz...  0.98 us
    pallas_call x1, Pallas kernels, local(): call(finish_kernel, 'finish', [vmem] * (3 + n_lon), (shaped(*wind_rows.sh...  0.92 us
  transfers between devices with their start and end apart: 10, of which 5 were waited for; matrix products, arithmetic and copies ran while one was open for 4% of the time, Pallas kernels for 26%

profile of v24, /device:TPU:0, one launch (start us, length us, event | category | flops | bytes accessed | tf_op | source)
XLA Modules:
  0.0 21.0 jit_solution(2144674551314447315)
XLA Ops:
  0.6 0.0 copy-start.3
  0.6 0.5 %collective-permute-start.1 = (f32[9,2,2880]{2,1,0:T(2,128)}, f32[9,2,2880]{2,1,0:T(2,128)S(1)}, u32[]{:S(2)}, u32[]{:S(2)}) collective-permute-start(f32[9,2,2880]{2,1,0:T(2,128)} %bitcast.3), channel_id=1, source_target_pairs={{0,4},{1,5},{2,6},{3,7},{4,0},{5,1},{6,2},{7,3},{8,12},{9,13},{10,... | collective-permute-start | bytes 622088 | tf_op jit(solution)/shard_map/ppermute | solution.py:628
  1.2 0.1 collective-permute-start
  1.2 1.2 %edges.1 = (f32[72,128]{1,0:T(8,128)S(1)}, f32[120,128]{1,0:T(8,128)S(1)}, f32[16,128]{1,0:T(8,128)S(1)}) custom-call(f32[9,2880]{1,0:T(8,128)} %h_ref.3, f32[9,2,2880]{2,1,0:T(2,128)} %bitcast.4, bf16[9,3,2880]{2,1,0:T(4,128)(2,1)} %bitcast.7), custom_call_target="tpu_custom_call" | custom-call | tf_op jit(solution)/shard_map/edges/pallas_call | solution.py:603
  2.4 0.4 %collective-permute-done.near_h_ref = f32[9,2880]{1,0:T(8,128)S(1)} collective-permute-done((f32[9,2880]{1,0:T(8,128)}, f32[9,2880]{1,0:T(8,128)S(1)}, u32[]{:S(2)}, u32[]{:S(2)}) %collective-permute-start) | collective-permute-done | bytes 103712 | tf_op jit(solution)/shard_map/ppermute | solution.py:627
  2.9 0.7 %polar.1 = (f32[152,128]{1,0:T(8,128)S(1)}, f32[152,128]{1,0:T(8,128)S(1)}, f32[152,128]{1,0:T(8,128)S(1)}, f32[152,128]{1,0:T(8,128)S(1)}) custom-call(f32[9,2880]{1,0:T(8,128)S(1)} %copy-done.2, f32[9,2,2880]{2,1,0:T(2,128)S(1)} %bitcast.5, f32[9,2880]{1,0:T(8,128)S(1)} %collective-permute-done.near_h_ref, ...), custom_call_target="tpu_custom_call" | custom-call | tf_op jit(solution)/shard_map/polar/pallas_call | solution.py:643
  3.5 3.8 %collective-permute-start.4 = (f32[152,128]{1,0:T(8,128)S(1)}, f32[152,128]{1,0:T(8,128)S(1)}, u32[]{:S(2)}, u32[]{:S(2)}) collective-permute-start(f32[152,128]{1,0:T(8,128)S(1)} %get-tuple-element.27), channel_id=1, source_target_pairs={{0,3},{1,2},{2,1},{3,0},{4,6},{5,7},{6,4},{7,5},{8,11},{9,10},{10,... | collective-permute-start | bytes 233480 | tf_op jit(solution)/shard_map/ppermute | solution.py:638
  7.3 0.5 %collective-permute-start.5 = (f32[152,128]{1,0:T(8,128)S(1)}, f32[152,128]{1,0:T(8,128)S(1)}, u32[]{:S(2)}, u32[]{:S(2)}) collective-permute-start(f32[152,128]{1,0:T(8,128)S(1)} %get-tuple-element.28), channel_id=1, source_target_pairs={{0,1},{1,0},{2,3},{3,2},{4,7},{5,6},{6,5},{7,4},{8,9},{9,8},{10,11... | collective-permute-start | bytes 233480 | tf_op jit(solution)/shard_map/ppermute | solution.py:638
  7.9 0.1 collective-permute-start.6
  8.0 1.9 %collective-permute-start.3 = (f32[120,128]{1,0:T(8,128)S(1)}, f32[120,128]{1,0:T(8,128)S(1)}, u32[]{:S(2)}, u32[]{:S(2)}) collective-permute-start(f32[120,128]{1,0:T(8,128)S(1)} %get-tuple-element.25), channel_id=1, source_target_pairs={{0,2},{1,3},{2,0},{3,1},{4,8},{5,9},{6,10},{7,11},{8,4},{9,5},{10,... | collective-permute-start | bytes 184328 | tf_op jit(solution)/shard_map/ppermute | solution.py:656
  9.9 0.2 collective-permute-start.2
  10.1 0.5 %copy-done.6 = s32[72]{0:T(128)S(1)} copy-done((s32[72]{0:T(128)S(1)}, s32[72]{0:T(128)}, u32[]{:S(2)}) %copy-start.6) | copy-done | bytes 312
  10.6 1.1 %weights.1 = (bf16[1152,96]{1,0:T(8,128)(2,1)S(1)}, f32[3,16,128]{2,1,0:T(8,128)S(1)}) custom-call(s32[72]{0:T(128)S(1)} %copy-done.6, f32[192,96]{1,0:T(8,128)S(1)} %copy-done.5, f32[192,96]{1,0:T(8,128)S(1)} %copy-done.4, f32[152,128]{1,0:T(8,128)S(1)} %get-tuple-element.22.after_ref.refs_0_), custom_call_target="tpu_custom_call" | custom-call | tf_op jit(solution)/shard_map/weights/pallas_call | solution.py:657
  11.7 0.3 %collective-permute-done.5.refs_2_ = f32[152,128]{1,0:T(8,128)S(1)} collective-permute-done((f32[152,128]{1,0:T(8,128)S(1)}, f32[152,128]{1,0:T(8,128)S(1)}, u32[]{:S(2)}, u32[]{:S(2)}) %collective-permute-start.5) | collective-permute-done | bytes 77856 | tf_op jit(solution)/shard_map/ppermute | solution.py:638
  12.1 0.2 %collective-permute-done.6.refs_3_ = f32[152,128]{1,0:T(8,128)S(1)} collective-permute-done((f32[152,128]{1,0:T(8,128)S(1)}, f32[152,128]{1,0:T(8,128)S(1)}, u32[]{:S(2)}, u32[]{:S(2)}) %collective-permute-start.6) | collective-permute-done | bytes 77856 | tf_op jit(solution)/shard_map/ppermute | solution.py:638
  12.3 1.0 %filter.1 = (f32[144,128]{1,0:T(8,128)S(1)}, f32[144,128]{1,0:T(8,128)S(1)}, f32[144,128]{1,0:T(8,128)S(1)}, f32[144,128]{1,0:T(8,128)S(1)}) custom-call(bf16[1152,96]{1,0:T(8,128)(2,1)S(1)} %get-tuple-element.26.weights_ref, f32[8,3,16,128]{3,2,1,0:T(8,128)S(1)} %copy-done.1, f32[152,128]{1,0:T(8,128)S(1)} %get-tuple-element.22.after_ref.refs_0_, ...), custom_call_target="tpu_custom_call" | custom-call | tf_op jit(solution)/shard_map/filter/pallas_call | solution.py:666
  13.3 1.8 %collective-permute-start.7 = (f32[144,128]{1,0:T(8,128)S(1)}, f32[144,128]{1,0:T(8,128)S(1)}, u32[]{:S(2)}, u32[]{:S(2)}) collective-permute-start(f32[144,128]{1,0:T(8,128)S(1)} %get-tuple-element.33), channel_id=1, source_target_pairs={{0,3},{1,2},{2,1},{3,0},{4,6},{5,7},{6,4},{7,5},{8,11},{9,10},{10,... | collective-permute-start | bytes 221192 | tf_op jit(solution)/shard_map/ppermute | solution.py:638
  15.0 0.4 %collective-permute-start.8 = (f32[144,128]{1,0:T(8,128)S(1)}, f32[144,128]{1,0:T(8,128)S(1)}, u32[]{:S(2)}, u32[]{:S(2)}) collective-permute-start(f32[144,128]{1,0:T(8,128)S(1)} %get-tuple-element.34), channel_id=1, source_target_pairs={{0,1},{1,0},{2,3},{3,2},{4,7},{5,6},{6,5},{7,4},{8,9},{9,8},{10,11... | collective-permute-start | bytes 221192 | tf_op jit(solution)/shard_map/ppermute | solution.py:638
  15.4 1.5 %collective-permute-start.9 = (f32[144,128]{1,0:T(8,128)S(1)}, f32[144,128]{1,0:T(8,128)S(1)}, u32[]{:S(2)}, u32[]{:S(2)}) collective-permute-start(f32[144,128]{1,0:T(8,128)S(1)} %pass.1), channel_id=1, source_target_pairs={{0,2},{1,3},{2,0},{3,1},{4,5},{5,4},{6,7},{7,6},{8,10},{9,11},{10,... | collective-permute-start | bytes 221192 | tf_op jit(solution)/shard_map/ppermute | solution.py:638
  16.9 2.1 %rest.1 = (f32[2,9,2880]{2,1,0:T(8,128)S(1)}, f32[9,2880]{1,0:T(8,128)S(1)}, bf16[3,9,2880]{2,1,0:T(8,128)(2,1)S(1)}) custom-call(f32[3,16,128]{2,1,0:T(8,128)S(1)} %get-tuple-element.23.masks_ref, f32[9,2880]{1,0:T(8,128)S(1)} %copy-done.2, f32[9,2,2880]{2,1,0:T(2,128)S(1)} %bitcast.6, bf16[3,9,2880]{2,1,0:T(8,128)(2,1)S(1)} %copy.11.q_ref, ...), custom_call_target="tpu_custom_call" | custom-call | tf_op jit(solution)/shard_map/rest/pallas_call | solution.py:677
  19.0 0.8 %copy.12 = bf16[3,9,2880]{2,0,1:T(4,128)(2,1)} copy(bf16[3,9,2880]{2,1,0:T(8,128)(2,1)S(1)} %get-tuple-element.41) | data formatting | bytes 311040
  19.8 0.1 collective-permute-done.8.refs_2_
  19.9 0.2 collective-permute-done.9.refs_3_
  20.1 0.9 %finish.1 = (f32[9,2,2880]{2,1,0:T(2,128)}, f32[9,2880]{1,0:T(8,128)}) custom-call(f32[3,16,128]{2,1,0:T(8,128)S(1)} %get-tuple-element.23.masks_ref, f32[2,9,2880]{2,1,0:T(8,128)S(1)} %get-tuple-element.31.base_w_ref, f32[9,2880]{1,0:T(8,128)S(1)} %get-tuple-element.32.base_h_ref, f32[144,128]{1,0:T(8,128)S(1)} %get-tuple-element.30.after_ref.refs_0_, ...), custom_call_target="tpu_custom_call" | custom-call | tf_op jit(solution)/shard_map/finish/pallas_call | solution.py:685
  (21 shorter events, 0.1 us)
Async XLA Ops:
  0.6 2.2 %copy-start.3 = (f32[2,24,128]{2,1,0:T(8,128)S(1)}, f32[2,24,128]{2,1,0:T(8,128)}, u32[]{:S(2)}) copy-start(f32[2,24,128]{2,1,0:T(8,128)} %constant.9.clone.wave_ref) | copy-start | bytes 73732
  0.6 2.2 %collective-permute-start.1 = (f32[9,2,2880]{2,1,0:T(2,128)}, f32[9,2,2880]{2,1,0:T(2,128)S(1)}, u32[]{:S(2)}, u32[]{:S(2)}) collective-permute-start(f32[9,2,2880]{2,1,0:T(2,128)} %bitcast.3), channel_id=1, source_target_pairs={{0,4},{1,5},{2,6},{3,7},{4,0},{5,1},{6,2},{7,3},{8,12},{9,13},{10,... | collective-permute-start | bytes 622088 | tf_op jit(solution)/shard_map/ppermute | solution.py:628
  1.2 1.6 %collective-permute-start = (f32[9,2880]{1,0:T(8,128)}, f32[9,2880]{1,0:T(8,128)S(1)}, u32[]{:S(2)}, u32[]{:S(2)}) collective-permute-start(f32[9,2880]{1,0:T(8,128)} %h_ref.3), channel_id=1, source_target_pairs={{0,4},{1,5},{2,6},{3,7},{4,0},{5,1},{6,2},{7,3},{8,12},{9,13},{10,... | collective-permute-start | bytes 311048 | tf_op jit(solution)/shard_map/ppermute | solution.py:627
  1.2 1.6 %copy-start = (f32[2,9,2880]{2,0,1:T(2,128)S(1)}, f32[2,9,2880]{2,0,1:T(2,128)}, u32[]{:S(2)}) copy-start(f32[2,9,2880]{2,0,1:T(2,128)} %param.8) | copy-start | bytes 622084
  1.2 1.6 %copy-start.1 = (f32[8,3,16,128]{3,2,1,0:T(8,128)S(1)}, f32[8,3,16,128]{3,2,1,0:T(8,128)}, u32[]{:S(2)}) copy-start(f32[8,3,16,128]{3,2,1,0:T(8,128)} %constant.8.clone.geo_ref) | copy-start | bytes 589828
  1.2 1.6 %copy-start.2 = (f32[9,2880]{1,0:T(8,128)S(1)}, f32[9,2880]{1,0:T(8,128)}, u32[]{:S(2)}) copy-start(f32[9,2880]{1,0:T(8,128)} %h_ref.3) | copy-start | bytes 311044
  2.8 7.2 %copy-start.4 = (f32[192,96]{1,0:T(8,128)S(1)}, f32[192,96]{1,0:T(8,128)}, u32[]{:S(2)}) copy-start(f32[192,96]{1,0:T(8,128)} %constant.11.clone.inverse_ref) | copy-start | bytes 221188
  2.8 7.2 %copy-start.5 = (f32[192,96]{1,0:T(8,128)S(1)}, f32[192,96]{1,0:T(8,128)}, u32[]{:S(2)}) copy-start(f32[192,96]{1,0:T(8,128)} %constant.10.clone.n_ref) | copy-start | bytes 221188
  3.5 8.2 %collective-permute-start.4 = (f32[152,128]{1,0:T(8,128)S(1)}, f32[152,128]{1,0:T(8,128)S(1)}, u32[]{:S(2)}, u32[]{:S(2)}) collective-permute-start(f32[152,128]{1,0:T(8,128)S(1)} %get-tuple-element.27), channel_id=1, source_target_pairs={{0,3},{1,2},{2,1},{3,0},{4,6},{5,7},{6,4},{7,5},{8,11},{9,10},{10,... | collective-permute-start | bytes 233480 | tf_op jit(solution)/shard_map/ppermute | solution.py:638
  7.3 4.7 %collective-permute-start.5 = (f32[152,128]{1,0:T(8,128)S(1)}, f32[152,128]{1,0:T(8,128)S(1)}, u32[]{:S(2)}, u32[]{:S(2)}) collective-permute-start(f32[152,128]{1,0:T(8,128)S(1)} %get-tuple-element.28), channel_id=1, source_target_pairs={{0,1},{1,0},{2,3},{3,2},{4,7},{5,6},{6,5},{7,4},{8,9},{9,8},{10,11... | collective-permute-start | bytes 233480 | tf_op jit(solution)/shard_map/ppermute | solution.py:638
  7.9 4.4 %collective-permute-start.6 = (f32[152,128]{1,0:T(8,128)S(1)}, f32[152,128]{1,0:T(8,128)S(1)}, u32[]{:S(2)}, u32[]{:S(2)}) collective-permute-start(f32[152,128]{1,0:T(8,128)S(1)} %get-tuple-element.29), channel_id=1, source_target_pairs={{0,2},{1,3},{2,0},{3,1},{4,5},{5,4},{6,7},{7,6},{8,10},{9,11},{10,... | collective-permute-start | bytes 233480 | tf_op jit(solution)/shard_map/ppermute | solution.py:638
  8.0 7.4 %collective-permute-start.3 = (f32[120,128]{1,0:T(8,128)S(1)}, f32[120,128]{1,0:T(8,128)S(1)}, u32[]{:S(2)}, u32[]{:S(2)}) collective-permute-start(f32[120,128]{1,0:T(8,128)S(1)} %get-tuple-element.25), channel_id=1, source_target_pairs={{0,2},{1,3},{2,0},{3,1},{4,8},{5,9},{6,10},{7,11},{8,4},{9,5},{10,... | collective-permute-start | bytes 184328 | tf_op jit(solution)/shard_map/ppermute | solution.py:656
  9.9 0.7 %copy-start.6 = (s32[72]{0:T(128)S(1)}, s32[72]{0:T(128)}, u32[]{:S(2)}) copy-start(s32[72]{0:T(128)} %cut_ref.1) | copy-start | bytes 868
  9.9 5.5 %collective-permute-start.2 = (f32[72,128]{1,0:T(8,128)S(1)}, f32[72,128]{1,0:T(8,128)S(1)}, u32[]{:S(2)}, u32[]{:S(2)}) collective-permute-start(f32[72,128]{1,0:T(8,128)S(1)} %get-tuple-element.24), channel_id=1, source_target_pairs={{0,4},{1,5},{2,6},{3,7},{4,0},{5,1},{6,2},{7,3},{8,12},{9,13},{10,... | collective-permute-start | bytes 110600 | tf_op jit(solution)/shard_map/ppermute | solution.py:655
  13.3 3.7 %copy-start.7 = (bf16[3,9,2880]{2,0,1:T(4,128)(2,1)S(1)}, bf16[3,9,2880]{2,0,1:T(4,128)(2,1)}, u32[]{:S(2)}) copy-start(bf16[3,9,2880]{2,0,1:T(4,128)(2,1)} %param.10) | copy-start | bytes 466564
  13.3 6.5 %collective-permute-start.7 = (f32[144,128]{1,0:T(8,128)S(1)}, f32[144,128]{1,0:T(8,128)S(1)}, u32[]{:S(2)}, u32[]{:S(2)}) collective-permute-start(f32[144,128]{1,0:T(8,128)S(1)} %get-tuple-element.33), channel_id=1, source_target_pairs={{0,3},{1,2},{2,1},{3,0},{4,6},{5,7},{6,4},{7,5},{8,11},{9,10},{10,... | collective-permute-start | bytes 221192 | tf_op jit(solution)/shard_map/ppermute | solution.py:638
  15.0 4.9 %collective-permute-start.8 = (f32[144,128]{1,0:T(8,128)S(1)}, f32[144,128]{1,0:T(8,128)S(1)}, u32[]{:S(2)}, u32[]{:S(2)}) collective-permute-start(f32[144,128]{1,0:T(8,128)S(1)} %get-tuple-element.34), channel_id=1, source_target_pairs={{0,1},{1,0},{2,3},{3,2},{4,7},{5,6},{6,5},{7,4},{8,9},{9,8},{10,11... | collective-permute-start | bytes 221192 | tf_op jit(solution)/shard_map/ppermute | solution.py:638
  15.4 4.7 %collective-permute-start.9 = (f32[144,128]{1,0:T(8,128)S(1)}, f32[144,128]{1,0:T(8,128)S(1)}, u32[]{:S(2)}, u32[]{:S(2)}) collective-permute-start(f32[144,128]{1,0:T(8,128)S(1)} %pass.1), channel_id=1, source_target_pairs={{0,2},{1,3},{2,0},{3,1},{4,5},{5,4},{6,7},{7,6},{8,10},{9,11},{10,... | collective-permute-start | bytes 221192 | tf_op jit(solution)/shard_map/ppermute | solution.py:638

commit v25 on v22

--- a/solution.py
+++ b/solution.py
@@ -455,9 +455,9 @@
 
 
 def sin_pi(y):
-    y = jnp.where(y > 0.5, 1.0 - y, jnp.where(y < -0.5, -1.0 - y, y))
+    y = jnp.maximum(jnp.minimum(y, 1.0 - y), -1.0 - y)
     s = y * y
-    series = [(-1) ** i * math.pi ** (2 * i + 1) / math.factorial(2 * i + 1) for i in range(7)]
+    series = [(-1) ** i * math.pi ** (2 * i + 1) / math.factorial(2 * i + 1) for i in range(6)]
     total = series[-1]
     for factor in reversed(series[:-1]):
         total = total * s + factor

time: 21.2 us -> 21.1 us (level)
  transfers between devices with their start and end apart: 10 -> 10, of which waited for: 5 -> 5; matrix products, arithmetic and copies ran while one was open for 4% -> 4% of each run, Pallas kernels for 26% -> 25%
where the time goes in v25:
time: 21.1 us; the launch traced here: 20.9 us
  starting transfers between devices  10.8 us (51%)
  Pallas kernels  6.88 us (33%)
  local copies, waits for them, and re-layouts  1.32 us (6%)
  waiting for transfers between devices  1.24 us (6%)
  between operations  0.74 us (4%)
    ppermute x6, starting transfers between devices, meetings(): lax.ppermute(shares[k], ('lat', 'lon'), [(b * n_lon + i, b * n_lon + j) f...  8.07 us
    pallas_call x1, Pallas kernels, local(): call(rest_kernel, 'rest', [vmem] * 10 + [anywhere] + [vmem] * n_lon, (sha...  2.07 us
    ppermute x1, starting transfers between devices, local(): lax.ppermute(far_rows, ('lat', 'lon'), far)  1.92 us
    unnamed x18, local copies, waits for them, and re-layouts  1.32 us
    pallas_call x1, Pallas kernels, local(): call(edges_kernel, 'edges', [hbm] * 3, (near_row, far_row, shaped(2 * SID...  1.17 us
    pallas_call x1, Pallas kernels, local(): call(weights_kernel, 'weights', [smem, vmem, vmem, anywhere], (jax.ShapeD...  1.07 us
    pallas_call x1, Pallas kernels, local(): call(filter_kernel, 'filter', [vmem] * 2 + [vmem] * n_lon, [shaped(sz.siz...  0.98 us
    pallas_call x1, Pallas kernels, local(): call(finish_kernel, 'finish', [vmem] * (3 + n_lon), (shaped(*wind_rows.sh...  0.92 us
  transfers between devices with their start and end apart: 10, of which 5 were waited for; matrix products, arithmetic and copies ran while one was open for 4% of the time, Pallas kernels for 25%

profile of v25, /device:TPU:0, one launch (start us, length us, event | category | flops | bytes accessed | tf_op | source)
XLA Modules:
  0.0 20.9 jit_solution(6578935540884688966)
XLA Ops:
  0.6 0.0 copy-start.3
  0.6 0.5 %collective-permute-start.1 = (f32[9,2,2880]{2,1,0:T(2,128)}, f32[9,2,2880]{2,1,0:T(2,128)S(1)}, u32[]{:S(2)}, u32[]{:S(2)}) collective-permute-start(f32[9,2,2880]{2,1,0:T(2,128)} %bitcast.3), channel_id=1, source_target_pairs={{0,4},{1,5},{2,6},{3,7},{4,0},{5,1},{6,2},{7,3},{8,12},{9,13},{10,... | collective-permute-start | bytes 622088 | tf_op jit(solution)/shard_map/ppermute | solution.py:631
  1.2 0.1 collective-permute-start
  1.2 1.2 %edges.1 = (f32[72,128]{1,0:T(8,128)S(1)}, f32[120,128]{1,0:T(8,128)S(1)}, f32[16,128]{1,0:T(8,128)S(1)}) custom-call(f32[9,2880]{1,0:T(8,128)} %h_ref.3, f32[9,2,2880]{2,1,0:T(2,128)} %bitcast.4, bf16[9,3,2880]{2,1,0:T(4,128)(2,1)} %bitcast.7), custom_call_target="tpu_custom_call" | custom-call | tf_op jit(solution)/shard_map/edges/pallas_call | solution.py:606
  2.4 0.4 %collective-permute-done.near_h_ref = f32[9,2880]{1,0:T(8,128)S(1)} collective-permute-done((f32[9,2880]{1,0:T(8,128)}, f32[9,2880]{1,0:T(8,128)S(1)}, u32[]{:S(2)}, u32[]{:S(2)}) %collective-permute-start) | collective-permute-done | bytes 103712 | tf_op jit(solution)/shard_map/ppermute | solution.py:630
  2.9 0.7 %polar.1 = (f32[152,128]{1,0:T(8,128)S(1)}, f32[152,128]{1,0:T(8,128)S(1)}, f32[152,128]{1,0:T(8,128)S(1)}, f32[152,128]{1,0:T(8,128)S(1)}, f32[120,128]{1,0:T(8,128)S(1)}, /*index=5*/f32[72,128]{1,0:T(8,128)S(1)}) custom-call(f32[9,2880]{1,0:T(8,128)S(1)} %copy-done.2, f32[9,2,2880]{2,1,0:T(2,128)S(1)} %bitcast.5, ...), custom_call_target="tpu_custom_call" | custom-call | tf_op jit(solution)/shard_map/polar/pallas_call | solution.py:646
  3.5 3.8 %collective-permute-start.4 = (f32[152,128]{1,0:T(8,128)S(1)}, f32[152,128]{1,0:T(8,128)S(1)}, u32[]{:S(2)}, u32[]{:S(2)}) collective-permute-start(f32[152,128]{1,0:T(8,128)S(1)} %get-tuple-element.31), channel_id=1, source_target_pairs={{0,3},{1,2},{2,1},{3,0},{4,6},{5,7},{6,4},{7,5},{8,11},{9,10},{10,... | collective-permute-start | bytes 233480 | tf_op jit(solution)/shard_map/ppermute | solution.py:641
  7.3 0.5 %collective-permute-start.5 = (f32[152,128]{1,0:T(8,128)S(1)}, f32[152,128]{1,0:T(8,128)S(1)}, u32[]{:S(2)}, u32[]{:S(2)}) collective-permute-start(f32[152,128]{1,0:T(8,128)S(1)} %get-tuple-element.32), channel_id=1, source_target_pairs={{0,1},{1,0},{2,3},{3,2},{4,7},{5,6},{6,5},{7,4},{8,9},{9,8},{10,11... | collective-permute-start | bytes 233480 | tf_op jit(solution)/shard_map/ppermute | solution.py:641
  7.9 0.1 collective-permute-start.6
  8.0 1.9 %collective-permute-start.3 = (f32[120,128]{1,0:T(8,128)S(1)}, f32[120,128]{1,0:T(8,128)S(1)}, u32[]{:S(2)}, u32[]{:S(2)}) collective-permute-start(f32[120,128]{1,0:T(8,128)S(1)} %get-tuple-element.29), channel_id=1, source_target_pairs={{0,2},{1,3},{2,0},{3,1},{4,8},{5,9},{6,10},{7,11},{8,4},{9,5},{10,... | collective-permute-start | bytes 184328 | tf_op jit(solution)/shard_map/ppermute | solution.py:659
  9.9 0.2 collective-permute-start.2
  10.1 0.5 %copy-done.6 = s32[72]{0:T(128)S(1)} copy-done((s32[72]{0:T(128)S(1)}, s32[72]{0:T(128)}, u32[]{:S(2)}) %copy-start.6) | copy-done | bytes 312
  10.6 1.1 %weights.1 = (bf16[1152,96]{1,0:T(8,128)(2,1)S(1)}, f32[3,16,128]{2,1,0:T(8,128)S(1)}) custom-call(s32[72]{0:T(128)S(1)} %copy-done.6, f32[192,96]{1,0:T(8,128)S(1)} %copy-done.5, f32[192,96]{1,0:T(8,128)S(1)} %copy-done.4, f32[152,128]{1,0:T(8,128)S(1)} %get-tuple-element.26.after_ref.refs_0_), custom_call_target="tpu_custom_call" | custom-call | tf_op jit(solution)/shard_map/weights/pallas_call | solution.py:660
  11.6 0.4 %collective-permute-done.5.refs_2_ = f32[152,128]{1,0:T(8,128)S(1)} collective-permute-done((f32[152,128]{1,0:T(8,128)S(1)}, f32[152,128]{1,0:T(8,128)S(1)}, u32[]{:S(2)}, u32[]{:S(2)}) %collective-permute-start.5) | collective-permute-done | bytes 77856 | tf_op jit(solution)/shard_map/ppermute | solution.py:641
  12.1 0.2 %collective-permute-done.6.refs_3_ = f32[152,128]{1,0:T(8,128)S(1)} collective-permute-done((f32[152,128]{1,0:T(8,128)S(1)}, f32[152,128]{1,0:T(8,128)S(1)}, u32[]{:S(2)}, u32[]{:S(2)}) %collective-permute-start.6) | collective-permute-done | bytes 77856 | tf_op jit(solution)/shard_map/ppermute | solution.py:641
  12.3 1.0 %filter.1 = (f32[144,128]{1,0:T(8,128)S(1)}, f32[144,128]{1,0:T(8,128)S(1)}, f32[144,128]{1,0:T(8,128)S(1)}, f32[144,128]{1,0:T(8,128)S(1)}) custom-call(bf16[1152,96]{1,0:T(8,128)(2,1)S(1)} %get-tuple-element.30.weights_ref, f32[8,3,16,128]{3,2,1,0:T(8,128)S(1)} %copy-done.1, f32[152,128]{1,0:T(8,128)S(1)} %get-tuple-element.26.after_ref.refs_0_, ...), custom_call_target="tpu_custom_call" | custom-call | tf_op jit(solution)/shard_map/filter/pallas_call | solution.py:669
  13.3 1.8 %collective-permute-start.7 = (f32[144,128]{1,0:T(8,128)S(1)}, f32[144,128]{1,0:T(8,128)S(1)}, u32[]{:S(2)}, u32[]{:S(2)}) collective-permute-start(f32[144,128]{1,0:T(8,128)S(1)} %get-tuple-element.37), channel_id=1, source_target_pairs={{0,3},{1,2},{2,1},{3,0},{4,6},{5,7},{6,4},{7,5},{8,11},{9,10},{10,... | collective-permute-start | bytes 221192 | tf_op jit(solution)/shard_map/ppermute | solution.py:641
  15.1 0.4 %collective-permute-start.8 = (f32[144,128]{1,0:T(8,128)S(1)}, f32[144,128]{1,0:T(8,128)S(1)}, u32[]{:S(2)}, u32[]{:S(2)}) collective-permute-start(f32[144,128]{1,0:T(8,128)S(1)} %get-tuple-element.38), channel_id=1, source_target_pairs={{0,1},{1,0},{2,3},{3,2},{4,7},{5,6},{6,5},{7,4},{8,9},{9,8},{10,11... | collective-permute-start | bytes 221192 | tf_op jit(solution)/shard_map/ppermute | solution.py:641
  15.4 1.5 %collective-permute-start.9 = (f32[144,128]{1,0:T(8,128)S(1)}, f32[144,128]{1,0:T(8,128)S(1)}, u32[]{:S(2)}, u32[]{:S(2)}) collective-permute-start(f32[144,128]{1,0:T(8,128)S(1)} %pass.1), channel_id=1, source_target_pairs={{0,2},{1,3},{2,0},{3,1},{4,5},{5,4},{6,7},{7,6},{8,10},{9,11},{10,... | collective-permute-start | bytes 221192 | tf_op jit(solution)/shard_map/ppermute | solution.py:641
  16.9 2.1 %rest.1 = (f32[2,9,2880]{2,1,0:T(8,128)S(1)}, f32[9,2880]{1,0:T(8,128)S(1)}, bf16[3,9,2880]{2,1,0:T(8,128)(2,1)S(1)}) custom-call(f32[3,16,128]{2,1,0:T(8,128)S(1)} %get-tuple-element.27.masks_ref, f32[9,2880]{1,0:T(8,128)S(1)} %copy-done.2, f32[9,2,2880]{2,1,0:T(2,128)S(1)} %bitcast.6, bf16[3,9,2880]{2,1,0:T(8,128)(2,1)S(1)} %copy.11.q_ref, ...), custom_call_target="tpu_custom_call" | custom-call | tf_op jit(solution)/shard_map/rest/pallas_call | solution.py:680
  19.0 0.8 %copy.12 = bf16[3,9,2880]{2,0,1:T(4,128)(2,1)} copy(bf16[3,9,2880]{2,1,0:T(8,128)(2,1)S(1)} %get-tuple-element.45) | data formatting | bytes 311040
  19.8 0.1 collective-permute-done.8.refs_2_
  19.9 0.2 collective-permute-done.9.refs_3_
  20.0 0.9 %finish.1 = (f32[9,2,2880]{2,1,0:T(2,128)}, f32[9,2880]{1,0:T(8,128)}) custom-call(f32[3,16,128]{2,1,0:T(8,128)S(1)} %get-tuple-element.27.masks_ref, f32[2,9,2880]{2,1,0:T(8,128)S(1)} %get-tuple-element.35.base_w_ref, f32[9,2880]{1,0:T(8,128)S(1)} %get-tuple-element.36.base_h_ref, f32[144,128]{1,0:T(8,128)S(1)} %get-tuple-element.34.after_ref.refs_0_, ...), custom_call_target="tpu_custom_call" | custom-call | tf_op jit(solution)/shard_map/finish/pallas_call | solution.py:688
  (21 shorter events, 0.1 us)
Async XLA Ops:
  0.6 2.2 %copy-start.3 = (f32[2,24,128]{2,1,0:T(8,128)S(1)}, f32[2,24,128]{2,1,0:T(8,128)}, u32[]{:S(2)}) copy-start(f32[2,24,128]{2,1,0:T(8,128)} %constant.9.clone.wave_ref) | copy-start | bytes 73732
  0.6 2.2 %collective-permute-start.1 = (f32[9,2,2880]{2,1,0:T(2,128)}, f32[9,2,2880]{2,1,0:T(2,128)S(1)}, u32[]{:S(2)}, u32[]{:S(2)}) collective-permute-start(f32[9,2,2880]{2,1,0:T(2,128)} %bitcast.3), channel_id=1, source_target_pairs={{0,4},{1,5},{2,6},{3,7},{4,0},{5,1},{6,2},{7,3},{8,12},{9,13},{10,... | collective-permute-start | bytes 622088 | tf_op jit(solution)/shard_map/ppermute | solution.py:631
  1.2 1.6 %collective-permute-start = (f32[9,2880]{1,0:T(8,128)}, f32[9,2880]{1,0:T(8,128)S(1)}, u32[]{:S(2)}, u32[]{:S(2)}) collective-permute-start(f32[9,2880]{1,0:T(8,128)} %h_ref.3), channel_id=1, source_target_pairs={{0,4},{1,5},{2,6},{3,7},{4,0},{5,1},{6,2},{7,3},{8,12},{9,13},{10,... | collective-permute-start | bytes 311048 | tf_op jit(solution)/shard_map/ppermute | solution.py:630
  1.2 1.6 %copy-start = (f32[2,9,2880]{2,0,1:T(2,128)S(1)}, f32[2,9,2880]{2,0,1:T(2,128)}, u32[]{:S(2)}) copy-start(f32[2,9,2880]{2,0,1:T(2,128)} %param.8) | copy-start | bytes 622084
  1.2 1.6 %copy-start.1 = (f32[8,3,16,128]{3,2,1,0:T(8,128)S(1)}, f32[8,3,16,128]{3,2,1,0:T(8,128)}, u32[]{:S(2)}) copy-start(f32[8,3,16,128]{3,2,1,0:T(8,128)} %constant.8.clone.geo_ref) | copy-start | bytes 589828
  1.2 1.6 %copy-start.2 = (f32[9,2880]{1,0:T(8,128)S(1)}, f32[9,2880]{1,0:T(8,128)}, u32[]{:S(2)}) copy-start(f32[9,2880]{1,0:T(8,128)} %h_ref.3) | copy-start | bytes 311044
  2.8 7.2 %copy-start.4 = (f32[192,96]{1,0:T(8,128)S(1)}, f32[192,96]{1,0:T(8,128)}, u32[]{:S(2)}) copy-start(f32[192,96]{1,0:T(8,128)} %constant.11.clone.inverse_ref) | copy-start | bytes 221188
  2.8 7.2 %copy-start.5 = (f32[192,96]{1,0:T(8,128)S(1)}, f32[192,96]{1,0:T(8,128)}, u32[]{:S(2)}) copy-start(f32[192,96]{1,0:T(8,128)} %constant.10.clone.n_ref) | copy-start | bytes 221188
  3.5 8.1 %collective-permute-start.4 = (f32[152,128]{1,0:T(8,128)S(1)}, f32[152,128]{1,0:T(8,128)S(1)}, u32[]{:S(2)}, u32[]{:S(2)}) collective-permute-start(f32[152,128]{1,0:T(8,128)S(1)} %get-tuple-element.31), channel_id=1, source_target_pairs={{0,3},{1,2},{2,1},{3,0},{4,6},{5,7},{6,4},{7,5},{8,11},{9,10},{10,... | collective-permute-start | bytes 233480 | tf_op jit(solution)/shard_map/ppermute | solution.py:641
  7.3 4.7 %collective-permute-start.5 = (f32[152,128]{1,0:T(8,128)S(1)}, f32[152,128]{1,0:T(8,128)S(1)}, u32[]{:S(2)}, u32[]{:S(2)}) collective-permute-start(f32[152,128]{1,0:T(8,128)S(1)} %get-tuple-element.32), channel_id=1, source_target_pairs={{0,1},{1,0},{2,3},{3,2},{4,7},{5,6},{6,5},{7,4},{8,9},{9,8},{10,11... | collective-permute-start | bytes 233480 | tf_op jit(solution)/shard_map/ppermute | solution.py:641
  7.9 4.4 %collective-permute-start.6 = (f32[152,128]{1,0:T(8,128)S(1)}, f32[152,128]{1,0:T(8,128)S(1)}, u32[]{:S(2)}, u32[]{:S(2)}) collective-permute-start(f32[152,128]{1,0:T(8,128)S(1)} %get-tuple-element.33), channel_id=1, source_target_pairs={{0,2},{1,3},{2,0},{3,1},{4,5},{5,4},{6,7},{7,6},{8,10},{9,11},{10,... | collective-permute-start | bytes 233480 | tf_op jit(solution)/shard_map/ppermute | solution.py:641
  8.0 7.5 %collective-permute-start.3 = (f32[120,128]{1,0:T(8,128)S(1)}, f32[120,128]{1,0:T(8,128)S(1)}, u32[]{:S(2)}, u32[]{:S(2)}) collective-permute-start(f32[120,128]{1,0:T(8,128)S(1)} %get-tuple-element.29), channel_id=1, source_target_pairs={{0,2},{1,3},{2,0},{3,1},{4,8},{5,9},{6,10},{7,11},{8,4},{9,5},{10,... | collective-permute-start | bytes 184328 | tf_op jit(solution)/shard_map/ppermute | solution.py:659
  9.9 0.7 %copy-start.6 = (s32[72]{0:T(128)S(1)}, s32[72]{0:T(128)}, u32[]{:S(2)}) copy-start(s32[72]{0:T(128)} %cut_ref.1) | copy-start | bytes 868
  9.9 5.5 %collective-permute-start.2 = (f32[72,128]{1,0:T(8,128)S(1)}, f32[72,128]{1,0:T(8,128)S(1)}, u32[]{:S(2)}, u32[]{:S(2)}) collective-permute-start(f32[72,128]{1,0:T(8,128)S(1)} %get-tuple-element.28), channel_id=1, source_target_pairs={{0,4},{1,5},{2,6},{3,7},{4,0},{5,1},{6,2},{7,3},{8,12},{9,13},{10,... | collective-permute-start | bytes 110600 | tf_op jit(solution)/shard_map/ppermute | solution.py:658
  13.3 3.7 %copy-start.7 = (bf16[3,9,2880]{2,0,1:T(4,128)(2,1)S(1)}, bf16[3,9,2880]{2,0,1:T(4,128)(2,1)}, u32[]{:S(2)}) copy-start(bf16[3,9,2880]{2,0,1:T(4,128)(2,1)} %param.10) | copy-start | bytes 466564
  13.3 6.5 %collective-permute-start.7 = (f32[144,128]{1,0:T(8,128)S(1)}, f32[144,128]{1,0:T(8,128)S(1)}, u32[]{:S(2)}, u32[]{:S(2)}) collective-permute-start(f32[144,128]{1,0:T(8,128)S(1)} %get-tuple-element.37), channel_id=1, source_target_pairs={{0,3},{1,2},{2,1},{3,0},{4,6},{5,7},{6,4},{7,5},{8,11},{9,10},{10,... | collective-permute-start | bytes 221192 | tf_op jit(solution)/shard_map/ppermute | solution.py:641
  15.1 4.8 %collective-permute-start.8 = (f32[144,128]{1,0:T(8,128)S(1)}, f32[144,128]{1,0:T(8,128)S(1)}, u32[]{:S(2)}, u32[]{:S(2)}) collective-permute-start(f32[144,128]{1,0:T(8,128)S(1)} %get-tuple-element.38), channel_id=1, source_target_pairs={{0,1},{1,0},{2,3},{3,2},{4,7},{5,6},{6,5},{7,4},{8,9},{9,8},{10,11... | collective-permute-start | bytes 221192 | tf_op jit(solution)/shard_map/ppermute | solution.py:641
  15.4 4.6 %collective-permute-start.9 = (f32[144,128]{1,0:T(8,128)S(1)}, f32[144,128]{1,0:T(8,128)S(1)}, u32[]{:S(2)}, u32[]{:S(2)}) collective-permute-start(f32[144,128]{1,0:T(8,128)S(1)} %pass.1), channel_id=1, source_target_pairs={{0,2},{1,3},{2,0},{3,1},{4,5},{5,4},{6,7},{7,6},{8,10},{9,11},{10,... | collective-permute-start | bytes 221192 | tf_op jit(solution)/shard_map/ppermute | solution.py:641

commit v26 on v23

--- a/solution.py
+++ b/solution.py
@@ -55,9 +55,7 @@
 
     def turns(self, odd, back):
         middle, last = list(range(1, self.n_lon - 1)), self.n_lon - 1
-        if odd and not back:
-            return [0, middle[-1], last] + middle[-2::-1]
-        return [0, last] + (middle[::-1] if odd else middle)
+        return [0, middle[-1], last] + middle[-2::-1] if odd != back else [0, last] + middle
 
     def partner(self, k, back=False):
         odd = lax.rem(lax.axis_index("lat"), 2) == 1
@@ -457,9 +455,9 @@
 
 
 def sin_pi(y):
-    y = jnp.maximum(jnp.minimum(y, 1.0 - y), -1.0 - y)
+    y = jnp.where(y > 0.5, 1.0 - y, jnp.where(y < -0.5, -1.0 - y, y))
     s = y * y
-    series = [(-1) ** i * math.pi ** (2 * i + 1) / math.factorial(2 * i + 1) for i in range(6)]
+    series = [(-1) ** i * math.pi ** (2 * i + 1) / math.factorial(2 * i + 1) for i in range(7)]
     total = series[-1]
     for factor in reversed(series[:-1]):
         total = total * s + factor

time: 21.1 us -> 21.8 us (1.033)
  waiting for transfers between devices: 1.28 us -> 1.87 us
    ppermute x6, waiting for transfers between devices: 0.89 us -> 1.49 us  [meetings(): lax.ppermute(shares[k], ('lat', 'lon'), [(b * n_lon + i, b * n_lon + j) f...]
where the time goes in v26:
time: 21.8 us; the launch traced here: 21.6 us
  starting transfers between devices  10.8 us (50%)
  Pallas kernels  6.96 us (32%)
  waiting for transfers between devices  1.87 us (9%)
  local copies, waits for them, and re-layouts  1.32 us (6%)
  between operations  0.74 us (3%)
    ppermute x6, starting transfers between devices, meetings(): lax.ppermute(shares[k], ('lat', 'lon'), [(b * n_lon + i, b * n_lon + j) f...  8.07 us
    pallas_call x1, Pallas kernels, local(): call(rest_kernel, 'rest', [vmem] * 10 + [anywhere] + [vmem] * n_lon, (sha...  2.07 us
    ppermute x1, starting transfers between devices, local(): lax.ppermute(far_rows, ('lat', 'lon'), far)  1.92 us
    ppermute x6, waiting for transfers between devices, meetings(): lax.ppermute(shares[k], ('lat', 'lon'), [(b * n_lon + i, b * n_lon + j) f...  1.49 us
    unnamed x18, local copies, waits for them, and re-layouts  1.32 us
    pallas_call x1, Pallas kernels, local(): call(edges_kernel, 'edges', [hbm] * 3, (near_row, far_row, shaped(2 * SID...  1.17 us
    pallas_call x1, Pallas kernels, local(): call(weights_kernel, 'weights', [smem, vmem, vmem, anywhere], (jax.ShapeD...  1.15 us
    pallas_call x1, Pallas kernels, local(): call(filter_kernel, 'filter', [vmem] * 2 + [vmem] * n_lon, [shaped(sz.siz...  0.98 us
  transfers between devices with their start and end apart: 10, of which 4 were waited for; matrix products, arithmetic and copies ran while one was open for 4% of the time, Pallas kernels for 25%

profile of v26, /device:TPU:0, one launch (start us, length us, event | category | flops | bytes accessed | tf_op | source)
XLA Modules:
  0.0 21.6 jit_solution(16088335004304746006)
XLA Ops:
  0.6 0.0 copy-start.3
  0.6 0.5 %collective-permute-start.1 = (f32[9,2,2880]{2,1,0:T(2,128)}, f32[9,2,2880]{2,1,0:T(2,128)S(1)}, u32[]{:S(2)}, u32[]{:S(2)}) collective-permute-start(f32[9,2,2880]{2,1,0:T(2,128)} %bitcast.3), channel_id=1, source_target_pairs={{0,4},{1,5},{2,6},{3,7},{4,0},{5,1},{6,2},{7,3},{8,12},{9,13},{10,... | collective-permute-start | bytes 622088 | tf_op jit(solution)/shard_map/ppermute | solution.py:631
  1.2 0.1 collective-permute-start
  1.2 1.2 %edges.1 = (f32[72,128]{1,0:T(8,128)S(1)}, f32[120,128]{1,0:T(8,128)S(1)}, f32[16,128]{1,0:T(8,128)S(1)}) custom-call(f32[9,2880]{1,0:T(8,128)} %h_ref.3, f32[9,2,2880]{2,1,0:T(2,128)} %bitcast.4, bf16[9,3,2880]{2,1,0:T(4,128)(2,1)} %bitcast.7), custom_call_target="tpu_custom_call" | custom-call | tf_op jit(solution)/shard_map/edges/pallas_call | solution.py:606
  2.4 0.4 %collective-permute-done.near_h_ref = f32[9,2880]{1,0:T(8,128)S(1)} collective-permute-done((f32[9,2880]{1,0:T(8,128)}, f32[9,2880]{1,0:T(8,128)S(1)}, u32[]{:S(2)}, u32[]{:S(2)}) %collective-permute-start) | collective-permute-done | bytes 103712 | tf_op jit(solution)/shard_map/ppermute | solution.py:630
  2.8 0.0 copy-start.5
  2.9 0.7 %polar.1 = (f32[152,128]{1,0:T(8,128)S(1)}, f32[152,128]{1,0:T(8,128)S(1)}, f32[152,128]{1,0:T(8,128)S(1)}, f32[152,128]{1,0:T(8,128)S(1)}, f32[120,128]{1,0:T(8,128)S(1)}, /*index=5*/f32[72,128]{1,0:T(8,128)S(1)}) custom-call(f32[9,2880]{1,0:T(8,128)S(1)} %copy-done.2, f32[9,2,2880]{2,1,0:T(2,128)S(1)} %bitcast.5, ...), custom_call_target="tpu_custom_call" | custom-call | tf_op jit(solution)/shard_map/polar/pallas_call | solution.py:645
  3.5 3.8 %collective-permute-start.4 = (f32[152,128]{1,0:T(8,128)S(1)}, f32[152,128]{1,0:T(8,128)S(1)}, u32[]{:S(2)}, u32[]{:S(2)}) collective-permute-start(f32[152,128]{1,0:T(8,128)S(1)} %get-tuple-element.31), channel_id=1, source_target_pairs={{0,3},{1,2},{2,1},{3,0},{4,6},{5,7},{6,4},{7,5},{8,11},{9,10},{10,... | collective-permute-start | bytes 233480 | tf_op jit(solution)/shard_map/ppermute | solution.py:640
  7.3 0.5 %collective-permute-start.5 = (f32[152,128]{1,0:T(8,128)S(1)}, f32[152,128]{1,0:T(8,128)S(1)}, u32[]{:S(2)}, u32[]{:S(2)}) collective-permute-start(f32[152,128]{1,0:T(8,128)S(1)} %get-tuple-element.32), channel_id=1, source_target_pairs={{0,1},{1,0},{2,3},{3,2},{4,7},{5,6},{6,5},{7,4},{8,9},{9,8},{10,11... | collective-permute-start | bytes 233480 | tf_op jit(solution)/shard_map/ppermute | solution.py:640
  7.9 0.1 collective-permute-start.6
  8.0 1.9 %collective-permute-start.3 = (f32[120,128]{1,0:T(8,128)S(1)}, f32[120,128]{1,0:T(8,128)S(1)}, u32[]{:S(2)}, u32[]{:S(2)}) collective-permute-start(f32[120,128]{1,0:T(8,128)S(1)} %get-tuple-element.29), channel_id=1, source_target_pairs={{0,2},{1,3},{2,0},{3,1},{4,8},{5,9},{6,10},{7,11},{8,4},{9,5},{10,... | collective-permute-start | bytes 184328 | tf_op jit(solution)/shard_map/ppermute | solution.py:658
  9.9 0.2 collective-permute-start.2
  10.1 0.5 %copy-done.6 = s32[72]{0:T(128)S(1)} copy-done((s32[72]{0:T(128)S(1)}, s32[72]{0:T(128)}, u32[]{:S(2)}) %copy-start.6) | copy-done | bytes 312
  10.6 1.1 %weights.1 = (bf16[1152,96]{1,0:T(8,128)(2,1)S(1)}, f32[3,16,128]{2,1,0:T(8,128)S(1)}) custom-call(s32[72]{0:T(128)S(1)} %copy-done.6, f32[192,96]{1,0:T(8,128)S(1)} %copy-done.5, f32[192,96]{1,0:T(8,128)S(1)} %copy-done.4, f32[152,128]{1,0:T(8,128)S(1)} %get-tuple-element.26.after_ref.refs_0_), custom_call_target="tpu_custom_call" | custom-call | tf_op jit(solution)/shard_map/weights/pallas_call | solution.py:659
  11.7 0.3 %collective-permute-done.5.refs_2_ = f32[152,128]{1,0:T(8,128)S(1)} collective-permute-done((f32[152,128]{1,0:T(8,128)S(1)}, f32[152,128]{1,0:T(8,128)S(1)}, u32[]{:S(2)}, u32[]{:S(2)}) %collective-permute-start.5) | collective-permute-done | bytes 77856 | tf_op jit(solution)/shard_map/ppermute | solution.py:640
  12.1 0.2 collective-permute-done.6.refs_3_
  12.3 1.0 %filter.1 = (f32[144,128]{1,0:T(8,128)S(1)}, f32[144,128]{1,0:T(8,128)S(1)}, f32[144,128]{1,0:T(8,128)S(1)}, f32[144,128]{1,0:T(8,128)S(1)}) custom-call(bf16[1152,96]{1,0:T(8,128)(2,1)S(1)} %get-tuple-element.30.weights_ref, f32[8,3,16,128]{3,2,1,0:T(8,128)S(1)} %copy-done.1, f32[152,128]{1,0:T(8,128)S(1)} %get-tuple-element.26.after_ref.refs_0_, ...), custom_call_target="tpu_custom_call" | custom-call | tf_op jit(solution)/shard_map/filter/pallas_call | solution.py:668
  13.3 0.7 %collective-permute-start.7 = (f32[144,128]{1,0:T(8,128)S(1)}, f32[144,128]{1,0:T(8,128)S(1)}, u32[]{:S(2)}, u32[]{:S(2)}) collective-permute-start(f32[144,128]{1,0:T(8,128)S(1)} %get-tuple-element.37), channel_id=1, source_target_pairs={{0,2},{1,3},{2,0},{3,1},{4,7},{5,6},{6,5},{7,4},{8,10},{9,11},{10,... | collective-permute-start | bytes 221192 | tf_op jit(solution)/shard_map/ppermute | solution.py:640
  14.0 2.3 %collective-permute-start.8 = (f32[144,128]{1,0:T(8,128)S(1)}, f32[144,128]{1,0:T(8,128)S(1)}, u32[]{:S(2)}, u32[]{:S(2)}) collective-permute-start(f32[144,128]{1,0:T(8,128)S(1)} %get-tuple-element.38), channel_id=1, source_target_pairs={{0,3},{1,2},{2,1},{3,0},{4,5},{5,4},{6,7},{7,6},{8,11},{9,10},{10,... | collective-permute-start | bytes 221192 | tf_op jit(solution)/shard_map/ppermute | solution.py:640
  16.3 0.6 %collective-permute-start.9 = (f32[144,128]{1,0:T(8,128)S(1)}, f32[144,128]{1,0:T(8,128)S(1)}, u32[]{:S(2)}, u32[]{:S(2)}) collective-permute-start(f32[144,128]{1,0:T(8,128)S(1)} %pass.1), channel_id=1, source_target_pairs={{0,1},{1,0},{2,3},{3,2},{4,6},{5,7},{6,4},{7,5},{8,9},{9,8},{10,11... | collective-permute-start | bytes 221192 | tf_op jit(solution)/shard_map/ppermute | solution.py:640
  16.9 2.1 %rest.1 = (f32[2,9,2880]{2,1,0:T(8,128)S(1)}, f32[9,2880]{1,0:T(8,128)S(1)}, bf16[3,9,2880]{2,1,0:T(8,128)(2,1)S(1)}) custom-call(f32[3,16,128]{2,1,0:T(8,128)S(1)} %get-tuple-element.27.masks_ref, f32[9,2880]{1,0:T(8,128)S(1)} %copy-done.2, f32[9,2,2880]{2,1,0:T(2,128)S(1)} %bitcast.6, bf16[3,9,2880]{2,1,0:T(8,128)(2,1)S(1)} %copy.11.q_ref, ...), custom_call_target="tpu_custom_call" | custom-call | tf_op jit(solution)/shard_map/rest/pallas_call | solution.py:679
  19.0 0.8 %copy.12 = bf16[3,9,2880]{2,0,1:T(4,128)(2,1)} copy(bf16[3,9,2880]{2,1,0:T(8,128)(2,1)S(1)} %get-tuple-element.45) | data formatting | bytes 311040
  19.8 0.9 %collective-permute-done.9.refs_3_ = f32[144,128]{1,0:T(8,128)S(1)} collective-permute-done((f32[144,128]{1,0:T(8,128)S(1)}, f32[144,128]{1,0:T(8,128)S(1)}, u32[]{:S(2)}, u32[]{:S(2)}) %collective-permute-start.9) | collective-permute-done | bytes 73760 | tf_op jit(solution)/shard_map/ppermute | solution.py:640
  20.7 0.9 %finish.1 = (f32[9,2,2880]{2,1,0:T(2,128)}, f32[9,2880]{1,0:T(8,128)}) custom-call(f32[3,16,128]{2,1,0:T(8,128)S(1)} %get-tuple-element.27.masks_ref, f32[2,9,2880]{2,1,0:T(8,128)S(1)} %get-tuple-element.35.base_w_ref, f32[9,2880]{1,0:T(8,128)S(1)} %get-tuple-element.36.base_h_ref, f32[144,128]{1,0:T(8,128)S(1)} %get-tuple-element.34.after_ref.refs_0_, ...), custom_call_target="tpu_custom_call" | custom-call | tf_op jit(solution)/shard_map/finish/pallas_call | solution.py:687
  (21 shorter events, 0.1 us)
Async XLA Ops:
  0.6 2.2 %copy-start.3 = (f32[2,24,128]{2,1,0:T(8,128)S(1)}, f32[2,24,128]{2,1,0:T(8,128)}, u32[]{:S(2)}) copy-start(f32[2,24,128]{2,1,0:T(8,128)} %constant.9.clone.wave_ref) | copy-start | bytes 73732
  0.6 2.2 %collective-permute-start.1 = (f32[9,2,2880]{2,1,0:T(2,128)}, f32[9,2,2880]{2,1,0:T(2,128)S(1)}, u32[]{:S(2)}, u32[]{:S(2)}) collective-permute-start(f32[9,2,2880]{2,1,0:T(2,128)} %bitcast.3), channel_id=1, source_target_pairs={{0,4},{1,5},{2,6},{3,7},{4,0},{5,1},{6,2},{7,3},{8,12},{9,13},{10,... | collective-permute-start | bytes 622088 | tf_op jit(solution)/shard_map/ppermute | solution.py:631
  1.2 1.6 %collective-permute-start = (f32[9,2880]{1,0:T(8,128)}, f32[9,2880]{1,0:T(8,128)S(1)}, u32[]{:S(2)}, u32[]{:S(2)}) collective-permute-start(f32[9,2880]{1,0:T(8,128)} %h_ref.3), channel_id=1, source_target_pairs={{0,4},{1,5},{2,6},{3,7},{4,0},{5,1},{6,2},{7,3},{8,12},{9,13},{10,... | collective-permute-start | bytes 311048 | tf_op jit(solution)/shard_map/ppermute | solution.py:630
  1.2 1.6 %copy-start = (f32[2,9,2880]{2,0,1:T(2,128)S(1)}, f32[2,9,2880]{2,0,1:T(2,128)}, u32[]{:S(2)}) copy-start(f32[2,9,2880]{2,0,1:T(2,128)} %param.8) | copy-start | bytes 622084
  1.2 1.6 %copy-start.1 = (f32[8,3,16,128]{3,2,1,0:T(8,128)S(1)}, f32[8,3,16,128]{3,2,1,0:T(8,128)}, u32[]{:S(2)}) copy-start(f32[8,3,16,128]{3,2,1,0:T(8,128)} %constant.8.clone.geo_ref) | copy-start | bytes 589828
  1.2 1.6 %copy-start.2 = (f32[9,2880]{1,0:T(8,128)S(1)}, f32[9,2880]{1,0:T(8,128)}, u32[]{:S(2)}) copy-start(f32[9,2880]{1,0:T(8,128)} %h_ref.3) | copy-start | bytes 311044
  2.8 7.2 %copy-start.4 = (f32[192,96]{1,0:T(8,128)S(1)}, f32[192,96]{1,0:T(8,128)}, u32[]{:S(2)}) copy-start(f32[192,96]{1,0:T(8,128)} %constant.11.clone.inverse_ref) | copy-start | bytes 221188
  2.8 7.2 %copy-start.5 = (f32[192,96]{1,0:T(8,128)S(1)}, f32[192,96]{1,0:T(8,128)}, u32[]{:S(2)}) copy-start(f32[192,96]{1,0:T(8,128)} %constant.10.clone.n_ref) | copy-start | bytes 221188
  3.5 8.2 %collective-permute-start.4 = (f32[152,128]{1,0:T(8,128)S(1)}, f32[152,128]{1,0:T(8,128)S(1)}, u32[]{:S(2)}, u32[]{:S(2)}) collective-permute-start(f32[152,128]{1,0:T(8,128)S(1)} %get-tuple-element.31), channel_id=1, source_target_pairs={{0,3},{1,2},{2,1},{3,0},{4,6},{5,7},{6,4},{7,5},{8,11},{9,10},{10,... | collective-permute-start | bytes 233480 | tf_op jit(solution)/shard_map/ppermute | solution.py:640
  7.3 4.7 %collective-permute-start.5 = (f32[152,128]{1,0:T(8,128)S(1)}, f32[152,128]{1,0:T(8,128)S(1)}, u32[]{:S(2)}, u32[]{:S(2)}) collective-permute-start(f32[152,128]{1,0:T(8,128)S(1)} %get-tuple-element.32), channel_id=1, source_target_pairs={{0,1},{1,0},{2,3},{3,2},{4,7},{5,6},{6,5},{7,4},{8,9},{9,8},{10,11... | collective-permute-start | bytes 233480 | tf_op jit(solution)/shard_map/ppermute | solution.py:640
  7.9 4.4 %collective-permute-start.6 = (f32[152,128]{1,0:T(8,128)S(1)}, f32[152,128]{1,0:T(8,128)S(1)}, u32[]{:S(2)}, u32[]{:S(2)}) collective-permute-start(f32[152,128]{1,0:T(8,128)S(1)} %get-tuple-element.33), channel_id=1, source_target_pairs={{0,2},{1,3},{2,0},{3,1},{4,5},{5,4},{6,7},{7,6},{8,10},{9,11},{10,... | collective-permute-start | bytes 233480 | tf_op jit(solution)/shard_map/ppermute | solution.py:640
  8.0 8.3 %collective-permute-start.3 = (f32[120,128]{1,0:T(8,128)S(1)}, f32[120,128]{1,0:T(8,128)S(1)}, u32[]{:S(2)}, u32[]{:S(2)}) collective-permute-start(f32[120,128]{1,0:T(8,128)S(1)} %get-tuple-element.29), channel_id=1, source_target_pairs={{0,2},{1,3},{2,0},{3,1},{4,8},{5,9},{6,10},{7,11},{8,4},{9,5},{10,... | collective-permute-start | bytes 184328 | tf_op jit(solution)/shard_map/ppermute | solution.py:658
  9.9 0.7 %copy-start.6 = (s32[72]{0:T(128)S(1)}, s32[72]{0:T(128)}, u32[]{:S(2)}) copy-start(s32[72]{0:T(128)} %cut_ref.1) | copy-start | bytes 868
  9.9 6.4 %collective-permute-start.2 = (f32[72,128]{1,0:T(8,128)S(1)}, f32[72,128]{1,0:T(8,128)S(1)}, u32[]{:S(2)}, u32[]{:S(2)}) collective-permute-start(f32[72,128]{1,0:T(8,128)S(1)} %get-tuple-element.28), channel_id=1, source_target_pairs={{0,4},{1,5},{2,6},{3,7},{4,0},{5,1},{6,2},{7,3},{8,12},{9,13},{10,... | collective-permute-start | bytes 110600 | tf_op jit(solution)/shard_map/ppermute | solution.py:657
  13.3 3.6 %copy-start.7 = (bf16[3,9,2880]{2,0,1:T(4,128)(2,1)S(1)}, bf16[3,9,2880]{2,0,1:T(4,128)(2,1)}, u32[]{:S(2)}) copy-start(bf16[3,9,2880]{2,0,1:T(4,128)(2,1)} %param.10) | copy-start | bytes 466564
  13.3 6.5 %collective-permute-start.7 = (f32[144,128]{1,0:T(8,128)S(1)}, f32[144,128]{1,0:T(8,128)S(1)}, u32[]{:S(2)}, u32[]{:S(2)}) collective-permute-start(f32[144,128]{1,0:T(8,128)S(1)} %get-tuple-element.37), channel_id=1, source_target_pairs={{0,2},{1,3},{2,0},{3,1},{4,7},{5,6},{6,5},{7,4},{8,10},{9,11},{10,... | collective-permute-start | bytes 221192 | tf_op jit(solution)/shard_map/ppermute | solution.py:640
  14.0 5.8 %collective-permute-start.8 = (f32[144,128]{1,0:T(8,128)S(1)}, f32[144,128]{1,0:T(8,128)S(1)}, u32[]{:S(2)}, u32[]{:S(2)}) collective-permute-start(f32[144,128]{1,0:T(8,128)S(1)} %get-tuple-element.38), channel_id=1, source_target_pairs={{0,3},{1,2},{2,1},{3,0},{4,5},{5,4},{6,7},{7,6},{8,11},{9,10},{10,... | collective-permute-start | bytes 221192 | tf_op jit(solution)/shard_map/ppermute | solution.py:640
  16.3 4.4 %collective-permute-start.9 = (f32[144,128]{1,0:T(8,128)S(1)}, f32[144,128]{1,0:T(8,128)S(1)}, u32[]{:S(2)}, u32[]{:S(2)}) collective-permute-start(f32[144,128]{1,0:T(8,128)S(1)} %pass.1), channel_id=1, source_target_pairs={{0,1},{1,0},{2,3},{3,2},{4,6},{5,7},{6,4},{7,5},{8,9},{9,8},{10,11... | collective-permute-start | bytes 221192 | tf_op jit(solution)/shard_map/ppermute | solution.py:640
